TPU v7x, 32 devices: a whole 2x2x4 slice. The times are simulated.
32 devices in a mesh: chan: 8 (over z, y), seg: 4 (over x, core).
Axes of the slice: x: 2, y: 2, z: 4, core: 2. Of those that a mesh axis runs over, the one named last changes fastest.
Arguments:
- recording: float32 [1024, 16384], P('chan', 'seg'), may hold values from -60 to 60
- filter_taps: float32 [64], replicated, may hold values from -0.75 to 0.75
- offsets: int32 [4], replicated, may hold values from -64 to 64, as said below
- loop_partner: int32 [8, 3], replicated, may hold values from 0 to 7, as said below
- loop_count: int32 [8], replicated, may hold values from 0 to 3, as said below
Outputs:
- near_corr: float32 [1024, 4, 256], P('chan', 'seg')
- loop_corr: float32 [8, 3, 128, 256], P('chan', None, 'seg')
Inputs may be any that keep to these rules, and one draw needn't show every extreme that they name: 4 distinct nonzero offsets; both -64 and 64 are among them. `loop_partner`: slots at or beyond a block's loop_count are ignored. `loop_count`: some block uses all 3 slots.
All inputs are finite; a program needn't handle non-finite values.
Results may differ from a plain program's by a relative error of at most 0.004.
Values may be sent and summed in bfloat16 or wider, within the bound.
No kernel may reach another device: no remote copies, remote signals or barrier semaphores. Data moves between devices by JAX's collectives and lax.ppermute only.
A program may use at most 64 MiB of HBM per device.

v0:
```python
import functools
import math

import jax
import jax.numpy as jnp
import numpy as np
from jax import lax
from jax.experimental import pallas as pl
from jax.experimental.pallas import tpu as pltpu
from jax.sharding import PartitionSpec as P

NFFT = 1024
LAGS = 256
TAPS = 64
DECIM = 4
HALFBAND = 10
BINS = 512
WATER = 0.2

LANES = 128
GROUP = 16
GROUPS = BINS // GROUP
OUT_BLOCK = 128
HALF = NFFT // 2

F32 = jnp.float32
BF16 = jnp.bfloat16


def bin_order():
    return np.concatenate([np.arange(0, BINS, 2), np.arange(1, BINS, 2)])


def split_np(table):
    high = table.astype(jnp.bfloat16)
    low = (table - high.astype(np.float64)).astype(jnp.bfloat16)
    return high, low


def forward_table():
    bins = bin_order().reshape(GROUPS, 1, GROUP)
    sample = np.arange(HALF)
    angles = (bins[..., None] * sample % NFFT) * (2.0 * np.pi / NFFT)
    rows = np.concatenate([np.cos(angles), -np.sin(angles)], axis=1)
    rows = rows * (bins != 0)[..., None]
    return rows.reshape(2, BINS, HALF)


def inverse_table(total_segs, order):
    lag = np.arange(LAGS) - LAGS // 2
    bins, part = order
    angles = (bins[None, :] * lag[:, None] % NFFT) * (2.0 * np.pi / NFFT)
    weights = np.where(bins == 0, 1.0, 2.0) / math.sqrt(2.0 * BINS * total_segs)
    return np.where(part[None, :] == 1, -np.sin(angles), np.cos(angles)) * weights[None, :]


def band_table():
    bins = bin_order()
    return (np.abs(bins[:, None] - bins[None, :]) <= HALFBAND).astype(jnp.bfloat16)


def split(value):
    high = value.astype(BF16)
    return high, (value - high.astype(F32)).astype(BF16)


def mm(a, b):
    return jnp.dot(a, b, preferred_element_type=F32)


def mm_nt(a, b):
    return lax.dot_general(a, b, (((1,), (1,)), ((), ())), preferred_element_type=F32)


def tap_rows(base_ref, rows):
    width = base_ref.shape[1]
    spread = jnp.broadcast_to(base_ref[0:1, :], (rows, width))
    return pltpu.roll(spread, 0, 1, stride=DECIM, stride_axis=0)


def spectrum_kernel(rec_ref, base_ref, tab_ref, spec_ref, mean_ref):
    length = rec_ref.shape[1]
    total = rec_ref[:, 0:LANES]
    for t in range(1, length // LANES):
        total = total + rec_ref[:, t * LANES : (t + 1) * LANES]
    mean = jnp.sum(total, axis=1, keepdims=True) * (1.0 / length)
    mean_ref[...] = jnp.broadcast_to(mean, mean_ref.shape)
    taps_high, taps_low = split(tap_rows(base_ref, OUT_BLOCK))
    taps_both = jnp.concatenate([taps_high, taps_low], axis=0)
    step = OUT_BLOCK * DECIM
    pieces = []
    for j in range(length // step):
        skip = LANES if j == 0 else 0
        window = rec_ref[:, j * step - LANES + skip : (j + 1) * step] - mean
        high, low = split(window)
        both = mm_nt(taps_both[:, skip:], high)
        pieces.append(both[:OUT_BLOCK] + both[OUT_BLOCK:] + mm_nt(taps_high[:, skip:], low))
    decimated = jnp.concatenate(pieces, axis=0)
    first, second = decimated[:HALF], decimated[HALF:]
    for parity, folded in enumerate((first + second, first - second)):
        high, low = split(folded)
        wide = mm(tab_ref[0, parity], jnp.concatenate([high, low], axis=1))
        rows = wide[:, :LANES] + wide[:, LANES:] + mm(tab_ref[1, parity], high)
        spec_ref[parity * BINS : (parity + 1) * BINS, :] = rows


def whiten_kernel(spec_ref, rim_ref, mean_ref, base_ref, edge_ref, band_ref, white_ref):
    head = tap_rows(base_ref, GROUP)[:, :LANES]
    rim = rim_ref[...] - mean_ref[...]
    history = lax.dot_general(
        head, rim, (((1,), (1,)), ((), ())),
        precision=lax.Precision.HIGHEST, preferred_element_type=F32,
    )
    high, low = split(history)
    stacked = jnp.concatenate([high, high, low], axis=0)
    spec = spec_ref[...] + mm(edge_ref[:, : 3 * GROUP], stacked)
    parted = spec.reshape(GROUPS, 2, GROUP, LANES)
    real, imag = parted[:, 0], parted[:, 1]
    amplitude = jnp.sqrt(real * real + imag * imag).reshape(BINS, LANES)
    high, low = split(amplitude)
    wide = mm(band_ref[...], jnp.concatenate([high, low], axis=1))
    row = lax.broadcasted_iota(jnp.int32, (BINS, LANES), 0)
    bins = jnp.where(row < BINS // 2, 2 * row, 2 * row - (BINS - 1))
    count = jnp.minimum(bins, HALFBAND) + jnp.minimum(BINS - 1 - bins, HALFBAND) + 1
    smoothed = (wide[:, :LANES] + wide[:, LANES:]) / count.astype(F32)
    level = jnp.sum(amplitude, axis=0, keepdims=True) * (1.0 / BINS)
    scale = 1.0 / (smoothed + WATER * level + 1e-06)
    white = parted * scale.reshape(GROUPS, 1, GROUP, LANES)
    white_ref[...] = white.astype(BF16)


def cross_kernel(offs_ref, partner_ref, count_ref, white_ref, out_ref, turned_ref):
    blocks, segs, _, bins, _ = white_ref.shape
    owners = out_ref.shape[1]
    noff = offs_ref.shape[0]
    slots = partner_ref.shape[1]
    near_tiles = noff // owners
    share = LANES // owners
    rows = segs * 2 * bins
    lane_in = lax.broadcasted_iota(jnp.int32, (LANES, LANES), 0)
    lane_out = lax.broadcasted_iota(jnp.int32, (LANES, LANES), 1)
    flip = (lane_in + lane_out == LANES - 1).astype(BF16)
    turned = mm(white_ref[...].reshape(blocks * rows, LANES), flip)
    turned_ref[...] = turned.reshape(turned_ref.shape)
    lane = lax.broadcasted_iota(jnp.int32, (rows, LANES), 1)
    pair_lane = lane[: 2 * bins]

    def products(own, far):
        real = jnp.sum(own[:, 0] * far[:, 0] + own[:, 1] * far[:, 1], axis=0)
        imag = jnp.sum(own[:, 1] * far[:, 0] - own[:, 0] * far[:, 1], axis=0)
        return real, imag

    def one_block(b, carry):
        flat = white_ref[b].astype(F32).reshape(rows, LANES)
        own = flat.reshape(segs, 2, bins, LANES)
        for o in range(noff):
            offset = offs_ref[o]
            ahead = offset > 0
            other = jnp.where(ahead, b + 1, b - 1)
            other = jnp.where(other < 0, blocks - 1, jnp.where(other >= blocks, 0, other))
            turn = jnp.where(ahead, offset, LANES + offset)
            mine = (lane >= turn) == ahead
            beside = white_ref[other].astype(F32).reshape(rows, LANES)
            far = pltpu.roll(jnp.where(mine, flat, beside), LANES - turn, 1)
            real, imag = products(own, far.reshape(own.shape))
            out_ref[b, o // near_tiles, o % near_tiles, 0] = real.astype(BF16)
            out_ref[b, o // near_tiles, o % near_tiles, 1] = imag.astype(BF16)
        live_count = count_ref[b]
        pairs = []
        for k in range(slots):
            partner = jnp.clip(partner_ref[b, k], 0, blocks - 1)
            live = (k < live_count).astype(F32)
            real, imag = products(own * live, turned_ref[partner])
            pairs.append(jnp.concatenate([real, imag], axis=0))
        for q in range(owners):
            packed = jnp.zeros_like(pairs[0])
            for k in range(slots):
                shift = (share * (k - q)) % LANES
                moved = pltpu.roll(pairs[k], shift, 1) if shift else pairs[k]
                inside = (pair_lane >= share * k) & (pair_lane < share * (k + 1))
                packed = jnp.where(inside, moved, packed)
            packed = packed.reshape(2, bins, LANES).astype(BF16)
            out_ref[b, q, near_tiles] = packed
        return carry

    lax.fori_loop(0, blocks, one_block, 0)


def lag_kernel(spec_ref, inv_ref, near_ref, loop_ref):
    tiles = spec_ref.shape[1]
    depth = inv_ref.shape[1]
    columns = [spec_ref[:, t].reshape(depth, LANES) for t in range(tiles)]
    both = mm(inv_ref[...], jnp.concatenate(columns, axis=1))
    lags = both[:LAGS] + both[LAGS:]
    for t in range(tiles - 1):
        near_ref[:, t, :] = lags[:, t * LANES : (t + 1) * LANES].T
    loop = lags[:, (tiles - 1) * LANES :].T
    loop_ref[...] = loop[: loop_ref.shape[0]]


def vmem(count):
    return [pl.BlockSpec(memory_space=pltpu.VMEM)] * count


def smem(count):
    return [pl.BlockSpec(memory_space=pltpu.SMEM)] * count


PARAMS = pltpu.CompilerParams(vmem_limit_bytes=48 * 1024 * 1024)


def cross_plain(white, offsets, loop_partner, loop_count, owners):
    blocks, segs, _, bins, chans = white.shape
    slots = loop_partner.shape[1]
    wide = white.astype(F32)
    flat = jnp.moveaxis(wide, 0, 3).reshape(segs, 2, bins, blocks * chans)

    def products(own, far):
        real = jnp.sum(own[:, 0] * far[:, 0] + own[:, 1] * far[:, 1], axis=0)
        imag = jnp.sum(own[:, 1] * far[:, 0] - own[:, 0] * far[:, 1], axis=0)
        return jnp.stack([real, imag])

    near = [products(flat, jnp.roll(flat, -offsets[o], axis=3)) for o in range(offsets.shape[0])]
    near = jnp.stack(near).reshape(owners, -1, 2, bins, blocks, chans)
    near = jnp.moveaxis(near, 4, 0)
    loops = []
    for k in range(slots):
        far = jnp.flip(wide[loop_partner[:, k]], axis=4)
        live = (k < loop_count).astype(F32)[:, None, None]
        pair = products(jnp.moveaxis(wide, 0, 2), jnp.moveaxis(far, 0, 2)) * live[None]
        loops.append(pair.reshape(2, blocks, bins, owners, chans // owners))
    loop = jnp.stack(loops)
    loop = jnp.transpose(loop, (2, 4, 1, 3, 0, 5))
    loop = loop.reshape(blocks, owners, 1, 2, bins, slots * (chans // owners))
    spare = chans - loop.shape[-1]
    loop = jnp.pad(loop, ((0, 0),) * 5 + ((0, spare),))
    return jnp.concatenate([near, loop], axis=2).astype(BF16)


def body(recording, filter_taps, offsets, loop_partner, loop_count):
    chan_count = lax.axis_size("chan")
    seg_count = lax.axis_size("seg")
    devices = chan_count * seg_count
    bins = BINS // devices
    chans, length = recording.shape
    noff, slots = offsets.shape[0], loop_partner.shape[1]
    share = chans // seg_count
    tiles = noff // seg_count + 1
    assert length == NFFT * DECIM and chans == LANES
    assert slots * share <= LANES and noff % seg_count == 0

    route = [(i, i + 1) for i in range(seg_count - 1)]
    rim = lax.ppermute(recording[:, length - LANES :], "seg", route)

    width = LANES + OUT_BLOCK * DECIM
    start = LANES + DECIM - TAPS
    base = jnp.pad(filter_taps[::-1], (start, width - start - TAPS))
    base = jnp.broadcast_to(base[None, :], (8, width))
    forward = forward_table()
    table = np.stack(split_np(forward))
    spec, mean = pl.pallas_call(
        spectrum_kernel,
        out_shape=[
            jax.ShapeDtypeStruct((2 * BINS, LANES), F32),
            jax.ShapeDtypeStruct((LANES, LANES), F32),
        ],
        in_specs=vmem(3),
        out_specs=vmem(2),
        compiler_params=PARAMS,
        cost_estimate=pl.CostEstimate(
            flops=1_000_000_000, bytes_accessed=5_000_000, transcendentals=0
        ),
        name="filter_and_transform",
    )(recording, base, table)

    first = forward.reshape(2 * BINS, HALF)[:, :GROUP]
    high, low = split_np(first)
    edge = np.concatenate([high, low, high], axis=1)
    edge = np.pad(edge.astype(np.float32), ((0, 0), (0, LANES - 3 * GROUP))).astype(jnp.bfloat16)
    white = pl.pallas_call(
        whiten_kernel,
        out_shape=jax.ShapeDtypeStruct((GROUPS, 2, GROUP, LANES), BF16),
        in_specs=vmem(6),
        out_specs=pl.BlockSpec(memory_space=pltpu.VMEM),
        compiler_params=PARAMS,
        name="whiten",
    )(spec, rim, mean, base, edge, band_table())

    if bins != GROUP:
        white = jnp.moveaxis(white, 1, 0).reshape(2, devices, bins, LANES)
        white = jnp.moveaxis(white, 0, 1)
    moved = lax.all_to_all(white, ("chan", "seg"), 0, 0, tiled=True)
    moved = moved.reshape(chan_count, seg_count, 2, bins, LANES)
    if bins % GROUP == 0:
        crossed = pl.pallas_call(
            cross_kernel,
            out_shape=jax.ShapeDtypeStruct(
                (chan_count, seg_count, tiles, 2, bins, LANES), BF16
            ),
            in_specs=smem(3) + vmem(1),
            out_specs=pl.BlockSpec(memory_space=pltpu.VMEM),
            scratch_shapes=[pltpu.VMEM((chan_count, seg_count, 2, bins, LANES), F32)],
            compiler_params=PARAMS,
            name="cross_spectra",
        )(offsets, loop_partner, loop_count, moved)
    else:
        crossed = cross_plain(moved, offsets, loop_partner, loop_count, seg_count)
    crossed = crossed.reshape(devices, tiles, 2, bins, LANES)
    summed = lax.all_to_all(crossed, ("chan", "seg"), 0, 0, tiled=True)

    if bins % GROUP:
        summed = jnp.transpose(summed, (1, 2, 0, 3, 4)).reshape(1, tiles, 2, BINS, LANES)
    sources, rows = summed.shape[0], summed.shape[3]
    order = np.broadcast_to(bin_order().reshape(sources, 1, rows), (sources, 2, rows))
    part = np.broadcast_to(np.arange(2).reshape(1, 2, 1), order.shape)
    inverse = inverse_table(seg_count, (order.reshape(-1), part.reshape(-1)))
    inverse = np.concatenate(split_np(inverse), axis=0)
    near, loop = pl.pallas_call(
        lag_kernel,
        out_shape=[
            jax.ShapeDtypeStruct((chans, tiles - 1, LAGS), F32),
            jax.ShapeDtypeStruct((slots * share, LAGS), F32),
        ],
        in_specs=vmem(2),
        out_specs=vmem(2),
        compiler_params=PARAMS,
        name="lags",
    )(summed, inverse)
    return near, loop.reshape(1, slots, share, LAGS)


def solution(mesh):
    in_specs = (P("chan", "seg"), P(), P(), P(), P())
    out_specs = (P("chan", "seg", None), P("chan", None, "seg", None))
    return jax.shard_map(body, mesh=mesh, in_specs=in_specs, out_specs=out_specs, check_vma=False)
```

profile of v0, /device:TPU:0, one launch (start us, length us, event | category | flops | bytes accessed | tf_op | source)
XLA Modules:
  0.0 50.3 jit_solution(16825123607825892116)
XLA Ops:
  0.6 0.8 %slice.3 = f32[128,128]{1,0:T(8,128)S(1)} slice(f32[128,4096]{1,0:T(8,128)} %rec_ref.1), slice={[0:128], [3968:4096]} | slice | bytes 131072 | tf_op jit(solution)/shard_map/slice | solution.py:253
  1.5 2.3 %collective-permute-start = (f32[128,128]{1,0:T(8,128)S(1)}, f32[128,128]{1,0:T(8,128)S(1)}, u32[]{:S(2)}, u32[]{:S(2)}) collective-permute-start(f32[128,128]{1,0:T(8,128)S(1)} %slice.3), channel_id=1, source_target_pairs={{0,1},{1,2},{2,3},{4,5},{5,6},{6,7},{8,9},{9,10},{10,11},{12,13},{... | collective-permute-start | bytes 196616 | tf_op jit(solution)/shard_map/ppermute | solution.py:253
  3.8 0.7 %rev.3 = f32[64]{0:T(128)S(1)} reverse(f32[64]{0:T(128)} %param.10), dimensions={0} | reverse | bytes 512 | tf_op jit(solution)/shard_map/rev | solution.py:257
  4.6 0.1 pad.4
  4.7 0.0 copy-start
  4.7 1.6 %copy-done = f32[128,4096]{1,0:T(8,128)S(1)} copy-done((f32[128,4096]{1,0:T(8,128)S(1)}, f32[128,4096]{1,0:T(8,128)}, u32[]{:S(2)}) %copy-start) | copy-done | bytes 2097176
  6.3 0.0 copy-start.1
  6.3 1.6 %copy-done.1 = bf16[2,2,512,512]{3,2,1,0:T(8,128)(2,1)S(1)} copy-done((bf16[2,2,512,512]{3,2,1,0:T(8,128)(2,1)S(1)}, bf16[2,2,512,512]{3,2,1,0:T(8,128)(2,1)}, u32[]{:S(2)}) %copy-start.1) | copy-done | bytes 2097176
  7.8 0.0 copy-start.3
  7.8 0.0 copy-start.4
  7.9 2.0 %filter_and_transform.1 = (f32[1024,128]{1,0:T(8,128)S(1)}, f32[128,128]{1,0:T(8,128)S(1)}) custom-call(f32[128,4096]{1,0:T(8,128)S(1)} %copy-done, f32[8,640]{1,0:T(8,128)S(1)} %broadcast_in_dim.2.base_ref, bf16[2,2,512,512]{3,2,1,0:T(8,128)(2,1)S(1)} %copy-done.1), custom_call_target="tpu_custom_call" | custom-call | flops 1000000000 | bytes 5000000 | tf_op jit(solution)/shard_map/filter_and_transform/pallas_call | solution.py:261
  9.9 0.0 copy-start.7
  9.9 0.0 copy-start.5
  9.9 0.0 copy-start.6
  9.9 0.0 copy-start.2
  9.9 0.0 collective-permute-done.rim_ref
  9.9 0.0 copy-done.3
  9.9 0.0 copy-done.4
  10.0 1.7 %whiten.1 = bf16[32,2,16,128]{3,2,1,0:T(8,128)(2,1)} custom-call(f32[1024,128]{1,0:T(8,128)S(1)} %get-tuple-element.6.spec_ref, f32[128,128]{1,0:T(8,128)S(1)} %collective-permute-done.rim_ref, f32[128,128]{1,0:T(8,128)S(1)} %get-tuple-element.7.mean_ref, f32[8,640]{1,0:T(8,128)S(1)} %broadcast_in_dim.2.base_ref, bf16[1024,128]{1,0:T(8,128)(2,1)S(1)} %copy-done.4, ...), custom_call_target="tpu_custom_call" | custom-call | tf_op jit(solution)/shard_map/whiten/pallas_call | solution.py:280
  11.6 7.1 %all-to-all-start = ((bf16[32,2,16,128]{3,2,1,0:T(8,128)(2,1)}), bf16[32,2,16,128]{3,2,1,0:T(8,128)(2,1)S(1)}, u32[]{:S(2)}, u32[]{:S(2)}) async-start(bf16[32,2,16,128]{3,2,1,0:T(8,128)(2,1)} %whiten.1), calls=%async_computation | async-start | bytes 524288 | tf_op jit(solution)/shard_map/all_to_all | solution.py:292
  18.8 0.0 copy-done.7
  18.8 0.1 copy.11.partner_ref
  18.9 10.5 %all-to-all-done = bf16[32,2,16,128]{3,2,1,0:T(8,128)(2,1)S(1)} async-done(((bf16[32,2,16,128]{3,2,1,0:T(8,128)(2,1)}), bf16[32,2,16,128]{3,2,1,0:T(8,128)(2,1)S(1)}, u32[]{:S(2)}, u32[]{:S(2)}) %all-to-all-start) | async-done | bytes 262176 | tf_op jit(solution)/shard_map/all_to_all | solution.py:292
  29.4 0.0 copy-done.5
  29.4 0.0 copy-done.6
  29.4 2.0 %cross_spectra.1 = bf16[8,4,2,2,16,128]{5,4,3,2,1,0:T(8,128)(2,1)S(1)} custom-call(s32[4]{0:T(128)S(1)} %copy-done.5, s32[8,3]{1,0:T(8,128)S(1)} %copy.11.partner_ref, s32[8]{0:T(128)S(1)} %copy-done.6, bf16[8,4,2,16,128]{4,3,2,1,0:T(8,128)(2,1)S(1)} %bitcast.4), custom_call_target="tpu_custom_call" | custom-call | tf_op jit(solution)/shard_map/cross_spectra/pallas_call | solution.py:295
  31.3 17.8 %all_to_all.10.spec_ref = bf16[32,2,2,16,128]{4,3,2,1,0:T(8,128)(2,1)S(1)} all-to-all(bf16[32,2,2,16,128]{4,3,2,1,0:T(8,128)(2,1)S(1)} %bitcast.3), channel_id=1, replica_groups=mesh['chan'=8,'seg'=4] {'chan','seg'}, dimensions={0} | all-to-all | bytes 1048576 | tf_op jit(solution)/shard_map/all_to_all | solution.py:309
  49.1 0.0 copy-done.2
  49.1 1.2 %lags.1 = (f32[128,1,256]{2,1,0:T(1,128)}, f32[96,256]{1,0:T(8,128)}) custom-call(bf16[32,2,2,16,128]{4,3,2,1,0:T(8,128)(2,1)S(1)} %all_to_all.10.spec_ref, bf16[512,1024]{1,0:T(8,128)(2,1)S(1)} %copy-done.2), custom_call_target="tpu_custom_call" | custom-call | tf_op jit(solution)/shard_map/lags/pallas_call | solution.py:318
  (1 shorter events, 0.0 us)
Async XLA Ops:
  1.5 8.4 %collective-permute-start = (f32[128,128]{1,0:T(8,128)S(1)}, f32[128,128]{1,0:T(8,128)S(1)}, u32[]{:S(2)}, u32[]{:S(2)}) collective-permute-start(f32[128,128]{1,0:T(8,128)S(1)} %slice.3), channel_id=1, source_target_pairs={{0,1},{1,2},{2,3},{4,5},{5,6},{6,7},{8,9},{9,10},{10,11},{12,13},{... | collective-permute-start | bytes 196616 | tf_op jit(solution)/shard_map/ppermute | solution.py:253
  4.7 1.6 %copy-start = (f32[128,4096]{1,0:T(8,128)S(1)}, f32[128,4096]{1,0:T(8,128)}, u32[]{:S(2)}) copy-start(f32[128,4096]{1,0:T(8,128)} %rec_ref.1) | copy-start | bytes 6291460
  6.3 1.6 %copy-start.1 = (bf16[2,2,512,512]{3,2,1,0:T(8,128)(2,1)S(1)}, bf16[2,2,512,512]{3,2,1,0:T(8,128)(2,1)}, u32[]{:S(2)}) copy-start(bf16[2,2,512,512]{3,2,1,0:T(8,128)(2,1)} %constant.11.clone.tab_ref) | copy-start | bytes 6291460
  7.8 2.1 %copy-start.3 = (bf16[512,512]{1,0:T(8,128)(2,1)S(1)}, bf16[512,512]{1,0:T(8,128)(2,1)}, u32[]{:S(2)}) copy-start(bf16[512,512]{1,0:T(8,128)(2,1)} %constant.13.clone.band_ref) | copy-start | bytes 1572868
  7.8 2.1 %copy-start.4 = (bf16[1024,128]{1,0:T(8,128)(2,1)S(1)}, bf16[1024,128]{1,0:T(8,128)(2,1)}, u32[]{:S(2)}) copy-start(bf16[1024,128]{1,0:T(8,128)(2,1)} %constant.12.clone.edge_ref) | copy-start | bytes 786436
  9.9 8.9 %copy-start.7 = (s32[8,3]{0,1:T(4,128)S(1)}, s32[8,3]{0,1:T(4,128)}, u32[]{:S(2)}) copy-start(s32[8,3]{0,1:T(4,128)} %param.12) | copy-start | bytes 292
  9.9 19.5 %copy-start.5 = (s32[4]{0:T(128)S(1)}, s32[4]{0:T(128)}, u32[]{:S(2)}) copy-start(s32[4]{0:T(128)} %offs_ref.1) | copy-start | bytes 52
  9.9 19.5 %copy-start.6 = (s32[8]{0:T(128)S(1)}, s32[8]{0:T(128)}, u32[]{:S(2)}) copy-start(s32[8]{0:T(128)} %count_ref.1) | copy-start | bytes 100
  9.9 39.2 %copy-start.2 = (bf16[512,1024]{1,0:T(8,128)(2,1)S(1)}, bf16[512,1024]{1,0:T(8,128)(2,1)}, u32[]{:S(2)}) copy-start(bf16[512,1024]{1,0:T(8,128)(2,1)} %constant.14.clone.inv_ref) | copy-start | bytes 3145732
  11.6 17.7 %all-to-all-start = ((bf16[32,2,16,128]{3,2,1,0:T(8,128)(2,1)}), bf16[32,2,16,128]{3,2,1,0:T(8,128)(2,1)S(1)}, u32[]{:S(2)}, u32[]{:S(2)}) async-start(bf16[32,2,16,128]{3,2,1,0:T(8,128)(2,1)} %whiten.1), calls=%async_computation | async-start | bytes 524288 | tf_op jit(solution)/shard_map/all_to_all | solution.py:292
where the time goes:
time: 50.6 us; the launch traced here: 50.3 us
  blocking collectives  17.8 us (35%)
  waiting for transfers between devices  10.5 us (21%)
  starting transfers between devices  9.48 us (19%)
  Pallas kernels  6.86 us (14%)
  local copies, waits for them, and re-layouts  4.97 us (10%)
  between operations  0.73 us (1%)
    all_to_all x1, blocking collectives, body(): summed = lax.all_to_all(crossed, ('chan', 'seg'), 0, 0, tiled=True)  17.8 us
    all_to_all x1, waiting for transfers between devices, body(): moved = lax.all_to_all(white, ('chan', 'seg'), 0, 0, tiled=True)  10.5 us
    all_to_all x1, starting transfers between devices, body(): moved = lax.all_to_all(white, ('chan', 'seg'), 0, 0, tiled=True)  7.13 us
    unnamed x17, local copies, waits for them, and re-layouts  3.3 us
    ppermute x1, starting transfers between devices, body(): rim = lax.ppermute(recording[:, length - LANES:], 'seg', route)  2.35 us
    pallas_call x1, Pallas kernels, body(): pl.pallas_call(spectrum_kernel, out_shape=[jax.ShapeDtypeStruct((2 * BINS...  2.02 us
    pallas_call x1, Pallas kernels, body(): pl.pallas_call(cross_kernel, out_shape=jax.ShapeDtypeStruct((chan_count,...  1.96 us
    pallas_call x1, Pallas kernels, body(): pl.pallas_call(whiten_kernel, out_shape=jax.ShapeDtypeStruct((GROUPS, 2,...  1.68 us
  transfers between devices with their start and end apart: 2, of which 1 were waited for; matrix products, arithmetic and copies ran while one was open for 2% of the time, Pallas kernels for 4%

commit v1 on v0

--- a/solution.py
+++ b/solution.py
@@ -72,31 +72,50 @@
     return lax.dot_general(a, b, (((1,), (1,)), ((), ())), preferred_element_type=F32)
 
 
-def tap_rows(base_ref, rows):
-    width = base_ref.shape[1]
-    spread = jnp.broadcast_to(base_ref[0:1, :], (rows, width))
+def tap_rows(taps_ref, rows):
+    width = LANES + OUT_BLOCK * DECIM
+    tap = lax.broadcasted_iota(jnp.int32, (TAPS, width), 0)
+    column = lax.broadcasted_iota(jnp.int32, (TAPS, width), 1)
+    placed = jnp.where(column == LANES + DECIM - 1 - tap, taps_ref[...], 0.0)
+    spread = jnp.broadcast_to(jnp.sum(placed, axis=0, keepdims=True), (rows, width))
     return pltpu.roll(spread, 0, 1, stride=DECIM, stride_axis=0)
 
 
-def spectrum_kernel(rec_ref, base_ref, tab_ref, spec_ref, mean_ref):
+def spectrum_kernel(rec_hbm, taps_ref, tab_hbm, spec_ref, mean_ref, rec_ref, tab_ref, sems):
     length = rec_ref.shape[1]
-    total = rec_ref[:, 0:LANES]
-    for t in range(1, length // LANES):
-        total = total + rec_ref[:, t * LANES : (t + 1) * LANES]
-    mean = jnp.sum(total, axis=1, keepdims=True) * (1.0 / length)
-    mean_ref[...] = jnp.broadcast_to(mean, mean_ref.shape)
-    taps_high, taps_low = split(tap_rows(base_ref, OUT_BLOCK))
+    step = OUT_BLOCK * DECIM
+    blocks = length // step
+    copies = []
+    for j in range(blocks):
+        part = pl.ds(j * step, step)
+        copies.append(
+            pltpu.make_async_copy(rec_hbm.at[:, part], rec_ref.at[:, part], sems.at[j])
+        )
+    for t in range(4):
+        place = (t // 2, t % 2)
+        copies.append(
+            pltpu.make_async_copy(tab_hbm.at[place], tab_ref.at[place], sems.at[blocks + t])
+        )
+    for copy in copies:
+        copy.start()
+    taps_high, taps_low = split(tap_rows(taps_ref, OUT_BLOCK))
     taps_both = jnp.concatenate([taps_high, taps_low], axis=0)
-    step = OUT_BLOCK * DECIM
     pieces = []
-    for j in range(length // step):
+    for j in range(blocks):
+        copies[j].wait()
         skip = LANES if j == 0 else 0
-        window = rec_ref[:, j * step - LANES + skip : (j + 1) * step] - mean
-        high, low = split(window)
+        window = rec_ref[:, j * step - LANES + skip : (j + 1) * step]
+        if j == 0:
+            mean = jnp.sum(window, axis=1, keepdims=True) * (1.0 / step)
+        high, low = split(window - mean)
         both = mm_nt(taps_both[:, skip:], high)
         pieces.append(both[:OUT_BLOCK] + both[OUT_BLOCK:] + mm_nt(taps_high[:, skip:], low))
+    mean_ref[...] = jnp.broadcast_to(mean, mean_ref.shape)
     decimated = jnp.concatenate(pieces, axis=0)
+    decimated = decimated - jnp.sum(decimated, axis=0, keepdims=True) * (1.0 / NFFT)
     first, second = decimated[:HALF], decimated[HALF:]
+    for copy in copies[blocks:]:
+        copy.wait()
     for parity, folded in enumerate((first + second, first - second)):
         high, low = split(folded)
         wide = mm(tab_ref[0, parity], jnp.concatenate([high, low], axis=1))
@@ -104,8 +123,8 @@
         spec_ref[parity * BINS : (parity + 1) * BINS, :] = rows
 
 
-def whiten_kernel(spec_ref, rim_ref, mean_ref, base_ref, edge_ref, band_ref, white_ref):
-    head = tap_rows(base_ref, GROUP)[:, :LANES]
+def whiten_kernel(spec_ref, rim_ref, mean_ref, taps_ref, edge_ref, band_ref, white_ref):
+    head = tap_rows(taps_ref, GROUP)[:, :LANES]
     rim = rim_ref[...] - mean_ref[...]
     history = lax.dot_general(
         head, rim, (((1,), (1,)), ((), ())),
@@ -202,11 +221,15 @@
     return [pl.BlockSpec(memory_space=pltpu.VMEM)] * count
 
 
+def in_hbm(array):
+    return pltpu.with_memory_space_constraint(array, pltpu.HBM)
+
+
 def smem(count):
     return [pl.BlockSpec(memory_space=pltpu.SMEM)] * count
 
 
-PARAMS = pltpu.CompilerParams(vmem_limit_bytes=48 * 1024 * 1024)
+PARAMS = pltpu.CompilerParams(vmem_limit_bytes=32 * 1024 * 1024)
 
 
 def cross_plain(white, offsets, loop_partner, loop_count, owners):
@@ -252,10 +275,7 @@
     route = [(i, i + 1) for i in range(seg_count - 1)]
     rim = lax.ppermute(recording[:, length - LANES :], "seg", route)
 
-    width = LANES + OUT_BLOCK * DECIM
-    start = LANES + DECIM - TAPS
-    base = jnp.pad(filter_taps[::-1], (start, width - start - TAPS))
-    base = jnp.broadcast_to(base[None, :], (8, width))
+    taps = filter_taps.reshape(TAPS, 1)
     forward = forward_table()
     table = np.stack(split_np(forward))
     spec, mean = pl.pallas_call(
@@ -264,14 +284,23 @@
             jax.ShapeDtypeStruct((2 * BINS, LANES), F32),
             jax.ShapeDtypeStruct((LANES, LANES), F32),
         ],
-        in_specs=vmem(3),
+        in_specs=[
+            pl.BlockSpec(memory_space=pltpu.HBM),
+            pl.BlockSpec(memory_space=pltpu.VMEM),
+            pl.BlockSpec(memory_space=pltpu.HBM),
+        ],
         out_specs=vmem(2),
+        scratch_shapes=[
+            pltpu.VMEM((chans, length), F32),
+            pltpu.VMEM((2, 2, HALF, HALF), BF16),
+            pltpu.SemaphoreType.DMA((length // (OUT_BLOCK * DECIM) + 4,)),
+        ],
         compiler_params=PARAMS,
         cost_estimate=pl.CostEstimate(
             flops=1_000_000_000, bytes_accessed=5_000_000, transcendentals=0
         ),
         name="filter_and_transform",
-    )(recording, base, table)
+    )(in_hbm(recording), taps, in_hbm(jnp.asarray(table)))
 
     first = forward.reshape(2 * BINS, HALF)[:, :GROUP]
     high, low = split_np(first)
@@ -284,7 +313,7 @@
         out_specs=pl.BlockSpec(memory_space=pltpu.VMEM),
         compiler_params=PARAMS,
         name="whiten",
-    )(spec, rim, mean, base, edge, band_table())
+    )(spec, rim, mean, taps, edge, band_table())
 
     if bins != GROUP:
         white = jnp.moveaxis(white, 1, 0).reshape(2, devices, bins, LANES)

time: 50.6 us -> 50 us (0.988)
  local copies, waits for them, and re-layouts: 4.97 us -> 1.71 us
  Pallas kernels: 6.86 us -> 9.56 us
    unnamed x17 -> x13, local copies, waits for them, and re-layouts: 3.3 us -> 0.12 us
    pallas_call x1, Pallas kernels: 2.02 us -> 4.63 us  [body(): pl.pallas_call(spectrum_kernel, out_shape=[jax.ShapeDtypeStruct((2 * BINS...]
    reshape x0 -> x1, local copies, waits for them, and re-layouts: none -> 0.75 us  [body(): taps = filter_taps.reshape(TAPS, 1)]
    rev x1 -> x0, local copies, waits for them, and re-layouts: 0.75 us -> none  [body(): base = jnp.pad(filter_taps[::-1], (start, width - start - TAPS))]
  transfers between devices with their start and end apart: 2 -> 2, of which waited for: 1 -> 1; matrix products, arithmetic and copies ran while one was open for 2% -> 2% of each run, Pallas kernels for 4% -> 9%
where the time goes in v1:
time: 50 us; the launch traced here: 49.7 us
  blocking collectives  17.8 us (36%)
  waiting for transfers between devices  10.5 us (21%)
  Pallas kernels  9.56 us (19%)
  starting transfers between devices  9.47 us (19%)
  local copies, waits for them, and re-layouts  1.71 us (3%)
  between operations  0.74 us (1%)
    all_to_all x1, blocking collectives, body(): summed = lax.all_to_all(crossed, ('chan', 'seg'), 0, 0, tiled=True)  17.8 us
    all_to_all x1, waiting for transfers between devices, body(): moved = lax.all_to_all(white, ('chan', 'seg'), 0, 0, tiled=True)  10.5 us
    all_to_all x1, starting transfers between devices, body(): moved = lax.all_to_all(white, ('chan', 'seg'), 0, 0, tiled=True)  7.12 us
    pallas_call x1, Pallas kernels, body(): pl.pallas_call(spectrum_kernel, out_shape=[jax.ShapeDtypeStruct((2 * BINS...  4.63 us
    ppermute x1, starting transfers between devices, body(): rim = lax.ppermute(recording[:, length - LANES:], 'seg', route)  2.35 us
    pallas_call x1, Pallas kernels, body(): pl.pallas_call(cross_kernel, out_shape=jax.ShapeDtypeStruct((chan_count,...  1.96 us
    pallas_call x1, Pallas kernels, body(): pl.pallas_call(whiten_kernel, out_shape=jax.ShapeDtypeStruct((GROUPS, 2,...  1.77 us
    pallas_call x1, Pallas kernels, body(): pl.pallas_call(lag_kernel, out_shape=[jax.ShapeDtypeStruct((chans, tiles...  1.2 us
  transfers between devices with their start and end apart: 2, of which 1 were waited for; matrix products, arithmetic and copies ran while one was open for 2% of the time, Pallas kernels for 9%

profile of v1, /device:TPU:0, one launch (start us, length us, event | category | flops | bytes accessed | tf_op | source)
XLA Modules:
  0.0 49.7 jit_solution(1735929337416929531)
XLA Ops:
  0.6 0.8 %slice.3 = f32[128,128]{1,0:T(8,128)S(1)} slice(f32[128,4096]{1,0:T(8,128)} %rec_hbm.1), slice={[0:128], [3968:4096]} | slice | bytes 131072 | tf_op jit(solution)/shard_map/slice | solution.py:276
  1.5 2.3 %collective-permute-start = (f32[128,128]{1,0:T(8,128)S(1)}, f32[128,128]{1,0:T(8,128)S(1)}, u32[]{:S(2)}, u32[]{:S(2)}) collective-permute-start(f32[128,128]{1,0:T(8,128)S(1)} %slice.3), channel_id=1, source_target_pairs={{0,1},{1,2},{2,3},{4,5},{5,6},{6,7},{8,9},{9,10},{10,11},{12,13},{... | collective-permute-start | bytes 196616 | tf_op jit(solution)/shard_map/ppermute | solution.py:276
  3.8 0.7 %copy.11.taps_ref = f32[64,1]{1,0:T(8,128)S(1)} copy(f32[64,1]{0,1:T(1,128)} %bitcast.6) | data formatting | bytes 512 | tf_op jit(solution)/shard_map/reshape | solution.py:278
  4.6 0.0 copy-start.1
  4.6 0.0 copy-start.2
  4.6 4.6 %filter_and_transform.1 = (f32[1024,128]{1,0:T(8,128)S(1)}, f32[128,128]{1,0:T(8,128)S(1)}) custom-call(f32[128,4096]{1,0:T(8,128)} %rec_hbm.1, f32[64,1]{1,0:T(8,128)S(1)} %copy.11.taps_ref, bf16[2,2,512,512]{3,2,1,0:T(8,128)(2,1)} %constant.8.clone.tab_hbm), custom_call_target="tpu_custom_call" | custom-call | flops 1000000000 | bytes 5000000 | tf_op jit(solution)/shard_map/filter_and_transform/pallas_call | solution.py:281
  9.2 0.0 copy-start.5
  9.2 0.0 copy-start.3
  9.3 0.0 copy-start.4
  9.3 0.0 copy-start
  9.3 0.0 collective-permute-done.rim_ref
  9.3 0.0 copy-done.1
  9.3 0.0 copy-done.2
  9.3 1.8 %whiten.1 = bf16[32,2,16,128]{3,2,1,0:T(8,128)(2,1)} custom-call(f32[1024,128]{1,0:T(8,128)S(1)} %get-tuple-element.6.spec_ref, f32[128,128]{1,0:T(8,128)S(1)} %collective-permute-done.rim_ref, f32[128,128]{1,0:T(8,128)S(1)} %get-tuple-element.7.mean_ref, f32[64,1]{1,0:T(8,128)S(1)} %copy.11.taps_ref, bf16[1024,128]{1,0:T(8,128)(2,1)S(1)} %copy-done.2, ...), custom_call_target="tpu_custom_call" | custom-call | tf_op jit(solution)/shard_map/whiten/pallas_call | solution.py:309
  11.1 7.1 %all-to-all-start = ((bf16[32,2,16,128]{3,2,1,0:T(8,128)(2,1)}), bf16[32,2,16,128]{3,2,1,0:T(8,128)(2,1)S(1)}, u32[]{:S(2)}, u32[]{:S(2)}) async-start(bf16[32,2,16,128]{3,2,1,0:T(8,128)(2,1)} %whiten.1), calls=%async_computation | async-start | bytes 524288 | tf_op jit(solution)/shard_map/all_to_all | solution.py:321
  18.2 0.0 copy-done.5
  18.2 0.1 copy.13.partner_ref
  18.3 10.5 %all-to-all-done = bf16[32,2,16,128]{3,2,1,0:T(8,128)(2,1)S(1)} async-done(((bf16[32,2,16,128]{3,2,1,0:T(8,128)(2,1)}), bf16[32,2,16,128]{3,2,1,0:T(8,128)(2,1)S(1)}, u32[]{:S(2)}, u32[]{:S(2)}) %all-to-all-start) | async-done | bytes 262176 | tf_op jit(solution)/shard_map/all_to_all | solution.py:321
  28.8 0.0 copy-done.3
  28.8 0.0 copy-done.4
  28.8 2.0 %cross_spectra.1 = bf16[8,4,2,2,16,128]{5,4,3,2,1,0:T(8,128)(2,1)S(1)} custom-call(s32[4]{0:T(128)S(1)} %copy-done.3, s32[8,3]{1,0:T(8,128)S(1)} %copy.13.partner_ref, s32[8]{0:T(128)S(1)} %copy-done.4, bf16[8,4,2,16,128]{4,3,2,1,0:T(8,128)(2,1)S(1)} %bitcast.5), custom_call_target="tpu_custom_call" | custom-call | tf_op jit(solution)/shard_map/cross_spectra/pallas_call | solution.py:324
  30.8 17.8 %all_to_all.10.spec_ref = bf16[32,2,2,16,128]{4,3,2,1,0:T(8,128)(2,1)S(1)} all-to-all(bf16[32,2,2,16,128]{4,3,2,1,0:T(8,128)(2,1)S(1)} %bitcast.4), channel_id=1, replica_groups=mesh['chan'=8,'seg'=4] {'chan','seg'}, dimensions={0} | all-to-all | bytes 1048576 | tf_op jit(solution)/shard_map/all_to_all | solution.py:338
  48.5 0.0 copy-done
  48.5 1.2 %lags.1 = (f32[128,1,256]{2,1,0:T(1,128)}, f32[96,256]{1,0:T(8,128)}) custom-call(bf16[32,2,2,16,128]{4,3,2,1,0:T(8,128)(2,1)S(1)} %all_to_all.10.spec_ref, bf16[512,1024]{1,0:T(8,128)(2,1)S(1)} %copy-done), custom_call_target="tpu_custom_call" | custom-call | tf_op jit(solution)/shard_map/lags/pallas_call | solution.py:347
Async XLA Ops:
  1.5 7.8 %collective-permute-start = (f32[128,128]{1,0:T(8,128)S(1)}, f32[128,128]{1,0:T(8,128)S(1)}, u32[]{:S(2)}, u32[]{:S(2)}) collective-permute-start(f32[128,128]{1,0:T(8,128)S(1)} %slice.3), channel_id=1, source_target_pairs={{0,1},{1,2},{2,3},{4,5},{5,6},{6,7},{8,9},{9,10},{10,11},{12,13},{... | collective-permute-start | bytes 196616 | tf_op jit(solution)/shard_map/ppermute | solution.py:276
  4.6 4.7 %copy-start.1 = (bf16[512,512]{1,0:T(8,128)(2,1)S(1)}, bf16[512,512]{1,0:T(8,128)(2,1)}, u32[]{:S(2)}) copy-start(bf16[512,512]{1,0:T(8,128)(2,1)} %constant.10.clone.band_ref) | copy-start | bytes 1572868
  4.6 4.7 %copy-start.2 = (bf16[1024,128]{1,0:T(8,128)(2,1)S(1)}, bf16[1024,128]{1,0:T(8,128)(2,1)}, u32[]{:S(2)}) copy-start(bf16[1024,128]{1,0:T(8,128)(2,1)} %constant.9.clone.edge_ref) | copy-start | bytes 786436
  9.2 9.0 %copy-start.5 = (s32[8,3]{0,1:T(4,128)S(1)}, s32[8,3]{0,1:T(4,128)}, u32[]{:S(2)}) copy-start(s32[8,3]{0,1:T(4,128)} %param.12) | copy-start | bytes 292
  9.2 19.6 %copy-start.3 = (s32[4]{0:T(128)S(1)}, s32[4]{0:T(128)}, u32[]{:S(2)}) copy-start(s32[4]{0:T(128)} %offs_ref.1) | copy-start | bytes 52
  9.3 19.6 %copy-start.4 = (s32[8]{0:T(128)S(1)}, s32[8]{0:T(128)}, u32[]{:S(2)}) copy-start(s32[8]{0:T(128)} %count_ref.1) | copy-start | bytes 100
  9.3 39.3 %copy-start = (bf16[512,1024]{1,0:T(8,128)(2,1)S(1)}, bf16[512,1024]{1,0:T(8,128)(2,1)}, u32[]{:S(2)}) copy-start(bf16[512,1024]{1,0:T(8,128)(2,1)} %constant.11.clone.inv_ref) | copy-start | bytes 3145732
  11.1 17.7 %all-to-all-start = ((bf16[32,2,16,128]{3,2,1,0:T(8,128)(2,1)}), bf16[32,2,16,128]{3,2,1,0:T(8,128)(2,1)S(1)}, u32[]{:S(2)}, u32[]{:S(2)}) async-start(bf16[32,2,16,128]{3,2,1,0:T(8,128)(2,1)} %whiten.1), calls=%async_computation | async-start | bytes 524288 | tf_op jit(solution)/shard_map/all_to_all | solution.py:321

commit v2 on v1

v2 whole, which is shorter than its diff:
```python
import functools
import math

import jax
import jax.numpy as jnp
import numpy as np
from jax import lax
from jax.experimental import pallas as pl
from jax.experimental.pallas import tpu as pltpu
from jax.sharding import PartitionSpec as P

NFFT = 1024
LAGS = 256
TAPS = 64
DECIM = 4
HALFBAND = 10
BINS = 512
WATER = 0.2

LANES = 128
GROUP = 16
GROUPS = BINS // GROUP
OUT_BLOCK = 128
STEP = OUT_BLOCK * DECIM
RADIX = 4
DEPTH = NFFT // RADIX
FAR_BINS = BINS // RADIX

F32 = jnp.float32
BF16 = jnp.bfloat16
MIB = 1024 * 1024
PARAMS = pltpu.CompilerParams(vmem_limit_bytes=32 * MIB)


def bin_order():
    return np.concatenate([np.arange(r, BINS, RADIX) for r in range(RADIX)])


def split_np(table):
    high = table.astype(jnp.bfloat16)
    low = (table - high.astype(np.float64)).astype(jnp.bfloat16)
    return high, low


def short_table():
    bins = np.arange(FAR_BINS).reshape(-1, 1, GROUP, 1)
    angles = (bins * np.arange(DEPTH) % DEPTH) * (2.0 * np.pi / DEPTH)
    rows = np.concatenate([np.cos(angles), np.sin(angles)], axis=1).reshape(-1, DEPTH)
    high, low = split_np(rows)
    return np.concatenate([high, high, low], axis=1)


def twiddle_table():
    angles = np.arange(DEPTH)[:, None] * np.arange(1, RADIX) * (2.0 * np.pi / NFFT)
    columns = np.stack([np.cos(angles), np.sin(angles)], axis=2).reshape(DEPTH, -1)
    return np.pad(columns, ((0, 0), (0, LANES - columns.shape[1]))).astype(np.float32)


def edge_table():
    bins = bin_order().reshape(GROUPS, 1, GROUP, 1)
    angles = (bins * np.arange(GROUP) % NFFT) * (2.0 * np.pi / NFFT)
    rows = np.concatenate([np.cos(angles), -np.sin(angles)], axis=1) * (bins != 0)
    high, low = split_np(rows.reshape(2 * BINS, GROUP))
    table = np.concatenate([high, high, low], axis=1)
    return np.pad(table.astype(np.float32), ((0, 0), (0, LANES - 3 * GROUP))).astype(jnp.bfloat16)


def inverse_table(total_segs, bins, part):
    lag = np.arange(LAGS) - LAGS // 2
    angles = (bins[None, :] * lag[:, None] % NFFT) * (2.0 * np.pi / NFFT)
    weights = np.where(bins == 0, 1.0, 2.0) / math.sqrt(2.0 * BINS * total_segs)
    return np.where(part[None, :] == 1, -np.sin(angles), np.cos(angles)) * weights[None, :]


def band_tables():
    bins = bin_order()
    inside = np.abs(bins[:, None] - bins[None, :]) <= HALFBAND
    share = np.broadcast_to(1.0 / inside.sum(axis=1, keepdims=True), (BINS, LANES))
    return inside.astype(jnp.bfloat16), share.astype(np.float32)


def split(value):
    high = value.astype(BF16)
    return high, (value - high.astype(F32)).astype(BF16)


def mm(a, b):
    return jnp.dot(a, b, preferred_element_type=F32)


def mm_nt(a, b):
    return lax.dot_general(a, b, (((1,), (1,)), ((), ())), preferred_element_type=F32)


def tap_rows(taps_ref, rows):
    width = LANES + STEP
    square = (TAPS, TAPS)
    diagonal = lax.broadcasted_iota(jnp.int32, square, 0) == lax.broadcasted_iota(jnp.int32, square, 1)
    column_taps = jnp.sum(jnp.where(diagonal, taps_ref[...], 0.0), axis=1, keepdims=True)
    tap = lax.broadcasted_iota(jnp.int32, (TAPS, width), 0)
    column = lax.broadcasted_iota(jnp.int32, (TAPS, width), 1)
    placed = jnp.where(column == LANES + DECIM - 1 - tap, column_taps, 0.0)
    spread = jnp.broadcast_to(jnp.sum(placed, axis=0, keepdims=True), (rows, width))
    return pltpu.roll(spread, 0, 1, stride=DECIM, stride_axis=0)


def spectrum_kernel(
    taps_ref, rec_hbm, tab_hbm, twist_hbm, spec_ref, mean_ref, rec_ref, tab_ref, twist_ref, sems
):
    blocks = rec_ref.shape[1] // STEP
    copies = []
    for j in range(blocks):
        part = pl.ds(j * STEP, STEP)
        copies.append((rec_hbm.at[:, part], rec_ref.at[:, part]))
    copies = copies + [(twist_hbm, twist_ref), (tab_hbm, tab_ref)]
    copies = [pltpu.make_async_copy(*c, sems.at[i]) for i, c in enumerate(copies)]
    for copy in copies:
        copy.start()
    taps_high, taps_low = split(tap_rows(taps_ref, OUT_BLOCK))
    taps = jnp.concatenate([taps_high, taps_high, taps_low], axis=1)
    before = [jnp.zeros((LANES, LANES), BF16)] * 2
    windows, pieces = [], []
    for j in range(blocks):
        copies[j].wait()
        chunk = rec_ref[:, j * STEP : (j + 1) * STEP]
        if j == 0:
            mean = jnp.sum(chunk, axis=1, keepdims=True) * (1.0 / STEP)
        high, low = split(chunk - mean)
        windows.append(jnp.concatenate([before[0], high, before[1], low, before[0], high], axis=1))
        before = [high[:, STEP - LANES :], low[:, STEP - LANES :]]
        if j % 2:
            pair = mm_nt(taps, jnp.concatenate(windows[-2:], axis=0))
            pieces.append(jnp.concatenate([pair[:, :LANES], pair[:, LANES:]], axis=0))
    mean_ref[...] = jnp.broadcast_to(mean, mean_ref.shape)
    even, odd = pieces[0] + pieces[2], pieces[1] + pieces[3]
    a, b = pieces[0] - pieces[2], pieces[1] - pieces[3]
    whole, half = even + odd, even - odd
    whole = whole - jnp.sum(whole, axis=0, keepdims=True) * (1.0 / DEPTH)
    copies[blocks].wait()
    c1, s1, c2, s2, c3, s3 = [twist_ref[:, i : i + 1] for i in range(6)]
    inputs = [
        whole,
        a * c1 - b * s1,
        -(a * s1 + b * c1),
        half * c2,
        -(half * s2),
        a * c3 + b * s3,
        b * c3 - a * s3,
    ]
    parts = [split(value) for value in inputs]
    high = jnp.concatenate([p[0] for p in parts], axis=1)
    low = jnp.concatenate([p[1] for p in parts], axis=1)
    copies[blocks + 1].wait()
    out = mm(tab_ref[...], jnp.concatenate([high, low, high], axis=0))
    out = out.reshape(FAR_BINS // GROUP, 2, GROUP, out.shape[1])
    rows = 2 * FAR_BINS
    for r in range(RADIX):
        first = max(2 * r - 1, 0) * LANES
        real_in = out[..., first : first + LANES]
        if r == 0:
            real, imag = real_in[:, 0], -real_in[:, 1]
        else:
            imag_in = out[..., first + LANES : first + 2 * LANES]
            real, imag = real_in[:, 0] + imag_in[:, 1], imag_in[:, 0] - real_in[:, 1]
        both = jnp.stack([real, imag], axis=1).reshape(rows, LANES)
        spec_ref[r * rows : (r + 1) * rows, :] = both


def whiten_kernel(
    spec_ref, rim_ref, mean_ref, taps_ref, edge_ref, band_ref, share_ref, white_ref
):
    head_high, head_low = split(tap_rows(taps_ref, GROUP)[:, :LANES])
    rim_high, rim_low = split(rim_ref[...] - mean_ref[...])
    history = mm_nt(
        jnp.concatenate([head_high, head_high, head_low], axis=1),
        jnp.concatenate([rim_high, rim_low, rim_high], axis=1),
    )
    high, low = split(history)
    stacked = jnp.concatenate([high, low, high], axis=0)
    spec = spec_ref[...] + mm(edge_ref[:, : 3 * GROUP], stacked)
    parted = spec.reshape(GROUPS, 2, GROUP, LANES)
    real, imag = parted[:, 0], parted[:, 1]
    amplitude = jnp.sqrt(real * real + imag * imag).reshape(BINS, LANES)
    high, low = split(amplitude)
    wide = mm(band_ref[...], jnp.concatenate([high, low], axis=1))
    smoothed = (wide[:, :LANES] + wide[:, LANES:]) * share_ref[...]
    level = jnp.sum(amplitude, axis=0, keepdims=True) * (1.0 / BINS)
    scale = 1.0 / (smoothed + (WATER * level + 1e-06))
    white = parted * scale.reshape(GROUPS, 1, GROUP, LANES)
    white_ref[...] = white.astype(BF16)


def moves_kernel(offs_ref, moves_ref):
    noff = offs_ref.shape[0]
    source = lax.broadcasted_iota(jnp.int32, (3 * LANES, LANES), 0)
    channel = lax.broadcasted_iota(jnp.int32, (3 * LANES, LANES), 1)
    for o in range(noff):
        hit = source == channel + (LANES + offs_ref[o])
        moves_ref[:, o * LANES : (o + 1) * LANES] = hit.astype(F32).astype(BF16)


def pack_matrix(owners):
    share = LANES // owners
    matrix = np.zeros((owners, owners, share, owners, owners, share), np.float32)
    for group in range(owners):
        for owner in range(owners):
            matrix[group, owner, :, owner, group, :] = np.eye(share)
    return matrix.reshape(owners * LANES, owners * LANES).astype(jnp.bfloat16)


def cross_kernel(
    partner_ref, count_ref, moves_ref, flip_ref, pack_ref, white_ref, out_ref, turned_ref
):
    blocks, segs, _, bins, _ = white_ref.shape
    owners = out_ref.shape[1]
    slots = partner_ref.shape[1]
    noff = moves_ref.shape[1] // LANES
    near_each = noff // owners
    rows = segs * 2 * bins
    packed_rows = 2 * bins // owners
    flats = [white_ref[b].reshape(rows, LANES) for b in range(blocks)]
    every = jnp.concatenate(flats, axis=0)
    turned_ref[...] = mm(every, flip_ref[...]).reshape(turned_ref.shape)
    before = jnp.concatenate(flats[-1:] + flats[:-1], axis=0)
    after = jnp.concatenate(flats[1:] + flats[:1], axis=0)
    moved = mm(jnp.concatenate([before, every, after], axis=1), moves_ref[...])

    def products(own, far):
        own = own.reshape(segs, 2, bins, LANES)
        far = far.reshape(segs, 2, bins, LANES)
        real = jnp.sum(own[:, 0] * far[:, 0] + own[:, 1] * far[:, 1], axis=0)
        imag = jnp.sum(own[:, 1] * far[:, 0] - own[:, 0] * far[:, 1], axis=0)
        return jnp.concatenate([real, imag], axis=0)

    near, loops = [], []
    for b in range(blocks):
        own = flats[b].astype(F32)
        far = moved[b * rows : (b + 1) * rows]
        near.append([products(own, far[:, o * LANES : (o + 1) * LANES]) for o in range(noff)])
        for k in range(slots):
            partner = jnp.clip(partner_ref[b, k], 0, blocks - 1)
            live = (k < count_ref[b]).astype(F32)
            pair = products(own, turned_ref[partner]) * live
            groups = [pair[g * packed_rows : (g + 1) * packed_rows] for g in range(owners)]
            loops.append(jnp.concatenate(groups, axis=1))
    packed = mm(jnp.concatenate(loops, axis=0).astype(BF16), pack_ref[...])
    depth = slots * packed_rows
    for b in range(blocks):
        for q in range(owners):
            tail = packed[b * depth : (b + 1) * depth, q * LANES : (q + 1) * LANES]
            mine = near[b][q * near_each : (q + 1) * near_each] + [tail]
            out_ref[b, q] = jnp.concatenate(mine, axis=0).astype(BF16)


def lag_kernel(slots, spec_ref, inv_ref, near_ref, loop_ref):
    sources = spec_ref.shape[0]
    rows = inv_ref.shape[1] // sources
    near_each = near_ref.shape[1]
    share = loop_ref.shape[0] // slots
    owners = LANES // share
    step = rows // owners
    columns = [
        spec_ref[:, t * rows : (t + 1) * rows].reshape(sources * rows, LANES)
        for t in range(near_each)
    ]
    loop = spec_ref[:, near_each * rows :].astype(F32)
    lane = lax.broadcasted_iota(jnp.int32, (sources, step, LANES), 2)
    for k in range(slots):
        tile = loop[:, k * step : (k + 1) * step]
        groups = [
            jnp.where((lane >= g * share) & (lane < (g + 1) * share), tile, 0.0)
            for g in range(owners)
        ]
        columns.append(jnp.concatenate(groups, axis=1).astype(BF16).reshape(sources * rows, LANES))
    both = mm(inv_ref[...], jnp.concatenate(columns, axis=1))
    lags = both[:LAGS] + both[LAGS:]
    for t in range(near_each):
        near_ref[:, t, :] = lags[:, t * LANES : (t + 1) * LANES].T
    for k in range(slots):
        first = (near_each + k) * LANES
        turned = lags[:, first : first + LANES].T
        loop_ref[k * share : (k + 1) * share] = sum(
            turned[g * share : (g + 1) * share] for g in range(owners)
        )


def vmem(count):
    return [pl.BlockSpec(memory_space=pltpu.VMEM)] * count


def smem(count):
    return [pl.BlockSpec(memory_space=pltpu.SMEM)] * count


def hbm(count):
    return [pl.BlockSpec(memory_space=pltpu.HBM)] * count


def in_hbm(array):
    return pltpu.with_memory_space_constraint(jnp.asarray(array), pltpu.HBM)


def finish_plain(white, offsets, loop_partner, loop_count, owners, total_segs):
    blocks, segs, _, bins, chans = white.shape
    devices = blocks * owners
    noff, slots = offsets.shape[0], loop_partner.shape[1]
    share = chans // owners
    wide = white.astype(F32)
    flat = jnp.moveaxis(wide, 0, 3).reshape(segs, 2, bins, blocks * chans)

    def products(own, far):
        real = jnp.sum(own[:, 0] * far[:, 0] + own[:, 1] * far[:, 1], axis=0)
        imag = jnp.sum(own[:, 1] * far[:, 0] - own[:, 0] * far[:, 1], axis=0)
        return jnp.stack([real, imag]).astype(BF16)

    near = [products(flat, jnp.roll(flat, -offsets[o], axis=3)) for o in range(noff)]
    near = jnp.stack(near).reshape(owners, noff // owners, 2, bins, blocks, chans)
    near = jnp.moveaxis(near, 4, 0).reshape(devices, noff // owners, 2 * bins, chans)
    loops = []
    for k in range(slots):
        far = jnp.flip(wide[loop_partner[:, k]], axis=4)
        live = (k < loop_count).astype(BF16)[:, None, None]
        pair = products(jnp.moveaxis(wide, 0, 2), jnp.moveaxis(far, 0, 2)) * live[None]
        loops.append(pair.reshape(2, blocks, bins, owners, share))
    loop = jnp.transpose(jnp.stack(loops), (2, 4, 0, 1, 3, 5))
    loop = loop.reshape(devices, slots, 2 * bins, share)
    order = np.repeat(bin_order().reshape(devices, 1, bins), 2, axis=1).reshape(-1)
    part = np.broadcast_to(np.arange(2).reshape(1, 2, 1), (devices, 2, bins)).reshape(-1)
    inverse = inverse_table(total_segs, order, part).astype(np.float32)
    inverse = inverse.reshape(LAGS, devices, 2 * bins)
    results = []
    for array in (near, loop):
        summed = lax.all_to_all(array, ("chan", "seg"), 0, 0, tiled=True).astype(F32)
        lags = jnp.einsum("dtvc,ldv->tcl", summed, inverse, precision=lax.Precision.HIGHEST)
        results.append(lags)
    return jnp.moveaxis(results[0], 0, 1), results[1][None]


def body(recording, filter_taps, offsets, loop_partner, loop_count):
    chan_count = lax.axis_size("chan")
    seg_count = lax.axis_size("seg")
    devices = chan_count * seg_count
    bins = BINS // devices
    chans, length = recording.shape
    noff, slots = offsets.shape[0], loop_partner.shape[1]
    share = chans // seg_count
    near_each = noff // seg_count
    assert length == NFFT * DECIM and chans == LANES and noff % seg_count == 0

    route = [(i, i + 1) for i in range(seg_count - 1)]
    rim = lax.ppermute(recording[:, length - LANES :], "seg", route)
    taps = filter_taps.reshape(1, TAPS)
    spec, mean = pl.pallas_call(
        spectrum_kernel,
        out_shape=[
            jax.ShapeDtypeStruct((2 * BINS, LANES), F32),
            jax.ShapeDtypeStruct((LANES, LANES), F32),
        ],
        in_specs=vmem(1) + hbm(3),
        out_specs=vmem(2),
        scratch_shapes=[
            pltpu.VMEM((chans, length), F32),
            pltpu.VMEM((2 * FAR_BINS, 3 * DEPTH), BF16),
            pltpu.VMEM((DEPTH, LANES), F32),
            pltpu.SemaphoreType.DMA((length // STEP + 2,)),
        ],
        compiler_params=PARAMS,
        cost_estimate=pl.CostEstimate(
            flops=1_000_000_000, bytes_accessed=5_000_000, transcendentals=0
        ),
        name="filter_and_transform",
    )(taps, in_hbm(recording), in_hbm(short_table()), in_hbm(twiddle_table()))

    band, band_share = band_tables()
    white = pl.pallas_call(
        whiten_kernel,
        out_shape=jax.ShapeDtypeStruct((GROUPS, 2, GROUP, LANES), BF16),
        in_specs=vmem(7),
        out_specs=pl.BlockSpec(memory_space=pltpu.VMEM),
        compiler_params=PARAMS,
        name="whiten",
    )(spec, rim, mean, taps, edge_table(), band, band_share)

    white, offsets = lax.optimization_barrier((white, offsets))
    if bins != GROUP:
        white = jnp.moveaxis(white, 1, 0).reshape(2, devices, bins, LANES)
        white = jnp.moveaxis(white, 0, 1)
    moved = lax.all_to_all(white, ("chan", "seg"), 0, 0, tiled=True)
    moved = moved.reshape(chan_count, seg_count, 2, bins, LANES)
    if bins % GROUP or 2 * bins % (8 * seg_count):
        return finish_plain(moved, offsets, loop_partner, loop_count, seg_count, seg_count)

    moves = pl.pallas_call(
        moves_kernel,
        out_shape=jax.ShapeDtypeStruct((3 * LANES, noff * LANES), BF16),
        in_specs=smem(1),
        out_specs=pl.BlockSpec(memory_space=pltpu.VMEM),
        compiler_params=PARAMS,
        name="offset_moves",
    )(offsets)
    flip = np.eye(LANES, dtype=np.float32)[::-1].astype(jnp.bfloat16)
    out_rows = near_each * 2 * bins + slots * (2 * bins // seg_count)
    crossed = pl.pallas_call(
        cross_kernel,
        out_shape=jax.ShapeDtypeStruct((chan_count, seg_count, out_rows, LANES), BF16),
        in_specs=smem(2) + vmem(4),
        out_specs=pl.BlockSpec(memory_space=pltpu.VMEM),
        scratch_shapes=[pltpu.VMEM((chan_count, seg_count * 2 * bins, LANES), F32)],
        compiler_params=PARAMS,
        name="cross_spectra",
    )(loop_partner, loop_count, moves, flip, pack_matrix(seg_count), moved)
    crossed = crossed.reshape(devices, out_rows, LANES)
    summed = lax.all_to_all(crossed, ("chan", "seg"), 0, 0, tiled=True)

    order = np.repeat(bin_order().reshape(devices, 1, bins), 2, axis=1).reshape(-1)
    part = np.broadcast_to(np.arange(2).reshape(1, 2, 1), (devices, 2, bins)).reshape(-1)
    inverse = np.concatenate(split_np(inverse_table(seg_count, order, part)), axis=0)
    near, loop = pl.pallas_call(
        functools.partial(lag_kernel, slots),
        out_shape=[
            jax.ShapeDtypeStruct((chans, near_each, LAGS), F32),
            jax.ShapeDtypeStruct((slots * share, LAGS), F32),
        ],
        in_specs=vmem(2),
        out_specs=vmem(2),
        compiler_params=PARAMS,
        name="lags",
    )(summed, inverse)
    return near, loop.reshape(1, slots, share, LAGS)


def solution(mesh):
    in_specs = (P("chan", "seg"), P(), P(), P(), P())
    out_specs = (P("chan", "seg", None), P("chan", None, "seg", None))
    return jax.shard_map(body, mesh=mesh, in_specs=in_specs, out_specs=out_specs, check_vma=False)
```

time: 50 us -> 48.8 us (0.976)
  blocking collectives: 17.8 us -> 16.6 us
  waiting for transfers between devices: 10.5 us -> 9.87 us
  Pallas kernels: 9.56 us -> 10.1 us
    all_to_all x1, blocking collectives: 17.8 us -> 16.6 us  [body(): summed = lax.all_to_all(crossed, ('chan', 'seg'), 0, 0, tiled=True)]
    pallas_call x1 -> x2, Pallas kernels: 1.2 us -> 2.16 us  [the longest x1 1.53 us: body(): pl.pallas_call(functools.partial(lag_kernel, slots), out_shape=[jax.Shape...]
    reshape x1 -> x0, local copies, waits for them, and re-layouts: 0.75 us -> none  [body(): taps = filter_taps.reshape(TAPS, 1)]
    unnamed x13 -> x21, local copies, waits for them, and re-layouts: 0.12 us -> 0.79 us
    all_to_all x1, waiting for transfers between devices: 10.5 us -> 9.87 us  [body(): moved = lax.all_to_all(white, ('chan', 'seg'), 0, 0, tiled=True)]
  transfers between devices with their start and end apart: 2 -> 2, of which waited for: 1 -> 1; matrix products, arithmetic and copies ran while one was open for 2% -> 0% of each run, Pallas kernels for 9% -> 11%
where the time goes in v2:
time: 48.8 us; the launch traced here: 48.5 us
  blocking collectives  16.6 us (34%)
  Pallas kernels  10.1 us (21%)
  waiting for transfers between devices  9.87 us (20%)
  starting transfers between devices  9.48 us (19%)
  local copies, waits for them, and re-layouts  1.72 us (4%)
  between operations  0.79 us (2%)
    all_to_all x1, blocking collectives, body(): summed = lax.all_to_all(crossed, ('chan', 'seg'), 0, 0, tiled=True)  16.6 us
    all_to_all x1, waiting for transfers between devices, body(): moved = lax.all_to_all(white, ('chan', 'seg'), 0, 0, tiled=True)  9.87 us
    all_to_all x1, starting transfers between devices, body(): moved = lax.all_to_all(white, ('chan', 'seg'), 0, 0, tiled=True)  7.13 us
    pallas_call x1, Pallas kernels, body(): pl.pallas_call(spectrum_kernel, out_shape=[jax.ShapeDtypeStruct((2 * BINS...  4.9 us
    ppermute x1, starting transfers between devices, body(): rim = lax.ppermute(recording[:, length - LANES:], 'seg', route)  2.35 us
    pallas_call x1, Pallas kernels, body(): pl.pallas_call(whiten_kernel, out_shape=jax.ShapeDtypeStruct((GROUPS, 2,...  1.55 us
    pallas_call x1, Pallas kernels, body(): pl.pallas_call(functools.partial(lag_kernel, slots), out_shape=[jax.Shape...  1.53 us
    pallas_call x1, Pallas kernels, body(): pl.pallas_call(cross_kernel, out_shape=jax.ShapeDtypeStruct((chan_count,...  1.52 us
  transfers between devices with their start and end apart: 2, of which 1 were waited for; matrix products, arithmetic and copies ran while one was open for 0% of the time, Pallas kernels for 11%

profile of v2, /device:TPU:0, one launch (start us, length us, event | category | flops | bytes accessed | tf_op | source)
XLA Modules:
  0.0 48.5 jit_solution(18013519125375937788)
XLA Ops:
  0.6 0.0 copy-start.3
  0.6 0.0 copy-start.1
  0.7 0.0 copy-start.4
  0.7 0.9 %slice.3 = f32[128,128]{1,0:T(8,128)S(1)} slice(f32[128,4096]{1,0:T(8,128)} %rec_hbm.1), slice={[0:128], [3968:4096]} | slice | bytes 131072 | tf_op jit(solution)/shard_map/slice | solution.py:351
  1.6 2.3 %collective-permute-start = (f32[128,128]{1,0:T(8,128)S(1)}, f32[128,128]{1,0:T(8,128)S(1)}, u32[]{:S(2)}, u32[]{:S(2)}) collective-permute-start(f32[128,128]{1,0:T(8,128)S(1)} %slice.3), channel_id=1, source_target_pairs={{0,1},{1,2},{2,3},{4,5},{5,6},{6,7},{8,9},{9,10},{10,11},{12,13},{... | collective-permute-start | bytes 196616 | tf_op jit(solution)/shard_map/ppermute | solution.py:351
  4.0 0.0 copy-start.6
  4.0 0.6 %copy-done.6 = f32[64]{0:T(128)S(1)} copy-done((f32[64]{0:T(128)S(1)}, f32[64]{0:T(128)}, u32[]{:S(2)}) %copy-start.6) | copy-done | bytes 280
  4.6 4.9 %filter_and_transform.1 = (f32[1024,128]{1,0:T(8,128)S(1)}, f32[128,128]{1,0:T(8,128)S(1)}) custom-call(f32[1,64]{1,0:T(1,128)S(1)} %bitcast.6, f32[128,4096]{1,0:T(8,128)} %rec_hbm.1, bf16[256,768]{1,0:T(8,128)(2,1)} %constant.16.clone.tab_hbm, f32[256,128]{1,0:T(8,128)} %constant.17.clone.twist_hbm), custom_call_target="tpu_custom_call" | custom-call | flops 1000000000 | bytes 5000000 | tf_op jit(solution)/shard_map/filter_and_transform/pallas_call | solution.py:353
  9.5 0.0 copy-start.9
  9.5 0.0 copy-start.7
  9.5 0.0 copy-start.2
  9.6 0.0 copy-start.5
  9.6 0.0 copy-start.8
  9.6 0.0 collective-permute-done.rim_ref
  9.6 0.0 copy-done.3
  9.6 0.0 copy-done.1
  9.6 0.0 copy-done.4
  9.6 1.5 %whiten.1 = bf16[32,2,16,128]{3,2,1,0:T(8,128)(2,1)} custom-call(f32[1024,128]{1,0:T(8,128)S(1)} %get-tuple-element.8.spec_ref, f32[128,128]{1,0:T(8,128)S(1)} %collective-permute-done.rim_ref, f32[128,128]{1,0:T(8,128)S(1)} %get-tuple-element.9.mean_ref, f32[1,64]{1,0:T(1,128)S(1)} %bitcast.7, bf16[1024,128]{1,0:T(8,128)(2,1)S(1)} %copy-done.4, ...), custom_call_target="tpu_custom_call" | custom-call | tf_op jit(solution)/shard_map/whiten/pallas_call | solution.py:375
  11.2 0.0 copy-start
  11.2 7.1 %all-to-all-start = ((bf16[32,2,16,128]{3,2,1,0:T(8,128)(2,1)}), bf16[32,2,16,128]{3,2,1,0:T(8,128)(2,1)S(1)}, u32[]{:S(2)}, u32[]{:S(2)}) async-start(bf16[32,2,16,128]{3,2,1,0:T(8,128)(2,1)} %whiten.1), calls=%async_computation | async-start | bytes 524288 | tf_op jit(solution)/shard_map/all_to_all | solution.py:388
  18.3 0.0 copy-done.9
  18.3 0.1 copy.15.partner_ref
  18.4 0.0 copy-done.7
  18.4 0.6 %offset_moves.1.moves_ref = bf16[384,512]{1,0:T(8,128)(2,1)S(1)} custom-call(s32[4]{0:T(128)S(1)} %copy-done.7), custom_call_target="tpu_custom_call" | custom-call | tf_op jit(solution)/shard_map/offset_moves/pallas_call | solution.py:393
  19.0 9.9 %all-to-all-done = bf16[32,2,16,128]{3,2,1,0:T(8,128)(2,1)S(1)} async-done(((bf16[32,2,16,128]{3,2,1,0:T(8,128)(2,1)}), bf16[32,2,16,128]{3,2,1,0:T(8,128)(2,1)S(1)}, u32[]{:S(2)}, u32[]{:S(2)}) %all-to-all-start) | async-done | bytes 262176 | tf_op jit(solution)/shard_map/all_to_all | solution.py:388
  28.9 0.0 copy-done.2
  28.9 0.0 copy-done.5
  28.9 0.0 copy-done.8
  28.9 1.5 %cross_spectra.1 = bf16[8,4,56,128]{3,2,1,0:T(8,128)(2,1)S(1)} custom-call(s32[8,3]{1,0:T(8,128)S(1)} %copy.15.partner_ref, s32[8]{0:T(128)S(1)} %copy-done.8, bf16[384,512]{1,0:T(8,128)(2,1)S(1)} %offset_moves.1.moves_ref, bf16[128,128]{1,0:T(8,128)(2,1)S(1)} %copy-done.5, bf16[512,512]{1,0:T(8,128)(2,1)S(1)} %copy-done.2, ...), custom_call_target="tpu_custom_call" | custom-call | tf_op jit(solution)/shard_map/cross_spectra/pallas_call | solution.py:403
  30.4 16.6 %all_to_all.10.spec_ref = bf16[32,56,128]{2,1,0:T(8,128)(2,1)S(1)} all-to-all(bf16[32,56,128]{2,1,0:T(8,128)(2,1)S(1)} %bitcast.4), channel_id=1, replica_groups=mesh['chan'=8,'seg'=4] {'chan','seg'}, dimensions={0} | all-to-all | bytes 917504 | tf_op jit(solution)/shard_map/all_to_all | solution.py:413
  47.0 0.0 copy-done
  47.0 1.5 %lags.1 = (f32[128,1,256]{2,1,0:T(1,128)}, f32[96,256]{1,0:T(8,128)}) custom-call(bf16[32,56,128]{2,1,0:T(8,128)(2,1)S(1)} %all_to_all.10.spec_ref, bf16[512,1024]{1,0:T(8,128)(2,1)S(1)} %copy-done), custom_call_target="tpu_custom_call" | custom-call | tf_op jit(solution)/shard_map/lags/pallas_call | solution.py:418
Async XLA Ops:
  0.6 9.0 %copy-start.3 = (f32[512,128]{1,0:T(8,128)S(1)}, f32[512,128]{1,0:T(8,128)}, u32[]{:S(2)}) copy-start(f32[512,128]{1,0:T(8,128)} %constant.20.clone.share_ref) | copy-start | bytes 786436
  0.6 9.0 %copy-start.1 = (bf16[512,512]{1,0:T(8,128)(2,1)S(1)}, bf16[512,512]{1,0:T(8,128)(2,1)}, u32[]{:S(2)}) copy-start(bf16[512,512]{1,0:T(8,128)(2,1)} %constant.19.clone.band_ref) | copy-start | bytes 1572868
  0.7 9.0 %copy-start.4 = (bf16[1024,128]{1,0:T(8,128)(2,1)S(1)}, bf16[1024,128]{1,0:T(8,128)(2,1)}, u32[]{:S(2)}) copy-start(bf16[1024,128]{1,0:T(8,128)(2,1)} %constant.18.clone.edge_ref) | copy-start | bytes 786436
  1.6 8.0 %collective-permute-start = (f32[128,128]{1,0:T(8,128)S(1)}, f32[128,128]{1,0:T(8,128)S(1)}, u32[]{:S(2)}, u32[]{:S(2)}) collective-permute-start(f32[128,128]{1,0:T(8,128)S(1)} %slice.3), channel_id=1, source_target_pairs={{0,1},{1,2},{2,3},{4,5},{5,6},{6,7},{8,9},{9,10},{10,11},{12,13},{... | collective-permute-start | bytes 196616 | tf_op jit(solution)/shard_map/ppermute | solution.py:351
  4.0 0.7 %copy-start.6 = (f32[64]{0:T(128)S(1)}, f32[64]{0:T(128)}, u32[]{:S(2)}) copy-start(f32[64]{0:T(128)} %param.14) | copy-start | bytes 772
  9.5 8.8 %copy-start.9 = (s32[8,3]{0,1:T(4,128)S(1)}, s32[8,3]{0,1:T(4,128)}, u32[]{:S(2)}) copy-start(s32[8,3]{0,1:T(4,128)} %param.16) | copy-start | bytes 292
  9.5 8.9 %copy-start.7 = (s32[4]{0:T(128)S(1)}, s32[4]{0:T(128)}, u32[]{:S(2)}) copy-start(s32[4]{0:T(128)} %offs_ref) | copy-start | bytes 52
  9.5 19.4 %copy-start.2 = (bf16[512,512]{1,0:T(8,128)(2,1)S(1)}, bf16[512,512]{1,0:T(8,128)(2,1)}, u32[]{:S(2)}) copy-start(bf16[512,512]{1,0:T(8,128)(2,1)} %constant.22.clone.pack_ref) | copy-start | bytes 1572868
  9.6 19.4 %copy-start.5 = (bf16[128,128]{1,0:T(8,128)(2,1)S(1)}, bf16[128,128]{1,0:T(8,128)(2,1)}, u32[]{:S(2)}) copy-start(bf16[128,128]{1,0:T(8,128)(2,1)} %constant.21.clone.flip_ref) | copy-start | bytes 98308
  9.6 19.3 %copy-start.8 = (s32[8]{0:T(128)S(1)}, s32[8]{0:T(128)}, u32[]{:S(2)}) copy-start(s32[8]{0:T(128)} %count_ref.1) | copy-start | bytes 100
  11.2 35.8 %copy-start = (bf16[512,1024]{1,0:T(8,128)(2,1)S(1)}, bf16[512,1024]{1,0:T(8,128)(2,1)}, u32[]{:S(2)}) copy-start(bf16[512,1024]{1,0:T(8,128)(2,1)} %constant.23.clone.inv_ref) | copy-start | bytes 3145732
  11.2 17.7 %all-to-all-start = ((bf16[32,2,16,128]{3,2,1,0:T(8,128)(2,1)}), bf16[32,2,16,128]{3,2,1,0:T(8,128)(2,1)S(1)}, u32[]{:S(2)}, u32[]{:S(2)}) async-start(bf16[32,2,16,128]{3,2,1,0:T(8,128)(2,1)} %whiten.1), calls=%async_computation | async-start | bytes 524288 | tf_op jit(solution)/shard_map/all_to_all | solution.py:388

commit v3 on v2

--- a/solution.py
+++ b/solution.py
@@ -92,23 +92,34 @@
     return lax.dot_general(a, b, (((1,), (1,)), ((), ())), preferred_element_type=F32)
 
 
-def tap_rows(taps_ref, rows):
+def tap_rows(taps):
     width = LANES + STEP
     square = (TAPS, TAPS)
     diagonal = lax.broadcasted_iota(jnp.int32, square, 0) == lax.broadcasted_iota(jnp.int32, square, 1)
-    column_taps = jnp.sum(jnp.where(diagonal, taps_ref[...], 0.0), axis=1, keepdims=True)
+    column_taps = jnp.sum(jnp.where(diagonal, taps, 0.0), axis=1, keepdims=True)
     tap = lax.broadcasted_iota(jnp.int32, (TAPS, width), 0)
     column = lax.broadcasted_iota(jnp.int32, (TAPS, width), 1)
     placed = jnp.where(column == LANES + DECIM - 1 - tap, column_taps, 0.0)
-    spread = jnp.broadcast_to(jnp.sum(placed, axis=0, keepdims=True), (rows, width))
+    spread = jnp.broadcast_to(jnp.sum(placed, axis=0, keepdims=True), (OUT_BLOCK, width))
     return pltpu.roll(spread, 0, 1, stride=DECIM, stride_axis=0)
 
 
 def spectrum_kernel(
-    taps_ref, rec_hbm, tab_hbm, twist_hbm, spec_ref, mean_ref, rec_ref, tab_ref, twist_ref, sems
+    taps_hbm,
+    rec_hbm,
+    tab_hbm,
+    twist_hbm,
+    spec_ref,
+    mean_ref,
+    head_ref,
+    taps_ref,
+    rec_ref,
+    tab_ref,
+    twist_ref,
+    sems,
 ):
     blocks = rec_ref.shape[1] // STEP
-    copies = []
+    copies = [(taps_hbm, taps_ref)]
     for j in range(blocks):
         part = pl.ds(j * STEP, STEP)
         copies.append((rec_hbm.at[:, part], rec_ref.at[:, part]))
@@ -116,27 +127,30 @@
     copies = [pltpu.make_async_copy(*c, sems.at[i]) for i, c in enumerate(copies)]
     for copy in copies:
         copy.start()
-    taps_high, taps_low = split(tap_rows(taps_ref, OUT_BLOCK))
-    taps = jnp.concatenate([taps_high, taps_high, taps_low], axis=1)
+    copies[0].wait()
+    table = tap_rows(taps_ref[...])
+    head_ref[...] = table[:GROUP, :LANES]
+    taps_high, taps_low = split(table.T)
+    taps_both = jnp.concatenate([taps_high, taps_low], axis=1)
     before = [jnp.zeros((LANES, LANES), BF16)] * 2
-    windows, pieces = [], []
+    outputs = []
     for j in range(blocks):
-        copies[j].wait()
+        copies[1 + j].wait()
         chunk = rec_ref[:, j * STEP : (j + 1) * STEP]
         if j == 0:
             mean = jnp.sum(chunk, axis=1, keepdims=True) * (1.0 / STEP)
         high, low = split(chunk - mean)
-        windows.append(jnp.concatenate([before[0], high, before[1], low, before[0], high], axis=1))
+        wide = mm(jnp.concatenate([before[0], high], axis=1), taps_both)
+        rest = mm(jnp.concatenate([before[1], low], axis=1), taps_high)
+        outputs.append((wide[:, :LANES] + wide[:, LANES:] + rest).T)
         before = [high[:, STEP - LANES :], low[:, STEP - LANES :]]
-        if j % 2:
-            pair = mm_nt(taps, jnp.concatenate(windows[-2:], axis=0))
-            pieces.append(jnp.concatenate([pair[:, :LANES], pair[:, LANES:]], axis=0))
+    pieces = [jnp.concatenate(outputs[j : j + 2], axis=0) for j in range(0, blocks, 2)]
     mean_ref[...] = jnp.broadcast_to(mean, mean_ref.shape)
     even, odd = pieces[0] + pieces[2], pieces[1] + pieces[3]
     a, b = pieces[0] - pieces[2], pieces[1] - pieces[3]
     whole, half = even + odd, even - odd
     whole = whole - jnp.sum(whole, axis=0, keepdims=True) * (1.0 / DEPTH)
-    copies[blocks].wait()
+    copies[blocks + 1].wait()
     c1, s1, c2, s2, c3, s3 = [twist_ref[:, i : i + 1] for i in range(6)]
     inputs = [
         whole,
@@ -150,7 +164,7 @@
     parts = [split(value) for value in inputs]
     high = jnp.concatenate([p[0] for p in parts], axis=1)
     low = jnp.concatenate([p[1] for p in parts], axis=1)
-    copies[blocks + 1].wait()
+    copies[blocks + 2].wait()
     out = mm(tab_ref[...], jnp.concatenate([high, low, high], axis=0))
     out = out.reshape(FAR_BINS // GROUP, 2, GROUP, out.shape[1])
     rows = 2 * FAR_BINS
@@ -167,9 +181,9 @@
 
 
 def whiten_kernel(
-    spec_ref, rim_ref, mean_ref, taps_ref, edge_ref, band_ref, share_ref, white_ref
+    spec_ref, rim_ref, mean_ref, head_ref, edge_ref, band_ref, share_ref, white_ref
 ):
-    head_high, head_low = split(tap_rows(taps_ref, GROUP)[:, :LANES])
+    head_high, head_low = split(head_ref[...])
     rim_high, rim_low = split(rim_ref[...] - mean_ref[...])
     history = mm_nt(
         jnp.concatenate([head_high, head_high, head_low], axis=1),
@@ -350,26 +364,28 @@
     route = [(i, i + 1) for i in range(seg_count - 1)]
     rim = lax.ppermute(recording[:, length - LANES :], "seg", route)
     taps = filter_taps.reshape(1, TAPS)
-    spec, mean = pl.pallas_call(
+    spec, mean, head = pl.pallas_call(
         spectrum_kernel,
         out_shape=[
             jax.ShapeDtypeStruct((2 * BINS, LANES), F32),
             jax.ShapeDtypeStruct((LANES, LANES), F32),
+            jax.ShapeDtypeStruct((GROUP, LANES), F32),
         ],
-        in_specs=vmem(1) + hbm(3),
-        out_specs=vmem(2),
+        in_specs=hbm(4),
+        out_specs=vmem(3),
         scratch_shapes=[
+            pltpu.VMEM((1, TAPS), F32),
             pltpu.VMEM((chans, length), F32),
             pltpu.VMEM((2 * FAR_BINS, 3 * DEPTH), BF16),
             pltpu.VMEM((DEPTH, LANES), F32),
-            pltpu.SemaphoreType.DMA((length // STEP + 2,)),
+            pltpu.SemaphoreType.DMA((length // STEP + 3,)),
         ],
         compiler_params=PARAMS,
         cost_estimate=pl.CostEstimate(
             flops=1_000_000_000, bytes_accessed=5_000_000, transcendentals=0
         ),
         name="filter_and_transform",
-    )(taps, in_hbm(recording), in_hbm(short_table()), in_hbm(twiddle_table()))
+    )(in_hbm(taps), in_hbm(recording), in_hbm(short_table()), in_hbm(twiddle_table()))
 
     band, band_share = band_tables()
     white = pl.pallas_call(
@@ -379,7 +395,7 @@
         out_specs=pl.BlockSpec(memory_space=pltpu.VMEM),
         compiler_params=PARAMS,
         name="whiten",
-    )(spec, rim, mean, taps, edge_table(), band, band_share)
+    )(spec, rim, mean, head, edge_table(), band, band_share)
 
     white, offsets = lax.optimization_barrier((white, offsets))
     if bins != GROUP:

time: 48.8 us -> 47.9 us (0.982)
  local copies, waits for them, and re-layouts: 1.72 us -> 1.07 us
    unnamed x21 -> x19, local copies, waits for them, and re-layouts: 0.79 us -> 0.14 us
where the time goes in v3:
time: 47.9 us; the launch traced here: 47.6 us
  blocking collectives  16.6 us (35%)
  waiting for transfers between devices  9.87 us (21%)
  Pallas kernels  9.84 us (21%)
  starting transfers between devices  9.47 us (20%)
  local copies, waits for them, and re-layouts  1.07 us (2%)
  between operations  0.78 us (2%)
    all_to_all x1, blocking collectives, body(): summed = lax.all_to_all(crossed, ('chan', 'seg'), 0, 0, tiled=True)  16.6 us
    all_to_all x1, waiting for transfers between devices, body(): moved = lax.all_to_all(white, ('chan', 'seg'), 0, 0, tiled=True)  9.87 us
    all_to_all x1, starting transfers between devices, body(): moved = lax.all_to_all(white, ('chan', 'seg'), 0, 0, tiled=True)  7.12 us
    pallas_call x1, Pallas kernels, body(): pl.pallas_call(spectrum_kernel, out_shape=[jax.ShapeDtypeStruct((2 * BINS...  4.76 us
    ppermute x1, starting transfers between devices, body(): rim = lax.ppermute(recording[:, length - LANES:], 'seg', route)  2.35 us
    pallas_call x1, Pallas kernels, body(): pl.pallas_call(functools.partial(lag_kernel, slots), out_shape=[jax.Shape...  1.53 us
    pallas_call x1, Pallas kernels, body(): pl.pallas_call(cross_kernel, out_shape=jax.ShapeDtypeStruct((chan_count,...  1.51 us
    pallas_call x1, Pallas kernels, body(): pl.pallas_call(whiten_kernel, out_shape=jax.ShapeDtypeStruct((GROUPS, 2,...  1.41 us
  transfers between devices with their start and end apart: 2, of which 1 were waited for; matrix products, arithmetic and copies ran while one was open for 0% of the time, Pallas kernels for 11%

profile of v3, /device:TPU:0, one launch (start us, length us, event | category | flops | bytes accessed | tf_op | source)
XLA Modules:
  0.0 47.6 jit_solution(13966516402959450967)
XLA Ops:
  0.6 0.0 copy-start.3
  0.6 0.0 copy-start.2
  0.7 0.0 copy-start.4
  0.7 0.9 %slice.3 = f32[128,128]{1,0:T(8,128)S(1)} slice(f32[128,4096]{1,0:T(8,128)} %rec_hbm.1), slice={[0:128], [3968:4096]} | slice | bytes 131072 | tf_op jit(solution)/shard_map/slice | solution.py:365
  1.6 2.3 %collective-permute-start = (f32[128,128]{1,0:T(8,128)S(1)}, f32[128,128]{1,0:T(8,128)S(1)}, u32[]{:S(2)}, u32[]{:S(2)}) collective-permute-start(f32[128,128]{1,0:T(8,128)S(1)} %slice.3), channel_id=1, source_target_pairs={{0,1},{1,2},{2,3},{4,5},{5,6},{6,7},{8,9},{9,10},{10,11},{12,13},{... | collective-permute-start | bytes 196616 | tf_op jit(solution)/shard_map/ppermute | solution.py:365
  4.0 4.8 %filter_and_transform.1 = (f32[1024,128]{1,0:T(8,128)S(1)}, f32[128,128]{1,0:T(8,128)S(1)}, f32[16,128]{1,0:T(8,128)S(1)}) custom-call(f32[1,64]{1,0:T(1,128)} %bitcast.7, f32[128,4096]{1,0:T(8,128)} %rec_hbm.1, bf16[256,768]{1,0:T(8,128)(2,1)} %constant.16.clone.tab_hbm, f32[256,128]{1,0:T(8,128)} %constant.17.clone.twist_hbm), custom_call_target="tpu_custom_call" | custom-call | flops 1000000000 | bytes 5000000 | tf_op jit(solution)/shard_map/filter_and_transform/pallas_call | solution.py:367
  8.7 0.0 copy-start.8
  8.7 0.0 copy-start.6
  8.7 0.0 copy-start.1
  8.8 0.0 copy-start.5
  8.8 0.0 copy-start.7
  8.8 0.0 collective-permute-done.rim_ref
  8.8 0.0 copy-done.3
  8.8 0.0 copy-done.2
  8.8 0.0 copy-done.4
  8.8 1.4 %whiten.1 = bf16[32,2,16,128]{3,2,1,0:T(8,128)(2,1)} custom-call(f32[1024,128]{1,0:T(8,128)S(1)} %get-tuple-element.9.spec_ref, f32[128,128]{1,0:T(8,128)S(1)} %collective-permute-done.rim_ref, f32[128,128]{1,0:T(8,128)S(1)} %get-tuple-element.10.mean_ref, f32[16,128]{1,0:T(8,128)S(1)} %get-tuple-element.11.head_ref, bf16[1024,128]{1,0:T(8,128)(2,1)S(1)} %copy-done.4, ...), custom_call_target="tpu_custom_call" | custom-call | tf_op jit(solution)/shard_map/whiten/pallas_call | solution.py:391
  10.2 0.0 copy-start
  10.2 7.1 %all-to-all-start = ((bf16[32,2,16,128]{3,2,1,0:T(8,128)(2,1)}), bf16[32,2,16,128]{3,2,1,0:T(8,128)(2,1)S(1)}, u32[]{:S(2)}, u32[]{:S(2)}) async-start(bf16[32,2,16,128]{3,2,1,0:T(8,128)(2,1)} %whiten.1), calls=%async_computation | async-start | bytes 524288 | tf_op jit(solution)/shard_map/all_to_all | solution.py:404
  17.4 0.0 copy-done.8
  17.4 0.1 copy.15.partner_ref
  17.5 0.0 copy-done.6
  17.5 0.6 %offset_moves.1.moves_ref = bf16[384,512]{1,0:T(8,128)(2,1)S(1)} custom-call(s32[4]{0:T(128)S(1)} %copy-done.6), custom_call_target="tpu_custom_call" | custom-call | tf_op jit(solution)/shard_map/offset_moves/pallas_call | solution.py:409
  18.1 9.9 %all-to-all-done = bf16[32,2,16,128]{3,2,1,0:T(8,128)(2,1)S(1)} async-done(((bf16[32,2,16,128]{3,2,1,0:T(8,128)(2,1)}), bf16[32,2,16,128]{3,2,1,0:T(8,128)(2,1)S(1)}, u32[]{:S(2)}, u32[]{:S(2)}) %all-to-all-start) | async-done | bytes 262176 | tf_op jit(solution)/shard_map/all_to_all | solution.py:404
  28.0 0.0 copy-done.1
  28.0 0.0 copy-done.5
  28.0 0.0 copy-done.7
  28.0 1.5 %cross_spectra.1 = bf16[8,4,56,128]{3,2,1,0:T(8,128)(2,1)S(1)} custom-call(s32[8,3]{1,0:T(8,128)S(1)} %copy.15.partner_ref, s32[8]{0:T(128)S(1)} %copy-done.7, bf16[384,512]{1,0:T(8,128)(2,1)S(1)} %offset_moves.1.moves_ref, bf16[128,128]{1,0:T(8,128)(2,1)S(1)} %copy-done.5, bf16[512,512]{1,0:T(8,128)(2,1)S(1)} %copy-done.1, ...), custom_call_target="tpu_custom_call" | custom-call | tf_op jit(solution)/shard_map/cross_spectra/pallas_call | solution.py:419
  29.5 16.6 %all_to_all.10.spec_ref = bf16[32,56,128]{2,1,0:T(8,128)(2,1)S(1)} all-to-all(bf16[32,56,128]{2,1,0:T(8,128)(2,1)S(1)} %bitcast.4), channel_id=1, replica_groups=mesh['chan'=8,'seg'=4] {'chan','seg'}, dimensions={0} | all-to-all | bytes 917504 | tf_op jit(solution)/shard_map/all_to_all | solution.py:429
  46.1 0.0 copy-done
  46.1 1.5 %lags.1 = (f32[128,1,256]{2,1,0:T(1,128)}, f32[96,256]{1,0:T(8,128)}) custom-call(bf16[32,56,128]{2,1,0:T(8,128)(2,1)S(1)} %all_to_all.10.spec_ref, bf16[512,1024]{1,0:T(8,128)(2,1)S(1)} %copy-done), custom_call_target="tpu_custom_call" | custom-call | tf_op jit(solution)/shard_map/lags/pallas_call | solution.py:434
Async XLA Ops:
  0.6 8.2 %copy-start.3 = (f32[512,128]{1,0:T(8,128)S(1)}, f32[512,128]{1,0:T(8,128)}, u32[]{:S(2)}) copy-start(f32[512,128]{1,0:T(8,128)} %constant.20.clone.share_ref) | copy-start | bytes 786436
  0.6 8.2 %copy-start.2 = (bf16[512,512]{1,0:T(8,128)(2,1)S(1)}, bf16[512,512]{1,0:T(8,128)(2,1)}, u32[]{:S(2)}) copy-start(bf16[512,512]{1,0:T(8,128)(2,1)} %constant.19.clone.band_ref) | copy-start | bytes 1572868
  0.7 8.2 %copy-start.4 = (bf16[1024,128]{1,0:T(8,128)(2,1)S(1)}, bf16[1024,128]{1,0:T(8,128)(2,1)}, u32[]{:S(2)}) copy-start(bf16[1024,128]{1,0:T(8,128)(2,1)} %constant.18.clone.edge_ref) | copy-start | bytes 786436
  1.6 7.2 %collective-permute-start = (f32[128,128]{1,0:T(8,128)S(1)}, f32[128,128]{1,0:T(8,128)S(1)}, u32[]{:S(2)}, u32[]{:S(2)}) collective-permute-start(f32[128,128]{1,0:T(8,128)S(1)} %slice.3), channel_id=1, source_target_pairs={{0,1},{1,2},{2,3},{4,5},{5,6},{6,7},{8,9},{9,10},{10,11},{12,13},{... | collective-permute-start | bytes 196616 | tf_op jit(solution)/shard_map/ppermute | solution.py:365
  8.7 8.6 %copy-start.8 = (s32[8,3]{0,1:T(4,128)S(1)}, s32[8,3]{0,1:T(4,128)}, u32[]{:S(2)}) copy-start(s32[8,3]{0,1:T(4,128)} %param.16) | copy-start | bytes 292
  8.7 8.7 %copy-start.6 = (s32[4]{0:T(128)S(1)}, s32[4]{0:T(128)}, u32[]{:S(2)}) copy-start(s32[4]{0:T(128)} %offs_ref) | copy-start | bytes 52
  8.7 19.2 %copy-start.1 = (bf16[512,512]{1,0:T(8,128)(2,1)S(1)}, bf16[512,512]{1,0:T(8,128)(2,1)}, u32[]{:S(2)}) copy-start(bf16[512,512]{1,0:T(8,128)(2,1)} %constant.22.clone.pack_ref) | copy-start | bytes 1572868
  8.8 19.2 %copy-start.5 = (bf16[128,128]{1,0:T(8,128)(2,1)S(1)}, bf16[128,128]{1,0:T(8,128)(2,1)}, u32[]{:S(2)}) copy-start(bf16[128,128]{1,0:T(8,128)(2,1)} %constant.21.clone.flip_ref) | copy-start | bytes 98308
  8.8 19.2 %copy-start.7 = (s32[8]{0:T(128)S(1)}, s32[8]{0:T(128)}, u32[]{:S(2)}) copy-start(s32[8]{0:T(128)} %count_ref.1) | copy-start | bytes 100
  10.2 35.8 %copy-start = (bf16[512,1024]{1,0:T(8,128)(2,1)S(1)}, bf16[512,1024]{1,0:T(8,128)(2,1)}, u32[]{:S(2)}) copy-start(bf16[512,1024]{1,0:T(8,128)(2,1)} %constant.23.clone.inv_ref) | copy-start | bytes 3145732
  10.2 17.7 %all-to-all-start = ((bf16[32,2,16,128]{3,2,1,0:T(8,128)(2,1)}), bf16[32,2,16,128]{3,2,1,0:T(8,128)(2,1)S(1)}, u32[]{:S(2)}, u32[]{:S(2)}) async-start(bf16[32,2,16,128]{3,2,1,0:T(8,128)(2,1)} %whiten.1), calls=%async_computation | async-start | bytes 524288 | tf_op jit(solution)/shard_map/all_to_all | solution.py:404

commit v4 on v3

--- a/solution.py
+++ b/solution.py
@@ -134,16 +134,21 @@
     taps_both = jnp.concatenate([taps_high, taps_low], axis=1)
     before = [jnp.zeros((LANES, LANES), BF16)] * 2
     outputs = []
-    for j in range(blocks):
-        copies[1 + j].wait()
-        chunk = rec_ref[:, j * STEP : (j + 1) * STEP]
-        if j == 0:
-            mean = jnp.sum(chunk, axis=1, keepdims=True) * (1.0 / STEP)
-        high, low = split(chunk - mean)
-        wide = mm(jnp.concatenate([before[0], high], axis=1), taps_both)
-        rest = mm(jnp.concatenate([before[1], low], axis=1), taps_high)
-        outputs.append((wide[:, :LANES] + wide[:, LANES:] + rest).T)
-        before = [high[:, STEP - LANES :], low[:, STEP - LANES :]]
+    for first in range(0, blocks, blocks // 2):
+        windows = ([], [])
+        for j in range(first, first + blocks // 2):
+            copies[1 + j].wait()
+        for j in range(first, first + blocks // 2):
+            chunk = rec_ref[:, j * STEP : (j + 1) * STEP]
+            if j == 0:
+                mean = jnp.sum(chunk, axis=1, keepdims=True) * (1.0 / STEP)
+            for i, value in enumerate(split(chunk - mean)):
+                windows[i].append(jnp.concatenate([before[i], value], axis=1))
+                before[i] = value[:, STEP - LANES :]
+        wide = mm(jnp.concatenate(windows[0], axis=0), taps_both)
+        rest = mm(jnp.concatenate(windows[1], axis=0), taps_high)
+        total = wide[:, :LANES] + wide[:, LANES:] + rest
+        outputs += [total[t * LANES : (t + 1) * LANES].T for t in range(blocks // 2)]
     pieces = [jnp.concatenate(outputs[j : j + 2], axis=0) for j in range(0, blocks, 2)]
     mean_ref[...] = jnp.broadcast_to(mean, mean_ref.shape)
     even, odd = pieces[0] + pieces[2], pieces[1] + pieces[3]

time: 47.9 us -> 46.7 us (0.975)
  Pallas kernels: 9.84 us -> 8.65 us
    pallas_call x1, Pallas kernels: 4.76 us -> 3.58 us  [body(): pl.pallas_call(spectrum_kernel, out_shape=[jax.ShapeDtypeStruct((2 * BINS...]
  transfers between devices with their start and end apart: 2 -> 2, of which waited for: 1 -> 1; matrix products, arithmetic and copies ran while one was open for 0% -> 0% of each run, Pallas kernels for 11% -> 9%
where the time goes in v4:
time: 46.7 us; the launch traced here: 46.4 us
  blocking collectives  16.6 us (36%)
  waiting for transfers between devices  9.87 us (21%)
  starting transfers between devices  9.47 us (20%)
  Pallas kernels  8.65 us (19%)
  local copies, waits for them, and re-layouts  1.07 us (2%)
  between operations  0.78 us (2%)
    all_to_all x1, blocking collectives, body(): summed = lax.all_to_all(crossed, ('chan', 'seg'), 0, 0, tiled=True)  16.6 us
    all_to_all x1, waiting for transfers between devices, body(): moved = lax.all_to_all(white, ('chan', 'seg'), 0, 0, tiled=True)  9.87 us
    all_to_all x1, starting transfers between devices, body(): moved = lax.all_to_all(white, ('chan', 'seg'), 0, 0, tiled=True)  7.12 us
    pallas_call x1, Pallas kernels, body(): pl.pallas_call(spectrum_kernel, out_shape=[jax.ShapeDtypeStruct((2 * BINS...  3.58 us
    ppermute x1, starting transfers between devices, body(): rim = lax.ppermute(recording[:, length - LANES:], 'seg', route)  2.35 us
    pallas_call x1, Pallas kernels, body(): pl.pallas_call(functools.partial(lag_kernel, slots), out_shape=[jax.Shape...  1.53 us
    pallas_call x1, Pallas kernels, body(): pl.pallas_call(cross_kernel, out_shape=jax.ShapeDtypeStruct((chan_count,...  1.51 us
    pallas_call x1, Pallas kernels, body(): pl.pallas_call(whiten_kernel, out_shape=jax.ShapeDtypeStruct((GROUPS, 2,...  1.41 us
  transfers between devices with their start and end apart: 2, of which 1 were waited for; matrix products, arithmetic and copies ran while one was open for 0% of the time, Pallas kernels for 9%

profile of v4, /device:TPU:0, one launch (start us, length us, event | category | flops | bytes accessed | tf_op | source)
XLA Modules:
  0.0 46.4 jit_solution(16587265932674998746)
XLA Ops:
  0.6 0.0 copy-start.3
  0.6 0.0 copy-start.2
  0.7 0.0 copy-start.4
  0.7 0.9 %slice.3 = f32[128,128]{1,0:T(8,128)S(1)} slice(f32[128,4096]{1,0:T(8,128)} %rec_hbm.1), slice={[0:128], [3968:4096]} | slice | bytes 131072 | tf_op jit(solution)/shard_map/slice | solution.py:370
  1.6 2.3 %collective-permute-start = (f32[128,128]{1,0:T(8,128)S(1)}, f32[128,128]{1,0:T(8,128)S(1)}, u32[]{:S(2)}, u32[]{:S(2)}) collective-permute-start(f32[128,128]{1,0:T(8,128)S(1)} %slice.3), channel_id=1, source_target_pairs={{0,1},{1,2},{2,3},{4,5},{5,6},{6,7},{8,9},{9,10},{10,11},{12,13},{... | collective-permute-start | bytes 196616 | tf_op jit(solution)/shard_map/ppermute | solution.py:370
  4.0 3.6 %filter_and_transform.1 = (f32[1024,128]{1,0:T(8,128)S(1)}, f32[128,128]{1,0:T(8,128)S(1)}, f32[16,128]{1,0:T(8,128)S(1)}) custom-call(f32[1,64]{1,0:T(1,128)} %bitcast.7, f32[128,4096]{1,0:T(8,128)} %rec_hbm.1, bf16[256,768]{1,0:T(8,128)(2,1)} %constant.16.clone.tab_hbm, f32[256,128]{1,0:T(8,128)} %constant.17.clone.twist_hbm), custom_call_target="tpu_custom_call" | custom-call | flops 1000000000 | bytes 5000000 | tf_op jit(solution)/shard_map/filter_and_transform/pallas_call | solution.py:372
  7.5 0.0 copy-start.8
  7.5 0.0 copy-start.6
  7.6 0.0 copy-start.1
  7.6 0.0 copy-start.5
  7.6 0.0 copy-start.7
  7.6 0.0 collective-permute-done.rim_ref
  7.6 0.0 copy-done.3
  7.6 0.0 copy-done.2
  7.6 0.0 copy-done.4
  7.6 1.4 %whiten.1 = bf16[32,2,16,128]{3,2,1,0:T(8,128)(2,1)} custom-call(f32[1024,128]{1,0:T(8,128)S(1)} %get-tuple-element.9.spec_ref, f32[128,128]{1,0:T(8,128)S(1)} %collective-permute-done.rim_ref, f32[128,128]{1,0:T(8,128)S(1)} %get-tuple-element.10.mean_ref, f32[16,128]{1,0:T(8,128)S(1)} %get-tuple-element.11.head_ref, bf16[1024,128]{1,0:T(8,128)(2,1)S(1)} %copy-done.4, ...), custom_call_target="tpu_custom_call" | custom-call | tf_op jit(solution)/shard_map/whiten/pallas_call | solution.py:396
  9.0 0.0 copy-start
  9.1 7.1 %all-to-all-start = ((bf16[32,2,16,128]{3,2,1,0:T(8,128)(2,1)}), bf16[32,2,16,128]{3,2,1,0:T(8,128)(2,1)S(1)}, u32[]{:S(2)}, u32[]{:S(2)}) async-start(bf16[32,2,16,128]{3,2,1,0:T(8,128)(2,1)} %whiten.1), calls=%async_computation | async-start | bytes 524288 | tf_op jit(solution)/shard_map/all_to_all | solution.py:409
  16.2 0.0 copy-done.8
  16.2 0.1 copy.15.partner_ref
  16.3 0.0 copy-done.6
  16.3 0.6 %offset_moves.1.moves_ref = bf16[384,512]{1,0:T(8,128)(2,1)S(1)} custom-call(s32[4]{0:T(128)S(1)} %copy-done.6), custom_call_target="tpu_custom_call" | custom-call | tf_op jit(solution)/shard_map/offset_moves/pallas_call | solution.py:414
  16.9 9.9 %all-to-all-done = bf16[32,2,16,128]{3,2,1,0:T(8,128)(2,1)S(1)} async-done(((bf16[32,2,16,128]{3,2,1,0:T(8,128)(2,1)}), bf16[32,2,16,128]{3,2,1,0:T(8,128)(2,1)S(1)}, u32[]{:S(2)}, u32[]{:S(2)}) %all-to-all-start) | async-done | bytes 262176 | tf_op jit(solution)/shard_map/all_to_all | solution.py:409
  26.8 0.0 copy-done.1
  26.8 0.0 copy-done.5
  26.8 0.0 copy-done.7
  26.8 1.5 %cross_spectra.1 = bf16[8,4,56,128]{3,2,1,0:T(8,128)(2,1)S(1)} custom-call(s32[8,3]{1,0:T(8,128)S(1)} %copy.15.partner_ref, s32[8]{0:T(128)S(1)} %copy-done.7, bf16[384,512]{1,0:T(8,128)(2,1)S(1)} %offset_moves.1.moves_ref, bf16[128,128]{1,0:T(8,128)(2,1)S(1)} %copy-done.5, bf16[512,512]{1,0:T(8,128)(2,1)S(1)} %copy-done.1, ...), custom_call_target="tpu_custom_call" | custom-call | tf_op jit(solution)/shard_map/cross_spectra/pallas_call | solution.py:424
  28.3 16.6 %all_to_all.10.spec_ref = bf16[32,56,128]{2,1,0:T(8,128)(2,1)S(1)} all-to-all(bf16[32,56,128]{2,1,0:T(8,128)(2,1)S(1)} %bitcast.4), channel_id=1, replica_groups=mesh['chan'=8,'seg'=4] {'chan','seg'}, dimensions={0} | all-to-all | bytes 917504 | tf_op jit(solution)/shard_map/all_to_all | solution.py:434
  44.9 0.0 copy-done
  44.9 1.5 %lags.1 = (f32[128,1,256]{2,1,0:T(1,128)}, f32[96,256]{1,0:T(8,128)}) custom-call(bf16[32,56,128]{2,1,0:T(8,128)(2,1)S(1)} %all_to_all.10.spec_ref, bf16[512,1024]{1,0:T(8,128)(2,1)S(1)} %copy-done), custom_call_target="tpu_custom_call" | custom-call | tf_op jit(solution)/shard_map/lags/pallas_call | solution.py:439
Async XLA Ops:
  0.6 7.0 %copy-start.3 = (f32[512,128]{1,0:T(8,128)S(1)}, f32[512,128]{1,0:T(8,128)}, u32[]{:S(2)}) copy-start(f32[512,128]{1,0:T(8,128)} %constant.20.clone.share_ref) | copy-start | bytes 786436
  0.6 7.0 %copy-start.2 = (bf16[512,512]{1,0:T(8,128)(2,1)S(1)}, bf16[512,512]{1,0:T(8,128)(2,1)}, u32[]{:S(2)}) copy-start(bf16[512,512]{1,0:T(8,128)(2,1)} %constant.19.clone.band_ref) | copy-start | bytes 1572868
  0.7 7.0 %copy-start.4 = (bf16[1024,128]{1,0:T(8,128)(2,1)S(1)}, bf16[1024,128]{1,0:T(8,128)(2,1)}, u32[]{:S(2)}) copy-start(bf16[1024,128]{1,0:T(8,128)(2,1)} %constant.18.clone.edge_ref) | copy-start | bytes 786436
  1.6 6.0 %collective-permute-start = (f32[128,128]{1,0:T(8,128)S(1)}, f32[128,128]{1,0:T(8,128)S(1)}, u32[]{:S(2)}, u32[]{:S(2)}) collective-permute-start(f32[128,128]{1,0:T(8,128)S(1)} %slice.3), channel_id=1, source_target_pairs={{0,1},{1,2},{2,3},{4,5},{5,6},{6,7},{8,9},{9,10},{10,11},{12,13},{... | collective-permute-start | bytes 196616 | tf_op jit(solution)/shard_map/ppermute | solution.py:370
  7.5 8.6 %copy-start.8 = (s32[8,3]{0,1:T(4,128)S(1)}, s32[8,3]{0,1:T(4,128)}, u32[]{:S(2)}) copy-start(s32[8,3]{0,1:T(4,128)} %param.16) | copy-start | bytes 292
  7.5 8.7 %copy-start.6 = (s32[4]{0:T(128)S(1)}, s32[4]{0:T(128)}, u32[]{:S(2)}) copy-start(s32[4]{0:T(128)} %offs_ref) | copy-start | bytes 52
  7.6 19.2 %copy-start.1 = (bf16[512,512]{1,0:T(8,128)(2,1)S(1)}, bf16[512,512]{1,0:T(8,128)(2,1)}, u32[]{:S(2)}) copy-start(bf16[512,512]{1,0:T(8,128)(2,1)} %constant.22.clone.pack_ref) | copy-start | bytes 1572868
  7.6 19.2 %copy-start.5 = (bf16[128,128]{1,0:T(8,128)(2,1)S(1)}, bf16[128,128]{1,0:T(8,128)(2,1)}, u32[]{:S(2)}) copy-start(bf16[128,128]{1,0:T(8,128)(2,1)} %constant.21.clone.flip_ref) | copy-start | bytes 98308
  7.6 19.2 %copy-start.7 = (s32[8]{0:T(128)S(1)}, s32[8]{0:T(128)}, u32[]{:S(2)}) copy-start(s32[8]{0:T(128)} %count_ref.1) | copy-start | bytes 100
  9.0 35.8 %copy-start = (bf16[512,1024]{1,0:T(8,128)(2,1)S(1)}, bf16[512,1024]{1,0:T(8,128)(2,1)}, u32[]{:S(2)}) copy-start(bf16[512,1024]{1,0:T(8,128)(2,1)} %constant.23.clone.inv_ref) | copy-start | bytes 3145732
  9.1 17.7 %all-to-all-start = ((bf16[32,2,16,128]{3,2,1,0:T(8,128)(2,1)}), bf16[32,2,16,128]{3,2,1,0:T(8,128)(2,1)S(1)}, u32[]{:S(2)}, u32[]{:S(2)}) async-start(bf16[32,2,16,128]{3,2,1,0:T(8,128)(2,1)} %whiten.1), calls=%async_computation | async-start | bytes 524288 | tf_op jit(solution)/shard_map/all_to_all | solution.py:409

commit v5 on v4

--- a/solution.py
+++ b/solution.py
@@ -186,10 +186,15 @@
 
 
 def whiten_kernel(
-    spec_ref, rim_ref, mean_ref, head_ref, edge_ref, band_ref, share_ref, white_ref
+    rims_hbm, spec_ref, mean_ref, head_ref, edge_ref, band_ref, share_ref, white_ref, rim_ref, sem
 ):
+    place = lax.axis_index("seg")
+    copy = pltpu.make_async_copy(rims_hbm.at[jnp.maximum(place - 1, 0)], rim_ref, sem)
+    copy.start()
     head_high, head_low = split(head_ref[...])
-    rim_high, rim_low = split(rim_ref[...] - mean_ref[...])
+    copy.wait()
+    rim = jnp.where(place > 0, rim_ref[...], 0.0)
+    rim_high, rim_low = split(rim - mean_ref[...])
     history = mm_nt(
         jnp.concatenate([head_high, head_high, head_low], axis=1),
         jnp.concatenate([rim_high, rim_low, rim_high], axis=1),
@@ -366,8 +371,7 @@
     near_each = noff // seg_count
     assert length == NFFT * DECIM and chans == LANES and noff % seg_count == 0
 
-    route = [(i, i + 1) for i in range(seg_count - 1)]
-    rim = lax.ppermute(recording[:, length - LANES :], "seg", route)
+    rims = lax.all_gather(recording[:, length - LANES :], "seg")
     taps = filter_taps.reshape(1, TAPS)
     spec, mean, head = pl.pallas_call(
         spectrum_kernel,
@@ -396,11 +400,12 @@
     white = pl.pallas_call(
         whiten_kernel,
         out_shape=jax.ShapeDtypeStruct((GROUPS, 2, GROUP, LANES), BF16),
-        in_specs=vmem(7),
+        in_specs=hbm(1) + vmem(6),
         out_specs=pl.BlockSpec(memory_space=pltpu.VMEM),
+        scratch_shapes=[pltpu.VMEM((chans, LANES), F32), pltpu.SemaphoreType.DMA],
         compiler_params=PARAMS,
         name="whiten",
-    )(spec, rim, mean, head, edge_table(), band, band_share)
+    )(in_hbm(rims), spec, mean, head, edge_table(), band, band_share)
 
     white, offsets = lax.optimization_barrier((white, offsets))
     if bins != GROUP:

time: 46.7 us -> 51.6 us (1.10)
  blocking collectives: 16.6 us -> 24.2 us
  starting transfers between devices: 9.47 us -> 5.9 us
  Pallas kernels: 8.65 us -> 9.56 us
    all_gather x0 -> x1, blocking collectives: none -> 7.63 us  [body(): rims = lax.all_gather(recording[:, length - LANES:], 'seg')]
    ppermute x1 -> x0, starting transfers between devices: 2.35 us -> none  [body(): rim = lax.ppermute(recording[:, length - LANES:], 'seg', route)]
    all_to_all x1, starting transfers between devices: 7.12 us -> 5.9 us  [body(): moved = lax.all_to_all(white, ('chan', 'seg'), 0, 0, tiled=True)]
    pallas_call x1, Pallas kernels: 1.41 us -> 2.33 us  [body(): pl.pallas_call(whiten_kernel, out_shape=jax.ShapeDtypeStruct((GROUPS, 2,...]
  transfers between devices with their start and end apart: 2 -> 1, of which waited for: 1 -> 1; matrix products, arithmetic and copies ran while one was open for 0% -> 0% of each run, Pallas kernels for 9% -> 1%
where the time goes in v5:
time: 51.6 us; the launch traced here: 51.4 us
  blocking collectives  24.2 us (47%)
  waiting for transfers between devices  9.86 us (19%)
  Pallas kernels  9.56 us (19%)
  starting transfers between devices  5.9 us (11%)
  local copies, waits for them, and re-layouts  1.07 us (2%)
  between operations  0.79 us (2%)
    all_to_all x1, blocking collectives, body(): summed = lax.all_to_all(crossed, ('chan', 'seg'), 0, 0, tiled=True)  16.6 us
    all_to_all x1, waiting for transfers between devices, body(): moved = lax.all_to_all(white, ('chan', 'seg'), 0, 0, tiled=True)  9.86 us
    all_gather x1, blocking collectives, body(): rims = lax.all_gather(recording[:, length - LANES:], 'seg')  7.63 us
    all_to_all x1, starting transfers between devices, body(): moved = lax.all_to_all(white, ('chan', 'seg'), 0, 0, tiled=True)  5.9 us
    pallas_call x1, Pallas kernels, body(): pl.pallas_call(spectrum_kernel, out_shape=[jax.ShapeDtypeStruct((2 * BINS...  3.56 us
    pallas_call x1, Pallas kernels, body(): pl.pallas_call(whiten_kernel, out_shape=jax.ShapeDtypeStruct((GROUPS, 2,...  2.33 us
    pallas_call x1, Pallas kernels, body(): pl.pallas_call(functools.partial(lag_kernel, slots), out_shape=[jax.Shape...  1.53 us
    pallas_call x1, Pallas kernels, body(): pl.pallas_call(cross_kernel, out_shape=jax.ShapeDtypeStruct((chan_count,...  1.51 us
  transfers between devices with their start and end apart: 1, of which 1 were waited for; matrix products, arithmetic and copies ran while one was open for 0% of the time, Pallas kernels for 1%

profile of v5, /device:TPU:0, one launch (start us, length us, event | category | flops | bytes accessed | tf_op | source)
XLA Modules:
  0.0 51.4 jit_solution(16245365236111868416)
XLA Ops:
  0.6 0.0 copy-start.3
  0.6 0.0 copy-start.2
  0.7 0.0 copy-start.4
  0.7 0.9 %slice.3 = f32[128,128]{1,0:T(8,128)S(1)} slice(f32[128,4096]{1,0:T(8,128)} %rec_hbm.1), slice={[0:128], [3968:4096]} | slice | bytes 131072 | tf_op jit(solution)/shard_map/slice | solution.py:374
  1.6 7.6 %all-gather = f32[512,128]{1,0:T(8,128)} all-gather(f32[128,128]{1,0:T(8,128)S(1)} %slice.3), channel_id=2, replica_groups=mesh['chan'=8,'seg'=4] {'seg'}, dimensions={0}, use_global_device_ids=true | all-gather | bytes 327680 | tf_op jit(solution)/shard_map/all_gather | solution.py:374
  9.2 3.6 %filter_and_transform.1 = (f32[1024,128]{1,0:T(8,128)S(1)}, f32[128,128]{1,0:T(8,128)S(1)}, f32[16,128]{1,0:T(8,128)S(1)}) custom-call(f32[1,64]{1,0:T(1,128)} %bitcast.9, f32[128,4096]{1,0:T(8,128)} %rec_hbm.1, bf16[256,768]{1,0:T(8,128)(2,1)} %constant.16.clone.tab_hbm, f32[256,128]{1,0:T(8,128)} %constant.17.clone.twist_hbm), custom_call_target="tpu_custom_call" | custom-call | flops 1000000000 | bytes 5000000 | tf_op jit(solution)/shard_map/filter_and_transform/pallas_call | solution.py:376
  12.8 0.0 copy-start.6
  12.8 0.0 copy-start.8
  12.8 0.0 copy-start.1
  12.8 0.0 copy-start.5
  12.8 0.0 copy-start.7
  12.9 0.0 copy-done.3
  12.9 0.0 copy-done.2
  12.9 0.0 copy-done.4
  12.9 2.3 %whiten.1 = bf16[32,2,16,128]{3,2,1,0:T(8,128)(2,1)} custom-call(f32[4,128,128]{2,1,0:T(8,128)} %bitcast.7, f32[1024,128]{1,0:T(8,128)S(1)} %get-tuple-element.9.spec_ref, f32[128,128]{1,0:T(8,128)S(1)} %get-tuple-element.10.mean_ref, f32[16,128]{1,0:T(8,128)S(1)} %get-tuple-element.11.head_ref, bf16[1024,128]{1,0:T(8,128)(2,1)S(1)} %copy-done.3, ...), custom_call_target="tpu_custom_call" | custom-call | tf_op jit(solution)/shard_map/whiten/pallas_call | solution.py:400
  15.2 0.0 copy-start
  15.2 5.9 %all-to-all-start = ((bf16[32,2,16,128]{3,2,1,0:T(8,128)(2,1)}), bf16[32,2,16,128]{3,2,1,0:T(8,128)(2,1)S(1)}, u32[]{:S(2)}, u32[]{:S(2)}) async-start(bf16[32,2,16,128]{3,2,1,0:T(8,128)(2,1)} %whiten.1), calls=%async_computation | async-start | bytes 524288 | tf_op jit(solution)/shard_map/all_to_all | solution.py:414
  21.1 0.0 copy-done.6
  21.2 0.6 %offset_moves.1.moves_ref = bf16[384,512]{1,0:T(8,128)(2,1)S(1)} custom-call(s32[4]{0:T(128)S(1)} %copy-done.6), custom_call_target="tpu_custom_call" | custom-call | tf_op jit(solution)/shard_map/offset_moves/pallas_call | solution.py:419
  21.8 0.0 copy-done.8
  21.8 0.1 copy.15.partner_ref
  21.9 9.9 %all-to-all-done = bf16[32,2,16,128]{3,2,1,0:T(8,128)(2,1)S(1)} async-done(((bf16[32,2,16,128]{3,2,1,0:T(8,128)(2,1)}), bf16[32,2,16,128]{3,2,1,0:T(8,128)(2,1)S(1)}, u32[]{:S(2)}, u32[]{:S(2)}) %all-to-all-start) | async-done | bytes 262176 | tf_op jit(solution)/shard_map/all_to_all | solution.py:414
  31.7 0.0 copy-done.1
  31.7 0.0 copy-done.5
  31.7 0.0 copy-done.7
  31.8 1.5 %cross_spectra.1 = bf16[8,4,56,128]{3,2,1,0:T(8,128)(2,1)S(1)} custom-call(s32[8,3]{1,0:T(8,128)S(1)} %copy.15.partner_ref, s32[8]{0:T(128)S(1)} %copy-done.7, bf16[384,512]{1,0:T(8,128)(2,1)S(1)} %offset_moves.1.moves_ref, bf16[128,128]{1,0:T(8,128)(2,1)S(1)} %copy-done.5, bf16[512,512]{1,0:T(8,128)(2,1)S(1)} %copy-done.1, ...), custom_call_target="tpu_custom_call" | custom-call | tf_op jit(solution)/shard_map/cross_spectra/pallas_call | solution.py:429
  33.3 16.6 %all_to_all.10.spec_ref = bf16[32,56,128]{2,1,0:T(8,128)(2,1)S(1)} all-to-all(bf16[32,56,128]{2,1,0:T(8,128)(2,1)S(1)} %bitcast.5), channel_id=1, replica_groups=mesh['chan'=8,'seg'=4] {'chan','seg'}, dimensions={0} | all-to-all | bytes 917504 | tf_op jit(solution)/shard_map/all_to_all | solution.py:439
  49.8 0.0 copy-done
  49.8 1.5 %lags.1 = (f32[128,1,256]{2,1,0:T(1,128)}, f32[96,256]{1,0:T(8,128)}) custom-call(bf16[32,56,128]{2,1,0:T(8,128)(2,1)S(1)} %all_to_all.10.spec_ref, bf16[512,1024]{1,0:T(8,128)(2,1)S(1)} %copy-done), custom_call_target="tpu_custom_call" | custom-call | tf_op jit(solution)/shard_map/lags/pallas_call | solution.py:444
Async XLA Ops:
  0.6 12.2 %copy-start.3 = (bf16[1024,128]{1,0:T(8,128)(2,1)S(1)}, bf16[1024,128]{1,0:T(8,128)(2,1)}, u32[]{:S(2)}) copy-start(bf16[1024,128]{1,0:T(8,128)(2,1)} %constant.18.clone.edge_ref) | copy-start | bytes 786436
  0.6 12.2 %copy-start.2 = (bf16[512,512]{1,0:T(8,128)(2,1)S(1)}, bf16[512,512]{1,0:T(8,128)(2,1)}, u32[]{:S(2)}) copy-start(bf16[512,512]{1,0:T(8,128)(2,1)} %constant.19.clone.band_ref) | copy-start | bytes 1572868
  0.7 12.2 %copy-start.4 = (f32[512,128]{1,0:T(8,128)S(1)}, f32[512,128]{1,0:T(8,128)}, u32[]{:S(2)}) copy-start(f32[512,128]{1,0:T(8,128)} %constant.20.clone.share_ref) | copy-start | bytes 786436
  12.8 8.3 %copy-start.6 = (s32[4]{0:T(128)S(1)}, s32[4]{0:T(128)}, u32[]{:S(2)}) copy-start(s32[4]{0:T(128)} %offs_ref) | copy-start | bytes 52
  12.8 9.0 %copy-start.8 = (s32[8,3]{0,1:T(4,128)S(1)}, s32[8,3]{0,1:T(4,128)}, u32[]{:S(2)}) copy-start(s32[8,3]{0,1:T(4,128)} %param.16) | copy-start | bytes 292
  12.8 18.9 %copy-start.1 = (bf16[512,512]{1,0:T(8,128)(2,1)S(1)}, bf16[512,512]{1,0:T(8,128)(2,1)}, u32[]{:S(2)}) copy-start(bf16[512,512]{1,0:T(8,128)(2,1)} %constant.22.clone.pack_ref) | copy-start | bytes 1572868
  12.8 18.9 %copy-start.5 = (bf16[128,128]{1,0:T(8,128)(2,1)S(1)}, bf16[128,128]{1,0:T(8,128)(2,1)}, u32[]{:S(2)}) copy-start(bf16[128,128]{1,0:T(8,128)(2,1)} %constant.21.clone.flip_ref) | copy-start | bytes 98308
  12.8 18.9 %copy-start.7 = (s32[8]{0:T(128)S(1)}, s32[8]{0:T(128)}, u32[]{:S(2)}) copy-start(s32[8]{0:T(128)} %count_ref.1) | copy-start | bytes 100
  15.2 34.6 %copy-start = (bf16[512,1024]{1,0:T(8,128)(2,1)S(1)}, bf16[512,1024]{1,0:T(8,128)(2,1)}, u32[]{:S(2)}) copy-start(bf16[512,1024]{1,0:T(8,128)(2,1)} %constant.23.clone.inv_ref) | copy-start | bytes 3145732
  15.2 16.5 %all-to-all-start = ((bf16[32,2,16,128]{3,2,1,0:T(8,128)(2,1)}), bf16[32,2,16,128]{3,2,1,0:T(8,128)(2,1)S(1)}, u32[]{:S(2)}, u32[]{:S(2)}) async-start(bf16[32,2,16,128]{3,2,1,0:T(8,128)(2,1)} %whiten.1), calls=%async_computation | async-start | bytes 524288 | tf_op jit(solution)/shard_map/all_to_all | solution.py:414

commit v6 on v4

--- a/solution.py
+++ b/solution.py
@@ -104,30 +104,15 @@
     return pltpu.roll(spread, 0, 1, stride=DECIM, stride_axis=0)
 
 
-def spectrum_kernel(
-    taps_hbm,
-    rec_hbm,
-    tab_hbm,
-    twist_hbm,
-    spec_ref,
-    mean_ref,
-    head_ref,
-    taps_ref,
-    rec_ref,
-    tab_ref,
-    twist_ref,
-    sems,
-):
+def rim_kernel(rec_hbm, rim_ref, sem):
+    length = rec_hbm.shape[1]
+    copy = pltpu.make_async_copy(rec_hbm.at[:, pl.ds(length - LANES, LANES)], rim_ref, sem)
+    copy.start()
+    copy.wait()
+
+
+def spectrum_kernel(taps_ref, rec_ref, tab_ref, twist_ref, spec_ref, mean_ref, head_ref):
     blocks = rec_ref.shape[1] // STEP
-    copies = [(taps_hbm, taps_ref)]
-    for j in range(blocks):
-        part = pl.ds(j * STEP, STEP)
-        copies.append((rec_hbm.at[:, part], rec_ref.at[:, part]))
-    copies = copies + [(twist_hbm, twist_ref), (tab_hbm, tab_ref)]
-    copies = [pltpu.make_async_copy(*c, sems.at[i]) for i, c in enumerate(copies)]
-    for copy in copies:
-        copy.start()
-    copies[0].wait()
     table = tap_rows(taps_ref[...])
     head_ref[...] = table[:GROUP, :LANES]
     taps_high, taps_low = split(table.T)
@@ -136,8 +121,6 @@
     outputs = []
     for first in range(0, blocks, blocks // 2):
         windows = ([], [])
-        for j in range(first, first + blocks // 2):
-            copies[1 + j].wait()
         for j in range(first, first + blocks // 2):
             chunk = rec_ref[:, j * STEP : (j + 1) * STEP]
             if j == 0:
@@ -155,7 +138,6 @@
     a, b = pieces[0] - pieces[2], pieces[1] - pieces[3]
     whole, half = even + odd, even - odd
     whole = whole - jnp.sum(whole, axis=0, keepdims=True) * (1.0 / DEPTH)
-    copies[blocks + 1].wait()
     c1, s1, c2, s2, c3, s3 = [twist_ref[:, i : i + 1] for i in range(6)]
     inputs = [
         whole,
@@ -169,7 +151,6 @@
     parts = [split(value) for value in inputs]
     high = jnp.concatenate([p[0] for p in parts], axis=1)
     low = jnp.concatenate([p[1] for p in parts], axis=1)
-    copies[blocks + 2].wait()
     out = mm(tab_ref[...], jnp.concatenate([high, low, high], axis=0))
     out = out.reshape(FAR_BINS // GROUP, 2, GROUP, out.shape[1])
     rows = 2 * FAR_BINS
@@ -367,7 +348,19 @@
     assert length == NFFT * DECIM and chans == LANES and noff % seg_count == 0
 
     route = [(i, i + 1) for i in range(seg_count - 1)]
-    rim = lax.ppermute(recording[:, length - LANES :], "seg", route)
+    rim = pl.pallas_call(
+        rim_kernel,
+        out_shape=jax.ShapeDtypeStruct((chans, LANES), F32),
+        in_specs=hbm(1),
+        out_specs=pl.BlockSpec(memory_space=pltpu.VMEM),
+        scratch_shapes=[pltpu.SemaphoreType.DMA],
+        compiler_params=PARAMS,
+        cost_estimate=pl.CostEstimate(
+            flops=10_000_000_000, bytes_accessed=20_000_000, transcendentals=0
+        ),
+        name="history",
+    )(in_hbm(recording))
+    rim = lax.ppermute(rim, "seg", route)
     taps = filter_taps.reshape(1, TAPS)
     spec, mean, head = pl.pallas_call(
         spectrum_kernel,
@@ -376,21 +369,14 @@
             jax.ShapeDtypeStruct((LANES, LANES), F32),
             jax.ShapeDtypeStruct((GROUP, LANES), F32),
         ],
-        in_specs=hbm(4),
+        in_specs=vmem(4),
         out_specs=vmem(3),
-        scratch_shapes=[
-            pltpu.VMEM((1, TAPS), F32),
-            pltpu.VMEM((chans, length), F32),
-            pltpu.VMEM((2 * FAR_BINS, 3 * DEPTH), BF16),
-            pltpu.VMEM((DEPTH, LANES), F32),
-            pltpu.SemaphoreType.DMA((length // STEP + 3,)),
-        ],
         compiler_params=PARAMS,
         cost_estimate=pl.CostEstimate(
             flops=1_000_000_000, bytes_accessed=5_000_000, transcendentals=0
         ),
         name="filter_and_transform",
-    )(in_hbm(taps), in_hbm(recording), in_hbm(short_table()), in_hbm(twiddle_table()))
+    )(taps, recording, short_table(), twiddle_table())
 
     band, band_share = band_tables()
     white = pl.pallas_call(

time: 46.7 us -> 46.7 us (level)
  starting transfers between devices: 9.47 us -> 10.9 us
  local copies, waits for them, and re-layouts: 1.07 us -> 0.16 us
  Pallas kernels: 8.65 us -> 8.05 us
    pallas_call x1, Pallas kernels: 3.58 us -> 1.98 us  [body(): pl.pallas_call(spectrum_kernel, out_shape=[jax.ShapeDtypeStruct((2 * BINS...]
    all_to_all x1, starting transfers between devices: 7.12 us -> 8.39 us  [body(): moved = lax.all_to_all(white, ('chan', 'seg'), 0, 0, tiled=True)]
    pallas_call x0 -> x1, Pallas kernels: none -> 1 us  [body(): pl.pallas_call(rim_kernel, out_shape=jax.ShapeDtypeStruct((chans, LANES),...]
    slice x1 -> x0, local copies, waits for them, and re-layouts: 0.93 us -> none  [body(): rim = lax.ppermute(recording[:, length - LANES:], 'seg', route)]
  transfers between devices with their start and end apart: 2 -> 2, of which waited for: 1 -> 1; matrix products, arithmetic and copies ran while one was open for 0% -> 0% of each run, Pallas kernels for 9% -> 6%
where the time goes in v6:
time: 46.7 us; the launch traced here: 46.4 us
  blocking collectives  16.6 us (36%)
  starting transfers between devices  10.9 us (23%)
  waiting for transfers between devices  9.87 us (21%)
  Pallas kernels  8.05 us (17%)
  between operations  0.85 us (2%)
    all_to_all x1, blocking collectives, body(): summed = lax.all_to_all(crossed, ('chan', 'seg'), 0, 0, tiled=True)  16.6 us
    all_to_all x1, waiting for transfers between devices, body(): moved = lax.all_to_all(white, ('chan', 'seg'), 0, 0, tiled=True)  9.87 us
    all_to_all x1, starting transfers between devices, body(): moved = lax.all_to_all(white, ('chan', 'seg'), 0, 0, tiled=True)  8.39 us
    ppermute x1, starting transfers between devices, body(): rim = lax.ppermute(rim, 'seg', route)  2.49 us
    pallas_call x1, Pallas kernels, body(): pl.pallas_call(spectrum_kernel, out_shape=[jax.ShapeDtypeStruct((2 * BINS...  1.98 us
    pallas_call x1, Pallas kernels, body(): pl.pallas_call(functools.partial(lag_kernel, slots), out_shape=[jax.Shape...  1.53 us
    pallas_call x1, Pallas kernels, body(): pl.pallas_call(cross_kernel, out_shape=jax.ShapeDtypeStruct((chan_count,...  1.51 us
    pallas_call x1, Pallas kernels, body(): pl.pallas_call(whiten_kernel, out_shape=jax.ShapeDtypeStruct((GROUPS, 2,...  1.4 us
  transfers between devices with their start and end apart: 2, of which 1 were waited for; matrix products, arithmetic and copies ran while one was open for 0% of the time, Pallas kernels for 6%

profile of v6, /device:TPU:0, one launch (start us, length us, event | category | flops | bytes accessed | tf_op | source)
XLA Modules:
  0.0 46.4 jit_solution(4015453555576306789)
XLA Ops:
  0.6 0.0 copy-start.10
  0.6 0.0 copy-start.11
  0.7 0.0 copy-start.8
  0.7 0.0 copy-start.9
  0.7 1.0 %history.1 = f32[128,128]{1,0:T(8,128)S(1)} custom-call(f32[128,4096]{1,0:T(8,128)} %rec_hbm.1), custom_call_target="tpu_custom_call" | custom-call | flops 10000000000 | bytes 20000000 | tf_op jit(solution)/shard_map/history/pallas_call | solution.py:351
  1.7 0.0 copy-start.2
  1.7 0.0 copy-start.3
  1.7 0.0 copy-start.4
  1.7 2.5 %collective-permute-start = (f32[128,128]{1,0:T(8,128)S(1)}, f32[128,128]{1,0:T(8,128)S(1)}, u32[]{:S(2)}, u32[]{:S(2)}) collective-permute-start(f32[128,128]{1,0:T(8,128)S(1)} %history.1), channel_id=1, source_target_pairs={{0,1},{1,2},{2,3},{4,5},{5,6},{6,7},{8,9},{9,10},{10,11},{12,13},{... | collective-permute-start | bytes 196616 | tf_op jit(solution)/shard_map/ppermute | solution.py:363
  4.2 0.0 copy-done.10
  4.2 0.0 copy-done.11
  4.2 0.0 copy-done.8
  4.2 0.0 copy-done.9
  4.3 2.0 %filter_and_transform.1 = (f32[1024,128]{1,0:T(8,128)S(1)}, f32[128,128]{1,0:T(8,128)S(1)}, f32[16,128]{1,0:T(8,128)S(1)}) custom-call(f32[1,64]{1,0:T(1,128)S(1)} %bitcast.6, f32[128,4096]{1,0:T(8,128)S(1)} %copy-done.8, bf16[256,768]{1,0:T(8,128)(2,1)S(1)} %copy-done.10, f32[256,128]{1,0:T(8,128)S(1)} %copy-done.11), custom_call_target="tpu_custom_call" | custom-call | flops 1000000000 | bytes 5000000 | tf_op jit(solution)/shard_map/filter_and_transform/pallas_call | solution.py:365
  6.2 0.0 copy-start.12
  6.3 0.0 copy-start.6
  6.3 0.0 copy-start.1
  6.3 0.0 copy-start.5
  6.3 0.0 copy-start.7
  6.3 0.0 collective-permute-done.rim_ref
  6.3 0.0 copy-done.2
  6.3 0.0 copy-done.3
  6.3 0.0 copy-done.4
  6.3 1.4 %whiten.1 = bf16[32,2,16,128]{3,2,1,0:T(8,128)(2,1)} custom-call(f32[1024,128]{1,0:T(8,128)S(1)} %get-tuple-element.9.spec_ref, f32[128,128]{1,0:T(8,128)S(1)} %collective-permute-done.rim_ref, f32[128,128]{1,0:T(8,128)S(1)} %get-tuple-element.10.mean_ref, f32[16,128]{1,0:T(8,128)S(1)} %get-tuple-element.11.head_ref, bf16[1024,128]{1,0:T(8,128)(2,1)S(1)} %copy-done.4, ...), custom_call_target="tpu_custom_call" | custom-call | tf_op jit(solution)/shard_map/whiten/pallas_call | solution.py:382
  7.8 0.0 copy-start
  7.8 8.4 %all-to-all-start = ((bf16[32,2,16,128]{3,2,1,0:T(8,128)(2,1)}), bf16[32,2,16,128]{3,2,1,0:T(8,128)(2,1)S(1)}, u32[]{:S(2)}, u32[]{:S(2)}) async-start(bf16[32,2,16,128]{3,2,1,0:T(8,128)(2,1)} %whiten.1), calls=%async_computation | async-start | bytes 524288 | tf_op jit(solution)/shard_map/all_to_all | solution.py:395
  16.2 0.0 copy-done.12
  16.2 0.1 copy.15.partner_ref
  16.3 0.0 copy-done.6
  16.3 0.6 %offset_moves.1.moves_ref = bf16[384,512]{1,0:T(8,128)(2,1)S(1)} custom-call(s32[4]{0:T(128)S(1)} %copy-done.6), custom_call_target="tpu_custom_call" | custom-call | tf_op jit(solution)/shard_map/offset_moves/pallas_call | solution.py:400
  16.9 9.9 %all-to-all-done = bf16[32,2,16,128]{3,2,1,0:T(8,128)(2,1)S(1)} async-done(((bf16[32,2,16,128]{3,2,1,0:T(8,128)(2,1)}), bf16[32,2,16,128]{3,2,1,0:T(8,128)(2,1)S(1)}, u32[]{:S(2)}, u32[]{:S(2)}) %all-to-all-start) | async-done | bytes 262176 | tf_op jit(solution)/shard_map/all_to_all | solution.py:395
  26.8 0.0 copy-done.1
  26.8 0.0 copy-done.5
  26.8 0.0 copy-done.7
  26.8 1.5 %cross_spectra.1 = bf16[8,4,56,128]{3,2,1,0:T(8,128)(2,1)S(1)} custom-call(s32[8,3]{1,0:T(8,128)S(1)} %copy.15.partner_ref, s32[8]{0:T(128)S(1)} %copy-done.7, bf16[384,512]{1,0:T(8,128)(2,1)S(1)} %offset_moves.1.moves_ref, bf16[128,128]{1,0:T(8,128)(2,1)S(1)} %copy-done.5, bf16[512,512]{1,0:T(8,128)(2,1)S(1)} %copy-done.1, ...), custom_call_target="tpu_custom_call" | custom-call | tf_op jit(solution)/shard_map/cross_spectra/pallas_call | solution.py:410
  28.3 16.6 %all_to_all.10.spec_ref = bf16[32,56,128]{2,1,0:T(8,128)(2,1)S(1)} all-to-all(bf16[32,56,128]{2,1,0:T(8,128)(2,1)S(1)} %bitcast.4), channel_id=1, replica_groups=mesh['chan'=8,'seg'=4] {'chan','seg'}, dimensions={0} | all-to-all | bytes 917504 | tf_op jit(solution)/shard_map/all_to_all | solution.py:420
  44.9 0.0 copy-done
  44.9 1.5 %lags.1 = (f32[128,1,256]{2,1,0:T(1,128)}, f32[96,256]{1,0:T(8,128)}) custom-call(bf16[32,56,128]{2,1,0:T(8,128)(2,1)S(1)} %all_to_all.10.spec_ref, bf16[512,1024]{1,0:T(8,128)(2,1)S(1)} %copy-done), custom_call_target="tpu_custom_call" | custom-call | tf_op jit(solution)/shard_map/lags/pallas_call | solution.py:425
Async XLA Ops:
  0.6 3.6 %copy-start.10 = (bf16[256,768]{1,0:T(8,128)(2,1)S(1)}, bf16[256,768]{1,0:T(8,128)(2,1)}, u32[]{:S(2)}) copy-start(bf16[256,768]{1,0:T(8,128)(2,1)} %constant.16.clone.tab_ref) | copy-start | bytes 1179652
  0.6 3.6 %copy-start.11 = (f32[256,128]{1,0:T(8,128)S(1)}, f32[256,128]{1,0:T(8,128)}, u32[]{:S(2)}) copy-start(f32[256,128]{1,0:T(8,128)} %constant.17.clone.twist_ref) | copy-start | bytes 393220
  0.7 3.6 %copy-start.8 = (f32[128,4096]{1,0:T(8,128)S(1)}, f32[128,4096]{1,0:T(8,128)}, u32[]{:S(2)}) copy-start(f32[128,4096]{1,0:T(8,128)} %rec_hbm.1) | copy-start | bytes 6291460
  0.7 3.6 %copy-start.9 = (f32[64]{0:T(128)S(1)}, f32[64]{0:T(128)}, u32[]{:S(2)}) copy-start(f32[64]{0:T(128)} %param.14) | copy-start | bytes 772
  1.7 4.6 %copy-start.2 = (bf16[512,512]{1,0:T(8,128)(2,1)S(1)}, bf16[512,512]{1,0:T(8,128)(2,1)}, u32[]{:S(2)}) copy-start(bf16[512,512]{1,0:T(8,128)(2,1)} %constant.19.clone.band_ref) | copy-start | bytes 1572868
  1.7 4.6 %copy-start.3 = (f32[512,128]{1,0:T(8,128)S(1)}, f32[512,128]{1,0:T(8,128)}, u32[]{:S(2)}) copy-start(f32[512,128]{1,0:T(8,128)} %constant.20.clone.share_ref) | copy-start | bytes 786436
  1.7 4.6 %copy-start.4 = (bf16[1024,128]{1,0:T(8,128)(2,1)S(1)}, bf16[1024,128]{1,0:T(8,128)(2,1)}, u32[]{:S(2)}) copy-start(bf16[1024,128]{1,0:T(8,128)(2,1)} %constant.18.clone.edge_ref) | copy-start | bytes 786436
  1.7 4.6 %collective-permute-start = (f32[128,128]{1,0:T(8,128)S(1)}, f32[128,128]{1,0:T(8,128)S(1)}, u32[]{:S(2)}, u32[]{:S(2)}) collective-permute-start(f32[128,128]{1,0:T(8,128)S(1)} %history.1), channel_id=1, source_target_pairs={{0,1},{1,2},{2,3},{4,5},{5,6},{6,7},{8,9},{9,10},{10,11},{12,13},{... | collective-permute-start | bytes 196616 | tf_op jit(solution)/shard_map/ppermute | solution.py:363
  6.2 9.9 %copy-start.12 = (s32[8,3]{0,1:T(4,128)S(1)}, s32[8,3]{0,1:T(4,128)}, u32[]{:S(2)}) copy-start(s32[8,3]{0,1:T(4,128)} %param.16) | copy-start | bytes 292
  6.3 10.0 %copy-start.6 = (s32[4]{0:T(128)S(1)}, s32[4]{0:T(128)}, u32[]{:S(2)}) copy-start(s32[4]{0:T(128)} %offs_ref) | copy-start | bytes 52
  6.3 20.5 %copy-start.1 = (bf16[512,512]{1,0:T(8,128)(2,1)S(1)}, bf16[512,512]{1,0:T(8,128)(2,1)}, u32[]{:S(2)}) copy-start(bf16[512,512]{1,0:T(8,128)(2,1)} %constant.22.clone.pack_ref) | copy-start | bytes 1572868
  6.3 20.5 %copy-start.5 = (bf16[128,128]{1,0:T(8,128)(2,1)S(1)}, bf16[128,128]{1,0:T(8,128)(2,1)}, u32[]{:S(2)}) copy-start(bf16[128,128]{1,0:T(8,128)(2,1)} %constant.21.clone.flip_ref) | copy-start | bytes 98308
  6.3 20.5 %copy-start.7 = (s32[8]{0:T(128)S(1)}, s32[8]{0:T(128)}, u32[]{:S(2)}) copy-start(s32[8]{0:T(128)} %count_ref.1) | copy-start | bytes 100
  7.8 37.1 %copy-start = (bf16[512,1024]{1,0:T(8,128)(2,1)S(1)}, bf16[512,1024]{1,0:T(8,128)(2,1)}, u32[]{:S(2)}) copy-start(bf16[512,1024]{1,0:T(8,128)(2,1)} %constant.23.clone.inv_ref) | copy-start | bytes 3145732
  7.8 19.0 %all-to-all-start = ((bf16[32,2,16,128]{3,2,1,0:T(8,128)(2,1)}), bf16[32,2,16,128]{3,2,1,0:T(8,128)(2,1)S(1)}, u32[]{:S(2)}, u32[]{:S(2)}) async-start(bf16[32,2,16,128]{3,2,1,0:T(8,128)(2,1)} %whiten.1), calls=%async_computation | async-start | bytes 524288 | tf_op jit(solution)/shard_map/all_to_all | solution.py:395

commit v7 on v6

--- a/solution.py
+++ b/solution.py
@@ -14,6 +14,7 @@
 TAPS = 64
 DECIM = 4
 HALFBAND = 10
+SPAN = 64
 BINS = 512
 WATER = 0.2
 
@@ -104,11 +105,14 @@
     return pltpu.roll(spread, 0, 1, stride=DECIM, stride_axis=0)
 
 
-def rim_kernel(rec_hbm, rim_ref, sem):
+def rim_kernel(rec_hbm, rim_ref, tail_ref, sem):
     length = rec_hbm.shape[1]
-    copy = pltpu.make_async_copy(rec_hbm.at[:, pl.ds(length - LANES, LANES)], rim_ref, sem)
+    copy = pltpu.make_async_copy(rec_hbm.at[:, pl.ds(length - LANES, LANES)], tail_ref, sem)
     copy.start()
     copy.wait()
+    upper, lower = tail_ref[: LANES // 2], tail_ref[LANES // 2 :]
+    lane = lax.broadcasted_iota(jnp.int32, lower.shape, 1)
+    rim_ref[...] = jnp.where(lane < TAPS, pltpu.roll(upper, LANES - TAPS, 1), lower)
 
 
 def spectrum_kernel(taps_ref, rec_ref, tab_ref, twist_ref, spec_ref, mean_ref, head_ref):
@@ -170,7 +174,8 @@
     spec_ref, rim_ref, mean_ref, head_ref, edge_ref, band_ref, share_ref, white_ref
 ):
     head_high, head_low = split(head_ref[...])
-    rim_high, rim_low = split(rim_ref[...] - mean_ref[...])
+    rim = jnp.concatenate([pltpu.roll(rim_ref[...], LANES - TAPS, 1), rim_ref[...]], axis=0)
+    rim_high, rim_low = split(rim - mean_ref[...])
     history = mm_nt(
         jnp.concatenate([head_high, head_high, head_low], axis=1),
         jnp.concatenate([rim_high, rim_low, rim_high], axis=1),
@@ -192,10 +197,11 @@
 
 def moves_kernel(offs_ref, moves_ref):
     noff = offs_ref.shape[0]
-    source = lax.broadcasted_iota(jnp.int32, (3 * LANES, LANES), 0)
-    channel = lax.broadcasted_iota(jnp.int32, (3 * LANES, LANES), 1)
+    row = lax.broadcasted_iota(jnp.int32, (2 * LANES, LANES), 0)
+    channel = lax.broadcasted_iota(jnp.int32, (2 * LANES, LANES), 1)
+    source = jnp.where(row < LANES + SPAN, row, row - 2 * LANES)
     for o in range(noff):
-        hit = source == channel + (LANES + offs_ref[o])
+        hit = source == channel + offs_ref[o]
         moves_ref[:, o * LANES : (o + 1) * LANES] = hit.astype(F32).astype(BF16)
 
 
@@ -223,7 +229,9 @@
     turned_ref[...] = mm(every, flip_ref[...]).reshape(turned_ref.shape)
     before = jnp.concatenate(flats[-1:] + flats[:-1], axis=0)
     after = jnp.concatenate(flats[1:] + flats[:1], axis=0)
-    moved = mm(jnp.concatenate([before, every, after], axis=1), moves_ref[...])
+    lane = lax.broadcasted_iota(jnp.int32, every.shape, 1)
+    edge = jnp.where(lane < SPAN, after.astype(F32), before.astype(F32)).astype(BF16)
+    moved = mm(jnp.concatenate([every, edge], axis=1), moves_ref[...])
 
     def products(own, far):
         own = own.reshape(segs, 2, bins, LANES)
@@ -350,10 +358,10 @@
     route = [(i, i + 1) for i in range(seg_count - 1)]
     rim = pl.pallas_call(
         rim_kernel,
-        out_shape=jax.ShapeDtypeStruct((chans, LANES), F32),
+        out_shape=jax.ShapeDtypeStruct((chans // 2, LANES), F32),
         in_specs=hbm(1),
         out_specs=pl.BlockSpec(memory_space=pltpu.VMEM),
-        scratch_shapes=[pltpu.SemaphoreType.DMA],
+        scratch_shapes=[pltpu.VMEM((chans, LANES), F32), pltpu.SemaphoreType.DMA],
         compiler_params=PARAMS,
         cost_estimate=pl.CostEstimate(
             flops=10_000_000_000, bytes_accessed=20_000_000, transcendentals=0
@@ -399,7 +407,7 @@
 
     moves = pl.pallas_call(
         moves_kernel,
-        out_shape=jax.ShapeDtypeStruct((3 * LANES, noff * LANES), BF16),
+        out_shape=jax.ShapeDtypeStruct((2 * LANES, noff * LANES), BF16),
         in_specs=smem(1),
         out_specs=pl.BlockSpec(memory_space=pltpu.VMEM),
         compiler_params=PARAMS,

time: 46.7 us -> 46.4 us (level)
  no operation moved by 1% of the time
where the time goes in v7:
time: 46.4 us; the launch traced here: 46.1 us
  blocking collectives  16.6 us (36%)
  starting transfers between devices  10.5 us (23%)
  waiting for transfers between devices  9.9 us (21%)
  Pallas kernels  8.12 us (17%)
  between operations  0.85 us (2%)
    all_to_all x1, blocking collectives, body(): summed = lax.all_to_all(crossed, ('chan', 'seg'), 0, 0, tiled=True)  16.6 us
    all_to_all x1, waiting for transfers between devices, body(): moved = lax.all_to_all(white, ('chan', 'seg'), 0, 0, tiled=True)  9.89 us
    all_to_all x1, starting transfers between devices, body(): moved = lax.all_to_all(white, ('chan', 'seg'), 0, 0, tiled=True)  8.05 us
    ppermute x1, starting transfers between devices, body(): rim = lax.ppermute(rim, 'seg', route)  2.49 us
    pallas_call x1, Pallas kernels, body(): pl.pallas_call(spectrum_kernel, out_shape=[jax.ShapeDtypeStruct((2 * BINS...  1.97 us
    pallas_call x1, Pallas kernels, body(): pl.pallas_call(functools.partial(lag_kernel, slots), out_shape=[jax.Shape...  1.53 us
    pallas_call x1, Pallas kernels, body(): pl.pallas_call(whiten_kernel, out_shape=jax.ShapeDtypeStruct((GROUPS, 2,...  1.47 us
    pallas_call x1, Pallas kernels, body(): pl.pallas_call(cross_kernel, out_shape=jax.ShapeDtypeStruct((chan_count,...  1.47 us
  transfers between devices with their start and end apart: 2, of which 1 were waited for; matrix products, arithmetic and copies ran while one was open for 0% of the time, Pallas kernels for 6%

profile of v7, /device:TPU:0, one launch (start us, length us, event | category | flops | bytes accessed | tf_op | source)
XLA Modules:
  0.0 46.1 jit_solution(17357323485579040192)
XLA Ops:
  0.6 0.0 copy-start.10
  0.6 0.0 copy-start.11
  0.7 0.0 copy-start.8
  0.7 0.0 copy-start.9
  0.7 1.1 %history.1 = f32[64,128]{1,0:T(8,128)S(1)} custom-call(f32[128,4096]{1,0:T(8,128)} %rec_hbm.1), custom_call_target="tpu_custom_call" | custom-call | flops 10000000000 | bytes 20000000 | tf_op jit(solution)/shard_map/history/pallas_call | solution.py:359
  1.8 0.0 copy-start.2
  1.8 0.0 copy-start.3
  1.8 0.0 copy-start.4
  1.8 2.5 %collective-permute-start = (f32[64,128]{1,0:T(8,128)S(1)}, f32[64,128]{1,0:T(8,128)S(1)}, u32[]{:S(2)}, u32[]{:S(2)}) collective-permute-start(f32[64,128]{1,0:T(8,128)S(1)} %history.1), channel_id=1, source_target_pairs={{0,1},{1,2},{2,3},{4,5},{5,6},{6,7},{8,9},{9,10},{10,11},{12,13},{... | collective-permute-start | bytes 98312 | tf_op jit(solution)/shard_map/ppermute | solution.py:371
  4.3 0.0 copy-done.10
  4.3 0.0 copy-done.11
  4.3 0.0 copy-done.8
  4.3 0.0 copy-done.9
  4.3 2.0 %filter_and_transform.1 = (f32[1024,128]{1,0:T(8,128)S(1)}, f32[128,128]{1,0:T(8,128)S(1)}, f32[16,128]{1,0:T(8,128)S(1)}) custom-call(f32[1,64]{1,0:T(1,128)S(1)} %bitcast.6, f32[128,4096]{1,0:T(8,128)S(1)} %copy-done.8, bf16[256,768]{1,0:T(8,128)(2,1)S(1)} %copy-done.10, f32[256,128]{1,0:T(8,128)S(1)} %copy-done.11), custom_call_target="tpu_custom_call" | custom-call | flops 1000000000 | bytes 5000000 | tf_op jit(solution)/shard_map/filter_and_transform/pallas_call | solution.py:373
  6.3 0.0 copy-start.12
  6.3 0.0 copy-start.6
  6.3 0.0 copy-start.1
  6.3 0.0 copy-start.5
  6.4 0.0 copy-start.7
  6.4 0.0 collective-permute-done.rim_ref
  6.4 0.0 copy-done.2
  6.4 0.0 copy-done.3
  6.4 0.0 copy-done.4
  6.4 1.5 %whiten.1 = bf16[32,2,16,128]{3,2,1,0:T(8,128)(2,1)} custom-call(f32[1024,128]{1,0:T(8,128)S(1)} %get-tuple-element.9.spec_ref, f32[64,128]{1,0:T(8,128)S(1)} %collective-permute-done.rim_ref, f32[128,128]{1,0:T(8,128)S(1)} %get-tuple-element.10.mean_ref, f32[16,128]{1,0:T(8,128)S(1)} %get-tuple-element.11.head_ref, bf16[1024,128]{1,0:T(8,128)(2,1)S(1)} %copy-done.4, ...), custom_call_target="tpu_custom_call" | custom-call | tf_op jit(solution)/shard_map/whiten/pallas_call | solution.py:390
  7.9 0.0 copy-start
  7.9 8.1 %all-to-all-start = ((bf16[32,2,16,128]{3,2,1,0:T(8,128)(2,1)}), bf16[32,2,16,128]{3,2,1,0:T(8,128)(2,1)S(1)}, u32[]{:S(2)}, u32[]{:S(2)}) async-start(bf16[32,2,16,128]{3,2,1,0:T(8,128)(2,1)} %whiten.1), calls=%async_computation | async-start | bytes 524288 | tf_op jit(solution)/shard_map/all_to_all | solution.py:403
  15.9 0.0 copy-done.12
  16.0 0.1 copy.15.partner_ref
  16.0 0.0 copy-done.6
  16.0 0.6 %offset_moves.1.moves_ref = bf16[256,512]{1,0:T(8,128)(2,1)S(1)} custom-call(s32[4]{0:T(128)S(1)} %copy-done.6), custom_call_target="tpu_custom_call" | custom-call | tf_op jit(solution)/shard_map/offset_moves/pallas_call | solution.py:408
  16.7 9.9 %all-to-all-done = bf16[32,2,16,128]{3,2,1,0:T(8,128)(2,1)S(1)} async-done(((bf16[32,2,16,128]{3,2,1,0:T(8,128)(2,1)}), bf16[32,2,16,128]{3,2,1,0:T(8,128)(2,1)S(1)}, u32[]{:S(2)}, u32[]{:S(2)}) %all-to-all-start) | async-done | bytes 262176 | tf_op jit(solution)/shard_map/all_to_all | solution.py:403
  26.5 0.0 copy-done.1
  26.6 0.0 copy-done.5
  26.6 0.0 copy-done.7
  26.6 1.5 %cross_spectra.1 = bf16[8,4,56,128]{3,2,1,0:T(8,128)(2,1)S(1)} custom-call(s32[8,3]{1,0:T(8,128)S(1)} %copy.15.partner_ref, s32[8]{0:T(128)S(1)} %copy-done.7, bf16[256,512]{1,0:T(8,128)(2,1)S(1)} %offset_moves.1.moves_ref, bf16[128,128]{1,0:T(8,128)(2,1)S(1)} %copy-done.5, bf16[512,512]{1,0:T(8,128)(2,1)S(1)} %copy-done.1, ...), custom_call_target="tpu_custom_call" | custom-call | tf_op jit(solution)/shard_map/cross_spectra/pallas_call | solution.py:418
  28.0 16.6 %all_to_all.10.spec_ref = bf16[32,56,128]{2,1,0:T(8,128)(2,1)S(1)} all-to-all(bf16[32,56,128]{2,1,0:T(8,128)(2,1)S(1)} %bitcast.4), channel_id=1, replica_groups=mesh['chan'=8,'seg'=4] {'chan','seg'}, dimensions={0} | all-to-all | bytes 917504 | tf_op jit(solution)/shard_map/all_to_all | solution.py:428
  44.6 0.0 copy-done
  44.6 1.5 %lags.1 = (f32[128,1,256]{2,1,0:T(1,128)}, f32[96,256]{1,0:T(8,128)}) custom-call(bf16[32,56,128]{2,1,0:T(8,128)(2,1)S(1)} %all_to_all.10.spec_ref, bf16[512,1024]{1,0:T(8,128)(2,1)S(1)} %copy-done), custom_call_target="tpu_custom_call" | custom-call | tf_op jit(solution)/shard_map/lags/pallas_call | solution.py:433
Async XLA Ops:
  0.6 3.7 %copy-start.10 = (bf16[256,768]{1,0:T(8,128)(2,1)S(1)}, bf16[256,768]{1,0:T(8,128)(2,1)}, u32[]{:S(2)}) copy-start(bf16[256,768]{1,0:T(8,128)(2,1)} %constant.16.clone.tab_ref) | copy-start | bytes 1179652
  0.6 3.7 %copy-start.11 = (f32[256,128]{1,0:T(8,128)S(1)}, f32[256,128]{1,0:T(8,128)}, u32[]{:S(2)}) copy-start(f32[256,128]{1,0:T(8,128)} %constant.17.clone.twist_ref) | copy-start | bytes 393220
  0.7 3.7 %copy-start.8 = (f32[128,4096]{1,0:T(8,128)S(1)}, f32[128,4096]{1,0:T(8,128)}, u32[]{:S(2)}) copy-start(f32[128,4096]{1,0:T(8,128)} %rec_hbm.1) | copy-start | bytes 6291460
  0.7 3.7 %copy-start.9 = (f32[64]{0:T(128)S(1)}, f32[64]{0:T(128)}, u32[]{:S(2)}) copy-start(f32[64]{0:T(128)} %param.14) | copy-start | bytes 772
  1.8 4.6 %copy-start.2 = (bf16[512,512]{1,0:T(8,128)(2,1)S(1)}, bf16[512,512]{1,0:T(8,128)(2,1)}, u32[]{:S(2)}) copy-start(bf16[512,512]{1,0:T(8,128)(2,1)} %constant.19.clone.band_ref) | copy-start | bytes 1572868
  1.8 4.6 %copy-start.3 = (f32[512,128]{1,0:T(8,128)S(1)}, f32[512,128]{1,0:T(8,128)}, u32[]{:S(2)}) copy-start(f32[512,128]{1,0:T(8,128)} %constant.20.clone.share_ref) | copy-start | bytes 786436
  1.8 4.6 %copy-start.4 = (bf16[1024,128]{1,0:T(8,128)(2,1)S(1)}, bf16[1024,128]{1,0:T(8,128)(2,1)}, u32[]{:S(2)}) copy-start(bf16[1024,128]{1,0:T(8,128)(2,1)} %constant.18.clone.edge_ref) | copy-start | bytes 786436
  1.8 4.6 %collective-permute-start = (f32[64,128]{1,0:T(8,128)S(1)}, f32[64,128]{1,0:T(8,128)S(1)}, u32[]{:S(2)}, u32[]{:S(2)}) collective-permute-start(f32[64,128]{1,0:T(8,128)S(1)} %history.1), channel_id=1, source_target_pairs={{0,1},{1,2},{2,3},{4,5},{5,6},{6,7},{8,9},{9,10},{10,11},{12,13},{... | collective-permute-start | bytes 98312 | tf_op jit(solution)/shard_map/ppermute | solution.py:371
  6.3 9.6 %copy-start.12 = (s32[8,3]{0,1:T(4,128)S(1)}, s32[8,3]{0,1:T(4,128)}, u32[]{:S(2)}) copy-start(s32[8,3]{0,1:T(4,128)} %param.16) | copy-start | bytes 292
  6.3 9.7 %copy-start.6 = (s32[4]{0:T(128)S(1)}, s32[4]{0:T(128)}, u32[]{:S(2)}) copy-start(s32[4]{0:T(128)} %offs_ref) | copy-start | bytes 52
  6.3 20.2 %copy-start.1 = (bf16[512,512]{1,0:T(8,128)(2,1)S(1)}, bf16[512,512]{1,0:T(8,128)(2,1)}, u32[]{:S(2)}) copy-start(bf16[512,512]{1,0:T(8,128)(2,1)} %constant.22.clone.pack_ref) | copy-start | bytes 1572868
  6.3 20.2 %copy-start.5 = (bf16[128,128]{1,0:T(8,128)(2,1)S(1)}, bf16[128,128]{1,0:T(8,128)(2,1)}, u32[]{:S(2)}) copy-start(bf16[128,128]{1,0:T(8,128)(2,1)} %constant.21.clone.flip_ref) | copy-start | bytes 98308
  6.4 20.2 %copy-start.7 = (s32[8]{0:T(128)S(1)}, s32[8]{0:T(128)}, u32[]{:S(2)}) copy-start(s32[8]{0:T(128)} %count_ref.1) | copy-start | bytes 100
  7.9 36.7 %copy-start = (bf16[512,1024]{1,0:T(8,128)(2,1)S(1)}, bf16[512,1024]{1,0:T(8,128)(2,1)}, u32[]{:S(2)}) copy-start(bf16[512,1024]{1,0:T(8,128)(2,1)} %constant.23.clone.inv_ref) | copy-start | bytes 3145732
  7.9 18.7 %all-to-all-start = ((bf16[32,2,16,128]{3,2,1,0:T(8,128)(2,1)}), bf16[32,2,16,128]{3,2,1,0:T(8,128)(2,1)S(1)}, u32[]{:S(2)}, u32[]{:S(2)}) async-start(bf16[32,2,16,128]{3,2,1,0:T(8,128)(2,1)} %whiten.1), calls=%async_computation | async-start | bytes 524288 | tf_op jit(solution)/shard_map/all_to_all | solution.py:403

commit v8 on v7

--- a/solution.py
+++ b/solution.py
@@ -214,65 +214,82 @@
     return matrix.reshape(owners * LANES, owners * LANES).astype(jnp.bfloat16)
 
 
-def cross_kernel(
-    partner_ref, count_ref, moves_ref, flip_ref, pack_ref, white_ref, out_ref, turned_ref
-):
+def halo_kernel(white_ref, up_ref, down_ref):
+    rows = white_ref.shape[0] * 2 * GROUP
+    white = white_ref[...].reshape(rows, LANES).astype(F32)
+    turned = pltpu.roll(white, SPAN, 1)
+    half = rows // 2
+    lane = lax.broadcasted_iota(jnp.int32, (half, LANES), 1)
+    up_ref[...] = jnp.where(lane < SPAN, turned[:half], white[half:]).astype(BF16)
+    down_ref[...] = jnp.where(lane < SPAN, white[:half], turned[half:]).astype(BF16)
+
+
+def near_kernel(white_ref, before_ref, after_ref, moves_ref, inv_ref, out_ref):
+    rows = white_ref.shape[0] * 2 * GROUP
+    half = rows // 2
+    noff = out_ref.shape[0]
+    before, after = before_ref[...].astype(F32), after_ref[...].astype(F32)
+    lane = lax.broadcasted_iota(jnp.int32, (half, LANES), 1)
+    upper = jnp.where(lane < SPAN, after, pltpu.roll(before, SPAN, 1))
+    lower = jnp.where(lane < SPAN, pltpu.roll(after, SPAN, 1), before)
+    edge = jnp.concatenate([upper, lower], axis=0).astype(BF16)
+    own = white_ref[...].reshape(rows, LANES)
+    far = mm(jnp.concatenate([own, edge], axis=1), moves_ref[...])
+    own = own.astype(F32).reshape(-1, 2, GROUP, LANES)
+    columns = []
+    for o in range(noff):
+        other = far[:, o * LANES : (o + 1) * LANES].reshape(own.shape)
+        real = own[:, 0] * other[:, 0] + own[:, 1] * other[:, 1]
+        imag = own[:, 1] * other[:, 0] - own[:, 0] * other[:, 1]
+        columns.append(jnp.stack([real, imag], axis=1).reshape(rows, LANES).astype(BF16))
+    both = mm(inv_ref[...], jnp.concatenate(columns, axis=1))
+    lags = both[:LAGS] + both[LAGS:]
+    for o in range(noff):
+        out_ref[o] = lags[:, o * LANES : (o + 1) * LANES]
+
+
+def turn_kernel(lags_ref, near_ref):
+    for t in range(lags_ref.shape[0]):
+        near_ref[:, t, :] = lags_ref[t].T
+
+
+def loop_kernel(partner_ref, count_ref, flip_ref, pack_ref, white_ref, out_ref, turned_ref):
     blocks, segs, _, bins, _ = white_ref.shape
     owners = out_ref.shape[1]
     slots = partner_ref.shape[1]
-    noff = moves_ref.shape[1] // LANES
-    near_each = noff // owners
     rows = segs * 2 * bins
     packed_rows = 2 * bins // owners
     flats = [white_ref[b].reshape(rows, LANES) for b in range(blocks)]
-    every = jnp.concatenate(flats, axis=0)
-    turned_ref[...] = mm(every, flip_ref[...]).reshape(turned_ref.shape)
-    before = jnp.concatenate(flats[-1:] + flats[:-1], axis=0)
-    after = jnp.concatenate(flats[1:] + flats[:1], axis=0)
-    lane = lax.broadcasted_iota(jnp.int32, every.shape, 1)
-    edge = jnp.where(lane < SPAN, after.astype(F32), before.astype(F32)).astype(BF16)
-    moved = mm(jnp.concatenate([every, edge], axis=1), moves_ref[...])
-
-    def products(own, far):
-        own = own.reshape(segs, 2, bins, LANES)
-        far = far.reshape(segs, 2, bins, LANES)
-        real = jnp.sum(own[:, 0] * far[:, 0] + own[:, 1] * far[:, 1], axis=0)
-        imag = jnp.sum(own[:, 1] * far[:, 0] - own[:, 0] * far[:, 1], axis=0)
-        return jnp.concatenate([real, imag], axis=0)
-
-    near, loops = [], []
+    turned_ref[...] = mm(jnp.concatenate(flats, axis=0), flip_ref[...]).reshape(turned_ref.shape)
+    loops = []
     for b in range(blocks):
-        own = flats[b].astype(F32)
-        far = moved[b * rows : (b + 1) * rows]
-        near.append([products(own, far[:, o * LANES : (o + 1) * LANES]) for o in range(noff)])
+        own = flats[b].astype(F32).reshape(segs, 2, bins, LANES)
         for k in range(slots):
             partner = jnp.clip(partner_ref[b, k], 0, blocks - 1)
             live = (k < count_ref[b]).astype(F32)
-            pair = products(own, turned_ref[partner]) * live
+            far = turned_ref[partner].reshape(segs, 2, bins, LANES)
+            real = jnp.sum(own[:, 0] * far[:, 0] + own[:, 1] * far[:, 1], axis=0)
+            imag = jnp.sum(own[:, 1] * far[:, 0] - own[:, 0] * far[:, 1], axis=0)
+            pair = jnp.concatenate([real, imag], axis=0) * live
             groups = [pair[g * packed_rows : (g + 1) * packed_rows] for g in range(owners)]
             loops.append(jnp.concatenate(groups, axis=1))
     packed = mm(jnp.concatenate(loops, axis=0).astype(BF16), pack_ref[...])
     depth = slots * packed_rows
     for b in range(blocks):
         for q in range(owners):
-            tail = packed[b * depth : (b + 1) * depth, q * LANES : (q + 1) * LANES]
-            mine = near[b][q * near_each : (q + 1) * near_each] + [tail]
-            out_ref[b, q] = jnp.concatenate(mine, axis=0).astype(BF16)
-
-
-def lag_kernel(slots, spec_ref, inv_ref, near_ref, loop_ref):
+            tile = packed[b * depth : (b + 1) * depth, q * LANES : (q + 1) * LANES]
+            out_ref[b, q] = tile.astype(BF16)
+
+
+def loop_lag_kernel(slots, spec_ref, inv_ref, loop_ref):
     sources = spec_ref.shape[0]
     rows = inv_ref.shape[1] // sources
-    near_each = near_ref.shape[1]
     share = loop_ref.shape[0] // slots
     owners = LANES // share
     step = rows // owners
-    columns = [
-        spec_ref[:, t * rows : (t + 1) * rows].reshape(sources * rows, LANES)
-        for t in range(near_each)
-    ]
-    loop = spec_ref[:, near_each * rows :].astype(F32)
+    loop = spec_ref[...].astype(F32)
     lane = lax.broadcasted_iota(jnp.int32, (sources, step, LANES), 2)
+    columns = []
     for k in range(slots):
         tile = loop[:, k * step : (k + 1) * step]
         groups = [
@@ -282,11 +299,8 @@
         columns.append(jnp.concatenate(groups, axis=1).astype(BF16).reshape(sources * rows, LANES))
     both = mm(inv_ref[...], jnp.concatenate(columns, axis=1))
     lags = both[:LAGS] + both[LAGS:]
-    for t in range(near_each):
-        near_ref[:, t, :] = lags[:, t * LANES : (t + 1) * LANES].T
     for k in range(slots):
-        first = (near_each + k) * LANES
-        turned = lags[:, first : first + LANES].T
+        turned = lags[:, k * LANES : (k + 1) * LANES].T
         loop_ref[k * share : (k + 1) * share] = sum(
             turned[g * share : (g + 1) * share] for g in range(owners)
         )
@@ -308,40 +322,26 @@
     return pltpu.with_memory_space_constraint(jnp.asarray(array), pltpu.HBM)
 
 
-def finish_plain(white, offsets, loop_partner, loop_count, owners, total_segs):
-    blocks, segs, _, bins, chans = white.shape
+def loops_plain(white, loop_partner, loop_count, owners, inverse):
+    blocks, _, _, bins, chans = white.shape
     devices = blocks * owners
-    noff, slots = offsets.shape[0], loop_partner.shape[1]
+    slots = loop_partner.shape[1]
     share = chans // owners
     wide = white.astype(F32)
-    flat = jnp.moveaxis(wide, 0, 3).reshape(segs, 2, bins, blocks * chans)
-
-    def products(own, far):
-        real = jnp.sum(own[:, 0] * far[:, 0] + own[:, 1] * far[:, 1], axis=0)
-        imag = jnp.sum(own[:, 1] * far[:, 0] - own[:, 0] * far[:, 1], axis=0)
-        return jnp.stack([real, imag]).astype(BF16)
-
-    near = [products(flat, jnp.roll(flat, -offsets[o], axis=3)) for o in range(noff)]
-    near = jnp.stack(near).reshape(owners, noff // owners, 2, bins, blocks, chans)
-    near = jnp.moveaxis(near, 4, 0).reshape(devices, noff // owners, 2 * bins, chans)
     loops = []
     for k in range(slots):
         far = jnp.flip(wide[loop_partner[:, k]], axis=4)
-        live = (k < loop_count).astype(BF16)[:, None, None]
-        pair = products(jnp.moveaxis(wide, 0, 2), jnp.moveaxis(far, 0, 2)) * live[None]
+        live = (k < loop_count).astype(F32)[:, None, None]
+        real = jnp.sum(wide[:, :, 0] * far[:, :, 0] + wide[:, :, 1] * far[:, :, 1], axis=1)
+        imag = jnp.sum(wide[:, :, 1] * far[:, :, 0] - wide[:, :, 0] * far[:, :, 1], axis=1)
+        pair = (jnp.stack([real, imag]) * live[None]).astype(BF16)
         loops.append(pair.reshape(2, blocks, bins, owners, share))
     loop = jnp.transpose(jnp.stack(loops), (2, 4, 0, 1, 3, 5))
     loop = loop.reshape(devices, slots, 2 * bins, share)
-    order = np.repeat(bin_order().reshape(devices, 1, bins), 2, axis=1).reshape(-1)
-    part = np.broadcast_to(np.arange(2).reshape(1, 2, 1), (devices, 2, bins)).reshape(-1)
-    inverse = inverse_table(total_segs, order, part).astype(np.float32)
-    inverse = inverse.reshape(LAGS, devices, 2 * bins)
-    results = []
-    for array in (near, loop):
-        summed = lax.all_to_all(array, ("chan", "seg"), 0, 0, tiled=True).astype(F32)
-        lags = jnp.einsum("dtvc,ldv->tcl", summed, inverse, precision=lax.Precision.HIGHEST)
-        results.append(lags)
-    return jnp.moveaxis(results[0], 0, 1), results[1][None]
+    summed = lax.all_to_all(loop, ("chan", "seg"), 0, 0, tiled=True).astype(F32)
+    table = inverse.astype(np.float32).reshape(LAGS, devices, 2 * bins)
+    lags = jnp.einsum("dtvc,ldv->tcl", summed, table, precision=lax.Precision.HIGHEST)
+    return lags[None]
 
 
 def body(recording, filter_taps, offsets, loop_partner, loop_count):
@@ -397,14 +397,25 @@
     )(spec, rim, mean, head, edge_table(), band, band_share)
 
     white, offsets = lax.optimization_barrier((white, offsets))
+    spread = white
     if bins != GROUP:
-        white = jnp.moveaxis(white, 1, 0).reshape(2, devices, bins, LANES)
-        white = jnp.moveaxis(white, 0, 1)
-    moved = lax.all_to_all(white, ("chan", "seg"), 0, 0, tiled=True)
+        spread = jnp.moveaxis(white, 1, 0).reshape(2, devices, bins, LANES)
+        spread = jnp.moveaxis(spread, 0, 1)
+    moved = lax.all_to_all(spread, ("chan", "seg"), 0, 0, tiled=True)
     moved = moved.reshape(chan_count, seg_count, 2, bins, LANES)
-    if bins % GROUP or 2 * bins % (8 * seg_count):
-        return finish_plain(moved, offsets, loop_partner, loop_count, seg_count, seg_count)
-
+
+    half = jax.ShapeDtypeStruct((BINS, LANES), BF16)
+    up, down = pl.pallas_call(
+        halo_kernel,
+        out_shape=[half, half],
+        in_specs=vmem(1),
+        out_specs=vmem(2),
+        compiler_params=PARAMS,
+        name="halo",
+    )(white)
+    ring = [(i, (i + 1) % chan_count) for i in range(chan_count)]
+    before = lax.ppermute(up, "chan", ring)
+    after = lax.ppermute(down, "chan", [(j, i) for i, j in ring])
     moves = pl.pallas_call(
         moves_kernel,
         out_shape=jax.ShapeDtypeStruct((2 * LANES, noff * LANES), BF16),
@@ -413,35 +424,56 @@
         compiler_params=PARAMS,
         name="offset_moves",
     )(offsets)
-    flip = np.eye(LANES, dtype=np.float32)[::-1].astype(jnp.bfloat16)
-    out_rows = near_each * 2 * bins + slots * (2 * bins // seg_count)
-    crossed = pl.pallas_call(
-        cross_kernel,
-        out_shape=jax.ShapeDtypeStruct((chan_count, seg_count, out_rows, LANES), BF16),
-        in_specs=smem(2) + vmem(4),
+    order = np.repeat(bin_order().reshape(GROUPS, 1, GROUP), 2, axis=1).reshape(-1)
+    part = np.broadcast_to(np.arange(2).reshape(1, 2, 1), (GROUPS, 2, GROUP)).reshape(-1)
+    inverse = np.concatenate(split_np(inverse_table(seg_count, order, part)), axis=0)
+    lags = pl.pallas_call(
+        near_kernel,
+        out_shape=jax.ShapeDtypeStruct((noff, LAGS, LANES), F32),
+        in_specs=vmem(5),
         out_specs=pl.BlockSpec(memory_space=pltpu.VMEM),
-        scratch_shapes=[pltpu.VMEM((chan_count, seg_count * 2 * bins, LANES), F32)],
-        compiler_params=PARAMS,
-        name="cross_spectra",
-    )(loop_partner, loop_count, moves, flip, pack_matrix(seg_count), moved)
-    crossed = crossed.reshape(devices, out_rows, LANES)
-    summed = lax.all_to_all(crossed, ("chan", "seg"), 0, 0, tiled=True)
-
-    order = np.repeat(bin_order().reshape(devices, 1, bins), 2, axis=1).reshape(-1)
-    part = np.broadcast_to(np.arange(2).reshape(1, 2, 1), (devices, 2, bins)).reshape(-1)
-    inverse = np.concatenate(split_np(inverse_table(seg_count, order, part)), axis=0)
-    near, loop = pl.pallas_call(
-        functools.partial(lag_kernel, slots),
-        out_shape=[
-            jax.ShapeDtypeStruct((chans, near_each, LAGS), F32),
-            jax.ShapeDtypeStruct((slots * share, LAGS), F32),
-        ],
-        in_specs=vmem(2),
-        out_specs=vmem(2),
-        compiler_params=PARAMS,
-        name="lags",
-    )(summed, inverse)
-    return near, loop.reshape(1, slots, share, LAGS)
+        compiler_params=PARAMS,
+        name="near_lags",
+    )(white, before, after, moves, inverse)
+    lags = lax.psum_scatter(lags, "seg", scatter_dimension=0, tiled=True)
+
+    if bins % GROUP or 2 * bins % (8 * seg_count):
+        order = np.repeat(bin_order().reshape(devices, 1, bins), 2, axis=1).reshape(-1)
+        part = np.broadcast_to(np.arange(2).reshape(1, 2, 1), (devices, 2, bins)).reshape(-1)
+        loop_inverse = inverse_table(seg_count, order, part)
+        loop = loops_plain(moved, loop_partner, loop_count, seg_count, loop_inverse)
+    else:
+        flip = np.eye(LANES, dtype=np.float32)[::-1].astype(jnp.bfloat16)
+        out_rows = slots * (2 * bins // seg_count)
+        crossed = pl.pallas_call(
+            loop_kernel,
+            out_shape=jax.ShapeDtypeStruct((chan_count, seg_count, out_rows, LANES), BF16),
+            in_specs=smem(2) + vmem(3),
+            out_specs=pl.BlockSpec(memory_space=pltpu.VMEM),
+            scratch_shapes=[pltpu.VMEM((chan_count, seg_count * 2 * bins, LANES), F32)],
+            compiler_params=PARAMS,
+            name="loop_spectra",
+        )(loop_partner, loop_count, flip, pack_matrix(seg_count), moved)
+        crossed = crossed.reshape(devices, out_rows, LANES)
+        summed = lax.all_to_all(crossed, ("chan", "seg"), 0, 0, tiled=True)
+        loop = pl.pallas_call(
+            functools.partial(loop_lag_kernel, slots),
+            out_shape=jax.ShapeDtypeStruct((slots * share, LAGS), F32),
+            in_specs=vmem(2),
+            out_specs=pl.BlockSpec(memory_space=pltpu.VMEM),
+            compiler_params=PARAMS,
+            name="loop_lags",
+        )(summed, inverse)
+        loop = loop.reshape(1, slots, share, LAGS)
+    near = pl.pallas_call(
+        turn_kernel,
+        out_shape=jax.ShapeDtypeStruct((chans, near_each, LAGS), F32),
+        in_specs=vmem(1),
+        out_specs=pl.BlockSpec(memory_space=pltpu.VMEM),
+        compiler_params=PARAMS,
+        name="near_turn",
+    )(lags)
+    return near, loop
 
 
 def solution(mesh):

time: 46.4 us -> 67.9 us (1.46)
  between operations: 0.85 us -> 14.2 us
  waiting for transfers between devices: 9.9 us -> 15.5 us
  blocking collectives: 16.6 us -> 11.1 us
  Pallas kernels: 8.12 us -> 12.6 us
  starting transfers between devices: 10.5 us -> 12.9 us
  local copies, waits for them, and re-layouts: 0.16 us -> 1.06 us
    ppermute x0 -> x2, starting transfers between devices: none -> 5.5 us  [the longest x1 3.1 us: body(): after = lax.ppermute(down, 'chan', [(j, i) for i, j in ring])]
    all_to_all x1, blocking collectives: 16.6 us -> 11.1 us  [body(): summed = lax.all_to_all(crossed, ('chan', 'seg'), 0, 0, tiled=True)]
    ppermute x0 -> x2, waiting for transfers between devices: none -> 5 us  [the longest x1 2.67 us: body(): before = lax.ppermute(up, 'chan', ring)]
    pallas_call x2 -> x5, Pallas kernels: 2.99 us -> 7.5 us  [the longest x1 2.8 us: body(): pl.pallas_call(near_kernel, out_shape=jax.ShapeDtypeStruct((noff, LAGS, L...]
    all_to_all x1, starting transfers between devices: 8.05 us -> 4.87 us  [body(): moved = lax.all_to_all(spread, ('chan', 'seg'), 0, 0, tiled=True)]
    unnamed x27 -> x29, local copies, waits for them, and re-layouts: 0.16 us -> 1.06 us
  transfers between devices with their start and end apart: 2 -> 5, of which waited for: 1 -> 3; matrix products, arithmetic and copies ran while one was open for 0% -> 0% of each run, Pallas kernels for 6% -> 8%
where the time goes in v8:
time: 67.9 us; the launch traced here: 67.5 us
  waiting for transfers between devices  15.5 us (23%)
  between operations  14.2 us (21%)
  starting transfers between devices  12.9 us (19%)
  Pallas kernels  12.6 us (19%)
  blocking collectives  11.1 us (16%)
  local copies, waits for them, and re-layouts  1.06 us (2%)
    all_to_all x1, blocking collectives, body(): summed = lax.all_to_all(crossed, ('chan', 'seg'), 0, 0, tiled=True)  11.1 us
    all_to_all x1, waiting for transfers between devices, body(): moved = lax.all_to_all(spread, ('chan', 'seg'), 0, 0, tiled=True)  10.5 us
    all_to_all x1, starting transfers between devices, body(): moved = lax.all_to_all(spread, ('chan', 'seg'), 0, 0, tiled=True)  4.87 us
    ppermute x1, starting transfers between devices, body(): after = lax.ppermute(down, 'chan', [(j, i) for i, j in ring])  3.1 us
    pallas_call x1, Pallas kernels, body(): pl.pallas_call(near_kernel, out_shape=jax.ShapeDtypeStruct((noff, LAGS, L...  2.8 us
    ppermute x1, waiting for transfers between devices, body(): before = lax.ppermute(up, 'chan', ring)  2.67 us
    ppermute x1, starting transfers between devices, body(): rim = lax.ppermute(rim, 'seg', route)  2.49 us
    ppermute x1, starting transfers between devices, body(): before = lax.ppermute(up, 'chan', ring)  2.4 us
  transfers between devices with their start and end apart: 5, of which 3 were waited for; matrix products, arithmetic and copies ran while one was open for 0% of the time, Pallas kernels for 8%

profile of v8, /device:TPU:0, one launch (start us, length us, event | category | flops | bytes accessed | tf_op | source)
XLA Modules:
  0.0 67.5 jit_solution(5697255696397305685)
XLA Ops:
  7.2 0.0 copy-start.11
  7.2 0.0 copy-start.12
  7.2 0.0 copy-start.10
  7.2 0.0 reduce-scatter.2.cloned.1.call-start
  7.2 0.0 copy-start.9
  7.3 1.1 %history.1 = f32[64,128]{1,0:T(8,128)S(1)} custom-call(f32[128,4096]{1,0:T(8,128)} %rec_hbm.1), custom_call_target="tpu_custom_call" | custom-call | flops 10000000000 | bytes 20000000 | tf_op jit(solution)/shard_map/history/pallas_call | solution.py:359
  8.3 0.0 copy-start.2
  8.3 0.0 copy-start.3
  8.4 0.0 copy-start.4
  8.4 2.5 %collective-permute-start = (f32[64,128]{1,0:T(8,128)S(1)}, f32[64,128]{1,0:T(8,128)S(1)}, u32[]{:S(2)}, u32[]{:S(2)}) collective-permute-start(f32[64,128]{1,0:T(8,128)S(1)} %history.1), channel_id=1, source_target_pairs={{0,1},{1,2},{2,3},{4,5},{5,6},{6,7},{8,9},{9,10},{10,11},{12,13},{... | collective-permute-start | bytes 98312 | tf_op jit(solution)/shard_map/ppermute | solution.py:371
  10.9 0.0 copy-done.11
  10.9 0.0 copy-done.12
  10.9 0.0 copy-done.10
  10.9 0.0 copy-done.9
  10.9 0.0 copy-start.8
  10.9 2.0 %filter_and_transform.1 = (f32[1024,128]{1,0:T(8,128)S(1)}, f32[128,128]{1,0:T(8,128)S(1)}, f32[16,128]{1,0:T(8,128)S(1)}) custom-call(f32[1,64]{1,0:T(1,128)S(1)} %bitcast.6, f32[128,4096]{1,0:T(8,128)S(1)} %copy-done.9, bf16[256,768]{1,0:T(8,128)(2,1)S(1)} %copy-done.11, f32[256,128]{1,0:T(8,128)S(1)} %copy-done.12), custom_call_target="tpu_custom_call" | custom-call | flops 1000000000 | bytes 5000000 | tf_op jit(solution)/shard_map/filter_and_transform/pallas_call | solution.py:373
  12.9 0.0 copy-start
  12.9 0.0 collective-permute-done.rim_ref
  12.9 0.0 copy-done.2
  12.9 0.0 copy-done.3
  13.0 0.0 copy-done.4
  13.0 1.5 %whiten.1.white_ref = bf16[32,2,16,128]{3,2,1,0:T(8,128)(2,1)} custom-call(f32[1024,128]{1,0:T(8,128)S(1)} %get-tuple-element.9.spec_ref, f32[64,128]{1,0:T(8,128)S(1)} %collective-permute-done.rim_ref, f32[128,128]{1,0:T(8,128)S(1)} %get-tuple-element.10.mean_ref, f32[16,128]{1,0:T(8,128)S(1)} %get-tuple-element.11.head_ref, ...), custom_call_target="tpu_custom_call" | custom-call | tf_op jit(solution)/shard_map/whiten/pallas_call | solution.py:390
  14.4 0.0 copy-start.13
  14.5 0.0 copy-start.1
  14.5 0.0 copy-start.6
  14.5 0.0 copy-start.7
  14.5 1.1 %halo.1 = (bf16[512,128]{1,0:T(8,128)(2,1)S(1)}, bf16[512,128]{1,0:T(8,128)(2,1)S(1)}) custom-call(bf16[32,2,16,128]{3,2,1,0:T(8,128)(2,1)} %whiten.1.white_ref), custom_call_target="tpu_custom_call" | custom-call | tf_op jit(solution)/shard_map/halo/pallas_call | solution.py:408
  15.6 2.4 %collective-permute-start.1 = (bf16[512,128]{1,0:T(8,128)(2,1)S(1)}, bf16[512,128]{1,0:T(8,128)(2,1)S(1)}, u32[]{:S(2)}, u32[]{:S(2)}) collective-permute-start(bf16[512,128]{1,0:T(8,128)(2,1)S(1)} %get-tuple-element.13), channel_id=1, source_target_pairs={{0,4},{4,8},{8,12},{12,16},{16,20},{20,24},{24,28},{28,0},{1,5},{5... | collective-permute-start | bytes 393224 | tf_op jit(solution)/shard_map/ppermute | solution.py:417
  18.0 3.1 %collective-permute-start.2 = (bf16[512,128]{1,0:T(8,128)(2,1)S(1)}, bf16[512,128]{1,0:T(8,128)(2,1)S(1)}, u32[]{:S(2)}, u32[]{:S(2)}) collective-permute-start(bf16[512,128]{1,0:T(8,128)(2,1)S(1)} %get-tuple-element.14), channel_id=1, source_target_pairs={{4,0},{8,4},{12,8},{16,12},{20,16},{24,20},{28,24},{0,28},{5,1},{9... | collective-permute-start | bytes 393224 | tf_op jit(solution)/shard_map/ppermute | solution.py:418
  21.1 0.0 copy-done.8
  21.1 0.6 offset_moves.1.moves_ref
  21.7 2.7 %collective-permute-done.1.before_ref = bf16[512,128]{1,0:T(8,128)(2,1)S(1)} collective-permute-done((bf16[512,128]{1,0:T(8,128)(2,1)S(1)}, bf16[512,128]{1,0:T(8,128)(2,1)S(1)}, u32[]{:S(2)}, u32[]{:S(2)}) %collective-permute-start.1) | collective-permute-done | bytes 131104 | tf_op jit(solution)/shard_map/ppermute | solution.py:417
  24.4 2.3 %collective-permute-done.2.after_ref = bf16[512,128]{1,0:T(8,128)(2,1)S(1)} collective-permute-done((bf16[512,128]{1,0:T(8,128)(2,1)S(1)}, bf16[512,128]{1,0:T(8,128)(2,1)S(1)}, u32[]{:S(2)}, u32[]{:S(2)}) %collective-permute-start.2) | collective-permute-done | bytes 131104 | tf_op jit(solution)/shard_map/ppermute | solution.py:418
  26.7 0.0 copy-done
  26.7 2.8 %near_lags.1 = f32[4,256,128]{2,1,0:T(8,128)} custom-call(bf16[32,2,16,128]{3,2,1,0:T(8,128)(2,1)} %whiten.1.white_ref, bf16[512,128]{1,0:T(8,128)(2,1)S(1)} %collective-permute-done.1.before_ref, bf16[512,128]{1,0:T(8,128)(2,1)S(1)} %collective-permute-done.2.after_ref, bf16[256,512]{1,0:T(8,128)(2,1)S(1)} %offset_moves.1.moves_ref, ...), custom_call_target="tpu_custom_call" | custom-call | tf_op jit(solution)/shard_map/near_lags/pallas_call | solution.py:430
  29.5 0.0 reduce-scatter.2.cloned.1.call-update
  29.6 4.9 %all-to-all-start = ((bf16[32,2,16,128]{3,2,1,0:T(8,128)(2,1)}), bf16[32,2,16,128]{3,2,1,0:T(8,128)(2,1)S(1)}, u32[]{:S(2)}, u32[]{:S(2)}) async-start(bf16[32,2,16,128]{3,2,1,0:T(8,128)(2,1)} %whiten.1.white_ref), calls=%async_computation.1 | async-start | bytes 524288 | tf_op jit(solution)/shard_map/all_to_all | solution.py:404
  34.4 0.0 copy-done.13
  34.4 0.1 copy.15.partner_ref
  34.5 10.5 %all-to-all-done = bf16[32,2,16,128]{3,2,1,0:T(8,128)(2,1)S(1)} async-done(((bf16[32,2,16,128]{3,2,1,0:T(8,128)(2,1)}), bf16[32,2,16,128]{3,2,1,0:T(8,128)(2,1)S(1)}, u32[]{:S(2)}, u32[]{:S(2)}) %all-to-all-start) | async-done | bytes 262176 | tf_op jit(solution)/shard_map/all_to_all | solution.py:404
  45.0 0.0 copy-done.1
  45.0 0.0 copy-done.6
  45.0 0.0 copy-done.7
  45.0 1.3 %loop_spectra.1 = bf16[8,4,24,128]{3,2,1,0:T(8,128)(2,1)S(1)} custom-call(s32[8,3]{1,0:T(8,128)S(1)} %copy.15.partner_ref, s32[8]{0:T(128)S(1)} %copy-done.7, bf16[128,128]{1,0:T(8,128)(2,1)S(1)} %copy-done.6, bf16[512,512]{1,0:T(8,128)(2,1)S(1)} %copy-done.1, bf16[8,4,2,16,128]{4,3,2,1,0:T(8,128)(2,1)S(1)} %bitcast.4), custom_call_target="tpu_custom_call" | custom-call | tf_op jit(solution)/shard_map/loop_spectra/pallas_call | solution.py:448
  46.3 11.1 %all_to_all.10.spec_ref = bf16[32,24,128]{2,1,0:T(8,128)(2,1)S(1)} all-to-all(bf16[32,24,128]{2,1,0:T(8,128)(2,1)S(1)} %bitcast.5), channel_id=1, replica_groups=mesh['chan'=8,'seg'=4] {'chan','seg'}, dimensions={0} | all-to-all | bytes 393216 | tf_op jit(solution)/shard_map/all_to_all | solution.py:458
  57.4 1.5 %loop_lags.1 = f32[96,256]{1,0:T(8,128)} custom-call(bf16[32,24,128]{2,1,0:T(8,128)(2,1)S(1)} %all_to_all.10.spec_ref, bf16[512,1024]{1,0:T(8,128)(2,1)S(1)} %copy-done), custom_call_target="tpu_custom_call" | custom-call | tf_op jit(solution)/shard_map/loop_lags/pallas_call | solution.py:459
  58.9 0.9 %copy-done.5 = f32[1,256,128]{2,1,0:T(8,128)S(1)} copy-done((f32[1,256,128]{2,1,0:T(8,128)S(1)}, f32[1,256,128]{2,1,0:T(8,128)}, u32[]{:S(2)}) %copy-start.5) | copy-done | bytes 131096
  59.8 0.8 %near_turn.1 = f32[128,1,256]{2,1,0:T(1,128)} custom-call(f32[1,256,128]{2,1,0:T(8,128)S(1)} %copy-done.5), custom_call_target="tpu_custom_call" | custom-call | tf_op jit(solution)/shard_map/near_turn/pallas_call | solution.py:468
  (2 shorter events, 0.0 us)
Async XLA Ops:
  7.2 3.7 %copy-start.11 = (bf16[256,768]{1,0:T(8,128)(2,1)S(1)}, bf16[256,768]{1,0:T(8,128)(2,1)}, u32[]{:S(2)}) copy-start(bf16[256,768]{1,0:T(8,128)(2,1)} %constant.16.clone.tab_ref) | copy-start | bytes 1179652
  7.2 3.7 %copy-start.12 = (f32[256,128]{1,0:T(8,128)S(1)}, f32[256,128]{1,0:T(8,128)}, u32[]{:S(2)}) copy-start(f32[256,128]{1,0:T(8,128)} %constant.17.clone.twist_ref) | copy-start | bytes 393220
  7.2 3.7 %copy-start.10 = (f32[64]{0:T(128)S(1)}, f32[64]{0:T(128)}, u32[]{:S(2)}) copy-start(f32[64]{0:T(128)} %param.14) | copy-start | bytes 772
  7.2 51.7 %reduce-scatter.2.cloned.1.call-start = ((), (), s32[]{:S(2)}) async-start(), calls=%async_computation.3 | async-start | bytes 655360 | tf_op jit(solution)/shard_map/reduce_scatter | solution.py:438
  7.2 3.7 %copy-start.9 = (f32[128,4096]{1,0:T(8,128)S(1)}, f32[128,4096]{1,0:T(8,128)}, u32[]{:S(2)}) copy-start(f32[128,4096]{1,0:T(8,128)} %rec_hbm.1) | copy-start | bytes 6291460
  8.3 4.6 %copy-start.2 = (bf16[512,512]{1,0:T(8,128)(2,1)S(1)}, bf16[512,512]{1,0:T(8,128)(2,1)}, u32[]{:S(2)}) copy-start(bf16[512,512]{1,0:T(8,128)(2,1)} %constant.19.clone.band_ref) | copy-start | bytes 1572868
  8.3 4.6 %copy-start.3 = (bf16[1024,128]{1,0:T(8,128)(2,1)S(1)}, bf16[1024,128]{1,0:T(8,128)(2,1)}, u32[]{:S(2)}) copy-start(bf16[1024,128]{1,0:T(8,128)(2,1)} %constant.18.clone.edge_ref) | copy-start | bytes 786436
  8.4 4.6 %copy-start.4 = (f32[512,128]{1,0:T(8,128)S(1)}, f32[512,128]{1,0:T(8,128)}, u32[]{:S(2)}) copy-start(f32[512,128]{1,0:T(8,128)} %constant.20.clone.share_ref) | copy-start | bytes 786436
  8.4 4.6 %collective-permute-start = (f32[64,128]{1,0:T(8,128)S(1)}, f32[64,128]{1,0:T(8,128)S(1)}, u32[]{:S(2)}, u32[]{:S(2)}) collective-permute-start(f32[64,128]{1,0:T(8,128)S(1)} %history.1), channel_id=1, source_target_pairs={{0,1},{1,2},{2,3},{4,5},{5,6},{6,7},{8,9},{9,10},{10,11},{12,13},{... | collective-permute-start | bytes 98312 | tf_op jit(solution)/shard_map/ppermute | solution.py:371
  10.9 10.2 %copy-start.8 = (s32[4]{0:T(128)S(1)}, s32[4]{0:T(128)}, u32[]{:S(2)}) copy-start(s32[4]{0:T(128)} %offs_ref) | copy-start | bytes 52
  12.9 13.8 %copy-start = (bf16[512,1024]{1,0:T(8,128)(2,1)S(1)}, bf16[512,1024]{1,0:T(8,128)(2,1)}, u32[]{:S(2)}) copy-start(bf16[512,1024]{1,0:T(8,128)(2,1)} %constant.21.clone.inv_ref) | copy-start | bytes 3145732
  14.4 20.0 %copy-start.13 = (s32[8,3]{0,1:T(4,128)S(1)}, s32[8,3]{0,1:T(4,128)}, u32[]{:S(2)}) copy-start(s32[8,3]{0,1:T(4,128)} %param.16) | copy-start | bytes 292
  14.5 30.6 %copy-start.1 = (bf16[512,512]{1,0:T(8,128)(2,1)S(1)}, bf16[512,512]{1,0:T(8,128)(2,1)}, u32[]{:S(2)}) copy-start(bf16[512,512]{1,0:T(8,128)(2,1)} %constant.23.clone.pack_ref) | copy-start | bytes 1572868
  14.5 30.6 %copy-start.6 = (bf16[128,128]{1,0:T(8,128)(2,1)S(1)}, bf16[128,128]{1,0:T(8,128)(2,1)}, u32[]{:S(2)}) copy-start(bf16[128,128]{1,0:T(8,128)(2,1)} %constant.22.clone.flip_ref) | copy-start | bytes 98308
  14.5 30.6 %copy-start.7 = (s32[8]{0:T(128)S(1)}, s32[8]{0:T(128)}, u32[]{:S(2)}) copy-start(s32[8]{0:T(128)} %count_ref.1) | copy-start | bytes 100
  15.6 8.8 %collective-permute-start.1 = (bf16[512,128]{1,0:T(8,128)(2,1)S(1)}, bf16[512,128]{1,0:T(8,128)(2,1)S(1)}, u32[]{:S(2)}, u32[]{:S(2)}) collective-permute-start(bf16[512,128]{1,0:T(8,128)(2,1)S(1)} %get-tuple-element.13), channel_id=1, source_target_pairs={{0,4},{4,8},{8,12},{12,16},{16,20},{20,24},{24,28},{28,0},{1,5},{5... | collective-permute-start | bytes 393224 | tf_op jit(solution)/shard_map/ppermute | solution.py:417
  18.0 8.7 %collective-permute-start.2 = (bf16[512,128]{1,0:T(8,128)(2,1)S(1)}, bf16[512,128]{1,0:T(8,128)(2,1)S(1)}, u32[]{:S(2)}, u32[]{:S(2)}) collective-permute-start(bf16[512,128]{1,0:T(8,128)(2,1)S(1)} %get-tuple-element.14), channel_id=1, source_target_pairs={{4,0},{8,4},{12,8},{16,12},{20,16},{24,20},{28,24},{0,28},{5,1},{9... | collective-permute-start | bytes 393224 | tf_op jit(solution)/shard_map/ppermute | solution.py:418
  29.6 15.5 %all-to-all-start = ((bf16[32,2,16,128]{3,2,1,0:T(8,128)(2,1)}), bf16[32,2,16,128]{3,2,1,0:T(8,128)(2,1)S(1)}, u32[]{:S(2)}, u32[]{:S(2)}) async-start(bf16[32,2,16,128]{3,2,1,0:T(8,128)(2,1)} %whiten.1.white_ref), calls=%async_computation.1 | async-start | bytes 524288 | tf_op jit(solution)/shard_map/all_to_all | solution.py:404
  58.9 0.9 %copy-start.5 = (f32[1,256,128]{2,1,0:T(8,128)S(1)}, f32[1,256,128]{2,1,0:T(8,128)}, u32[]{:S(2)}) copy-start(f32[1,256,128]{2,1,0:T(8,128)} %reduce-scatter.2.cloned.1.call-done.lags_ref) | copy-start | bytes 393220
Sparse Core Ops, SparseCore 0:
  29.7 21.9 reduce-scatter.1

commit v9 on v8

--- a/solution.py
+++ b/solution.py
@@ -171,7 +171,16 @@
 
 
 def whiten_kernel(
-    spec_ref, rim_ref, mean_ref, head_ref, edge_ref, band_ref, share_ref, white_ref
+    spec_ref,
+    rim_ref,
+    mean_ref,
+    head_ref,
+    edge_ref,
+    band_ref,
+    share_ref,
+    white_ref,
+    up_ref,
+    down_ref,
 ):
     head_high, head_low = split(head_ref[...])
     rim = jnp.concatenate([pltpu.roll(rim_ref[...], LANES - TAPS, 1), rim_ref[...]], axis=0)
@@ -193,6 +202,11 @@
     scale = 1.0 / (smoothed + (WATER * level + 1e-06))
     white = parted * scale.reshape(GROUPS, 1, GROUP, LANES)
     white_ref[...] = white.astype(BF16)
+    flat = white.reshape(2 * BINS, LANES)
+    turned = pltpu.roll(flat, SPAN, 1)
+    lane = lax.broadcasted_iota(jnp.int32, (BINS, LANES), 1)
+    up_ref[...] = jnp.where(lane < SPAN, turned[:BINS], flat[BINS:]).astype(BF16)
+    down_ref[...] = jnp.where(lane < SPAN, flat[:BINS], turned[BINS:]).astype(BF16)
 
 
 def moves_kernel(offs_ref, moves_ref):
@@ -214,20 +228,11 @@
     return matrix.reshape(owners * LANES, owners * LANES).astype(jnp.bfloat16)
 
 
-def halo_kernel(white_ref, up_ref, down_ref):
-    rows = white_ref.shape[0] * 2 * GROUP
-    white = white_ref[...].reshape(rows, LANES).astype(F32)
-    turned = pltpu.roll(white, SPAN, 1)
-    half = rows // 2
-    lane = lax.broadcasted_iota(jnp.int32, (half, LANES), 1)
-    up_ref[...] = jnp.where(lane < SPAN, turned[:half], white[half:]).astype(BF16)
-    down_ref[...] = jnp.where(lane < SPAN, white[:half], turned[half:]).astype(BF16)
-
-
-def near_kernel(white_ref, before_ref, after_ref, moves_ref, inv_ref, out_ref):
+def near_kernel(white_ref, before_ref, after_ref, moves_ref, inv_ref, *refs):
+    out_refs, lags_ref = refs[:-1], refs[-1]
     rows = white_ref.shape[0] * 2 * GROUP
     half = rows // 2
-    noff = out_ref.shape[0]
+    noff = lags_ref.shape[0]
     before, after = before_ref[...].astype(F32), after_ref[...].astype(F32)
     lane = lax.broadcasted_iota(jnp.int32, (half, LANES), 1)
     upper = jnp.where(lane < SPAN, after, pltpu.roll(before, SPAN, 1))
@@ -245,12 +250,20 @@
     both = mm(inv_ref[...], jnp.concatenate(columns, axis=1))
     lags = both[:LAGS] + both[LAGS:]
     for o in range(noff):
-        out_ref[o] = lags[:, o * LANES : (o + 1) * LANES]
-
-
-def turn_kernel(lags_ref, near_ref):
-    for t in range(lags_ref.shape[0]):
-        near_ref[:, t, :] = lags_ref[t].T
+        lags_ref[o] = lags[:, o * LANES : (o + 1) * LANES]
+    owners = len(out_refs)
+    each = noff // owners
+    place = lax.axis_index("seg")
+    for r in range(owners):
+        first = lax.rem(place + r, owners) * each
+        out_refs[r][...] = lags_ref[pl.ds(first, each)].astype(BF16)
+
+
+def turn_kernel(*refs):
+    near_ref = refs[-1]
+    total = sum(ref[...].astype(F32) for ref in refs[:-1])
+    for t in range(near_ref.shape[1]):
+        near_ref[:, t, :] = total[t].T
 
 
 def loop_kernel(partner_ref, count_ref, flip_ref, pack_ref, white_ref, out_ref, turned_ref):
@@ -387,11 +400,12 @@
     )(taps, recording, short_table(), twiddle_table())
 
     band, band_share = band_tables()
-    white = pl.pallas_call(
+    half = jax.ShapeDtypeStruct((BINS, LANES), BF16)
+    white, up, down = pl.pallas_call(
         whiten_kernel,
-        out_shape=jax.ShapeDtypeStruct((GROUPS, 2, GROUP, LANES), BF16),
+        out_shape=[jax.ShapeDtypeStruct((GROUPS, 2, GROUP, LANES), BF16), half, half],
         in_specs=vmem(7),
-        out_specs=pl.BlockSpec(memory_space=pltpu.VMEM),
+        out_specs=vmem(3),
         compiler_params=PARAMS,
         name="whiten",
     )(spec, rim, mean, head, edge_table(), band, band_share)
@@ -404,15 +418,6 @@
     moved = lax.all_to_all(spread, ("chan", "seg"), 0, 0, tiled=True)
     moved = moved.reshape(chan_count, seg_count, 2, bins, LANES)
 
-    half = jax.ShapeDtypeStruct((BINS, LANES), BF16)
-    up, down = pl.pallas_call(
-        halo_kernel,
-        out_shape=[half, half],
-        in_specs=vmem(1),
-        out_specs=vmem(2),
-        compiler_params=PARAMS,
-        name="halo",
-    )(white)
     ring = [(i, (i + 1) % chan_count) for i in range(chan_count)]
     before = lax.ppermute(up, "chan", ring)
     after = lax.ppermute(down, "chan", [(j, i) for i, j in ring])
@@ -429,13 +434,20 @@
     inverse = np.concatenate(split_np(inverse_table(seg_count, order, part)), axis=0)
     lags = pl.pallas_call(
         near_kernel,
-        out_shape=jax.ShapeDtypeStruct((noff, LAGS, LANES), F32),
+        out_shape=[jax.ShapeDtypeStruct((near_each, LAGS, LANES), BF16)] * seg_count,
         in_specs=vmem(5),
-        out_specs=pl.BlockSpec(memory_space=pltpu.VMEM),
-        compiler_params=PARAMS,
+        out_specs=vmem(seg_count),
+        scratch_shapes=[pltpu.VMEM((noff, LAGS, LANES), F32)],
+        compiler_params=PARAMS,
+        cost_estimate=pl.CostEstimate(
+            flops=10_000_000_000, bytes_accessed=20_000_000, transcendentals=0
+        ),
         name="near_lags",
     )(white, before, after, moves, inverse)
-    lags = lax.psum_scatter(lags, "seg", scatter_dimension=0, tiled=True)
+    lags = list(lags)
+    for r in range(1, seg_count):
+        route = [(i, (i + r) % seg_count) for i in range(seg_count)]
+        lags[r] = lax.ppermute(lags[r], "seg", route)
 
     if bins % GROUP or 2 * bins % (8 * seg_count):
         order = np.repeat(bin_order().reshape(devices, 1, bins), 2, axis=1).reshape(-1)
@@ -468,11 +480,11 @@
     near = pl.pallas_call(
         turn_kernel,
         out_shape=jax.ShapeDtypeStruct((chans, near_each, LAGS), F32),
-        in_specs=vmem(1),
+        in_specs=vmem(seg_count),
         out_specs=pl.BlockSpec(memory_space=pltpu.VMEM),
         compiler_params=PARAMS,
         name="near_turn",
-    )(lags)
+    )(*lags)
     return near, loop
 
 

time: 67.9 us -> 44.5 us (0.66)
  between operations: 14.2 us -> 0.88 us
  blocking collectives: 11.1 us -> 0 us
  starting transfers between devices: 12.9 us -> 23 us
  waiting for transfers between devices: 15.5 us -> 8.2 us
  Pallas kernels: 12.6 us -> 11.4 us
  local copies, waits for them, and re-layouts: 1.06 us -> 0.16 us
    all_to_all x1 -> x0, blocking collectives: 11.1 us -> none  [body(): summed = lax.all_to_all(crossed, ('chan', 'seg'), 0, 0, tiled=True)]
    all_to_all x1, waiting for transfers between devices: 10.5 us -> 5.49 us  [body(): moved = lax.all_to_all(spread, ('chan', 'seg'), 0, 0, tiled=True)]
    all_to_all x0 -> x1, starting transfers between devices: none -> 4.42 us  [body(): summed = lax.all_to_all(crossed, ('chan', 'seg'), 0, 0, tiled=True)]
    ppermute x0 -> x3, starting transfers between devices: none -> 3.31 us  [body(): lags[r] = lax.ppermute(lags[r], 'seg', route)]
    all_to_all x1, starting transfers between devices: 4.87 us -> 8.04 us  [body(): moved = lax.all_to_all(spread, ('chan', 'seg'), 0, 0, tiled=True)]
    ppermute x1, waiting for transfers between devices: 2.67 us -> 0.01 us  [body(): before = lax.ppermute(up, 'chan', ring)]
    ppermute x0 -> x3, waiting for transfers between devices: none -> 2.37 us  [body(): lags[r] = lax.ppermute(lags[r], 'seg', route)]
    ppermute x1, waiting for transfers between devices: 2.33 us -> 0.01 us  [body(): after = lax.ppermute(down, 'chan', [(j, i) for i, j in ring])]
  transfers between devices with their start and end apart: 5 -> 8, of which waited for: 3 -> 5; matrix products, arithmetic and copies ran while one was open for 0% -> 0% of each run, Pallas kernels for 8% -> 17%
where the time goes in v9:
time: 44.5 us; the launch traced here: 43.7 us
  starting transfers between devices  23 us (52%)
  Pallas kernels  11.4 us (26%)
  waiting for transfers between devices  8.2 us (18%)
  between operations  0.88 us (2%)
    all_to_all x1, starting transfers between devices, body(): moved = lax.all_to_all(spread, ('chan', 'seg'), 0, 0, tiled=True)  8.04 us
    all_to_all x1, waiting for transfers between devices, body(): moved = lax.all_to_all(spread, ('chan', 'seg'), 0, 0, tiled=True)  5.49 us
    all_to_all x1, starting transfers between devices, body(): summed = lax.all_to_all(crossed, ('chan', 'seg'), 0, 0, tiled=True)  4.42 us
    ppermute x3, starting transfers between devices, body(): lags[r] = lax.ppermute(lags[r], 'seg', route)  3.31 us
    ppermute x1, starting transfers between devices, body(): after = lax.ppermute(down, 'chan', [(j, i) for i, j in ring])  2.95 us
    ppermute x1, starting transfers between devices, body(): rim = lax.ppermute(rim, 'seg', route)  2.49 us
    ppermute x3, waiting for transfers between devices, body(): lags[r] = lax.ppermute(lags[r], 'seg', route)  2.37 us
    pallas_call x1, Pallas kernels, body(): pl.pallas_call(near_kernel, out_shape=[jax.ShapeDtypeStruct((near_each, L...  2.06 us
  transfers between devices with their start and end apart: 8, of which 5 were waited for; matrix products, arithmetic and copies ran while one was open for 0% of the time, Pallas kernels for 17%

profile of v9, /device:TPU:0, one launch (start us, length us, event | category | flops | bytes accessed | tf_op | source)
XLA Modules:
  0.0 43.7 jit_solution(13670884999326973300)
XLA Ops:
  0.6 0.0 copy-start.10
  0.6 0.0 copy-start.11
  0.7 0.0 copy-start.8
  0.7 0.0 copy-start.9
  0.7 1.1 %history.1 = f32[64,128]{1,0:T(8,128)S(1)} custom-call(f32[128,4096]{1,0:T(8,128)} %rec_hbm.1), custom_call_target="tpu_custom_call" | custom-call | flops 10000000000 | bytes 20000000 | tf_op jit(solution)/shard_map/history/pallas_call | solution.py:372
  1.8 0.0 copy-start.1
  1.8 0.0 copy-start.3
  1.8 0.0 copy-start.4
  1.8 2.5 %collective-permute-start = (f32[64,128]{1,0:T(8,128)S(1)}, f32[64,128]{1,0:T(8,128)S(1)}, u32[]{:S(2)}, u32[]{:S(2)}) collective-permute-start(f32[64,128]{1,0:T(8,128)S(1)} %history.1), channel_id=1, source_target_pairs={{0,1},{1,2},{2,3},{4,5},{5,6},{6,7},{8,9},{9,10},{10,11},{12,13},{... | collective-permute-start | bytes 98312 | tf_op jit(solution)/shard_map/ppermute | solution.py:384
  4.3 0.0 copy-done.10
  4.3 0.0 copy-done.11
  4.3 0.0 copy-done.8
  4.3 0.0 copy-done.9
  4.3 0.0 copy-start.12
  4.3 0.0 copy-start.7
  4.4 2.0 %filter_and_transform.1 = (f32[1024,128]{1,0:T(8,128)S(1)}, f32[128,128]{1,0:T(8,128)S(1)}, f32[16,128]{1,0:T(8,128)S(1)}) custom-call(f32[1,64]{1,0:T(1,128)S(1)} %bitcast.5, f32[128,4096]{1,0:T(8,128)S(1)} %copy-done.8, bf16[256,768]{1,0:T(8,128)(2,1)S(1)} %copy-done.10, f32[256,128]{1,0:T(8,128)S(1)} %copy-done.11), custom_call_target="tpu_custom_call" | custom-call | flops 1000000000 | bytes 5000000 | tf_op jit(solution)/shard_map/filter_and_transform/pallas_call | solution.py:386
  6.3 0.0 copy-start.2
  6.3 0.0 copy-start.5
  6.4 0.0 copy-start.6
  6.4 0.0 copy-start
  6.4 0.0 collective-permute-done.rim_ref
  6.4 0.0 copy-done.1
  6.4 0.0 copy-done.3
  6.4 0.0 copy-done.4
  6.4 1.5 %whiten.1 = (bf16[32,2,16,128]{3,2,1,0:T(8,128)(2,1)}, bf16[512,128]{1,0:T(8,128)(2,1)S(1)}, bf16[512,128]{1,0:T(8,128)(2,1)S(1)}) custom-call(f32[1024,128]{1,0:T(8,128)S(1)} %get-tuple-element.14.spec_ref, f32[64,128]{1,0:T(8,128)S(1)} %collective-permute-done.rim_ref, f32[128,128]{1,0:T(8,128)S(1)} %get-tuple-element.15.mean_ref, ...), custom_call_target="tpu_custom_call" | custom-call | tf_op jit(solution)/shard_map/whiten/pallas_call | solution.py:404
  7.9 8.0 %all-to-all-start = ((bf16[32,2,16,128]{3,2,1,0:T(8,128)(2,1)}), bf16[32,2,16,128]{3,2,1,0:T(8,128)(2,1)S(1)}, u32[]{:S(2)}, u32[]{:S(2)}) async-start(bf16[32,2,16,128]{3,2,1,0:T(8,128)(2,1)} %get-tuple-element.18.white_ref), calls=%async_computation | async-start | bytes 524288 | tf_op jit(solution)/shard_map/all_to_all | solution.py:418
  16.0 1.8 %collective-permute-start.1 = (bf16[512,128]{1,0:T(8,128)(2,1)S(1)}, bf16[512,128]{1,0:T(8,128)(2,1)S(1)}, u32[]{:S(2)}, u32[]{:S(2)}) collective-permute-start(bf16[512,128]{1,0:T(8,128)(2,1)S(1)} %get-tuple-element.19), channel_id=1, source_target_pairs={{0,4},{4,8},{8,12},{12,16},{16,20},{20,24},{24,28},{28,0},{1,5},{5... | collective-permute-start | bytes 393224 | tf_op jit(solution)/shard_map/ppermute | solution.py:422
  17.8 3.0 %collective-permute-start.2 = (bf16[512,128]{1,0:T(8,128)(2,1)S(1)}, bf16[512,128]{1,0:T(8,128)(2,1)S(1)}, u32[]{:S(2)}, u32[]{:S(2)}) collective-permute-start(bf16[512,128]{1,0:T(8,128)(2,1)S(1)} %get-tuple-element.20), channel_id=1, source_target_pairs={{4,0},{8,4},{12,8},{16,12},{20,16},{24,20},{28,24},{0,28},{5,1},{9... | collective-permute-start | bytes 393224 | tf_op jit(solution)/shard_map/ppermute | solution.py:423
  20.7 0.0 copy-done.12
  20.7 0.1 copy.15.partner_ref
  20.8 0.6 %offset_moves.1.moves_ref = bf16[256,512]{1,0:T(8,128)(2,1)S(1)} custom-call(s32[4]{0:T(128)S(1)} %copy-done.7), custom_call_target="tpu_custom_call" | custom-call | tf_op jit(solution)/shard_map/offset_moves/pallas_call | solution.py:424
  21.4 5.5 %all-to-all-done = bf16[32,2,16,128]{3,2,1,0:T(8,128)(2,1)S(1)} async-done(((bf16[32,2,16,128]{3,2,1,0:T(8,128)(2,1)}), bf16[32,2,16,128]{3,2,1,0:T(8,128)(2,1)S(1)}, u32[]{:S(2)}, u32[]{:S(2)}) %all-to-all-start) | async-done | bytes 262176 | tf_op jit(solution)/shard_map/all_to_all | solution.py:418
  26.9 0.0 copy-done.2
  26.9 0.0 copy-done.6
  26.9 2.0 %loop_spectra.1 = bf16[8,4,24,128]{3,2,1,0:T(8,128)(2,1)} custom-call(s32[8,3]{1,0:T(8,128)S(1)} %copy.15.partner_ref, s32[8]{0:T(128)S(1)} %copy-done.6, bf16[128,128]{1,0:T(8,128)(2,1)S(1)} %copy-done.5, bf16[512,512]{1,0:T(8,128)(2,1)S(1)} %copy-done.2, bf16[8,4,2,16,128]{4,3,2,1,0:T(8,128)(2,1)S(1)} %bitcast.4), custom_call_target="tpu_custom_call" | custom-call | tf_op jit(solution)/shard_map/loop_spectra/pallas_call | solution.py:460
  28.9 4.4 %all-to-all-start.1 = ((bf16[32,24,128]{2,1,0:T(8,128)(2,1)}), bf16[32,24,128]{2,1,0:T(8,128)(2,1)S(1)}, u32[]{:S(2)}, u32[]{:S(2)}) async-start(bf16[32,24,128]{2,1,0:T(8,128)(2,1)} %bitcast.2), calls=%async_computation.1 | async-start | bytes 393216 | tf_op jit(solution)/shard_map/all_to_all | solution.py:470
  33.4 0.0 collective-permute-done.1.before_ref
  33.4 0.0 collective-permute-done.2.after_ref
  33.4 2.1 %near_lags.1 = (bf16[1,256,128]{2,1,0:T(8,128)(2,1)S(1)}, bf16[1,256,128]{2,1,0:T(8,128)(2,1)S(1)}, bf16[1,256,128]{2,1,0:T(8,128)(2,1)S(1)}, bf16[1,256,128]{2,1,0:T(8,128)(2,1)S(1)}) custom-call(bf16[32,2,16,128]{3,2,1,0:T(8,128)(2,1)} %get-tuple-element.18.white_ref, bf16[512,128]{1,0:T(8,128)(2,1)S(1)} %collective-permute-done.1.before_ref, ...), custom_call_target="tpu_custom_call" | custom-call | flops 10000000000 | bytes 20000000 | tf_op jit(solution)/shard_map/near_lags/pallas_call | solution.py:435
  35.4 0.3 collective-permute-start.3
  35.8 1.7 %collective-permute-start.4 = (bf16[1,256,128]{2,1,0:T(8,128)(2,1)S(1)}, bf16[1,256,128]{2,1,0:T(8,128)(2,1)S(1)}, u32[]{:S(2)}, u32[]{:S(2)}) collective-permute-start(bf16[1,256,128]{2,1,0:T(8,128)(2,1)S(1)} %get-tuple-element.24), channel_id=1, source_target_pairs={{0,2},{1,3},{2,0},{3,1},{4,6},{5,7},{6,4},{7,5},{8,10},{9,11},{10,... | collective-permute-start | bytes 196616 | tf_op jit(solution)/shard_map/ppermute | solution.py:450
  37.5 1.3 %collective-permute-start.5 = (bf16[1,256,128]{2,1,0:T(8,128)(2,1)S(1)}, bf16[1,256,128]{2,1,0:T(8,128)(2,1)S(1)}, u32[]{:S(2)}, u32[]{:S(2)}) collective-permute-start(bf16[1,256,128]{2,1,0:T(8,128)(2,1)S(1)} %get-tuple-element.25), channel_id=1, source_target_pairs={{0,3},{1,0},{2,1},{3,2},{4,7},{5,4},{6,5},{7,6},{8,11},{9,8},{10,9... | collective-permute-start | bytes 196616 | tf_op jit(solution)/shard_map/ppermute | solution.py:450
  38.8 1.0 %collective-permute-done.3.refs_1_ = bf16[1,256,128]{2,1,0:T(8,128)(2,1)S(1)} collective-permute-done((bf16[1,256,128]{2,1,0:T(8,128)(2,1)S(1)}, bf16[1,256,128]{2,1,0:T(8,128)(2,1)S(1)}, u32[]{:S(2)}, u32[]{:S(2)}) %collective-permute-start.3) | collective-permute-done | bytes 65568 | tf_op jit(solution)/shard_map/ppermute | solution.py:450
  39.8 1.2 %collective-permute-done.4.refs_2_ = bf16[1,256,128]{2,1,0:T(8,128)(2,1)S(1)} collective-permute-done((bf16[1,256,128]{2,1,0:T(8,128)(2,1)S(1)}, bf16[1,256,128]{2,1,0:T(8,128)(2,1)S(1)}, u32[]{:S(2)}, u32[]{:S(2)}) %collective-permute-start.4) | collective-permute-done | bytes 65568 | tf_op jit(solution)/shard_map/ppermute | solution.py:450
  41.0 0.2 collective-permute-done.5.refs_3_
  41.1 0.8 %near_turn.1 = f32[128,1,256]{2,1,0:T(1,128)} custom-call(bf16[1,256,128]{2,1,0:T(8,128)(2,1)S(1)} %get-tuple-element.22.refs_0_, bf16[1,256,128]{2,1,0:T(8,128)(2,1)S(1)} %collective-permute-done.3.refs_1_, bf16[1,256,128]{2,1,0:T(8,128)(2,1)S(1)} %collective-permute-done.4.refs_2_, bf16[1,256,128]{2,1,0:T(8,128)(2,1)S(1)} %collective-permute-done.5.refs_3_), custom_call_target="tpu_custom_call" | custom-call | tf_op jit(solution)/shard_map/near_turn/pallas_call | solution.py:480
  41.9 0.3 all-to-all-done.1.spec_ref
  42.2 1.5 %loop_lags.1 = f32[96,256]{1,0:T(8,128)} custom-call(bf16[32,24,128]{2,1,0:T(8,128)(2,1)S(1)} %all-to-all-done.1.spec_ref, bf16[512,1024]{1,0:T(8,128)(2,1)S(1)} %copy-done), custom_call_target="tpu_custom_call" | custom-call | tf_op jit(solution)/shard_map/loop_lags/pallas_call | solution.py:471
  (3 shorter events, 0.0 us)
Async XLA Ops:
  0.6 3.7 %copy-start.10 = (bf16[256,768]{1,0:T(8,128)(2,1)S(1)}, bf16[256,768]{1,0:T(8,128)(2,1)}, u32[]{:S(2)}) copy-start(bf16[256,768]{1,0:T(8,128)(2,1)} %constant.16.clone.tab_ref) | copy-start | bytes 1179652
  0.6 3.7 %copy-start.11 = (f32[256,128]{1,0:T(8,128)S(1)}, f32[256,128]{1,0:T(8,128)}, u32[]{:S(2)}) copy-start(f32[256,128]{1,0:T(8,128)} %constant.17.clone.twist_ref) | copy-start | bytes 393220
  0.7 3.7 %copy-start.8 = (f32[128,4096]{1,0:T(8,128)S(1)}, f32[128,4096]{1,0:T(8,128)}, u32[]{:S(2)}) copy-start(f32[128,4096]{1,0:T(8,128)} %rec_hbm.1) | copy-start | bytes 6291460
  0.7 3.7 %copy-start.9 = (f32[64]{0:T(128)S(1)}, f32[64]{0:T(128)}, u32[]{:S(2)}) copy-start(f32[64]{0:T(128)} %param.14) | copy-start | bytes 772
  1.8 4.6 %copy-start.1 = (bf16[512,512]{1,0:T(8,128)(2,1)S(1)}, bf16[512,512]{1,0:T(8,128)(2,1)}, u32[]{:S(2)}) copy-start(bf16[512,512]{1,0:T(8,128)(2,1)} %constant.19.clone.band_ref) | copy-start | bytes 1572868
  1.8 4.6 %copy-start.3 = (bf16[1024,128]{1,0:T(8,128)(2,1)S(1)}, bf16[1024,128]{1,0:T(8,128)(2,1)}, u32[]{:S(2)}) copy-start(bf16[1024,128]{1,0:T(8,128)(2,1)} %constant.18.clone.edge_ref) | copy-start | bytes 786436
  1.8 4.6 %copy-start.4 = (f32[512,128]{1,0:T(8,128)S(1)}, f32[512,128]{1,0:T(8,128)}, u32[]{:S(2)}) copy-start(f32[512,128]{1,0:T(8,128)} %constant.20.clone.share_ref) | copy-start | bytes 786436
  1.8 4.6 %collective-permute-start = (f32[64,128]{1,0:T(8,128)S(1)}, f32[64,128]{1,0:T(8,128)S(1)}, u32[]{:S(2)}, u32[]{:S(2)}) collective-permute-start(f32[64,128]{1,0:T(8,128)S(1)} %history.1), channel_id=1, source_target_pairs={{0,1},{1,2},{2,3},{4,5},{5,6},{6,7},{8,9},{9,10},{10,11},{12,13},{... | collective-permute-start | bytes 98312 | tf_op jit(solution)/shard_map/ppermute | solution.py:384
  4.3 16.4 %copy-start.12 = (s32[8,3]{0,1:T(4,128)S(1)}, s32[8,3]{0,1:T(4,128)}, u32[]{:S(2)}) copy-start(s32[8,3]{0,1:T(4,128)} %param.16) | copy-start | bytes 292
  4.3 16.5 %copy-start.7 = (s32[4]{0:T(128)S(1)}, s32[4]{0:T(128)}, u32[]{:S(2)}) copy-start(s32[4]{0:T(128)} %offs_ref) | copy-start | bytes 52
  6.3 20.6 %copy-start.2 = (bf16[512,512]{1,0:T(8,128)(2,1)S(1)}, bf16[512,512]{1,0:T(8,128)(2,1)}, u32[]{:S(2)}) copy-start(bf16[512,512]{1,0:T(8,128)(2,1)} %constant.23.clone.pack_ref) | copy-start | bytes 1572868
  6.3 20.6 %copy-start.5 = (bf16[128,128]{1,0:T(8,128)(2,1)S(1)}, bf16[128,128]{1,0:T(8,128)(2,1)}, u32[]{:S(2)}) copy-start(bf16[128,128]{1,0:T(8,128)(2,1)} %constant.22.clone.flip_ref) | copy-start | bytes 98308
  6.4 20.6 %copy-start.6 = (s32[8]{0:T(128)S(1)}, s32[8]{0:T(128)}, u32[]{:S(2)}) copy-start(s32[8]{0:T(128)} %count_ref.1) | copy-start | bytes 100
  6.4 27.0 %copy-start = (bf16[512,1024]{1,0:T(8,128)(2,1)S(1)}, bf16[512,1024]{1,0:T(8,128)(2,1)}, u32[]{:S(2)}) copy-start(bf16[512,1024]{1,0:T(8,128)(2,1)} %constant.21.clone.inv_ref) | copy-start | bytes 3145732
  7.9 19.0 %all-to-all-start = ((bf16[32,2,16,128]{3,2,1,0:T(8,128)(2,1)}), bf16[32,2,16,128]{3,2,1,0:T(8,128)(2,1)S(1)}, u32[]{:S(2)}, u32[]{:S(2)}) async-start(bf16[32,2,16,128]{3,2,1,0:T(8,128)(2,1)} %get-tuple-element.18.white_ref), calls=%async_computation | async-start | bytes 524288 | tf_op jit(solution)/shard_map/all_to_all | solution.py:418
  16.0 17.4 %collective-permute-start.1 = (bf16[512,128]{1,0:T(8,128)(2,1)S(1)}, bf16[512,128]{1,0:T(8,128)(2,1)S(1)}, u32[]{:S(2)}, u32[]{:S(2)}) collective-permute-start(bf16[512,128]{1,0:T(8,128)(2,1)S(1)} %get-tuple-element.19), channel_id=1, source_target_pairs={{0,4},{4,8},{8,12},{12,16},{16,20},{20,24},{24,28},{28,0},{1,5},{5... | collective-permute-start | bytes 393224 | tf_op jit(solution)/shard_map/ppermute | solution.py:422
  17.8 15.6 %collective-permute-start.2 = (bf16[512,128]{1,0:T(8,128)(2,1)S(1)}, bf16[512,128]{1,0:T(8,128)(2,1)S(1)}, u32[]{:S(2)}, u32[]{:S(2)}) collective-permute-start(bf16[512,128]{1,0:T(8,128)(2,1)S(1)} %get-tuple-element.20), channel_id=1, source_target_pairs={{4,0},{8,4},{12,8},{16,12},{20,16},{24,20},{28,24},{0,28},{5,1},{9... | collective-permute-start | bytes 393224 | tf_op jit(solution)/shard_map/ppermute | solution.py:423
  28.9 13.3 %all-to-all-start.1 = ((bf16[32,24,128]{2,1,0:T(8,128)(2,1)}), bf16[32,24,128]{2,1,0:T(8,128)(2,1)S(1)}, u32[]{:S(2)}, u32[]{:S(2)}) async-start(bf16[32,24,128]{2,1,0:T(8,128)(2,1)} %bitcast.2), calls=%async_computation.1 | async-start | bytes 393216 | tf_op jit(solution)/shard_map/all_to_all | solution.py:470
  35.4 4.3 %collective-permute-start.3 = (bf16[1,256,128]{2,1,0:T(8,128)(2,1)S(1)}, bf16[1,256,128]{2,1,0:T(8,128)(2,1)S(1)}, u32[]{:S(2)}, u32[]{:S(2)}) collective-permute-start(bf16[1,256,128]{2,1,0:T(8,128)(2,1)S(1)} %get-tuple-element.23), channel_id=1, source_target_pairs={{0,1},{1,2},{2,3},{3,0},{4,5},{5,6},{6,7},{7,4},{8,9},{9,10},{10,1... | collective-permute-start | bytes 196616 | tf_op jit(solution)/shard_map/ppermute | solution.py:450
  35.8 5.2 %collective-permute-start.4 = (bf16[1,256,128]{2,1,0:T(8,128)(2,1)S(1)}, bf16[1,256,128]{2,1,0:T(8,128)(2,1)S(1)}, u32[]{:S(2)}, u32[]{:S(2)}) collective-permute-start(bf16[1,256,128]{2,1,0:T(8,128)(2,1)S(1)} %get-tuple-element.24), channel_id=1, source_target_pairs={{0,2},{1,3},{2,0},{3,1},{4,6},{5,7},{6,4},{7,5},{8,10},{9,11},{10,... | collective-permute-start | bytes 196616 | tf_op jit(solution)/shard_map/ppermute | solution.py:450
  37.5 3.7 %collective-permute-start.5 = (bf16[1,256,128]{2,1,0:T(8,128)(2,1)S(1)}, bf16[1,256,128]{2,1,0:T(8,128)(2,1)S(1)}, u32[]{:S(2)}, u32[]{:S(2)}) collective-permute-start(bf16[1,256,128]{2,1,0:T(8,128)(2,1)S(1)} %get-tuple-element.25), channel_id=1, source_target_pairs={{0,3},{1,0},{2,1},{3,2},{4,7},{5,4},{6,5},{7,6},{8,11},{9,8},{10,9... | collective-permute-start | bytes 196616 | tf_op jit(solution)/shard_map/ppermute | solution.py:450

commit v10 on v9

--- a/solution.py
+++ b/solution.py
@@ -296,27 +296,16 @@
 
 def loop_lag_kernel(slots, spec_ref, inv_ref, loop_ref):
     sources = spec_ref.shape[0]
-    rows = inv_ref.shape[1] // sources
+    step = spec_ref.shape[1] // slots
     share = loop_ref.shape[0] // slots
-    owners = LANES // share
-    step = rows // owners
     loop = spec_ref[...].astype(F32)
-    lane = lax.broadcasted_iota(jnp.int32, (sources, step, LANES), 2)
-    columns = []
+    rows = []
     for k in range(slots):
-        tile = loop[:, k * step : (k + 1) * step]
-        groups = [
-            jnp.where((lane >= g * share) & (lane < (g + 1) * share), tile, 0.0)
-            for g in range(owners)
-        ]
-        columns.append(jnp.concatenate(groups, axis=1).astype(BF16).reshape(sources * rows, LANES))
-    both = mm(inv_ref[...], jnp.concatenate(columns, axis=1))
-    lags = both[:LAGS] + both[LAGS:]
-    for k in range(slots):
-        turned = lags[:, k * LANES : (k + 1) * LANES].T
-        loop_ref[k * share : (k + 1) * share] = sum(
-            turned[g * share : (g + 1) * share] for g in range(owners)
-        )
+        turned = loop[:, k * step : (k + 1) * step].reshape(sources * step, LANES).T
+        groups = [turned[g * share : (g + 1) * share] for g in range(LANES // share)]
+        rows.append(jnp.concatenate(groups, axis=1))
+    both = mm(jnp.concatenate(rows, axis=0).astype(BF16), inv_ref[...])
+    loop_ref[...] = both[:, :LAGS] + both[:, LAGS:]
 
 
 def vmem(count):
@@ -440,14 +429,11 @@
         scratch_shapes=[pltpu.VMEM((noff, LAGS, LANES), F32)],
         compiler_params=PARAMS,
         cost_estimate=pl.CostEstimate(
-            flops=10_000_000_000, bytes_accessed=20_000_000, transcendentals=0
+            flops=3_000_000_000, bytes_accessed=4_000_000, transcendentals=0
         ),
         name="near_lags",
     )(white, before, after, moves, inverse)
-    lags = list(lags)
-    for r in range(1, seg_count):
-        route = [(i, (i + r) % seg_count) for i in range(seg_count)]
-        lags[r] = lax.ppermute(lags[r], "seg", route)
+    moved, *lags = lax.optimization_barrier((moved, *lags))
 
     if bins % GROUP or 2 * bins % (8 * seg_count):
         order = np.repeat(bin_order().reshape(devices, 1, bins), 2, axis=1).reshape(-1)
@@ -466,8 +452,12 @@
             compiler_params=PARAMS,
             name="loop_spectra",
         )(loop_partner, loop_count, flip, pack_matrix(seg_count), moved)
+        crossed, *lags = lax.optimization_barrier((crossed, *lags))
         crossed = crossed.reshape(devices, out_rows, LANES)
         summed = lax.all_to_all(crossed, ("chan", "seg"), 0, 0, tiled=True)
+        columns = np.arange(2 * BINS).reshape(devices, seg_count, -1).swapaxes(0, 1).reshape(-1)
+        loop_inverse = inverse_table(seg_count, order[columns], part[columns]).T
+        loop_inverse = np.concatenate(split_np(loop_inverse), axis=1)
         loop = pl.pallas_call(
             functools.partial(loop_lag_kernel, slots),
             out_shape=jax.ShapeDtypeStruct((slots * share, LAGS), F32),
@@ -475,8 +465,11 @@
             out_specs=pl.BlockSpec(memory_space=pltpu.VMEM),
             compiler_params=PARAMS,
             name="loop_lags",
-        )(summed, inverse)
+        )(summed, loop_inverse)
         loop = loop.reshape(1, slots, share, LAGS)
+    for r in range(1, seg_count):
+        route = [(i, (i + r) % seg_count) for i in range(seg_count)]
+        lags[r] = lax.ppermute(lags[r], "seg", route)
     near = pl.pallas_call(
         turn_kernel,
         out_shape=jax.ShapeDtypeStruct((chans, near_each, LAGS), F32),

time: 44.5 us -> 46.3 us (1.040)
  waiting for transfers between devices: 8.2 us -> 12.1 us
  starting transfers between devices: 23 us -> 21.7 us
    ppermute x1, waiting for transfers between devices: 0.01 us -> 7.32 us  [body(): before = lax.ppermute(up, 'chan', ring)]
    all_to_all x1, waiting for transfers between devices: 5.49 us -> 0.01 us  [body(): moved = lax.all_to_all(spread, ('chan', 'seg'), 0, 0, tiled=True)]
    all_to_all x1, starting transfers between devices: 4.42 us -> 3.07 us  [body(): summed = lax.all_to_all(crossed, ('chan', 'seg'), 0, 0, tiled=True)]
    all_to_all x1, waiting for transfers between devices: 0.33 us -> 1.59 us  [body(): summed = lax.all_to_all(crossed, ('chan', 'seg'), 0, 0, tiled=True)]
    ppermute x3, waiting for transfers between devices: 2.37 us -> 3.23 us  [body(): lags[r] = lax.ppermute(lags[r], 'seg', route)]
    pallas_call x1, Pallas kernels: 1.49 us -> 1.01 us  [body(): pl.pallas_call(functools.partial(loop_lag_kernel, slots), out_shape=jax.S...]
  transfers between devices with their start and end apart: 8 -> 8, of which waited for: 5 -> 5; matrix products, arithmetic and copies ran while one was open for 0% -> 0% of each run, Pallas kernels for 17% -> 12%
where the time goes in v10:
time: 46.3 us; the launch traced here: 45.9 us
  starting transfers between devices  21.7 us (47%)
  waiting for transfers between devices  12.1 us (26%)
  Pallas kernels  11 us (24%)
  between operations  0.9 us (2%)
    all_to_all x1, starting transfers between devices, body(): moved = lax.all_to_all(spread, ('chan', 'seg'), 0, 0, tiled=True)  8.07 us
    ppermute x1, waiting for transfers between devices, body(): before = lax.ppermute(up, 'chan', ring)  7.32 us
    ppermute x3, starting transfers between devices, body(): lags[r] = lax.ppermute(lags[r], 'seg', route)  3.3 us
    ppermute x3, waiting for transfers between devices, body(): lags[r] = lax.ppermute(lags[r], 'seg', route)  3.23 us
    all_to_all x1, starting transfers between devices, body(): summed = lax.all_to_all(crossed, ('chan', 'seg'), 0, 0, tiled=True)  3.07 us
    ppermute x1, starting transfers between devices, body(): after = lax.ppermute(down, 'chan', [(j, i) for i, j in ring])  2.95 us
    ppermute x1, starting transfers between devices, body(): rim = lax.ppermute(rim, 'seg', route)  2.49 us
    pallas_call x1, Pallas kernels, body(): pl.pallas_call(near_kernel, out_shape=[jax.ShapeDtypeStruct((near_each, L...  2.08 us
  transfers between devices with their start and end apart: 8, of which 5 were waited for; matrix products, arithmetic and copies ran while one was open for 0% of the time, Pallas kernels for 12%

profile of v10, /device:TPU:0, one launch (start us, length us, event | category | flops | bytes accessed | tf_op | source)
XLA Modules:
  0.0 45.9 jit_solution(15079094717455852120)
XLA Ops:
  0.6 0.0 copy-start.11
  0.6 0.0 copy-start.12
  0.7 0.0 copy-start.8
  0.7 0.0 copy-start.9
  0.7 1.1 %history.1 = f32[64,128]{1,0:T(8,128)S(1)} custom-call(f32[128,4096]{1,0:T(8,128)} %rec_hbm.1), custom_call_target="tpu_custom_call" | custom-call | flops 10000000000 | bytes 20000000 | tf_op jit(solution)/shard_map/history/pallas_call | solution.py:361
  1.8 0.0 copy-start.1
  1.8 0.0 copy-start.3
  1.8 0.0 copy-start.4
  1.8 2.5 %collective-permute-start = (f32[64,128]{1,0:T(8,128)S(1)}, f32[64,128]{1,0:T(8,128)S(1)}, u32[]{:S(2)}, u32[]{:S(2)}) collective-permute-start(f32[64,128]{1,0:T(8,128)S(1)} %history.1), channel_id=1, source_target_pairs={{0,1},{1,2},{2,3},{4,5},{5,6},{6,7},{8,9},{9,10},{10,11},{12,13},{... | collective-permute-start | bytes 98312 | tf_op jit(solution)/shard_map/ppermute | solution.py:373
  4.3 0.0 copy-done.11
  4.3 0.0 copy-done.12
  4.3 0.0 copy-done.8
  4.3 0.0 copy-done.9
  4.3 0.0 copy-start.13
  4.3 0.0 copy-start.7
  4.4 2.0 %filter_and_transform.1 = (f32[1024,128]{1,0:T(8,128)S(1)}, f32[128,128]{1,0:T(8,128)S(1)}, f32[16,128]{1,0:T(8,128)S(1)}) custom-call(f32[1,64]{1,0:T(1,128)S(1)} %bitcast.5, f32[128,4096]{1,0:T(8,128)S(1)} %copy-done.8, bf16[256,768]{1,0:T(8,128)(2,1)S(1)} %copy-done.11, f32[256,128]{1,0:T(8,128)S(1)} %copy-done.12), custom_call_target="tpu_custom_call" | custom-call | flops 1000000000 | bytes 5000000 | tf_op jit(solution)/shard_map/filter_and_transform/pallas_call | solution.py:375
  6.3 0.0 copy-start.10
  6.4 0.0 collective-permute-done.rim_ref
  6.4 1.5 %whiten.1 = (bf16[32,2,16,128]{3,2,1,0:T(8,128)(2,1)}, bf16[512,128]{1,0:T(8,128)(2,1)S(1)}, bf16[512,128]{1,0:T(8,128)(2,1)S(1)}) custom-call(f32[1024,128]{1,0:T(8,128)S(1)} %get-tuple-element.24.spec_ref, f32[64,128]{1,0:T(8,128)S(1)} %collective-permute-done.rim_ref, f32[128,128]{1,0:T(8,128)S(1)} %get-tuple-element.25.mean_ref, ...), custom_call_target="tpu_custom_call" | custom-call | tf_op jit(solution)/shard_map/whiten/pallas_call | solution.py:393
  7.9 8.1 %all-to-all-start = ((bf16[32,2,16,128]{3,2,1,0:T(8,128)(2,1)}), bf16[32,2,16,128]{3,2,1,0:T(8,128)(2,1)S(1)}, u32[]{:S(2)}, u32[]{:S(2)}) async-start(bf16[32,2,16,128]{3,2,1,0:T(8,128)(2,1)} %get-tuple-element.28.white_ref), calls=%async_computation | async-start | bytes 524288 | tf_op jit(solution)/shard_map/all_to_all | solution.py:407
  16.0 1.8 %collective-permute-start.1 = (bf16[512,128]{1,0:T(8,128)(2,1)S(1)}, bf16[512,128]{1,0:T(8,128)(2,1)S(1)}, u32[]{:S(2)}, u32[]{:S(2)}) collective-permute-start(bf16[512,128]{1,0:T(8,128)(2,1)S(1)} %get-tuple-element.29), channel_id=1, source_target_pairs={{0,4},{4,8},{8,12},{12,16},{16,20},{20,24},{24,28},{28,0},{1,5},{5... | collective-permute-start | bytes 393224 | tf_op jit(solution)/shard_map/ppermute | solution.py:411
  17.8 3.0 %collective-permute-start.2 = (bf16[512,128]{1,0:T(8,128)(2,1)S(1)}, bf16[512,128]{1,0:T(8,128)(2,1)S(1)}, u32[]{:S(2)}, u32[]{:S(2)}) collective-permute-start(bf16[512,128]{1,0:T(8,128)(2,1)S(1)} %get-tuple-element.30), channel_id=1, source_target_pairs={{4,0},{8,4},{12,8},{16,12},{20,16},{24,20},{28,24},{0,28},{5,1},{9... | collective-permute-start | bytes 393224 | tf_op jit(solution)/shard_map/ppermute | solution.py:412
  20.7 0.0 copy-done.13
  20.8 0.1 copy.16.partner_ref
  20.8 0.0 copy-done.7
  20.8 0.6 %offset_moves.1.moves_ref = bf16[256,512]{1,0:T(8,128)(2,1)S(1)} custom-call(s32[4]{0:T(128)S(1)} %copy-done.7), custom_call_target="tpu_custom_call" | custom-call | tf_op jit(solution)/shard_map/offset_moves/pallas_call | solution.py:413
  21.4 0.0 copy-start.2
  21.5 0.0 copy-start.5
  21.5 0.0 copy-start.6
  21.5 7.3 %collective-permute-done.1.before_ref = bf16[512,128]{1,0:T(8,128)(2,1)S(1)} collective-permute-done((bf16[512,128]{1,0:T(8,128)(2,1)S(1)}, bf16[512,128]{1,0:T(8,128)(2,1)S(1)}, u32[]{:S(2)}, u32[]{:S(2)}) %collective-permute-start.1) | collective-permute-done | bytes 131104 | tf_op jit(solution)/shard_map/ppermute | solution.py:411
  28.8 0.0 collective-permute-done.2.after_ref
  28.8 2.1 %near_lags.1 = (bf16[1,256,128]{2,1,0:T(8,128)(2,1)S(1)}, bf16[1,256,128]{2,1,0:T(8,128)(2,1)S(1)}, bf16[1,256,128]{2,1,0:T(8,128)(2,1)S(1)}, bf16[1,256,128]{2,1,0:T(8,128)(2,1)S(1)}) custom-call(bf16[32,2,16,128]{3,2,1,0:T(8,128)(2,1)} %get-tuple-element.28.white_ref, bf16[512,128]{1,0:T(8,128)(2,1)S(1)} %collective-permute-done.1.before_ref, ...), custom_call_target="tpu_custom_call" | custom-call | flops 3000000000 | bytes 4000000 | tf_op jit(solution)/shard_map/near_lags/pallas_call | solution.py:424
  30.9 0.0 copy-start
  30.9 0.0 all-to-all-done
  30.9 0.0 copy-done.2
  30.9 0.0 copy-done.5
  30.9 0.0 copy-done.6
  30.9 2.0 %loop_spectra.1 = bf16[8,4,24,128]{3,2,1,0:T(8,128)(2,1)} custom-call(s32[8,3]{1,0:T(8,128)S(1)} %copy.16.partner_ref, s32[8]{0:T(128)S(1)} %copy-done.6, bf16[128,128]{1,0:T(8,128)(2,1)S(1)} %copy-done.5, bf16[512,512]{1,0:T(8,128)(2,1)S(1)} %copy-done.2, bf16[8,4,2,16,128]{4,3,2,1,0:T(8,128)(2,1)S(1)} %bitcast.4), custom_call_target="tpu_custom_call" | custom-call | tf_op jit(solution)/shard_map/loop_spectra/pallas_call | solution.py:446
  32.9 3.1 %all-to-all-start.1 = ((bf16[32,24,128]{2,1,0:T(8,128)(2,1)}), bf16[32,24,128]{2,1,0:T(8,128)(2,1)S(1)}, u32[]{:S(2)}, u32[]{:S(2)}) async-start(bf16[32,24,128]{2,1,0:T(8,128)(2,1)} %bitcast.2), calls=%async_computation.1 | async-start | bytes 393216 | tf_op jit(solution)/shard_map/all_to_all | solution.py:457
  36.0 0.3 collective-permute-start.3
  36.3 1.7 %collective-permute-start.4 = (bf16[1,256,128]{2,1,0:T(8,128)(2,1)S(1)}, bf16[1,256,128]{2,1,0:T(8,128)(2,1)S(1)}, u32[]{:S(2)}, u32[]{:S(2)}) collective-permute-start(bf16[1,256,128]{2,1,0:T(8,128)(2,1)S(1)} %get-tuple-element.43), channel_id=1, source_target_pairs={{0,2},{1,3},{2,0},{3,1},{4,6},{5,7},{6,4},{7,5},{8,10},{9,11},{10,... | collective-permute-start | bytes 196616 | tf_op jit(solution)/shard_map/ppermute | solution.py:472
  38.0 1.3 %collective-permute-start.5 = (bf16[1,256,128]{2,1,0:T(8,128)(2,1)S(1)}, bf16[1,256,128]{2,1,0:T(8,128)(2,1)S(1)}, u32[]{:S(2)}, u32[]{:S(2)}) collective-permute-start(bf16[1,256,128]{2,1,0:T(8,128)(2,1)S(1)} %get-tuple-element.44), channel_id=1, source_target_pairs={{0,3},{1,0},{2,1},{3,2},{4,7},{5,4},{6,5},{7,6},{8,11},{9,8},{10,9... | collective-permute-start | bytes 196616 | tf_op jit(solution)/shard_map/ppermute | solution.py:472
  39.3 1.4 %collective-permute-done.3.refs_1_ = bf16[1,256,128]{2,1,0:T(8,128)(2,1)S(1)} collective-permute-done((bf16[1,256,128]{2,1,0:T(8,128)(2,1)S(1)}, bf16[1,256,128]{2,1,0:T(8,128)(2,1)S(1)}, u32[]{:S(2)}, u32[]{:S(2)}) %collective-permute-start.3) | collective-permute-done | bytes 65568 | tf_op jit(solution)/shard_map/ppermute | solution.py:472
  40.7 1.7 %collective-permute-done.4.refs_2_ = bf16[1,256,128]{2,1,0:T(8,128)(2,1)S(1)} collective-permute-done((bf16[1,256,128]{2,1,0:T(8,128)(2,1)S(1)}, bf16[1,256,128]{2,1,0:T(8,128)(2,1)S(1)}, u32[]{:S(2)}, u32[]{:S(2)}) %collective-permute-start.4) | collective-permute-done | bytes 65568 | tf_op jit(solution)/shard_map/ppermute | solution.py:472
  42.4 0.1 collective-permute-done.5.refs_3_
  42.5 0.8 %near_turn.1 = f32[128,1,256]{2,1,0:T(1,128)} custom-call(bf16[1,256,128]{2,1,0:T(8,128)(2,1)S(1)} %get-tuple-element.41.refs_0_, bf16[1,256,128]{2,1,0:T(8,128)(2,1)S(1)} %collective-permute-done.3.refs_1_, bf16[1,256,128]{2,1,0:T(8,128)(2,1)S(1)} %collective-permute-done.4.refs_2_, bf16[1,256,128]{2,1,0:T(8,128)(2,1)S(1)} %collective-permute-done.5.refs_3_), custom_call_target="tpu_custom_call" | custom-call | tf_op jit(solution)/shard_map/near_turn/pallas_call | solution.py:473
  43.3 1.6 %all-to-all-done.1.spec_ref = bf16[32,24,128]{2,1,0:T(8,128)(2,1)S(1)} async-done(((bf16[32,24,128]{2,1,0:T(8,128)(2,1)}), bf16[32,24,128]{2,1,0:T(8,128)(2,1)S(1)}, u32[]{:S(2)}, u32[]{:S(2)}) %all-to-all-start.1) | async-done | bytes 196640 | tf_op jit(solution)/shard_map/all_to_all | solution.py:457
  44.9 1.0 %loop_lags.1 = f32[96,256]{1,0:T(8,128)} custom-call(bf16[32,24,128]{2,1,0:T(8,128)(2,1)S(1)} %all-to-all-done.1.spec_ref, bf16[1024,512]{1,0:T(8,128)(2,1)S(1)} %copy-done), custom_call_target="tpu_custom_call" | custom-call | tf_op jit(solution)/shard_map/loop_lags/pallas_call | solution.py:461
  (5 shorter events, 0.0 us)
Async XLA Ops:
  0.6 3.7 %copy-start.11 = (bf16[256,768]{1,0:T(8,128)(2,1)S(1)}, bf16[256,768]{1,0:T(8,128)(2,1)}, u32[]{:S(2)}) copy-start(bf16[256,768]{1,0:T(8,128)(2,1)} %constant.18.clone.tab_ref) | copy-start | bytes 1179652
  0.6 3.7 %copy-start.12 = (f32[256,128]{1,0:T(8,128)S(1)}, f32[256,128]{1,0:T(8,128)}, u32[]{:S(2)}) copy-start(f32[256,128]{1,0:T(8,128)} %constant.19.clone.twist_ref) | copy-start | bytes 393220
  0.7 3.7 %copy-start.8 = (f32[128,4096]{1,0:T(8,128)S(1)}, f32[128,4096]{1,0:T(8,128)}, u32[]{:S(2)}) copy-start(f32[128,4096]{1,0:T(8,128)} %rec_hbm.1) | copy-start | bytes 6291460
  0.7 3.7 %copy-start.9 = (f32[64]{0:T(128)S(1)}, f32[64]{0:T(128)}, u32[]{:S(2)}) copy-start(f32[64]{0:T(128)} %param.15) | copy-start | bytes 772
  1.8 4.6 %copy-start.1 = (bf16[512,512]{1,0:T(8,128)(2,1)S(1)}, bf16[512,512]{1,0:T(8,128)(2,1)}, u32[]{:S(2)}) copy-start(bf16[512,512]{1,0:T(8,128)(2,1)} %constant.21.clone.band_ref) | copy-start | bytes 1572868
  1.8 4.6 %copy-start.3 = (bf16[1024,128]{1,0:T(8,128)(2,1)S(1)}, bf16[1024,128]{1,0:T(8,128)(2,1)}, u32[]{:S(2)}) copy-start(bf16[1024,128]{1,0:T(8,128)(2,1)} %constant.20.clone.edge_ref) | copy-start | bytes 786436
  1.8 4.6 %copy-start.4 = (f32[512,128]{1,0:T(8,128)S(1)}, f32[512,128]{1,0:T(8,128)}, u32[]{:S(2)}) copy-start(f32[512,128]{1,0:T(8,128)} %constant.22.clone.share_ref) | copy-start | bytes 786436
  1.8 4.6 %collective-permute-start = (f32[64,128]{1,0:T(8,128)S(1)}, f32[64,128]{1,0:T(8,128)S(1)}, u32[]{:S(2)}, u32[]{:S(2)}) collective-permute-start(f32[64,128]{1,0:T(8,128)S(1)} %history.1), channel_id=1, source_target_pairs={{0,1},{1,2},{2,3},{4,5},{5,6},{6,7},{8,9},{9,10},{10,11},{12,13},{... | collective-permute-start | bytes 98312 | tf_op jit(solution)/shard_map/ppermute | solution.py:373
  4.3 16.4 %copy-start.13 = (s32[8,3]{0,1:T(4,128)S(1)}, s32[8,3]{0,1:T(4,128)}, u32[]{:S(2)}) copy-start(s32[8,3]{0,1:T(4,128)} %param.17) | copy-start | bytes 292
  4.3 16.5 %copy-start.7 = (s32[4]{0:T(128)S(1)}, s32[4]{0:T(128)}, u32[]{:S(2)}) copy-start(s32[4]{0:T(128)} %offs_ref) | copy-start | bytes 52
  6.3 22.5 %copy-start.10 = (bf16[512,1024]{1,0:T(8,128)(2,1)S(1)}, bf16[512,1024]{1,0:T(8,128)(2,1)}, u32[]{:S(2)}) copy-start(bf16[512,1024]{1,0:T(8,128)(2,1)} %constant.23.clone.inv_ref) | copy-start | bytes 3145732
  7.9 23.0 %all-to-all-start = ((bf16[32,2,16,128]{3,2,1,0:T(8,128)(2,1)}), bf16[32,2,16,128]{3,2,1,0:T(8,128)(2,1)S(1)}, u32[]{:S(2)}, u32[]{:S(2)}) async-start(bf16[32,2,16,128]{3,2,1,0:T(8,128)(2,1)} %get-tuple-element.28.white_ref), calls=%async_computation | async-start | bytes 524288 | tf_op jit(solution)/shard_map/all_to_all | solution.py:407
  16.0 12.8 %collective-permute-start.1 = (bf16[512,128]{1,0:T(8,128)(2,1)S(1)}, bf16[512,128]{1,0:T(8,128)(2,1)S(1)}, u32[]{:S(2)}, u32[]{:S(2)}) collective-permute-start(bf16[512,128]{1,0:T(8,128)(2,1)S(1)} %get-tuple-element.29), channel_id=1, source_target_pairs={{0,4},{4,8},{8,12},{12,16},{16,20},{20,24},{24,28},{28,0},{1,5},{5... | collective-permute-start | bytes 393224 | tf_op jit(solution)/shard_map/ppermute | solution.py:411
  17.8 11.0 %collective-permute-start.2 = (bf16[512,128]{1,0:T(8,128)(2,1)S(1)}, bf16[512,128]{1,0:T(8,128)(2,1)S(1)}, u32[]{:S(2)}, u32[]{:S(2)}) collective-permute-start(bf16[512,128]{1,0:T(8,128)(2,1)S(1)} %get-tuple-element.30), channel_id=1, source_target_pairs={{4,0},{8,4},{12,8},{16,12},{20,16},{24,20},{28,24},{0,28},{5,1},{9... | collective-permute-start | bytes 393224 | tf_op jit(solution)/shard_map/ppermute | solution.py:412
  21.4 9.5 %copy-start.2 = (bf16[512,512]{1,0:T(8,128)(2,1)S(1)}, bf16[512,512]{1,0:T(8,128)(2,1)}, u32[]{:S(2)}) copy-start(bf16[512,512]{1,0:T(8,128)(2,1)} %constant.25.clone.pack_ref) | copy-start | bytes 1572868
  21.5 9.5 %copy-start.5 = (bf16[128,128]{1,0:T(8,128)(2,1)S(1)}, bf16[128,128]{1,0:T(8,128)(2,1)}, u32[]{:S(2)}) copy-start(bf16[128,128]{1,0:T(8,128)(2,1)} %constant.24.clone.flip_ref) | copy-start | bytes 98308
  21.5 9.5 %copy-start.6 = (s32[8]{0:T(128)S(1)}, s32[8]{0:T(128)}, u32[]{:S(2)}) copy-start(s32[8]{0:T(128)} %count_ref.1) | copy-start | bytes 100
  30.9 14.0 %copy-start = (bf16[1024,512]{1,0:T(8,128)(2,1)S(1)}, bf16[1024,512]{1,0:T(8,128)(2,1)}, u32[]{:S(2)}) copy-start(bf16[1024,512]{1,0:T(8,128)(2,1)} %constant.26.clone.inv_ref) | copy-start | bytes 3145732
  32.9 12.0 %all-to-all-start.1 = ((bf16[32,24,128]{2,1,0:T(8,128)(2,1)}), bf16[32,24,128]{2,1,0:T(8,128)(2,1)S(1)}, u32[]{:S(2)}, u32[]{:S(2)}) async-start(bf16[32,24,128]{2,1,0:T(8,128)(2,1)} %bitcast.2), calls=%async_computation.1 | async-start | bytes 393216 | tf_op jit(solution)/shard_map/all_to_all | solution.py:457
  36.0 4.7 %collective-permute-start.3 = (bf16[1,256,128]{2,1,0:T(8,128)(2,1)S(1)}, bf16[1,256,128]{2,1,0:T(8,128)(2,1)S(1)}, u32[]{:S(2)}, u32[]{:S(2)}) collective-permute-start(bf16[1,256,128]{2,1,0:T(8,128)(2,1)S(1)} %get-tuple-element.42), channel_id=1, source_target_pairs={{0,1},{1,2},{2,3},{3,0},{4,5},{5,6},{6,7},{7,4},{8,9},{9,10},{10,1... | collective-permute-start | bytes 196616 | tf_op jit(solution)/shard_map/ppermute | solution.py:472
  36.3 6.1 %collective-permute-start.4 = (bf16[1,256,128]{2,1,0:T(8,128)(2,1)S(1)}, bf16[1,256,128]{2,1,0:T(8,128)(2,1)S(1)}, u32[]{:S(2)}, u32[]{:S(2)}) collective-permute-start(bf16[1,256,128]{2,1,0:T(8,128)(2,1)S(1)} %get-tuple-element.43), channel_id=1, source_target_pairs={{0,2},{1,3},{2,0},{3,1},{4,6},{5,7},{6,4},{7,5},{8,10},{9,11},{10,... | collective-permute-start | bytes 196616 | tf_op jit(solution)/shard_map/ppermute | solution.py:472
  38.0 4.6 %collective-permute-start.5 = (bf16[1,256,128]{2,1,0:T(8,128)(2,1)S(1)}, bf16[1,256,128]{2,1,0:T(8,128)(2,1)S(1)}, u32[]{:S(2)}, u32[]{:S(2)}) collective-permute-start(bf16[1,256,128]{2,1,0:T(8,128)(2,1)S(1)} %get-tuple-element.44), channel_id=1, source_target_pairs={{0,3},{1,0},{2,1},{3,2},{4,7},{5,4},{6,5},{7,6},{8,11},{9,8},{10,9... | collective-permute-start | bytes 196616 | tf_op jit(solution)/shard_map/ppermute | solution.py:472

commit v11 on v10

--- a/solution.py
+++ b/solution.py
@@ -228,6 +228,10 @@
     return matrix.reshape(owners * LANES, owners * LANES).astype(jnp.bfloat16)
 
 
+def partner_of(place, r, owners):
+    return place ^ r if owners & (owners - 1) == 0 else (place + r) % owners
+
+
 def near_kernel(white_ref, before_ref, after_ref, moves_ref, inv_ref, *refs):
     out_refs, lags_ref = refs[:-1], refs[-1]
     rows = white_ref.shape[0] * 2 * GROUP
@@ -255,7 +259,7 @@
     each = noff // owners
     place = lax.axis_index("seg")
     for r in range(owners):
-        first = lax.rem(place + r, owners) * each
+        first = partner_of(place, r, owners) * each
         out_refs[r][...] = lags_ref[pl.ds(first, each)].astype(BF16)
 
 
@@ -392,7 +396,7 @@
     half = jax.ShapeDtypeStruct((BINS, LANES), BF16)
     white, up, down = pl.pallas_call(
         whiten_kernel,
-        out_shape=[jax.ShapeDtypeStruct((GROUPS, 2, GROUP, LANES), BF16), half, half],
+        out_shape=[pltpu.VMEM((GROUPS, 2, GROUP, LANES), BF16), half, half],
         in_specs=vmem(7),
         out_specs=vmem(3),
         compiler_params=PARAMS,
@@ -429,7 +433,7 @@
         scratch_shapes=[pltpu.VMEM((noff, LAGS, LANES), F32)],
         compiler_params=PARAMS,
         cost_estimate=pl.CostEstimate(
-            flops=3_000_000_000, bytes_accessed=4_000_000, transcendentals=0
+            flops=20_000_000_000, bytes_accessed=20_000_000, transcendentals=0
         ),
         name="near_lags",
     )(white, before, after, moves, inverse)
@@ -445,7 +449,7 @@
         out_rows = slots * (2 * bins // seg_count)
         crossed = pl.pallas_call(
             loop_kernel,
-            out_shape=jax.ShapeDtypeStruct((chan_count, seg_count, out_rows, LANES), BF16),
+            out_shape=pltpu.VMEM((chan_count, seg_count, out_rows, LANES), BF16),
             in_specs=smem(2) + vmem(3),
             out_specs=pl.BlockSpec(memory_space=pltpu.VMEM),
             scratch_shapes=[pltpu.VMEM((chan_count, seg_count * 2 * bins, LANES), F32)],
@@ -467,8 +471,8 @@
             name="loop_lags",
         )(summed, loop_inverse)
         loop = loop.reshape(1, slots, share, LAGS)
-    for r in range(1, seg_count):
-        route = [(i, (i + r) % seg_count) for i in range(seg_count)]
+    for r in range(seg_count - 1, 0, -1):
+        route = [(i, partner_of(i, r, seg_count)) for i in range(seg_count)]
         lags[r] = lax.ppermute(lags[r], "seg", route)
     near = pl.pallas_call(
         turn_kernel,

time: 46.3 us -> 44.2 us (0.955)
  starting transfers between devices: 21.7 us -> 17.1 us
  waiting for transfers between devices: 12.1 us -> 14.6 us
    all_to_all x1, waiting for transfers between devices: 0.01 us -> 8.24 us  [body(): moved = lax.all_to_all(spread, ('chan', 'seg'), 0, 0, tiled=True)]
    ppermute x1, waiting for transfers between devices: 7.32 us -> 0.01 us  [body(): before = lax.ppermute(up, 'chan', ring)]
    all_to_all x1, starting transfers between devices: 8.07 us -> 4.71 us  [body(): moved = lax.all_to_all(spread, ('chan', 'seg'), 0, 0, tiled=True)]
    ppermute x3, waiting for transfers between devices: 3.23 us -> 5.16 us  [body(): lags[r] = lax.ppermute(lags[r], 'seg', route)]
    ppermute x3, starting transfers between devices: 3.3 us -> 1.96 us  [body(): lags[r] = lax.ppermute(lags[r], 'seg', route)]
    all_to_all x1, waiting for transfers between devices: 1.59 us -> 1 us  [body(): summed = lax.all_to_all(crossed, ('chan', 'seg'), 0, 0, tiled=True)]
    ppermute x1, starting transfers between devices: 1.82 us -> 2.35 us  [body(): before = lax.ppermute(up, 'chan', ring)]
    all_to_all x1, starting transfers between devices: 3.07 us -> 2.58 us  [body(): summed = lax.all_to_all(crossed, ('chan', 'seg'), 0, 0, tiled=True)]
where the time goes in v11:
time: 44.2 us; the launch traced here: 43.8 us
  starting transfers between devices  17.1 us (39%)
  waiting for transfers between devices  14.6 us (33%)
  Pallas kernels  11 us (25%)
  between operations  0.88 us (2%)
    all_to_all x1, waiting for transfers between devices, body(): moved = lax.all_to_all(spread, ('chan', 'seg'), 0, 0, tiled=True)  8.24 us
    ppermute x3, waiting for transfers between devices, body(): lags[r] = lax.ppermute(lags[r], 'seg', route)  5.16 us
    all_to_all x1, starting transfers between devices, body(): moved = lax.all_to_all(spread, ('chan', 'seg'), 0, 0, tiled=True)  4.71 us
    ppermute x1, starting transfers between devices, body(): after = lax.ppermute(down, 'chan', [(j, i) for i, j in ring])  3.03 us
    all_to_all x1, starting transfers between devices, body(): summed = lax.all_to_all(crossed, ('chan', 'seg'), 0, 0, tiled=True)  2.58 us
    ppermute x1, starting transfers between devices, body(): rim = lax.ppermute(rim, 'seg', route)  2.49 us
    ppermute x1, starting transfers between devices, body(): before = lax.ppermute(up, 'chan', ring)  2.35 us
    pallas_call x1, Pallas kernels, body(): pl.pallas_call(near_kernel, out_shape=[jax.ShapeDtypeStruct((near_each, L...  2.05 us
  transfers between devices with their start and end apart: 8, of which 5 were waited for; matrix products, arithmetic and copies ran while one was open for 0% of the time, Pallas kernels for 12%

profile of v11, /device:TPU:0, one launch (start us, length us, event | category | flops | bytes accessed | tf_op | source)
XLA Modules:
  0.0 43.8 jit_solution(12125124128316997828)
XLA Ops:
  0.6 0.0 copy-start.11
  0.6 0.0 copy-start.12
  0.7 0.0 copy-start.8
  0.7 0.0 copy-start.9
  0.7 1.1 %history.1 = f32[64,128]{1,0:T(8,128)S(1)} custom-call(f32[128,4096]{1,0:T(8,128)} %rec_hbm.1), custom_call_target="tpu_custom_call" | custom-call | flops 10000000000 | bytes 20000000 | tf_op jit(solution)/shard_map/history/pallas_call | solution.py:365
  1.8 0.0 copy-start.1
  1.8 0.0 copy-start.3
  1.8 0.0 copy-start.4
  1.8 2.5 %collective-permute-start = (f32[64,128]{1,0:T(8,128)S(1)}, f32[64,128]{1,0:T(8,128)S(1)}, u32[]{:S(2)}, u32[]{:S(2)}) collective-permute-start(f32[64,128]{1,0:T(8,128)S(1)} %history.1), channel_id=1, source_target_pairs={{0,1},{1,2},{2,3},{4,5},{5,6},{6,7},{8,9},{9,10},{10,11},{12,13},{... | collective-permute-start | bytes 98312 | tf_op jit(solution)/shard_map/ppermute | solution.py:377
  4.3 0.0 copy-done.11
  4.3 0.0 copy-done.12
  4.3 0.0 copy-done.8
  4.3 0.0 copy-done.9
  4.3 0.0 copy-start.13
  4.3 0.0 copy-start.7
  4.4 2.0 %filter_and_transform.1 = (f32[1024,128]{1,0:T(8,128)S(1)}, f32[128,128]{1,0:T(8,128)S(1)}, f32[16,128]{1,0:T(8,128)S(1)}) custom-call(f32[1,64]{1,0:T(1,128)S(1)} %bitcast.5, f32[128,4096]{1,0:T(8,128)S(1)} %copy-done.8, bf16[256,768]{1,0:T(8,128)(2,1)S(1)} %copy-done.11, f32[256,128]{1,0:T(8,128)S(1)} %copy-done.12), custom_call_target="tpu_custom_call" | custom-call | flops 1000000000 | bytes 5000000 | tf_op jit(solution)/shard_map/filter_and_transform/pallas_call | solution.py:379
  6.3 0.0 copy-start.10
  6.4 0.0 collective-permute-done.rim_ref
  6.4 0.0 copy-done.1
  6.4 0.0 copy-done.3
  6.4 0.0 copy-done.4
  6.4 1.5 %whiten.1 = (bf16[32,2,16,128]{3,2,1,0:T(8,128)(2,1)}, bf16[512,128]{1,0:T(8,128)(2,1)S(1)}, bf16[512,128]{1,0:T(8,128)(2,1)S(1)}) custom-call(f32[1024,128]{1,0:T(8,128)S(1)} %get-tuple-element.24.spec_ref, f32[64,128]{1,0:T(8,128)S(1)} %collective-permute-done.rim_ref, f32[128,128]{1,0:T(8,128)S(1)} %get-tuple-element.25.mean_ref, ...), custom_call_target="tpu_custom_call" | custom-call | tf_op jit(solution)/shard_map/whiten/pallas_call | solution.py:397
  7.9 2.4 %collective-permute-start.1 = (bf16[512,128]{1,0:T(8,128)(2,1)S(1)}, bf16[512,128]{1,0:T(8,128)(2,1)S(1)}, u32[]{:S(2)}, u32[]{:S(2)}) collective-permute-start(bf16[512,128]{1,0:T(8,128)(2,1)S(1)} %get-tuple-element.29), channel_id=1, source_target_pairs={{0,4},{4,8},{8,12},{12,16},{16,20},{20,24},{24,28},{28,0},{1,5},{5... | collective-permute-start | bytes 393224 | tf_op jit(solution)/shard_map/ppermute | solution.py:415
  10.2 3.0 %collective-permute-start.2 = (bf16[512,128]{1,0:T(8,128)(2,1)S(1)}, bf16[512,128]{1,0:T(8,128)(2,1)S(1)}, u32[]{:S(2)}, u32[]{:S(2)}) collective-permute-start(bf16[512,128]{1,0:T(8,128)(2,1)S(1)} %get-tuple-element.30), channel_id=1, source_target_pairs={{4,0},{8,4},{12,8},{16,12},{20,16},{24,20},{28,24},{0,28},{5,1},{9... | collective-permute-start | bytes 393224 | tf_op jit(solution)/shard_map/ppermute | solution.py:416
  13.3 0.0 copy-done.13
  13.3 0.1 copy.16.partner_ref
  13.4 0.0 copy-done.7
  13.4 0.6 %offset_moves.1.moves_ref = bf16[256,512]{1,0:T(8,128)(2,1)S(1)} custom-call(s32[4]{0:T(128)S(1)} %copy-done.7), custom_call_target="tpu_custom_call" | custom-call | tf_op jit(solution)/shard_map/offset_moves/pallas_call | solution.py:417
  14.0 4.7 %all-to-all-start = ((bf16[32,2,16,128]{3,2,1,0:T(8,128)(2,1)}), bf16[32,2,16,128]{3,2,1,0:T(8,128)(2,1)S(1)}, u32[]{:S(2)}, u32[]{:S(2)}) async-start(bf16[32,2,16,128]{3,2,1,0:T(8,128)(2,1)} %get-tuple-element.28.white_ref), calls=%async_computation | async-start | bytes 524288 | tf_op jit(solution)/shard_map/all_to_all | solution.py:411
  18.7 0.0 copy-start.2
  18.7 0.0 copy-start.5
  18.7 0.0 copy-start.6
  18.7 0.0 collective-permute-done.1.before_ref
  18.7 0.2 collective-permute-done.2.after_ref
  19.0 2.1 %near_lags.1 = (bf16[1,256,128]{2,1,0:T(8,128)(2,1)S(1)}, bf16[1,256,128]{2,1,0:T(8,128)(2,1)S(1)}, bf16[1,256,128]{2,1,0:T(8,128)(2,1)S(1)}, bf16[1,256,128]{2,1,0:T(8,128)(2,1)S(1)}) custom-call(bf16[32,2,16,128]{3,2,1,0:T(8,128)(2,1)} %get-tuple-element.28.white_ref, bf16[512,128]{1,0:T(8,128)(2,1)S(1)} %collective-permute-done.1.before_ref, ...), custom_call_target="tpu_custom_call" | custom-call | flops 20000000000 | bytes 20000000 | tf_op jit(solution)/shard_map/near_lags/pallas_call | solution.py:428
  21.0 0.0 copy-start
  21.1 8.2 %all-to-all-done = bf16[32,2,16,128]{3,2,1,0:T(8,128)(2,1)S(1)} async-done(((bf16[32,2,16,128]{3,2,1,0:T(8,128)(2,1)}), bf16[32,2,16,128]{3,2,1,0:T(8,128)(2,1)S(1)}, u32[]{:S(2)}, u32[]{:S(2)}) %all-to-all-start) | async-done | bytes 262176 | tf_op jit(solution)/shard_map/all_to_all | solution.py:411
  29.3 2.0 %loop_spectra.1 = bf16[8,4,24,128]{3,2,1,0:T(8,128)(2,1)} custom-call(s32[8,3]{1,0:T(8,128)S(1)} %copy.16.partner_ref, s32[8]{0:T(128)S(1)} %copy-done.6, bf16[128,128]{1,0:T(8,128)(2,1)S(1)} %copy-done.5, bf16[512,512]{1,0:T(8,128)(2,1)S(1)} %copy-done.2, bf16[8,4,2,16,128]{4,3,2,1,0:T(8,128)(2,1)S(1)} %bitcast.4), custom_call_target="tpu_custom_call" | custom-call | tf_op jit(solution)/shard_map/loop_spectra/pallas_call | solution.py:450
  31.3 2.6 %all-to-all-start.1 = ((bf16[32,24,128]{2,1,0:T(8,128)(2,1)}), bf16[32,24,128]{2,1,0:T(8,128)(2,1)S(1)}, u32[]{:S(2)}, u32[]{:S(2)}) async-start(bf16[32,24,128]{2,1,0:T(8,128)(2,1)} %bitcast.2), calls=%async_computation.1 | async-start | bytes 393216 | tf_op jit(solution)/shard_map/all_to_all | solution.py:461
  33.9 0.2 collective-permute-start.3
  34.1 1.7 %collective-permute-start.4 = (bf16[1,256,128]{2,1,0:T(8,128)(2,1)S(1)}, bf16[1,256,128]{2,1,0:T(8,128)(2,1)S(1)}, u32[]{:S(2)}, u32[]{:S(2)}) collective-permute-start(bf16[1,256,128]{2,1,0:T(8,128)(2,1)S(1)} %get-tuple-element.43), channel_id=1, source_target_pairs={{0,2},{1,3},{2,0},{3,1},{4,6},{5,7},{6,4},{7,5},{8,10},{9,11},{10,... | collective-permute-start | bytes 196616 | tf_op jit(solution)/shard_map/ppermute | solution.py:476
  35.8 0.1 collective-permute-start.5
  35.8 0.0 collective-permute-done.3.refs_1_
  35.8 4.3 %collective-permute-done.4.refs_2_ = bf16[1,256,128]{2,1,0:T(8,128)(2,1)S(1)} collective-permute-done((bf16[1,256,128]{2,1,0:T(8,128)(2,1)S(1)}, bf16[1,256,128]{2,1,0:T(8,128)(2,1)S(1)}, u32[]{:S(2)}, u32[]{:S(2)}) %collective-permute-start.4) | collective-permute-done | bytes 65568 | tf_op jit(solution)/shard_map/ppermute | solution.py:476
  40.2 0.8 %collective-permute-done.5.refs_3_ = bf16[1,256,128]{2,1,0:T(8,128)(2,1)S(1)} collective-permute-done((bf16[1,256,128]{2,1,0:T(8,128)(2,1)S(1)}, bf16[1,256,128]{2,1,0:T(8,128)(2,1)S(1)}, u32[]{:S(2)}, u32[]{:S(2)}) %collective-permute-start.5) | collective-permute-done | bytes 65568 | tf_op jit(solution)/shard_map/ppermute | solution.py:476
  41.0 0.8 %near_turn.1 = f32[128,1,256]{2,1,0:T(1,128)} custom-call(bf16[1,256,128]{2,1,0:T(8,128)(2,1)S(1)} %get-tuple-element.41.refs_0_, bf16[1,256,128]{2,1,0:T(8,128)(2,1)S(1)} %collective-permute-done.3.refs_1_, bf16[1,256,128]{2,1,0:T(8,128)(2,1)S(1)} %collective-permute-done.4.refs_2_, bf16[1,256,128]{2,1,0:T(8,128)(2,1)S(1)} %collective-permute-done.5.refs_3_), custom_call_target="tpu_custom_call" | custom-call | tf_op jit(solution)/shard_map/near_turn/pallas_call | solution.py:477
  41.8 1.0 %all-to-all-done.1.spec_ref = bf16[32,24,128]{2,1,0:T(8,128)(2,1)S(1)} async-done(((bf16[32,24,128]{2,1,0:T(8,128)(2,1)}), bf16[32,24,128]{2,1,0:T(8,128)(2,1)S(1)}, u32[]{:S(2)}, u32[]{:S(2)}) %all-to-all-start.1) | async-done | bytes 196640 | tf_op jit(solution)/shard_map/all_to_all | solution.py:461
  42.8 1.0 %loop_lags.1 = f32[96,256]{1,0:T(8,128)} custom-call(bf16[32,24,128]{2,1,0:T(8,128)(2,1)S(1)} %all-to-all-done.1.spec_ref, bf16[1024,512]{1,0:T(8,128)(2,1)S(1)} %copy-done), custom_call_target="tpu_custom_call" | custom-call | tf_op jit(solution)/shard_map/loop_lags/pallas_call | solution.py:465
  (5 shorter events, 0.0 us)
Async XLA Ops:
  0.6 3.7 %copy-start.11 = (bf16[256,768]{1,0:T(8,128)(2,1)S(1)}, bf16[256,768]{1,0:T(8,128)(2,1)}, u32[]{:S(2)}) copy-start(bf16[256,768]{1,0:T(8,128)(2,1)} %constant.18.clone.tab_ref) | copy-start | bytes 1179652
  0.6 3.7 %copy-start.12 = (f32[256,128]{1,0:T(8,128)S(1)}, f32[256,128]{1,0:T(8,128)}, u32[]{:S(2)}) copy-start(f32[256,128]{1,0:T(8,128)} %constant.19.clone.twist_ref) | copy-start | bytes 393220
  0.7 3.7 %copy-start.8 = (f32[128,4096]{1,0:T(8,128)S(1)}, f32[128,4096]{1,0:T(8,128)}, u32[]{:S(2)}) copy-start(f32[128,4096]{1,0:T(8,128)} %rec_hbm.1) | copy-start | bytes 6291460
  0.7 3.7 %copy-start.9 = (f32[64]{0:T(128)S(1)}, f32[64]{0:T(128)}, u32[]{:S(2)}) copy-start(f32[64]{0:T(128)} %param.15) | copy-start | bytes 772
  1.8 4.6 %copy-start.1 = (bf16[512,512]{1,0:T(8,128)(2,1)S(1)}, bf16[512,512]{1,0:T(8,128)(2,1)}, u32[]{:S(2)}) copy-start(bf16[512,512]{1,0:T(8,128)(2,1)} %constant.21.clone.band_ref) | copy-start | bytes 1572868
  1.8 4.6 %copy-start.3 = (bf16[1024,128]{1,0:T(8,128)(2,1)S(1)}, bf16[1024,128]{1,0:T(8,128)(2,1)}, u32[]{:S(2)}) copy-start(bf16[1024,128]{1,0:T(8,128)(2,1)} %constant.20.clone.edge_ref) | copy-start | bytes 786436
  1.8 4.6 %copy-start.4 = (f32[512,128]{1,0:T(8,128)S(1)}, f32[512,128]{1,0:T(8,128)}, u32[]{:S(2)}) copy-start(f32[512,128]{1,0:T(8,128)} %constant.22.clone.share_ref) | copy-start | bytes 786436
  1.8 4.6 %collective-permute-start = (f32[64,128]{1,0:T(8,128)S(1)}, f32[64,128]{1,0:T(8,128)S(1)}, u32[]{:S(2)}, u32[]{:S(2)}) collective-permute-start(f32[64,128]{1,0:T(8,128)S(1)} %history.1), channel_id=1, source_target_pairs={{0,1},{1,2},{2,3},{4,5},{5,6},{6,7},{8,9},{9,10},{10,11},{12,13},{... | collective-permute-start | bytes 98312 | tf_op jit(solution)/shard_map/ppermute | solution.py:377
  4.3 9.0 %copy-start.13 = (s32[8,3]{0,1:T(4,128)S(1)}, s32[8,3]{0,1:T(4,128)}, u32[]{:S(2)}) copy-start(s32[8,3]{0,1:T(4,128)} %param.17) | copy-start | bytes 292
  4.3 9.0 %copy-start.7 = (s32[4]{0:T(128)S(1)}, s32[4]{0:T(128)}, u32[]{:S(2)}) copy-start(s32[4]{0:T(128)} %offs_ref) | copy-start | bytes 52
  6.3 12.6 %copy-start.10 = (bf16[512,1024]{1,0:T(8,128)(2,1)S(1)}, bf16[512,1024]{1,0:T(8,128)(2,1)}, u32[]{:S(2)}) copy-start(bf16[512,1024]{1,0:T(8,128)(2,1)} %constant.23.clone.inv_ref) | copy-start | bytes 3145732
  7.9 10.8 %collective-permute-start.1 = (bf16[512,128]{1,0:T(8,128)(2,1)S(1)}, bf16[512,128]{1,0:T(8,128)(2,1)S(1)}, u32[]{:S(2)}, u32[]{:S(2)}) collective-permute-start(bf16[512,128]{1,0:T(8,128)(2,1)S(1)} %get-tuple-element.29), channel_id=1, source_target_pairs={{0,4},{4,8},{8,12},{12,16},{16,20},{20,24},{24,28},{28,0},{1,5},{5... | collective-permute-start | bytes 393224 | tf_op jit(solution)/shard_map/ppermute | solution.py:415
  10.2 8.7 %collective-permute-start.2 = (bf16[512,128]{1,0:T(8,128)(2,1)S(1)}, bf16[512,128]{1,0:T(8,128)(2,1)S(1)}, u32[]{:S(2)}, u32[]{:S(2)}) collective-permute-start(bf16[512,128]{1,0:T(8,128)(2,1)S(1)} %get-tuple-element.30), channel_id=1, source_target_pairs={{4,0},{8,4},{12,8},{16,12},{20,16},{24,20},{28,24},{0,28},{5,1},{9... | collective-permute-start | bytes 393224 | tf_op jit(solution)/shard_map/ppermute | solution.py:416
  14.0 15.3 %all-to-all-start = ((bf16[32,2,16,128]{3,2,1,0:T(8,128)(2,1)}), bf16[32,2,16,128]{3,2,1,0:T(8,128)(2,1)S(1)}, u32[]{:S(2)}, u32[]{:S(2)}) async-start(bf16[32,2,16,128]{3,2,1,0:T(8,128)(2,1)} %get-tuple-element.28.white_ref), calls=%async_computation | async-start | bytes 524288 | tf_op jit(solution)/shard_map/all_to_all | solution.py:411
  18.7 10.6 %copy-start.2 = (bf16[512,512]{1,0:T(8,128)(2,1)S(1)}, bf16[512,512]{1,0:T(8,128)(2,1)}, u32[]{:S(2)}) copy-start(bf16[512,512]{1,0:T(8,128)(2,1)} %constant.25.clone.pack_ref) | copy-start | bytes 1572868
  18.7 10.6 %copy-start.5 = (bf16[128,128]{1,0:T(8,128)(2,1)S(1)}, bf16[128,128]{1,0:T(8,128)(2,1)}, u32[]{:S(2)}) copy-start(bf16[128,128]{1,0:T(8,128)(2,1)} %constant.24.clone.flip_ref) | copy-start | bytes 98308
  18.7 10.6 %copy-start.6 = (s32[8]{0:T(128)S(1)}, s32[8]{0:T(128)}, u32[]{:S(2)}) copy-start(s32[8]{0:T(128)} %count_ref.1) | copy-start | bytes 100
  21.0 21.7 %copy-start = (bf16[1024,512]{1,0:T(8,128)(2,1)S(1)}, bf16[1024,512]{1,0:T(8,128)(2,1)}, u32[]{:S(2)}) copy-start(bf16[1024,512]{1,0:T(8,128)(2,1)} %constant.26.clone.inv_ref) | copy-start | bytes 3145732
  31.3 11.5 %all-to-all-start.1 = ((bf16[32,24,128]{2,1,0:T(8,128)(2,1)}), bf16[32,24,128]{2,1,0:T(8,128)(2,1)S(1)}, u32[]{:S(2)}, u32[]{:S(2)}) async-start(bf16[32,24,128]{2,1,0:T(8,128)(2,1)} %bitcast.2), calls=%async_computation.1 | async-start | bytes 393216 | tf_op jit(solution)/shard_map/all_to_all | solution.py:461
  33.9 2.0 %collective-permute-start.3 = (bf16[1,256,128]{2,1,0:T(8,128)(2,1)S(1)}, bf16[1,256,128]{2,1,0:T(8,128)(2,1)S(1)}, u32[]{:S(2)}, u32[]{:S(2)}) collective-permute-start(bf16[1,256,128]{2,1,0:T(8,128)(2,1)S(1)} %get-tuple-element.42), channel_id=1, source_target_pairs={{0,1},{1,0},{2,3},{3,2},{4,5},{5,4},{6,7},{7,6},{8,9},{9,8},{10,11... | collective-permute-start | bytes 196616 | tf_op jit(solution)/shard_map/ppermute | solution.py:476
  34.1 6.1 %collective-permute-start.4 = (bf16[1,256,128]{2,1,0:T(8,128)(2,1)S(1)}, bf16[1,256,128]{2,1,0:T(8,128)(2,1)S(1)}, u32[]{:S(2)}, u32[]{:S(2)}) collective-permute-start(bf16[1,256,128]{2,1,0:T(8,128)(2,1)S(1)} %get-tuple-element.43), channel_id=1, source_target_pairs={{0,2},{1,3},{2,0},{3,1},{4,6},{5,7},{6,4},{7,5},{8,10},{9,11},{10,... | collective-permute-start | bytes 196616 | tf_op jit(solution)/shard_map/ppermute | solution.py:476
  35.8 5.3 %collective-permute-start.5 = (bf16[1,256,128]{2,1,0:T(8,128)(2,1)S(1)}, bf16[1,256,128]{2,1,0:T(8,128)(2,1)S(1)}, u32[]{:S(2)}, u32[]{:S(2)}) collective-permute-start(bf16[1,256,128]{2,1,0:T(8,128)(2,1)S(1)} %get-tuple-element.44), channel_id=1, source_target_pairs={{0,3},{1,2},{2,1},{3,0},{4,7},{5,6},{6,5},{7,4},{8,11},{9,10},{10,... | collective-permute-start | bytes 196616 | tf_op jit(solution)/shard_map/ppermute | solution.py:476

commit v12 on v11

--- a/solution.py
+++ b/solution.py
@@ -209,14 +209,12 @@
     down_ref[...] = jnp.where(lane < SPAN, flat[:BINS], turned[BINS:]).astype(BF16)
 
 
-def moves_kernel(offs_ref, moves_ref):
-    noff = offs_ref.shape[0]
+def offset_moves(offs_ref):
     row = lax.broadcasted_iota(jnp.int32, (2 * LANES, LANES), 0)
     channel = lax.broadcasted_iota(jnp.int32, (2 * LANES, LANES), 1)
-    source = jnp.where(row < LANES + SPAN, row, row - 2 * LANES)
-    for o in range(noff):
-        hit = source == channel + offs_ref[o]
-        moves_ref[:, o * LANES : (o + 1) * LANES] = hit.astype(F32).astype(BF16)
+    distance = jnp.where(row < LANES + SPAN, row, row - 2 * LANES) - channel
+    hits = [(distance == offs_ref[o]).astype(F32) for o in range(offs_ref.shape[0])]
+    return jnp.concatenate(hits, axis=1).astype(BF16)
 
 
 def pack_matrix(owners):
@@ -232,7 +230,7 @@
     return place ^ r if owners & (owners - 1) == 0 else (place + r) % owners
 
 
-def near_kernel(white_ref, before_ref, after_ref, moves_ref, inv_ref, *refs):
+def near_kernel(offs_ref, white_ref, before_ref, after_ref, inv_ref, *refs):
     out_refs, lags_ref = refs[:-1], refs[-1]
     rows = white_ref.shape[0] * 2 * GROUP
     half = rows // 2
@@ -243,7 +241,7 @@
     lower = jnp.where(lane < SPAN, pltpu.roll(after, SPAN, 1), before)
     edge = jnp.concatenate([upper, lower], axis=0).astype(BF16)
     own = white_ref[...].reshape(rows, LANES)
-    far = mm(jnp.concatenate([own, edge], axis=1), moves_ref[...])
+    far = mm(jnp.concatenate([own, edge], axis=1), offset_moves(offs_ref))
     own = own.astype(F32).reshape(-1, 2, GROUP, LANES)
     columns = []
     for o in range(noff):
@@ -273,7 +271,7 @@
 def loop_kernel(partner_ref, count_ref, flip_ref, pack_ref, white_ref, out_ref, turned_ref):
     blocks, segs, _, bins, _ = white_ref.shape
     owners = out_ref.shape[1]
-    slots = partner_ref.shape[1]
+    slots = partner_ref.shape[0]
     rows = segs * 2 * bins
     packed_rows = 2 * bins // owners
     flats = [white_ref[b].reshape(rows, LANES) for b in range(blocks)]
@@ -282,7 +280,7 @@
     for b in range(blocks):
         own = flats[b].astype(F32).reshape(segs, 2, bins, LANES)
         for k in range(slots):
-            partner = jnp.clip(partner_ref[b, k], 0, blocks - 1)
+            partner = jnp.clip(partner_ref[k, b], 0, blocks - 1)
             live = (k < count_ref[b]).astype(F32)
             far = turned_ref[partner].reshape(segs, 2, bins, LANES)
             real = jnp.sum(own[:, 0] * far[:, 0] + own[:, 1] * far[:, 1], axis=0)
@@ -396,14 +394,13 @@
     half = jax.ShapeDtypeStruct((BINS, LANES), BF16)
     white, up, down = pl.pallas_call(
         whiten_kernel,
-        out_shape=[pltpu.VMEM((GROUPS, 2, GROUP, LANES), BF16), half, half],
+        out_shape=[jax.ShapeDtypeStruct((GROUPS, 2, GROUP, LANES), BF16), half, half],
         in_specs=vmem(7),
         out_specs=vmem(3),
         compiler_params=PARAMS,
         name="whiten",
     )(spec, rim, mean, head, edge_table(), band, band_share)
 
-    white, offsets = lax.optimization_barrier((white, offsets))
     spread = white
     if bins != GROUP:
         spread = jnp.moveaxis(white, 1, 0).reshape(2, devices, bins, LANES)
@@ -414,21 +411,13 @@
     ring = [(i, (i + 1) % chan_count) for i in range(chan_count)]
     before = lax.ppermute(up, "chan", ring)
     after = lax.ppermute(down, "chan", [(j, i) for i, j in ring])
-    moves = pl.pallas_call(
-        moves_kernel,
-        out_shape=jax.ShapeDtypeStruct((2 * LANES, noff * LANES), BF16),
-        in_specs=smem(1),
-        out_specs=pl.BlockSpec(memory_space=pltpu.VMEM),
-        compiler_params=PARAMS,
-        name="offset_moves",
-    )(offsets)
     order = np.repeat(bin_order().reshape(GROUPS, 1, GROUP), 2, axis=1).reshape(-1)
     part = np.broadcast_to(np.arange(2).reshape(1, 2, 1), (GROUPS, 2, GROUP)).reshape(-1)
     inverse = np.concatenate(split_np(inverse_table(seg_count, order, part)), axis=0)
     lags = pl.pallas_call(
         near_kernel,
         out_shape=[jax.ShapeDtypeStruct((near_each, LAGS, LANES), BF16)] * seg_count,
-        in_specs=vmem(5),
+        in_specs=smem(1) + vmem(4),
         out_specs=vmem(seg_count),
         scratch_shapes=[pltpu.VMEM((noff, LAGS, LANES), F32)],
         compiler_params=PARAMS,
@@ -436,7 +425,7 @@
             flops=20_000_000_000, bytes_accessed=20_000_000, transcendentals=0
         ),
         name="near_lags",
-    )(white, before, after, moves, inverse)
+    )(offsets, white, before, after, inverse)
     moved, *lags = lax.optimization_barrier((moved, *lags))
 
     if bins % GROUP or 2 * bins % (8 * seg_count):
@@ -449,14 +438,13 @@
         out_rows = slots * (2 * bins // seg_count)
         crossed = pl.pallas_call(
             loop_kernel,
-            out_shape=pltpu.VMEM((chan_count, seg_count, out_rows, LANES), BF16),
+            out_shape=jax.ShapeDtypeStruct((chan_count, seg_count, out_rows, LANES), BF16),
             in_specs=smem(2) + vmem(3),
             out_specs=pl.BlockSpec(memory_space=pltpu.VMEM),
             scratch_shapes=[pltpu.VMEM((chan_count, seg_count * 2 * bins, LANES), F32)],
             compiler_params=PARAMS,
             name="loop_spectra",
-        )(loop_partner, loop_count, flip, pack_matrix(seg_count), moved)
-        crossed, *lags = lax.optimization_barrier((crossed, *lags))
+        )(loop_partner.T, loop_count, flip, pack_matrix(seg_count), moved)
         crossed = crossed.reshape(devices, out_rows, LANES)
         summed = lax.all_to_all(crossed, ("chan", "seg"), 0, 0, tiled=True)
         columns = np.arange(2 * BINS).reshape(devices, seg_count, -1).swapaxes(0, 1).reshape(-1)

time: 44.2 us -> 43.5 us (0.984)
  Pallas kernels: 11 us -> 10.4 us
    all_to_all x1, waiting for transfers between devices: 8.24 us -> 7.55 us  [body(): moved = lax.all_to_all(spread, ('chan', 'seg'), 0, 0, tiled=True)]
    ppermute x1, waiting for transfers between devices: 0.23 us -> 0.9 us  [body(): after = lax.ppermute(down, 'chan', [(j, i) for i, j in ring])]
    pallas_call x3 -> x2, Pallas kernels: 4.09 us -> 3.45 us  [the longest x1 1.96 us: body(): pl.pallas_call(loop_kernel, out_shape=jax.ShapeDtypeStruct((chan_count, s...]
  transfers between devices with their start and end apart: 8 -> 8, of which waited for: 5 -> 5; matrix products, arithmetic and copies ran while one was open for 0% -> 0% of each run, Pallas kernels for 12% -> 11%
where the time goes in v12:
time: 43.5 us; the launch traced here: 43.1 us
  starting transfers between devices  17.1 us (39%)
  waiting for transfers between devices  14.6 us (34%)
  Pallas kernels  10.4 us (24%)
  between operations  0.88 us (2%)
    all_to_all x1, waiting for transfers between devices, body(): moved = lax.all_to_all(spread, ('chan', 'seg'), 0, 0, tiled=True)  7.55 us
    ppermute x3, waiting for transfers between devices, body(): lags[r] = lax.ppermute(lags[r], 'seg', route)  5.16 us
    all_to_all x1, starting transfers between devices, body(): moved = lax.all_to_all(spread, ('chan', 'seg'), 0, 0, tiled=True)  4.72 us
    ppermute x1, starting transfers between devices, body(): after = lax.ppermute(down, 'chan', [(j, i) for i, j in ring])  3.04 us
    all_to_all x1, starting transfers between devices, body(): summed = lax.all_to_all(crossed, ('chan', 'seg'), 0, 0, tiled=True)  2.58 us
    ppermute x1, starting transfers between devices, body(): rim = lax.ppermute(rim, 'seg', route)  2.49 us
    ppermute x1, starting transfers between devices, body(): before = lax.ppermute(up, 'chan', ring)  2.35 us
    pallas_call x1, Pallas kernels, body(): pl.pallas_call(near_kernel, out_shape=[jax.ShapeDtypeStruct((near_each, L...  2.06 us
  transfers between devices with their start and end apart: 8, of which 5 were waited for; matrix products, arithmetic and copies ran while one was open for 0% of the time, Pallas kernels for 11%

profile of v12, /device:TPU:0, one launch (start us, length us, event | category | flops | bytes accessed | tf_op | source)
XLA Modules:
  0.0 43.1 jit_solution(9000217753555040685)
XLA Ops:
  0.6 0.0 copy-start.12
  0.6 0.0 copy-start.13
  0.7 0.0 copy-start.8
  0.7 0.0 copy-start.9
  0.7 1.1 %history.1 = f32[64,128]{1,0:T(8,128)S(1)} custom-call(f32[128,4096]{1,0:T(8,128)} %rec_hbm.1), custom_call_target="tpu_custom_call" | custom-call | flops 10000000000 | bytes 20000000 | tf_op jit(solution)/shard_map/history/pallas_call | solution.py:363
  1.8 0.0 copy-start.1
  1.8 0.0 copy-start.3
  1.8 0.0 copy-start.4
  1.8 2.5 %collective-permute-start = (f32[64,128]{1,0:T(8,128)S(1)}, f32[64,128]{1,0:T(8,128)S(1)}, u32[]{:S(2)}, u32[]{:S(2)}) collective-permute-start(f32[64,128]{1,0:T(8,128)S(1)} %history.1), channel_id=1, source_target_pairs={{0,1},{1,2},{2,3},{4,5},{5,6},{6,7},{8,9},{9,10},{10,11},{12,13},{... | collective-permute-start | bytes 98312 | tf_op jit(solution)/shard_map/ppermute | solution.py:375
  4.3 0.0 copy-done.12
  4.3 0.0 copy-done.13
  4.3 0.0 copy-done.8
  4.3 0.0 copy-done.9
  4.3 0.0 copy-start.10
  4.3 0.0 copy-start.11
  4.4 2.0 %filter_and_transform.1 = (f32[1024,128]{1,0:T(8,128)S(1)}, f32[128,128]{1,0:T(8,128)S(1)}, f32[16,128]{1,0:T(8,128)S(1)}) custom-call(f32[1,64]{1,0:T(1,128)S(1)} %bitcast.7, f32[128,4096]{1,0:T(8,128)S(1)} %copy-done.8, bf16[256,768]{1,0:T(8,128)(2,1)S(1)} %copy-done.12, f32[256,128]{1,0:T(8,128)S(1)} %copy-done.13), custom_call_target="tpu_custom_call" | custom-call | flops 1000000000 | bytes 5000000 | tf_op jit(solution)/shard_map/filter_and_transform/pallas_call | solution.py:377
  6.3 0.0 collective-permute-done.rim_ref
  6.4 0.0 copy-done.1
  6.4 0.0 copy-done.3
  6.4 0.0 copy-done.4
  6.4 1.5 %whiten.1 = (bf16[32,2,16,128]{3,2,1,0:T(8,128)(2,1)}, bf16[512,128]{1,0:T(8,128)(2,1)S(1)}, bf16[512,128]{1,0:T(8,128)(2,1)S(1)}) custom-call(f32[1024,128]{1,0:T(8,128)S(1)} %get-tuple-element.17.spec_ref, f32[64,128]{1,0:T(8,128)S(1)} %collective-permute-done.rim_ref, f32[128,128]{1,0:T(8,128)S(1)} %get-tuple-element.18.mean_ref, ...), custom_call_target="tpu_custom_call" | custom-call | tf_op jit(solution)/shard_map/whiten/pallas_call | solution.py:395
  7.9 2.3 %collective-permute-start.1 = (bf16[512,128]{1,0:T(8,128)(2,1)S(1)}, bf16[512,128]{1,0:T(8,128)(2,1)S(1)}, u32[]{:S(2)}, u32[]{:S(2)}) collective-permute-start(bf16[512,128]{1,0:T(8,128)(2,1)S(1)} %get-tuple-element.21), channel_id=1, source_target_pairs={{0,4},{4,8},{8,12},{12,16},{16,20},{20,24},{24,28},{28,0},{1,5},{5... | collective-permute-start | bytes 393224 | tf_op jit(solution)/shard_map/ppermute | solution.py:412
  10.2 3.0 %collective-permute-start.2 = (bf16[512,128]{1,0:T(8,128)(2,1)S(1)}, bf16[512,128]{1,0:T(8,128)(2,1)S(1)}, u32[]{:S(2)}, u32[]{:S(2)}) collective-permute-start(bf16[512,128]{1,0:T(8,128)(2,1)S(1)} %get-tuple-element.22), channel_id=1, source_target_pairs={{4,0},{8,4},{12,8},{16,12},{20,16},{24,20},{28,24},{0,28},{5,1},{9... | collective-permute-start | bytes 393224 | tf_op jit(solution)/shard_map/ppermute | solution.py:413
  13.3 4.7 %all-to-all-start = ((bf16[32,2,16,128]{3,2,1,0:T(8,128)(2,1)}), bf16[32,2,16,128]{3,2,1,0:T(8,128)(2,1)S(1)}, u32[]{:S(2)}, u32[]{:S(2)}) async-start(bf16[32,2,16,128]{3,2,1,0:T(8,128)(2,1)} %get-tuple-element.20.white_ref), calls=%async_computation | async-start | bytes 524288 | tf_op jit(solution)/shard_map/all_to_all | solution.py:408
  18.0 0.0 copy-start.2
  18.0 0.0 copy-start.5
  18.0 0.0 copy-start.6
  18.0 0.0 copy-start.7
  18.0 0.0 collective-permute-done.1.before_ref
  18.1 0.9 %collective-permute-done.2.after_ref = bf16[512,128]{1,0:T(8,128)(2,1)S(1)} collective-permute-done((bf16[512,128]{1,0:T(8,128)(2,1)S(1)}, bf16[512,128]{1,0:T(8,128)(2,1)S(1)}, u32[]{:S(2)}, u32[]{:S(2)}) %collective-permute-start.2) | collective-permute-done | bytes 131104 | tf_op jit(solution)/shard_map/ppermute | solution.py:413
  19.0 0.0 copy-done.10
  19.0 0.0 copy-done.11
  19.0 2.1 %near_lags.1 = (bf16[1,256,128]{2,1,0:T(8,128)(2,1)S(1)}, bf16[1,256,128]{2,1,0:T(8,128)(2,1)S(1)}, bf16[1,256,128]{2,1,0:T(8,128)(2,1)S(1)}, bf16[1,256,128]{2,1,0:T(8,128)(2,1)S(1)}) custom-call(s32[4]{0:T(128)S(1)} %copy-done.10, bf16[32,2,16,128]{3,2,1,0:T(8,128)(2,1)} %get-tuple-element.20.white_ref, ...), custom_call_target="tpu_custom_call" | custom-call | flops 20000000000 | bytes 20000000 | tf_op jit(solution)/shard_map/near_lags/pallas_call | solution.py:417
  21.0 0.0 copy-start
  21.0 7.5 %all-to-all-done = bf16[32,2,16,128]{3,2,1,0:T(8,128)(2,1)S(1)} async-done(((bf16[32,2,16,128]{3,2,1,0:T(8,128)(2,1)}), bf16[32,2,16,128]{3,2,1,0:T(8,128)(2,1)S(1)}, u32[]{:S(2)}, u32[]{:S(2)}) %all-to-all-start) | async-done | bytes 262176 | tf_op jit(solution)/shard_map/all_to_all | solution.py:408
  28.6 0.0 copy-done.5
  28.6 2.0 %loop_spectra.1 = bf16[8,4,24,128]{3,2,1,0:T(8,128)(2,1)} custom-call(s32[3,8]{1,0:T(4,128)S(1)} %bitcast.6, s32[8]{0:T(128)S(1)} %copy-done.7, bf16[128,128]{1,0:T(8,128)(2,1)S(1)} %copy-done.5, bf16[512,512]{1,0:T(8,128)(2,1)S(1)} %copy-done.2, bf16[8,4,2,16,128]{4,3,2,1,0:T(8,128)(2,1)S(1)} %bitcast.5), custom_call_target="tpu_custom_call" | custom-call | tf_op jit(solution)/shard_map/loop_spectra/pallas_call | solution.py:439
  30.6 2.6 %all-to-all-start.1 = ((bf16[32,24,128]{2,1,0:T(8,128)(2,1)}), bf16[32,24,128]{2,1,0:T(8,128)(2,1)S(1)}, u32[]{:S(2)}, u32[]{:S(2)}) async-start(bf16[32,24,128]{2,1,0:T(8,128)(2,1)} %bitcast.3), calls=%async_computation.1 | async-start | bytes 393216 | tf_op jit(solution)/shard_map/all_to_all | solution.py:449
  33.2 0.2 collective-permute-start.3
  33.3 1.7 %collective-permute-start.4 = (bf16[1,256,128]{2,1,0:T(8,128)(2,1)S(1)}, bf16[1,256,128]{2,1,0:T(8,128)(2,1)S(1)}, u32[]{:S(2)}, u32[]{:S(2)}) collective-permute-start(bf16[1,256,128]{2,1,0:T(8,128)(2,1)S(1)} %get-tuple-element.29), channel_id=1, source_target_pairs={{0,2},{1,3},{2,0},{3,1},{4,6},{5,7},{6,4},{7,5},{8,10},{9,11},{10,... | collective-permute-start | bytes 196616 | tf_op jit(solution)/shard_map/ppermute | solution.py:464
  35.0 0.1 collective-permute-start.5
  35.1 0.0 collective-permute-done.3.refs_1_
  35.1 4.3 %collective-permute-done.4.refs_2_ = bf16[1,256,128]{2,1,0:T(8,128)(2,1)S(1)} collective-permute-done((bf16[1,256,128]{2,1,0:T(8,128)(2,1)S(1)}, bf16[1,256,128]{2,1,0:T(8,128)(2,1)S(1)}, u32[]{:S(2)}, u32[]{:S(2)}) %collective-permute-start.4) | collective-permute-done | bytes 65568 | tf_op jit(solution)/shard_map/ppermute | solution.py:464
  39.4 0.8 %collective-permute-done.5.refs_3_ = bf16[1,256,128]{2,1,0:T(8,128)(2,1)S(1)} collective-permute-done((bf16[1,256,128]{2,1,0:T(8,128)(2,1)S(1)}, bf16[1,256,128]{2,1,0:T(8,128)(2,1)S(1)}, u32[]{:S(2)}, u32[]{:S(2)}) %collective-permute-start.5) | collective-permute-done | bytes 65568 | tf_op jit(solution)/shard_map/ppermute | solution.py:464
  40.3 0.8 %near_turn.1 = f32[128,1,256]{2,1,0:T(1,128)} custom-call(bf16[1,256,128]{2,1,0:T(8,128)(2,1)S(1)} %get-tuple-element.27.refs_0_, bf16[1,256,128]{2,1,0:T(8,128)(2,1)S(1)} %collective-permute-done.3.refs_1_, bf16[1,256,128]{2,1,0:T(8,128)(2,1)S(1)} %collective-permute-done.4.refs_2_, bf16[1,256,128]{2,1,0:T(8,128)(2,1)S(1)} %collective-permute-done.5.refs_3_), custom_call_target="tpu_custom_call" | custom-call | tf_op jit(solution)/shard_map/near_turn/pallas_call | solution.py:465
  41.1 1.0 %all-to-all-done.1.spec_ref = bf16[32,24,128]{2,1,0:T(8,128)(2,1)S(1)} async-done(((bf16[32,24,128]{2,1,0:T(8,128)(2,1)}), bf16[32,24,128]{2,1,0:T(8,128)(2,1)S(1)}, u32[]{:S(2)}, u32[]{:S(2)}) %all-to-all-start.1) | async-done | bytes 196640 | tf_op jit(solution)/shard_map/all_to_all | solution.py:449
  42.0 0.0 copy-done
  42.1 1.0 %loop_lags.1 = f32[96,256]{1,0:T(8,128)} custom-call(bf16[32,24,128]{2,1,0:T(8,128)(2,1)S(1)} %all-to-all-done.1.spec_ref, bf16[1024,512]{1,0:T(8,128)(2,1)S(1)} %copy-done), custom_call_target="tpu_custom_call" | custom-call | tf_op jit(solution)/shard_map/loop_lags/pallas_call | solution.py:453
  (3 shorter events, 0.0 us)
Async XLA Ops:
  0.6 3.7 %copy-start.12 = (bf16[256,768]{1,0:T(8,128)(2,1)S(1)}, bf16[256,768]{1,0:T(8,128)(2,1)}, u32[]{:S(2)}) copy-start(bf16[256,768]{1,0:T(8,128)(2,1)} %constant.18.clone.tab_ref) | copy-start | bytes 1179652
  0.6 3.7 %copy-start.13 = (f32[256,128]{1,0:T(8,128)S(1)}, f32[256,128]{1,0:T(8,128)}, u32[]{:S(2)}) copy-start(f32[256,128]{1,0:T(8,128)} %constant.19.clone.twist_ref) | copy-start | bytes 393220
  0.7 3.7 %copy-start.8 = (f32[128,4096]{1,0:T(8,128)S(1)}, f32[128,4096]{1,0:T(8,128)}, u32[]{:S(2)}) copy-start(f32[128,4096]{1,0:T(8,128)} %rec_hbm.1) | copy-start | bytes 6291460
  0.7 3.7 %copy-start.9 = (f32[64]{0:T(128)S(1)}, f32[64]{0:T(128)}, u32[]{:S(2)}) copy-start(f32[64]{0:T(128)} %param.15) | copy-start | bytes 772
  1.8 4.6 %copy-start.1 = (bf16[512,512]{1,0:T(8,128)(2,1)S(1)}, bf16[512,512]{1,0:T(8,128)(2,1)}, u32[]{:S(2)}) copy-start(bf16[512,512]{1,0:T(8,128)(2,1)} %constant.21.clone.band_ref) | copy-start | bytes 1572868
  1.8 4.6 %copy-start.3 = (f32[512,128]{1,0:T(8,128)S(1)}, f32[512,128]{1,0:T(8,128)}, u32[]{:S(2)}) copy-start(f32[512,128]{1,0:T(8,128)} %constant.22.clone.share_ref) | copy-start | bytes 786436
  1.8 4.6 %copy-start.4 = (bf16[1024,128]{1,0:T(8,128)(2,1)S(1)}, bf16[1024,128]{1,0:T(8,128)(2,1)}, u32[]{:S(2)}) copy-start(bf16[1024,128]{1,0:T(8,128)(2,1)} %constant.20.clone.edge_ref) | copy-start | bytes 786436
  1.8 4.6 %collective-permute-start = (f32[64,128]{1,0:T(8,128)S(1)}, f32[64,128]{1,0:T(8,128)S(1)}, u32[]{:S(2)}, u32[]{:S(2)}) collective-permute-start(f32[64,128]{1,0:T(8,128)S(1)} %history.1), channel_id=1, source_target_pairs={{0,1},{1,2},{2,3},{4,5},{5,6},{6,7},{8,9},{9,10},{10,11},{12,13},{... | collective-permute-start | bytes 98312 | tf_op jit(solution)/shard_map/ppermute | solution.py:375
  4.3 14.6 %copy-start.10 = (s32[4]{0:T(128)S(1)}, s32[4]{0:T(128)}, u32[]{:S(2)}) copy-start(s32[4]{0:T(128)} %offs_ref.1) | copy-start | bytes 52
  4.3 14.6 %copy-start.11 = (bf16[512,1024]{1,0:T(8,128)(2,1)S(1)}, bf16[512,1024]{1,0:T(8,128)(2,1)}, u32[]{:S(2)}) copy-start(bf16[512,1024]{1,0:T(8,128)(2,1)} %constant.23.clone.inv_ref) | copy-start | bytes 3145732
  7.9 10.2 %collective-permute-start.1 = (bf16[512,128]{1,0:T(8,128)(2,1)S(1)}, bf16[512,128]{1,0:T(8,128)(2,1)S(1)}, u32[]{:S(2)}, u32[]{:S(2)}) collective-permute-start(bf16[512,128]{1,0:T(8,128)(2,1)S(1)} %get-tuple-element.21), channel_id=1, source_target_pairs={{0,4},{4,8},{8,12},{12,16},{16,20},{20,24},{24,28},{28,0},{1,5},{5... | collective-permute-start | bytes 393224 | tf_op jit(solution)/shard_map/ppermute | solution.py:412
  10.2 8.7 %collective-permute-start.2 = (bf16[512,128]{1,0:T(8,128)(2,1)S(1)}, bf16[512,128]{1,0:T(8,128)(2,1)S(1)}, u32[]{:S(2)}, u32[]{:S(2)}) collective-permute-start(bf16[512,128]{1,0:T(8,128)(2,1)S(1)} %get-tuple-element.22), channel_id=1, source_target_pairs={{4,0},{8,4},{12,8},{16,12},{20,16},{24,20},{28,24},{0,28},{5,1},{9... | collective-permute-start | bytes 393224 | tf_op jit(solution)/shard_map/ppermute | solution.py:413
  13.3 15.3 %all-to-all-start = ((bf16[32,2,16,128]{3,2,1,0:T(8,128)(2,1)}), bf16[32,2,16,128]{3,2,1,0:T(8,128)(2,1)S(1)}, u32[]{:S(2)}, u32[]{:S(2)}) async-start(bf16[32,2,16,128]{3,2,1,0:T(8,128)(2,1)} %get-tuple-element.20.white_ref), calls=%async_computation | async-start | bytes 524288 | tf_op jit(solution)/shard_map/all_to_all | solution.py:408
  18.0 10.6 %copy-start.2 = (bf16[512,512]{1,0:T(8,128)(2,1)S(1)}, bf16[512,512]{1,0:T(8,128)(2,1)}, u32[]{:S(2)}) copy-start(bf16[512,512]{1,0:T(8,128)(2,1)} %constant.25.clone.pack_ref) | copy-start | bytes 1572868
  18.0 10.6 %copy-start.5 = (bf16[128,128]{1,0:T(8,128)(2,1)S(1)}, bf16[128,128]{1,0:T(8,128)(2,1)}, u32[]{:S(2)}) copy-start(bf16[128,128]{1,0:T(8,128)(2,1)} %constant.24.clone.flip_ref) | copy-start | bytes 98308
  18.0 10.6 %copy-start.6 = (s32[8,3]{0,1:T(4,128)S(1)}, s32[8,3]{0,1:T(4,128)}, u32[]{:S(2)}) copy-start(s32[8,3]{0,1:T(4,128)} %param.17) | copy-start | bytes 292
  18.0 10.6 %copy-start.7 = (s32[8]{0:T(128)S(1)}, s32[8]{0:T(128)}, u32[]{:S(2)}) copy-start(s32[8]{0:T(128)} %count_ref.1) | copy-start | bytes 100
  21.0 21.0 %copy-start = (bf16[1024,512]{1,0:T(8,128)(2,1)S(1)}, bf16[1024,512]{1,0:T(8,128)(2,1)}, u32[]{:S(2)}) copy-start(bf16[1024,512]{1,0:T(8,128)(2,1)} %constant.26.clone.inv_ref) | copy-start | bytes 3145732
  30.6 11.5 %all-to-all-start.1 = ((bf16[32,24,128]{2,1,0:T(8,128)(2,1)}), bf16[32,24,128]{2,1,0:T(8,128)(2,1)S(1)}, u32[]{:S(2)}, u32[]{:S(2)}) async-start(bf16[32,24,128]{2,1,0:T(8,128)(2,1)} %bitcast.3), calls=%async_computation.1 | async-start | bytes 393216 | tf_op jit(solution)/shard_map/all_to_all | solution.py:449
  33.2 2.0 %collective-permute-start.3 = (bf16[1,256,128]{2,1,0:T(8,128)(2,1)S(1)}, bf16[1,256,128]{2,1,0:T(8,128)(2,1)S(1)}, u32[]{:S(2)}, u32[]{:S(2)}) collective-permute-start(bf16[1,256,128]{2,1,0:T(8,128)(2,1)S(1)} %get-tuple-element.28), channel_id=1, source_target_pairs={{0,1},{1,0},{2,3},{3,2},{4,5},{5,4},{6,7},{7,6},{8,9},{9,8},{10,11... | collective-permute-start | bytes 196616 | tf_op jit(solution)/shard_map/ppermute | solution.py:464
  33.3 6.1 %collective-permute-start.4 = (bf16[1,256,128]{2,1,0:T(8,128)(2,1)S(1)}, bf16[1,256,128]{2,1,0:T(8,128)(2,1)S(1)}, u32[]{:S(2)}, u32[]{:S(2)}) collective-permute-start(bf16[1,256,128]{2,1,0:T(8,128)(2,1)S(1)} %get-tuple-element.29), channel_id=1, source_target_pairs={{0,2},{1,3},{2,0},{3,1},{4,6},{5,7},{6,4},{7,5},{8,10},{9,11},{10,... | collective-permute-start | bytes 196616 | tf_op jit(solution)/shard_map/ppermute | solution.py:464
  35.0 5.3 %collective-permute-start.5 = (bf16[1,256,128]{2,1,0:T(8,128)(2,1)S(1)}, bf16[1,256,128]{2,1,0:T(8,128)(2,1)S(1)}, u32[]{:S(2)}, u32[]{:S(2)}) collective-permute-start(bf16[1,256,128]{2,1,0:T(8,128)(2,1)S(1)} %get-tuple-element.30), channel_id=1, source_target_pairs={{0,3},{1,2},{2,1},{3,0},{4,7},{5,6},{6,5},{7,4},{8,11},{9,10},{10,... | collective-permute-start | bytes 196616 | tf_op jit(solution)/shard_map/ppermute | solution.py:464

commit v13 on v12

--- a/solution.py
+++ b/solution.py
@@ -178,9 +178,11 @@
     edge_ref,
     band_ref,
     share_ref,
-    white_ref,
+    white_hbm,
     up_ref,
     down_ref,
+    white_ref,
+    sems,
 ):
     head_high, head_low = split(head_ref[...])
     rim = jnp.concatenate([pltpu.roll(rim_ref[...], LANES - TAPS, 1), rim_ref[...]], axis=0)
@@ -200,13 +202,20 @@
     smoothed = (wide[:, :LANES] + wide[:, LANES:]) * share_ref[...]
     level = jnp.sum(amplitude, axis=0, keepdims=True) * (1.0 / BINS)
     scale = 1.0 / (smoothed + (WATER * level + 1e-06))
-    white = parted * scale.reshape(GROUPS, 1, GROUP, LANES)
-    white_ref[...] = white.astype(BF16)
-    flat = white.reshape(2 * BINS, LANES)
-    turned = pltpu.roll(flat, SPAN, 1)
+    scale = scale.reshape(GROUPS, 1, GROUP, LANES)
+    halves, copies = [], []
+    for i in range(2):
+        part = slice(i * GROUPS // 2, (i + 1) * GROUPS // 2)
+        white = parted[part] * scale[part]
+        white_ref[part] = white.astype(BF16)
+        copies.append(pltpu.make_async_copy(white_ref.at[part], white_hbm.at[part], sems.at[i]))
+        copies[i].start()
+        halves.append(white.reshape(BINS, LANES))
     lane = lax.broadcasted_iota(jnp.int32, (BINS, LANES), 1)
-    up_ref[...] = jnp.where(lane < SPAN, turned[:BINS], flat[BINS:]).astype(BF16)
-    down_ref[...] = jnp.where(lane < SPAN, flat[:BINS], turned[BINS:]).astype(BF16)
+    up_ref[...] = jnp.where(lane < SPAN, pltpu.roll(halves[0], SPAN, 1), halves[1]).astype(BF16)
+    down_ref[...] = jnp.where(lane < SPAN, halves[0], pltpu.roll(halves[1], SPAN, 1)).astype(BF16)
+    for copy in copies:
+        copy.wait()
 
 
 def offset_moves(offs_ref):
@@ -268,7 +277,9 @@
         near_ref[:, t, :] = total[t].T
 
 
-def loop_kernel(partner_ref, count_ref, flip_ref, pack_ref, white_ref, out_ref, turned_ref):
+def loop_kernel(
+    partner_ref, count_ref, flip_ref, pack_ref, white_ref, out_hbm, out_ref, turned_ref, sems
+):
     blocks, segs, _, bins, _ = white_ref.shape
     owners = out_ref.shape[1]
     slots = partner_ref.shape[0]
@@ -276,24 +287,32 @@
     packed_rows = 2 * bins // owners
     flats = [white_ref[b].reshape(rows, LANES) for b in range(blocks)]
     turned_ref[...] = mm(jnp.concatenate(flats, axis=0), flip_ref[...]).reshape(turned_ref.shape)
-    loops = []
-    for b in range(blocks):
-        own = flats[b].astype(F32).reshape(segs, 2, bins, LANES)
-        for k in range(slots):
-            partner = jnp.clip(partner_ref[k, b], 0, blocks - 1)
-            live = (k < count_ref[b]).astype(F32)
-            far = turned_ref[partner].reshape(segs, 2, bins, LANES)
-            real = jnp.sum(own[:, 0] * far[:, 0] + own[:, 1] * far[:, 1], axis=0)
-            imag = jnp.sum(own[:, 1] * far[:, 0] - own[:, 0] * far[:, 1], axis=0)
-            pair = jnp.concatenate([real, imag], axis=0) * live
-            groups = [pair[g * packed_rows : (g + 1) * packed_rows] for g in range(owners)]
-            loops.append(jnp.concatenate(groups, axis=1))
-    packed = mm(jnp.concatenate(loops, axis=0).astype(BF16), pack_ref[...])
     depth = slots * packed_rows
-    for b in range(blocks):
-        for q in range(owners):
-            tile = packed[b * depth : (b + 1) * depth, q * LANES : (q + 1) * LANES]
-            out_ref[b, q] = tile.astype(BF16)
+    copies = []
+    for i in range(2):
+        part = range(i * blocks // 2, (i + 1) * blocks // 2)
+        loops = []
+        for b in part:
+            own = flats[b].astype(F32).reshape(segs, 2, bins, LANES)
+            for k in range(slots):
+                partner = jnp.clip(partner_ref[k, b], 0, blocks - 1)
+                live = (k < count_ref[b]).astype(F32)
+                far = turned_ref[partner].reshape(segs, 2, bins, LANES)
+                real = jnp.sum(own[:, 0] * far[:, 0] + own[:, 1] * far[:, 1], axis=0)
+                imag = jnp.sum(own[:, 1] * far[:, 0] - own[:, 0] * far[:, 1], axis=0)
+                pair = jnp.concatenate([real, imag], axis=0) * live
+                groups = [pair[g * packed_rows : (g + 1) * packed_rows] for g in range(owners)]
+                loops.append(jnp.concatenate(groups, axis=1))
+        packed = mm(jnp.concatenate(loops, axis=0).astype(BF16), pack_ref[...])
+        for n, b in enumerate(part):
+            for q in range(owners):
+                tile = packed[n * depth : (n + 1) * depth, q * LANES : (q + 1) * LANES]
+                out_ref[b, q] = tile.astype(BF16)
+        place = slice(part[0], part[-1] + 1)
+        copies.append(pltpu.make_async_copy(out_ref.at[place], out_hbm.at[place], sems.at[i]))
+        copies[i].start()
+    for copy in copies:
+        copy.wait()
 
 
 def loop_lag_kernel(slots, spec_ref, inv_ref, loop_ref):
@@ -396,7 +415,11 @@
         whiten_kernel,
         out_shape=[jax.ShapeDtypeStruct((GROUPS, 2, GROUP, LANES), BF16), half, half],
         in_specs=vmem(7),
-        out_specs=vmem(3),
+        out_specs=hbm(1) + vmem(2),
+        scratch_shapes=[
+            pltpu.VMEM((GROUPS, 2, GROUP, LANES), BF16),
+            pltpu.SemaphoreType.DMA((2,)),
+        ],
         compiler_params=PARAMS,
         name="whiten",
     )(spec, rim, mean, head, edge_table(), band, band_share)
@@ -440,8 +463,12 @@
             loop_kernel,
             out_shape=jax.ShapeDtypeStruct((chan_count, seg_count, out_rows, LANES), BF16),
             in_specs=smem(2) + vmem(3),
-            out_specs=pl.BlockSpec(memory_space=pltpu.VMEM),
-            scratch_shapes=[pltpu.VMEM((chan_count, seg_count * 2 * bins, LANES), F32)],
+            out_specs=pl.BlockSpec(memory_space=pltpu.HBM),
+            scratch_shapes=[
+                pltpu.VMEM((chan_count, seg_count, out_rows, LANES), BF16),
+                pltpu.VMEM((chan_count, seg_count * 2 * bins, LANES), F32),
+                pltpu.SemaphoreType.DMA((2,)),
+            ],
             compiler_params=PARAMS,
             name="loop_spectra",
         )(loop_partner.T, loop_count, flip, pack_matrix(seg_count), moved)
@@ -468,6 +495,9 @@
         in_specs=vmem(seg_count),
         out_specs=pl.BlockSpec(memory_space=pltpu.VMEM),
         compiler_params=PARAMS,
+        cost_estimate=pl.CostEstimate(
+            flops=20_000_000_000, bytes_accessed=20_000_000, transcendentals=0
+        ),
         name="near_turn",
     )(*lags)
     return near, loop

time: 43.5 us -> 45.5 us (1.046)
  waiting for transfers between devices: 14.6 us -> 16.5 us
    all_to_all x1, waiting for transfers between devices: 1 us -> 8.07 us  [body(): summed = lax.all_to_all(crossed, ('chan', 'seg'), 0, 0, tiled=True)]
    ppermute x3, waiting for transfers between devices: 5.16 us -> 0.01 us  [body(): lags[r] = lax.ppermute(lags[r], 'seg', route)]
  transfers between devices with their start and end apart: 8 -> 8, of which waited for: 5 -> 3; matrix products, arithmetic and copies ran while one was open for 0% -> 0% of each run, Pallas kernels for 11% -> 15%
where the time goes in v13:
time: 45.5 us; the launch traced here: 45 us
  starting transfers between devices  17.1 us (38%)
  waiting for transfers between devices  16.5 us (36%)
  Pallas kernels  10.4 us (23%)
  between operations  0.91 us (2%)
    all_to_all x1, waiting for transfers between devices, body(): summed = lax.all_to_all(crossed, ('chan', 'seg'), 0, 0, tiled=True)  8.07 us
    all_to_all x1, waiting for transfers between devices, body(): moved = lax.all_to_all(spread, ('chan', 'seg'), 0, 0, tiled=True)  7.57 us
    all_to_all x1, starting transfers between devices, body(): moved = lax.all_to_all(spread, ('chan', 'seg'), 0, 0, tiled=True)  4.66 us
    ppermute x1, starting transfers between devices, body(): after = lax.ppermute(down, 'chan', [(j, i) for i, j in ring])  3.1 us
    all_to_all x1, starting transfers between devices, body(): summed = lax.all_to_all(crossed, ('chan', 'seg'), 0, 0, tiled=True)  2.6 us
    ppermute x1, starting transfers between devices, body(): rim = lax.ppermute(rim, 'seg', route)  2.49 us
    ppermute x1, starting transfers between devices, body(): before = lax.ppermute(up, 'chan', ring)  2.4 us
    pallas_call x1, Pallas kernels, body(): pl.pallas_call(near_kernel, out_shape=[jax.ShapeDtypeStruct((near_each, L...  2.06 us
  transfers between devices with their start and end apart: 8, of which 3 were waited for; matrix products, arithmetic and copies ran while one was open for 0% of the time, Pallas kernels for 15%

profile of v13, /device:TPU:0, one launch (start us, length us, event | category | flops | bytes accessed | tf_op | source)
XLA Modules:
  0.0 45.0 jit_solution(10730275786070581270)
XLA Ops:
  0.6 0.0 copy-start.12
  0.6 0.0 copy-start.13
  0.7 0.0 copy-start.8
  0.7 0.0 copy-start.9
  0.7 1.1 %history.1 = f32[64,128]{1,0:T(8,128)S(1)} custom-call(f32[128,4096]{1,0:T(8,128)} %rec_hbm.1), custom_call_target="tpu_custom_call" | custom-call | flops 10000000000 | bytes 20000000 | tf_op jit(solution)/shard_map/history/pallas_call | solution.py:382
  1.8 0.0 copy-start.1
  1.8 0.0 copy-start.3
  1.8 0.0 copy-start.4
  1.8 2.5 %collective-permute-start = (f32[64,128]{1,0:T(8,128)S(1)}, f32[64,128]{1,0:T(8,128)S(1)}, u32[]{:S(2)}, u32[]{:S(2)}) collective-permute-start(f32[64,128]{1,0:T(8,128)S(1)} %history.1), channel_id=1, source_target_pairs={{0,1},{1,2},{2,3},{4,5},{5,6},{6,7},{8,9},{9,10},{10,11},{12,13},{... | collective-permute-start | bytes 98312 | tf_op jit(solution)/shard_map/ppermute | solution.py:394
  4.3 0.0 copy-done.12
  4.3 0.0 copy-done.13
  4.3 0.0 copy-done.8
  4.3 0.0 copy-done.9
  4.3 0.0 copy-start.10
  4.3 0.0 copy-start.11
  4.4 2.0 %filter_and_transform.1 = (f32[1024,128]{1,0:T(8,128)S(1)}, f32[128,128]{1,0:T(8,128)S(1)}, f32[16,128]{1,0:T(8,128)S(1)}) custom-call(f32[1,64]{1,0:T(1,128)S(1)} %bitcast.7, f32[128,4096]{1,0:T(8,128)S(1)} %copy-done.8, bf16[256,768]{1,0:T(8,128)(2,1)S(1)} %copy-done.12, f32[256,128]{1,0:T(8,128)S(1)} %copy-done.13), custom_call_target="tpu_custom_call" | custom-call | flops 1000000000 | bytes 5000000 | tf_op jit(solution)/shard_map/filter_and_transform/pallas_call | solution.py:396
  6.3 0.0 collective-permute-done.rim_ref
  6.4 0.0 copy-done.1
  6.4 0.0 copy-done.3
  6.4 0.0 copy-done.4
  6.4 1.5 %whiten.1 = (bf16[32,2,16,128]{3,2,1,0:T(8,128)(2,1)}, bf16[512,128]{1,0:T(8,128)(2,1)S(1)}, bf16[512,128]{1,0:T(8,128)(2,1)S(1)}) custom-call(f32[1024,128]{1,0:T(8,128)S(1)} %get-tuple-element.17.spec_ref, f32[64,128]{1,0:T(8,128)S(1)} %collective-permute-done.rim_ref, f32[128,128]{1,0:T(8,128)S(1)} %get-tuple-element.18.mean_ref, ...), custom_call_target="tpu_custom_call" | custom-call | tf_op jit(solution)/shard_map/whiten/pallas_call | solution.py:414
  7.9 2.4 %collective-permute-start.1 = (bf16[512,128]{1,0:T(8,128)(2,1)S(1)}, bf16[512,128]{1,0:T(8,128)(2,1)S(1)}, u32[]{:S(2)}, u32[]{:S(2)}) collective-permute-start(bf16[512,128]{1,0:T(8,128)(2,1)S(1)} %get-tuple-element.21), channel_id=1, source_target_pairs={{0,4},{4,8},{8,12},{12,16},{16,20},{20,24},{24,28},{28,0},{1,5},{5... | collective-permute-start | bytes 393224 | tf_op jit(solution)/shard_map/ppermute | solution.py:435
  10.3 3.1 %collective-permute-start.2 = (bf16[512,128]{1,0:T(8,128)(2,1)S(1)}, bf16[512,128]{1,0:T(8,128)(2,1)S(1)}, u32[]{:S(2)}, u32[]{:S(2)}) collective-permute-start(bf16[512,128]{1,0:T(8,128)(2,1)S(1)} %get-tuple-element.22), channel_id=1, source_target_pairs={{4,0},{8,4},{12,8},{16,12},{20,16},{24,20},{28,24},{0,28},{5,1},{9... | collective-permute-start | bytes 393224 | tf_op jit(solution)/shard_map/ppermute | solution.py:436
  13.4 4.7 %all-to-all-start = ((bf16[32,2,16,128]{3,2,1,0:T(8,128)(2,1)}), bf16[32,2,16,128]{3,2,1,0:T(8,128)(2,1)S(1)}, u32[]{:S(2)}, u32[]{:S(2)}) async-start(bf16[32,2,16,128]{3,2,1,0:T(8,128)(2,1)} %get-tuple-element.20.white_ref), calls=%async_computation | async-start | bytes 524288 | tf_op jit(solution)/shard_map/all_to_all | solution.py:431
  18.0 0.0 copy-start.2
  18.1 0.0 copy-start.5
  18.1 0.0 copy-start.6
  18.1 0.0 copy-start.7
  18.1 0.0 collective-permute-done.1.before_ref
  18.1 0.9 %collective-permute-done.2.after_ref = bf16[512,128]{1,0:T(8,128)(2,1)S(1)} collective-permute-done((bf16[512,128]{1,0:T(8,128)(2,1)S(1)}, bf16[512,128]{1,0:T(8,128)(2,1)S(1)}, u32[]{:S(2)}, u32[]{:S(2)}) %collective-permute-start.2) | collective-permute-done | bytes 131104 | tf_op jit(solution)/shard_map/ppermute | solution.py:436
  19.0 0.0 copy-done.10
  19.0 0.0 copy-done.11
  19.0 2.1 %near_lags.1 = (bf16[1,256,128]{2,1,0:T(8,128)(2,1)S(1)}, bf16[1,256,128]{2,1,0:T(8,128)(2,1)S(1)}, bf16[1,256,128]{2,1,0:T(8,128)(2,1)S(1)}, bf16[1,256,128]{2,1,0:T(8,128)(2,1)S(1)}) custom-call(s32[4]{0:T(128)S(1)} %copy-done.10, bf16[32,2,16,128]{3,2,1,0:T(8,128)(2,1)} %get-tuple-element.20.white_ref, ...), custom_call_target="tpu_custom_call" | custom-call | flops 20000000000 | bytes 20000000 | tf_op jit(solution)/shard_map/near_lags/pallas_call | solution.py:440
  21.1 7.6 %all-to-all-done = bf16[32,2,16,128]{3,2,1,0:T(8,128)(2,1)S(1)} async-done(((bf16[32,2,16,128]{3,2,1,0:T(8,128)(2,1)}), bf16[32,2,16,128]{3,2,1,0:T(8,128)(2,1)S(1)}, u32[]{:S(2)}, u32[]{:S(2)}) %all-to-all-start) | async-done | bytes 262176 | tf_op jit(solution)/shard_map/all_to_all | solution.py:431
  28.6 0.0 collective-permute-start.3
  28.6 0.8 %collective-permute-start.4 = (bf16[1,256,128]{2,1,0:T(8,128)(2,1)S(1)}, bf16[1,256,128]{2,1,0:T(8,128)(2,1)S(1)}, u32[]{:S(2)}, u32[]{:S(2)}) collective-permute-start(bf16[1,256,128]{2,1,0:T(8,128)(2,1)S(1)} %get-tuple-element.29), channel_id=1, source_target_pairs={{0,2},{1,3},{2,0},{3,1},{4,6},{5,7},{6,4},{7,5},{8,10},{9,11},{10,... | collective-permute-start | bytes 196616 | tf_op jit(solution)/shard_map/ppermute | solution.py:491
  29.5 1.0 %collective-permute-start.5 = (bf16[1,256,128]{2,1,0:T(8,128)(2,1)S(1)}, bf16[1,256,128]{2,1,0:T(8,128)(2,1)S(1)}, u32[]{:S(2)}, u32[]{:S(2)}) collective-permute-start(bf16[1,256,128]{2,1,0:T(8,128)(2,1)S(1)} %get-tuple-element.30), channel_id=1, source_target_pairs={{0,3},{1,2},{2,1},{3,0},{4,7},{5,6},{6,5},{7,4},{8,11},{9,10},{10,... | collective-permute-start | bytes 196616 | tf_op jit(solution)/shard_map/ppermute | solution.py:491
  30.5 0.0 copy-done.2
  30.5 0.0 copy-done.5
  30.5 2.0 %loop_spectra.1 = bf16[8,4,24,128]{3,2,1,0:T(8,128)(2,1)} custom-call(s32[3,8]{1,0:T(4,128)S(1)} %bitcast.6, s32[8]{0:T(128)S(1)} %copy-done.7, bf16[128,128]{1,0:T(8,128)(2,1)S(1)} %copy-done.5, bf16[512,512]{1,0:T(8,128)(2,1)S(1)} %copy-done.2, bf16[8,4,2,16,128]{4,3,2,1,0:T(8,128)(2,1)S(1)} %bitcast.5), custom_call_target="tpu_custom_call" | custom-call | tf_op jit(solution)/shard_map/loop_spectra/pallas_call | solution.py:462
  32.5 2.6 %all-to-all-start.1 = ((bf16[32,24,128]{2,1,0:T(8,128)(2,1)}), bf16[32,24,128]{2,1,0:T(8,128)(2,1)S(1)}, u32[]{:S(2)}, u32[]{:S(2)}) async-start(bf16[32,24,128]{2,1,0:T(8,128)(2,1)} %bitcast.3), calls=%async_computation.1 | async-start | bytes 393216 | tf_op jit(solution)/shard_map/all_to_all | solution.py:476
  35.1 0.0 copy-start
  35.1 0.0 collective-permute-done.3.refs_1_
  35.2 0.0 collective-permute-done.4.refs_2_
  35.2 0.0 collective-permute-done.5.refs_3_
  35.2 0.8 %near_turn.1 = f32[128,1,256]{2,1,0:T(1,128)} custom-call(bf16[1,256,128]{2,1,0:T(8,128)(2,1)S(1)} %get-tuple-element.27.refs_0_, bf16[1,256,128]{2,1,0:T(8,128)(2,1)S(1)} %collective-permute-done.3.refs_1_, bf16[1,256,128]{2,1,0:T(8,128)(2,1)S(1)} %collective-permute-done.4.refs_2_, bf16[1,256,128]{2,1,0:T(8,128)(2,1)S(1)} %collective-permute-done.5.refs_3_), custom_call_target="tpu_custom_call" | custom-call | flops 20000000000 | bytes 20000000 | tf_op jit(solution)/shard_map/near_turn/pallas_call | solution.py:492
  36.0 8.1 %all-to-all-done.1.spec_ref = bf16[32,24,128]{2,1,0:T(8,128)(2,1)S(1)} async-done(((bf16[32,24,128]{2,1,0:T(8,128)(2,1)}), bf16[32,24,128]{2,1,0:T(8,128)(2,1)S(1)}, u32[]{:S(2)}, u32[]{:S(2)}) %all-to-all-start.1) | async-done | bytes 196640 | tf_op jit(solution)/shard_map/all_to_all | solution.py:476
  44.0 1.0 %loop_lags.1 = f32[96,256]{1,0:T(8,128)} custom-call(bf16[32,24,128]{2,1,0:T(8,128)(2,1)S(1)} %all-to-all-done.1.spec_ref, bf16[1024,512]{1,0:T(8,128)(2,1)S(1)} %copy-done), custom_call_target="tpu_custom_call" | custom-call | tf_op jit(solution)/shard_map/loop_lags/pallas_call | solution.py:480
  (3 shorter events, 0.0 us)
Async XLA Ops:
  0.6 3.7 %copy-start.12 = (bf16[256,768]{1,0:T(8,128)(2,1)S(1)}, bf16[256,768]{1,0:T(8,128)(2,1)}, u32[]{:S(2)}) copy-start(bf16[256,768]{1,0:T(8,128)(2,1)} %constant.18.clone.tab_ref) | copy-start | bytes 1179652
  0.6 3.7 %copy-start.13 = (f32[256,128]{1,0:T(8,128)S(1)}, f32[256,128]{1,0:T(8,128)}, u32[]{:S(2)}) copy-start(f32[256,128]{1,0:T(8,128)} %constant.19.clone.twist_ref) | copy-start | bytes 393220
  0.7 3.7 %copy-start.8 = (f32[128,4096]{1,0:T(8,128)S(1)}, f32[128,4096]{1,0:T(8,128)}, u32[]{:S(2)}) copy-start(f32[128,4096]{1,0:T(8,128)} %rec_hbm.1) | copy-start | bytes 6291460
  0.7 3.7 %copy-start.9 = (f32[64]{0:T(128)S(1)}, f32[64]{0:T(128)}, u32[]{:S(2)}) copy-start(f32[64]{0:T(128)} %param.15) | copy-start | bytes 772
  1.8 4.6 %copy-start.1 = (bf16[512,512]{1,0:T(8,128)(2,1)S(1)}, bf16[512,512]{1,0:T(8,128)(2,1)}, u32[]{:S(2)}) copy-start(bf16[512,512]{1,0:T(8,128)(2,1)} %constant.21.clone.band_ref) | copy-start | bytes 1572868
  1.8 4.6 %copy-start.3 = (f32[512,128]{1,0:T(8,128)S(1)}, f32[512,128]{1,0:T(8,128)}, u32[]{:S(2)}) copy-start(f32[512,128]{1,0:T(8,128)} %constant.22.clone.share_ref) | copy-start | bytes 786436
  1.8 4.6 %copy-start.4 = (bf16[1024,128]{1,0:T(8,128)(2,1)S(1)}, bf16[1024,128]{1,0:T(8,128)(2,1)}, u32[]{:S(2)}) copy-start(bf16[1024,128]{1,0:T(8,128)(2,1)} %constant.20.clone.edge_ref) | copy-start | bytes 786436
  1.8 4.6 %collective-permute-start = (f32[64,128]{1,0:T(8,128)S(1)}, f32[64,128]{1,0:T(8,128)S(1)}, u32[]{:S(2)}, u32[]{:S(2)}) collective-permute-start(f32[64,128]{1,0:T(8,128)S(1)} %history.1), channel_id=1, source_target_pairs={{0,1},{1,2},{2,3},{4,5},{5,6},{6,7},{8,9},{9,10},{10,11},{12,13},{... | collective-permute-start | bytes 98312 | tf_op jit(solution)/shard_map/ppermute | solution.py:394
  4.3 14.7 %copy-start.10 = (s32[4]{0:T(128)S(1)}, s32[4]{0:T(128)}, u32[]{:S(2)}) copy-start(s32[4]{0:T(128)} %offs_ref.1) | copy-start | bytes 52
  4.3 14.7 %copy-start.11 = (bf16[512,1024]{1,0:T(8,128)(2,1)S(1)}, bf16[512,1024]{1,0:T(8,128)(2,1)}, u32[]{:S(2)}) copy-start(bf16[512,1024]{1,0:T(8,128)(2,1)} %constant.23.clone.inv_ref) | copy-start | bytes 3145732
  7.9 10.2 %collective-permute-start.1 = (bf16[512,128]{1,0:T(8,128)(2,1)S(1)}, bf16[512,128]{1,0:T(8,128)(2,1)S(1)}, u32[]{:S(2)}, u32[]{:S(2)}) collective-permute-start(bf16[512,128]{1,0:T(8,128)(2,1)S(1)} %get-tuple-element.21), channel_id=1, source_target_pairs={{0,4},{4,8},{8,12},{12,16},{16,20},{20,24},{24,28},{28,0},{1,5},{5... | collective-permute-start | bytes 393224 | tf_op jit(solution)/shard_map/ppermute | solution.py:435
  10.3 8.7 %collective-permute-start.2 = (bf16[512,128]{1,0:T(8,128)(2,1)S(1)}, bf16[512,128]{1,0:T(8,128)(2,1)S(1)}, u32[]{:S(2)}, u32[]{:S(2)}) collective-permute-start(bf16[512,128]{1,0:T(8,128)(2,1)S(1)} %get-tuple-element.22), channel_id=1, source_target_pairs={{4,0},{8,4},{12,8},{16,12},{20,16},{24,20},{28,24},{0,28},{5,1},{9... | collective-permute-start | bytes 393224 | tf_op jit(solution)/shard_map/ppermute | solution.py:436
  13.4 15.3 %all-to-all-start = ((bf16[32,2,16,128]{3,2,1,0:T(8,128)(2,1)}), bf16[32,2,16,128]{3,2,1,0:T(8,128)(2,1)S(1)}, u32[]{:S(2)}, u32[]{:S(2)}) async-start(bf16[32,2,16,128]{3,2,1,0:T(8,128)(2,1)} %get-tuple-element.20.white_ref), calls=%async_computation | async-start | bytes 524288 | tf_op jit(solution)/shard_map/all_to_all | solution.py:431
  18.0 12.5 %copy-start.2 = (bf16[512,512]{1,0:T(8,128)(2,1)S(1)}, bf16[512,512]{1,0:T(8,128)(2,1)}, u32[]{:S(2)}) copy-start(bf16[512,512]{1,0:T(8,128)(2,1)} %constant.25.clone.pack_ref) | copy-start | bytes 1572868
  18.1 12.5 %copy-start.5 = (bf16[128,128]{1,0:T(8,128)(2,1)S(1)}, bf16[128,128]{1,0:T(8,128)(2,1)}, u32[]{:S(2)}) copy-start(bf16[128,128]{1,0:T(8,128)(2,1)} %constant.24.clone.flip_ref) | copy-start | bytes 98308
  18.1 12.4 %copy-start.6 = (s32[8,3]{0,1:T(4,128)S(1)}, s32[8,3]{0,1:T(4,128)}, u32[]{:S(2)}) copy-start(s32[8,3]{0,1:T(4,128)} %param.17) | copy-start | bytes 292
  18.1 12.4 %copy-start.7 = (s32[8]{0:T(128)S(1)}, s32[8]{0:T(128)}, u32[]{:S(2)}) copy-start(s32[8]{0:T(128)} %count_ref.1) | copy-start | bytes 100
  28.6 6.5 %collective-permute-start.3 = (bf16[1,256,128]{2,1,0:T(8,128)(2,1)S(1)}, bf16[1,256,128]{2,1,0:T(8,128)(2,1)S(1)}, u32[]{:S(2)}, u32[]{:S(2)}) collective-permute-start(bf16[1,256,128]{2,1,0:T(8,128)(2,1)S(1)} %get-tuple-element.28), channel_id=1, source_target_pairs={{0,1},{1,0},{2,3},{3,2},{4,5},{5,4},{6,7},{7,6},{8,9},{9,8},{10,11... | collective-permute-start | bytes 196616 | tf_op jit(solution)/shard_map/ppermute | solution.py:491
  28.6 6.5 %collective-permute-start.4 = (bf16[1,256,128]{2,1,0:T(8,128)(2,1)S(1)}, bf16[1,256,128]{2,1,0:T(8,128)(2,1)S(1)}, u32[]{:S(2)}, u32[]{:S(2)}) collective-permute-start(bf16[1,256,128]{2,1,0:T(8,128)(2,1)S(1)} %get-tuple-element.29), channel_id=1, source_target_pairs={{0,2},{1,3},{2,0},{3,1},{4,6},{5,7},{6,4},{7,5},{8,10},{9,11},{10,... | collective-permute-start | bytes 196616 | tf_op jit(solution)/shard_map/ppermute | solution.py:491
  29.5 5.7 %collective-permute-start.5 = (bf16[1,256,128]{2,1,0:T(8,128)(2,1)S(1)}, bf16[1,256,128]{2,1,0:T(8,128)(2,1)S(1)}, u32[]{:S(2)}, u32[]{:S(2)}) collective-permute-start(bf16[1,256,128]{2,1,0:T(8,128)(2,1)S(1)} %get-tuple-element.30), channel_id=1, source_target_pairs={{0,3},{1,2},{2,1},{3,0},{4,7},{5,6},{6,5},{7,4},{8,11},{9,10},{10,... | collective-permute-start | bytes 196616 | tf_op jit(solution)/shard_map/ppermute | solution.py:491
  32.5 11.5 %all-to-all-start.1 = ((bf16[32,24,128]{2,1,0:T(8,128)(2,1)}), bf16[32,24,128]{2,1,0:T(8,128)(2,1)S(1)}, u32[]{:S(2)}, u32[]{:S(2)}) async-start(bf16[32,24,128]{2,1,0:T(8,128)(2,1)} %bitcast.3), calls=%async_computation.1 | async-start | bytes 393216 | tf_op jit(solution)/shard_map/all_to_all | solution.py:476
  35.1 8.9 %copy-start = (bf16[1024,512]{1,0:T(8,128)(2,1)S(1)}, bf16[1024,512]{1,0:T(8,128)(2,1)}, u32[]{:S(2)}) copy-start(bf16[1024,512]{1,0:T(8,128)(2,1)} %constant.26.clone.inv_ref) | copy-start | bytes 3145732

commit v14 on v12

--- a/solution.py
+++ b/solution.py
@@ -310,6 +310,11 @@
     loop_ref[...] = both[:, :LAGS] + both[:, LAGS:]
 
 
+def last_kernel(slots, spec_ref, inv_ref, *refs):
+    turn_kernel(*refs[:-1])
+    loop_lag_kernel(slots, spec_ref, inv_ref, refs[-1])
+
+
 def vmem(count):
     return [pl.BlockSpec(memory_space=pltpu.VMEM)] * count
 
@@ -426,51 +431,54 @@
         ),
         name="near_lags",
     )(offsets, white, before, after, inverse)
-    moved, *lags = lax.optimization_barrier((moved, *lags))
-
+    lags = list(lags)
+    for r in range(seg_count - 1, 0, -1):
+        route = [(i, partner_of(i, r, seg_count)) for i in range(seg_count)]
+        lags[r] = lax.ppermute(lags[r], "seg", route)
+    moved, lags[0] = lax.optimization_barrier((moved, lags[0]))
+
+    near_shape = jax.ShapeDtypeStruct((chans, near_each, LAGS), F32)
     if bins % GROUP or 2 * bins % (8 * seg_count):
         order = np.repeat(bin_order().reshape(devices, 1, bins), 2, axis=1).reshape(-1)
         part = np.broadcast_to(np.arange(2).reshape(1, 2, 1), (devices, 2, bins)).reshape(-1)
         loop_inverse = inverse_table(seg_count, order, part)
         loop = loops_plain(moved, loop_partner, loop_count, seg_count, loop_inverse)
-    else:
-        flip = np.eye(LANES, dtype=np.float32)[::-1].astype(jnp.bfloat16)
-        out_rows = slots * (2 * bins // seg_count)
-        crossed = pl.pallas_call(
-            loop_kernel,
-            out_shape=jax.ShapeDtypeStruct((chan_count, seg_count, out_rows, LANES), BF16),
-            in_specs=smem(2) + vmem(3),
-            out_specs=pl.BlockSpec(memory_space=pltpu.VMEM),
-            scratch_shapes=[pltpu.VMEM((chan_count, seg_count * 2 * bins, LANES), F32)],
-            compiler_params=PARAMS,
-            name="loop_spectra",
-        )(loop_partner.T, loop_count, flip, pack_matrix(seg_count), moved)
-        crossed = crossed.reshape(devices, out_rows, LANES)
-        summed = lax.all_to_all(crossed, ("chan", "seg"), 0, 0, tiled=True)
-        columns = np.arange(2 * BINS).reshape(devices, seg_count, -1).swapaxes(0, 1).reshape(-1)
-        loop_inverse = inverse_table(seg_count, order[columns], part[columns]).T
-        loop_inverse = np.concatenate(split_np(loop_inverse), axis=1)
-        loop = pl.pallas_call(
-            functools.partial(loop_lag_kernel, slots),
-            out_shape=jax.ShapeDtypeStruct((slots * share, LAGS), F32),
-            in_specs=vmem(2),
+        near = pl.pallas_call(
+            turn_kernel,
+            out_shape=near_shape,
+            in_specs=vmem(seg_count),
             out_specs=pl.BlockSpec(memory_space=pltpu.VMEM),
             compiler_params=PARAMS,
-            name="loop_lags",
-        )(summed, loop_inverse)
-        loop = loop.reshape(1, slots, share, LAGS)
-    for r in range(seg_count - 1, 0, -1):
-        route = [(i, partner_of(i, r, seg_count)) for i in range(seg_count)]
-        lags[r] = lax.ppermute(lags[r], "seg", route)
-    near = pl.pallas_call(
-        turn_kernel,
-        out_shape=jax.ShapeDtypeStruct((chans, near_each, LAGS), F32),
-        in_specs=vmem(seg_count),
+            name="near_turn",
+        )(*lags)
+        return near, loop
+
+    flip = np.eye(LANES, dtype=np.float32)[::-1].astype(jnp.bfloat16)
+    out_rows = slots * (2 * bins // seg_count)
+    crossed = pl.pallas_call(
+        loop_kernel,
+        out_shape=jax.ShapeDtypeStruct((chan_count, seg_count, out_rows, LANES), BF16),
+        in_specs=smem(2) + vmem(3),
         out_specs=pl.BlockSpec(memory_space=pltpu.VMEM),
-        compiler_params=PARAMS,
-        name="near_turn",
-    )(*lags)
-    return near, loop
+        scratch_shapes=[pltpu.VMEM((chan_count, seg_count * 2 * bins, LANES), F32)],
+        compiler_params=PARAMS,
+        name="loop_spectra",
+    )(loop_partner.T, loop_count, flip, pack_matrix(seg_count), moved)
+    crossed, *lags[1:] = lax.optimization_barrier((crossed, *lags[1:]))
+    crossed = crossed.reshape(devices, out_rows, LANES)
+    summed = lax.all_to_all(crossed, ("chan", "seg"), 0, 0, tiled=True)
+    columns = np.arange(2 * BINS).reshape(devices, seg_count, -1).swapaxes(0, 1).reshape(-1)
+    loop_inverse = inverse_table(seg_count, order[columns], part[columns]).T
+    loop_inverse = np.concatenate(split_np(loop_inverse), axis=1)
+    near, loop = pl.pallas_call(
+        functools.partial(last_kernel, slots),
+        out_shape=[near_shape, jax.ShapeDtypeStruct((slots * share, LAGS), F32)],
+        in_specs=vmem(2 + seg_count),
+        out_specs=vmem(2),
+        compiler_params=PARAMS,
+        name="lags",
+    )(summed, loop_inverse, *lags)
+    return near, loop.reshape(1, slots, share, LAGS)
 
 
 def solution(mesh):

time: 43.5 us -> 42.4 us (0.975)
  blocking collectives: 0 us -> 11.1 us
  waiting for transfers between devices: 14.6 us -> 6.54 us
  starting transfers between devices: 17.1 us -> 14.5 us
  Pallas kernels: 10.4 us -> 8.9 us
    all_to_all x0 -> x1, blocking collectives: none -> 11.1 us  [body(): summed = lax.all_to_all(crossed, ('chan', 'seg'), 0, 0, tiled=True)]
    ppermute x3, waiting for transfers between devices: 5.16 us -> 0.01 us  [body(): lags[r] = lax.ppermute(lags[r], 'seg', route)]
    all_to_all x1 -> x0, starting transfers between devices: 2.58 us -> none  [body(): summed = lax.all_to_all(crossed, ('chan', 'seg'), 0, 0, tiled=True)]
    all_to_all x1, waiting for transfers between devices: 7.55 us -> 5.62 us  [body(): moved = lax.all_to_all(spread, ('chan', 'seg'), 0, 0, tiled=True)]
    all_to_all x1 -> x0, waiting for transfers between devices: 1 us -> none  [body(): summed = lax.all_to_all(crossed, ('chan', 'seg'), 0, 0, tiled=True)]
    pallas_call x2 -> x1, Pallas kernels: 1.78 us -> 1.01 us  [body(): pl.pallas_call(functools.partial(last_kernel, slots), out_shape=[near_sha...]
    pallas_call x1, Pallas kernels: 1.96 us -> 1.27 us  [body(): pl.pallas_call(loop_kernel, out_shape=jax.ShapeDtypeStruct((chan_count, s...]
  transfers between devices with their start and end apart: 8 -> 7, of which waited for: 5 -> 2; matrix products, arithmetic and copies ran while one was open for 0% -> 0% of each run, Pallas kernels for 11% -> 13%
where the time goes in v14:
time: 42.4 us; the launch traced here: 42 us
  starting transfers between devices  14.5 us (34%)
  blocking collectives  11.1 us (26%)
  Pallas kernels  8.9 us (21%)
  waiting for transfers between devices  6.54 us (15%)
  between operations  0.89 us (2%)
    all_to_all x1, blocking collectives, body(): summed = lax.all_to_all(crossed, ('chan', 'seg'), 0, 0, tiled=True)  11.1 us
    all_to_all x1, waiting for transfers between devices, body(): moved = lax.all_to_all(spread, ('chan', 'seg'), 0, 0, tiled=True)  5.62 us
    all_to_all x1, starting transfers between devices, body(): moved = lax.all_to_all(spread, ('chan', 'seg'), 0, 0, tiled=True)  4.72 us
    ppermute x1, starting transfers between devices, body(): after = lax.ppermute(down, 'chan', [(j, i) for i, j in ring])  3.04 us
    ppermute x1, starting transfers between devices, body(): rim = lax.ppermute(rim, 'seg', route)  2.49 us
    ppermute x1, starting transfers between devices, body(): before = lax.ppermute(up, 'chan', ring)  2.35 us
    pallas_call x1, Pallas kernels, body(): pl.pallas_call(near_kernel, out_shape=[jax.ShapeDtypeStruct((near_each, L...  2.06 us
    pallas_call x1, Pallas kernels, body(): pl.pallas_call(spectrum_kernel, out_shape=[jax.ShapeDtypeStruct((2 * BINS...  1.98 us
  transfers between devices with their start and end apart: 7, of which 2 were waited for; matrix products, arithmetic and copies ran while one was open for 0% of the time, Pallas kernels for 13%

profile of v14, /device:TPU:0, one launch (start us, length us, event | category | flops | bytes accessed | tf_op | source)
XLA Modules:
  0.0 42.0 jit_solution(6661409250259829861)
XLA Ops:
  0.6 0.0 copy-start.12
  0.6 0.0 copy-start.13
  0.7 0.0 copy-start.8
  0.7 0.0 copy-start.9
  0.7 1.1 %history.1 = f32[64,128]{1,0:T(8,128)S(1)} custom-call(f32[128,4096]{1,0:T(8,128)} %rec_hbm.1), custom_call_target="tpu_custom_call" | custom-call | flops 10000000000 | bytes 20000000 | tf_op jit(solution)/shard_map/history/pallas_call | solution.py:368
  1.8 0.0 copy-start.1
  1.8 0.0 copy-start.3
  1.8 0.0 copy-start.4
  1.8 2.5 %collective-permute-start = (f32[64,128]{1,0:T(8,128)S(1)}, f32[64,128]{1,0:T(8,128)S(1)}, u32[]{:S(2)}, u32[]{:S(2)}) collective-permute-start(f32[64,128]{1,0:T(8,128)S(1)} %history.1), channel_id=1, source_target_pairs={{0,1},{1,2},{2,3},{4,5},{5,6},{6,7},{8,9},{9,10},{10,11},{12,13},{... | collective-permute-start | bytes 98312 | tf_op jit(solution)/shard_map/ppermute | solution.py:380
  4.3 0.0 copy-done.12
  4.3 0.0 copy-done.13
  4.3 0.0 copy-done.8
  4.3 0.0 copy-done.9
  4.3 0.0 copy-start.10
  4.3 0.0 copy-start.11
  4.4 2.0 %filter_and_transform.1 = (f32[1024,128]{1,0:T(8,128)S(1)}, f32[128,128]{1,0:T(8,128)S(1)}, f32[16,128]{1,0:T(8,128)S(1)}) custom-call(f32[1,64]{1,0:T(1,128)S(1)} %bitcast.8, f32[128,4096]{1,0:T(8,128)S(1)} %copy-done.8, bf16[256,768]{1,0:T(8,128)(2,1)S(1)} %copy-done.12, f32[256,128]{1,0:T(8,128)S(1)} %copy-done.13), custom_call_target="tpu_custom_call" | custom-call | flops 1000000000 | bytes 5000000 | tf_op jit(solution)/shard_map/filter_and_transform/pallas_call | solution.py:382
  6.3 0.0 collective-permute-done.rim_ref
  6.4 0.0 copy-done.1
  6.4 0.0 copy-done.3
  6.4 0.0 copy-done.4
  6.4 1.5 %whiten.1 = (bf16[32,2,16,128]{3,2,1,0:T(8,128)(2,1)}, bf16[512,128]{1,0:T(8,128)(2,1)S(1)}, bf16[512,128]{1,0:T(8,128)(2,1)S(1)}) custom-call(f32[1024,128]{1,0:T(8,128)S(1)} %get-tuple-element.20.spec_ref, f32[64,128]{1,0:T(8,128)S(1)} %collective-permute-done.rim_ref, f32[128,128]{1,0:T(8,128)S(1)} %get-tuple-element.21.mean_ref, ...), custom_call_target="tpu_custom_call" | custom-call | tf_op jit(solution)/shard_map/whiten/pallas_call | solution.py:400
  7.9 2.3 %collective-permute-start.1 = (bf16[512,128]{1,0:T(8,128)(2,1)S(1)}, bf16[512,128]{1,0:T(8,128)(2,1)S(1)}, u32[]{:S(2)}, u32[]{:S(2)}) collective-permute-start(bf16[512,128]{1,0:T(8,128)(2,1)S(1)} %get-tuple-element.24), channel_id=1, source_target_pairs={{0,4},{4,8},{8,12},{12,16},{16,20},{20,24},{24,28},{28,0},{1,5},{5... | collective-permute-start | bytes 393224 | tf_op jit(solution)/shard_map/ppermute | solution.py:417
  10.2 3.0 %collective-permute-start.2 = (bf16[512,128]{1,0:T(8,128)(2,1)S(1)}, bf16[512,128]{1,0:T(8,128)(2,1)S(1)}, u32[]{:S(2)}, u32[]{:S(2)}) collective-permute-start(bf16[512,128]{1,0:T(8,128)(2,1)S(1)} %get-tuple-element.25), channel_id=1, source_target_pairs={{4,0},{8,4},{12,8},{16,12},{20,16},{24,20},{28,24},{0,28},{5,1},{9... | collective-permute-start | bytes 393224 | tf_op jit(solution)/shard_map/ppermute | solution.py:418
  13.3 4.7 %all-to-all-start = ((bf16[32,2,16,128]{3,2,1,0:T(8,128)(2,1)}), bf16[32,2,16,128]{3,2,1,0:T(8,128)(2,1)S(1)}, u32[]{:S(2)}, u32[]{:S(2)}) async-start(bf16[32,2,16,128]{3,2,1,0:T(8,128)(2,1)} %get-tuple-element.23.white_ref), calls=%async_computation | async-start | bytes 524288 | tf_op jit(solution)/shard_map/all_to_all | solution.py:413
  18.0 0.0 copy-start.2
  18.0 0.0 copy-start.5
  18.0 0.0 copy-start.6
  18.0 0.0 copy-start.7
  18.0 0.0 collective-permute-done.1.before_ref
  18.1 0.9 %collective-permute-done.2.after_ref = bf16[512,128]{1,0:T(8,128)(2,1)S(1)} collective-permute-done((bf16[512,128]{1,0:T(8,128)(2,1)S(1)}, bf16[512,128]{1,0:T(8,128)(2,1)S(1)}, u32[]{:S(2)}, u32[]{:S(2)}) %collective-permute-start.2) | collective-permute-done | bytes 131104 | tf_op jit(solution)/shard_map/ppermute | solution.py:418
  19.0 0.0 copy-done.10
  19.0 0.0 copy-done.11
  19.0 2.1 %near_lags.1 = (bf16[1,256,128]{2,1,0:T(8,128)(2,1)S(1)}, bf16[1,256,128]{2,1,0:T(8,128)(2,1)S(1)}, bf16[1,256,128]{2,1,0:T(8,128)(2,1)S(1)}, bf16[1,256,128]{2,1,0:T(8,128)(2,1)S(1)}) custom-call(s32[4]{0:T(128)S(1)} %copy-done.10, bf16[32,2,16,128]{3,2,1,0:T(8,128)(2,1)} %get-tuple-element.23.white_ref, ...), custom_call_target="tpu_custom_call" | custom-call | flops 20000000000 | bytes 20000000 | tf_op jit(solution)/shard_map/near_lags/pallas_call | solution.py:422
  21.0 0.0 copy-start
  21.0 0.4 collective-permute-start.3
  21.4 0.8 %collective-permute-start.4 = (bf16[1,256,128]{2,1,0:T(8,128)(2,1)S(1)}, bf16[1,256,128]{2,1,0:T(8,128)(2,1)S(1)}, u32[]{:S(2)}, u32[]{:S(2)}) collective-permute-start(bf16[1,256,128]{2,1,0:T(8,128)(2,1)S(1)} %get-tuple-element.29), channel_id=1, source_target_pairs={{0,2},{1,3},{2,0},{3,1},{4,6},{5,7},{6,4},{7,5},{8,10},{9,11},{10,... | collective-permute-start | bytes 196616 | tf_op jit(solution)/shard_map/ppermute | solution.py:437
  22.2 0.7 %collective-permute-start.5 = (bf16[1,256,128]{2,1,0:T(8,128)(2,1)S(1)}, bf16[1,256,128]{2,1,0:T(8,128)(2,1)S(1)}, u32[]{:S(2)}, u32[]{:S(2)}) collective-permute-start(bf16[1,256,128]{2,1,0:T(8,128)(2,1)S(1)} %get-tuple-element.30), channel_id=1, source_target_pairs={{0,3},{1,2},{2,1},{3,0},{4,7},{5,6},{6,5},{7,4},{8,11},{9,10},{10,... | collective-permute-start | bytes 196616 | tf_op jit(solution)/shard_map/ppermute | solution.py:437
  23.0 5.6 %all-to-all-done = bf16[32,2,16,128]{3,2,1,0:T(8,128)(2,1)S(1)} async-done(((bf16[32,2,16,128]{3,2,1,0:T(8,128)(2,1)}), bf16[32,2,16,128]{3,2,1,0:T(8,128)(2,1)S(1)}, u32[]{:S(2)}, u32[]{:S(2)}) %all-to-all-start) | async-done | bytes 262176 | tf_op jit(solution)/shard_map/all_to_all | solution.py:413
  28.6 0.0 copy-done.2
  28.6 0.0 copy-done.5
  28.6 0.0 copy-done.6
  28.6 0.0 copy-done.7
  28.6 1.3 %loop_spectra.1 = bf16[8,4,24,128]{3,2,1,0:T(8,128)(2,1)S(1)} custom-call(s32[3,8]{1,0:T(4,128)S(1)} %bitcast.7, s32[8]{0:T(128)S(1)} %copy-done.7, bf16[128,128]{1,0:T(8,128)(2,1)S(1)} %copy-done.5, bf16[512,512]{1,0:T(8,128)(2,1)S(1)} %copy-done.2, bf16[8,4,2,16,128]{4,3,2,1,0:T(8,128)(2,1)S(1)} %bitcast.5), custom_call_target="tpu_custom_call" | custom-call | tf_op jit(solution)/shard_map/loop_spectra/pallas_call | solution.py:458
  29.9 0.0 collective-permute-done.3.refs_1_
  29.9 0.0 collective-permute-done.4.refs_2_
  29.9 0.0 collective-permute-done.5.refs_3_
  29.9 11.1 %all_to_all.10.spec_ref = bf16[32,24,128]{2,1,0:T(8,128)(2,1)S(1)} all-to-all(bf16[32,24,128]{2,1,0:T(8,128)(2,1)S(1)} %bitcast.6), channel_id=1, replica_groups=mesh['chan'=8,'seg'=4] {'chan','seg'}, dimensions={0} | all-to-all | bytes 393216 | tf_op jit(solution)/shard_map/all_to_all | solution.py:469
  41.0 1.0 %lags.1 = (f32[128,1,256]{2,1,0:T(1,128)}, f32[96,256]{1,0:T(8,128)}) custom-call(bf16[32,24,128]{2,1,0:T(8,128)(2,1)S(1)} %all_to_all.10.spec_ref, bf16[1024,512]{1,0:T(8,128)(2,1)S(1)} %copy-done, bf16[1,256,128]{2,1,0:T(8,128)(2,1)S(1)} %get-tuple-element.32.refs_0_, bf16[1,256,128]{2,1,0:T(8,128)(2,1)S(1)} %collective-permute-done.3.refs_1_, ...), custom_call_target="tpu_custom_call" | custom-call | tf_op jit(solution)/shard_map/lags/pallas_call | solution.py:473
  (1 shorter events, 0.0 us)
Async XLA Ops:
  0.6 3.7 %copy-start.12 = (bf16[256,768]{1,0:T(8,128)(2,1)S(1)}, bf16[256,768]{1,0:T(8,128)(2,1)}, u32[]{:S(2)}) copy-start(bf16[256,768]{1,0:T(8,128)(2,1)} %constant.18.clone.tab_ref) | copy-start | bytes 1179652
  0.6 3.7 %copy-start.13 = (f32[256,128]{1,0:T(8,128)S(1)}, f32[256,128]{1,0:T(8,128)}, u32[]{:S(2)}) copy-start(f32[256,128]{1,0:T(8,128)} %constant.19.clone.twist_ref) | copy-start | bytes 393220
  0.7 3.7 %copy-start.8 = (f32[128,4096]{1,0:T(8,128)S(1)}, f32[128,4096]{1,0:T(8,128)}, u32[]{:S(2)}) copy-start(f32[128,4096]{1,0:T(8,128)} %rec_hbm.1) | copy-start | bytes 6291460
  0.7 3.7 %copy-start.9 = (f32[64]{0:T(128)S(1)}, f32[64]{0:T(128)}, u32[]{:S(2)}) copy-start(f32[64]{0:T(128)} %param.15) | copy-start | bytes 772
  1.8 4.6 %copy-start.1 = (bf16[512,512]{1,0:T(8,128)(2,1)S(1)}, bf16[512,512]{1,0:T(8,128)(2,1)}, u32[]{:S(2)}) copy-start(bf16[512,512]{1,0:T(8,128)(2,1)} %constant.21.clone.band_ref) | copy-start | bytes 1572868
  1.8 4.6 %copy-start.3 = (f32[512,128]{1,0:T(8,128)S(1)}, f32[512,128]{1,0:T(8,128)}, u32[]{:S(2)}) copy-start(f32[512,128]{1,0:T(8,128)} %constant.22.clone.share_ref) | copy-start | bytes 786436
  1.8 4.6 %copy-start.4 = (bf16[1024,128]{1,0:T(8,128)(2,1)S(1)}, bf16[1024,128]{1,0:T(8,128)(2,1)}, u32[]{:S(2)}) copy-start(bf16[1024,128]{1,0:T(8,128)(2,1)} %constant.20.clone.edge_ref) | copy-start | bytes 786436
  1.8 4.6 %collective-permute-start = (f32[64,128]{1,0:T(8,128)S(1)}, f32[64,128]{1,0:T(8,128)S(1)}, u32[]{:S(2)}, u32[]{:S(2)}) collective-permute-start(f32[64,128]{1,0:T(8,128)S(1)} %history.1), channel_id=1, source_target_pairs={{0,1},{1,2},{2,3},{4,5},{5,6},{6,7},{8,9},{9,10},{10,11},{12,13},{... | collective-permute-start | bytes 98312 | tf_op jit(solution)/shard_map/ppermute | solution.py:380
  4.3 14.6 %copy-start.10 = (s32[4]{0:T(128)S(1)}, s32[4]{0:T(128)}, u32[]{:S(2)}) copy-start(s32[4]{0:T(128)} %offs_ref.1) | copy-start | bytes 52
  4.3 14.6 %copy-start.11 = (bf16[512,1024]{1,0:T(8,128)(2,1)S(1)}, bf16[512,1024]{1,0:T(8,128)(2,1)}, u32[]{:S(2)}) copy-start(bf16[512,1024]{1,0:T(8,128)(2,1)} %constant.23.clone.inv_ref) | copy-start | bytes 3145732
  7.9 10.2 %collective-permute-start.1 = (bf16[512,128]{1,0:T(8,128)(2,1)S(1)}, bf16[512,128]{1,0:T(8,128)(2,1)S(1)}, u32[]{:S(2)}, u32[]{:S(2)}) collective-permute-start(bf16[512,128]{1,0:T(8,128)(2,1)S(1)} %get-tuple-element.24), channel_id=1, source_target_pairs={{0,4},{4,8},{8,12},{12,16},{16,20},{20,24},{24,28},{28,0},{1,5},{5... | collective-permute-start | bytes 393224 | tf_op jit(solution)/shard_map/ppermute | solution.py:417
  10.2 8.7 %collective-permute-start.2 = (bf16[512,128]{1,0:T(8,128)(2,1)S(1)}, bf16[512,128]{1,0:T(8,128)(2,1)S(1)}, u32[]{:S(2)}, u32[]{:S(2)}) collective-permute-start(bf16[512,128]{1,0:T(8,128)(2,1)S(1)} %get-tuple-element.25), channel_id=1, source_target_pairs={{4,0},{8,4},{12,8},{16,12},{20,16},{24,20},{28,24},{0,28},{5,1},{9... | collective-permute-start | bytes 393224 | tf_op jit(solution)/shard_map/ppermute | solution.py:418
  13.3 15.3 %all-to-all-start = ((bf16[32,2,16,128]{3,2,1,0:T(8,128)(2,1)}), bf16[32,2,16,128]{3,2,1,0:T(8,128)(2,1)S(1)}, u32[]{:S(2)}, u32[]{:S(2)}) async-start(bf16[32,2,16,128]{3,2,1,0:T(8,128)(2,1)} %get-tuple-element.23.white_ref), calls=%async_computation | async-start | bytes 524288 | tf_op jit(solution)/shard_map/all_to_all | solution.py:413
  18.0 10.6 %copy-start.2 = (bf16[512,512]{1,0:T(8,128)(2,1)S(1)}, bf16[512,512]{1,0:T(8,128)(2,1)}, u32[]{:S(2)}) copy-start(bf16[512,512]{1,0:T(8,128)(2,1)} %constant.25.clone.pack_ref) | copy-start | bytes 1572868
  18.0 10.6 %copy-start.5 = (bf16[128,128]{1,0:T(8,128)(2,1)S(1)}, bf16[128,128]{1,0:T(8,128)(2,1)}, u32[]{:S(2)}) copy-start(bf16[128,128]{1,0:T(8,128)(2,1)} %constant.24.clone.flip_ref) | copy-start | bytes 98308
  18.0 10.6 %copy-start.6 = (s32[8,3]{0,1:T(4,128)S(1)}, s32[8,3]{0,1:T(4,128)}, u32[]{:S(2)}) copy-start(s32[8,3]{0,1:T(4,128)} %param.17) | copy-start | bytes 292
  18.0 10.6 %copy-start.7 = (s32[8]{0:T(128)S(1)}, s32[8]{0:T(128)}, u32[]{:S(2)}) copy-start(s32[8]{0:T(128)} %count_ref.1) | copy-start | bytes 100
  21.0 20.0 %copy-start = (bf16[1024,512]{1,0:T(8,128)(2,1)S(1)}, bf16[1024,512]{1,0:T(8,128)(2,1)}, u32[]{:S(2)}) copy-start(bf16[1024,512]{1,0:T(8,128)(2,1)} %constant.26.clone.inv_ref) | copy-start | bytes 3145732
  21.0 8.8 %collective-permute-start.3 = (bf16[1,256,128]{2,1,0:T(8,128)(2,1)S(1)}, bf16[1,256,128]{2,1,0:T(8,128)(2,1)S(1)}, u32[]{:S(2)}, u32[]{:S(2)}) collective-permute-start(bf16[1,256,128]{2,1,0:T(8,128)(2,1)S(1)} %get-tuple-element.28), channel_id=1, source_target_pairs={{0,1},{1,0},{2,3},{3,2},{4,5},{5,4},{6,7},{7,6},{8,9},{9,8},{10,11... | collective-permute-start | bytes 196616 | tf_op jit(solution)/shard_map/ppermute | solution.py:437
  21.4 8.5 %collective-permute-start.4 = (bf16[1,256,128]{2,1,0:T(8,128)(2,1)S(1)}, bf16[1,256,128]{2,1,0:T(8,128)(2,1)S(1)}, u32[]{:S(2)}, u32[]{:S(2)}) collective-permute-start(bf16[1,256,128]{2,1,0:T(8,128)(2,1)S(1)} %get-tuple-element.29), channel_id=1, source_target_pairs={{0,2},{1,3},{2,0},{3,1},{4,6},{5,7},{6,4},{7,5},{8,10},{9,11},{10,... | collective-permute-start | bytes 196616 | tf_op jit(solution)/shard_map/ppermute | solution.py:437
  22.2 7.7 %collective-permute-start.5 = (bf16[1,256,128]{2,1,0:T(8,128)(2,1)S(1)}, bf16[1,256,128]{2,1,0:T(8,128)(2,1)S(1)}, u32[]{:S(2)}, u32[]{:S(2)}) collective-permute-start(bf16[1,256,128]{2,1,0:T(8,128)(2,1)S(1)} %get-tuple-element.30), channel_id=1, source_target_pairs={{0,3},{1,2},{2,1},{3,0},{4,7},{5,6},{6,5},{7,4},{8,11},{9,10},{10,... | collective-permute-start | bytes 196616 | tf_op jit(solution)/shard_map/ppermute | solution.py:437

commit v15 on v14

--- a/solution.py
+++ b/solution.py
@@ -94,15 +94,21 @@
 
 
 def tap_rows(taps):
-    width = LANES + STEP
+    width, period = 2 * LANES, LANES // DECIM
     square = (TAPS, TAPS)
     diagonal = lax.broadcasted_iota(jnp.int32, square, 0) == lax.broadcasted_iota(jnp.int32, square, 1)
     column_taps = jnp.sum(jnp.where(diagonal, taps, 0.0), axis=1, keepdims=True)
     tap = lax.broadcasted_iota(jnp.int32, (TAPS, width), 0)
     column = lax.broadcasted_iota(jnp.int32, (TAPS, width), 1)
     placed = jnp.where(column == LANES + DECIM - 1 - tap, column_taps, 0.0)
-    spread = jnp.broadcast_to(jnp.sum(placed, axis=0, keepdims=True), (OUT_BLOCK, width))
-    return pltpu.roll(spread, 0, 1, stride=DECIM, stride_axis=0)
+    spread = jnp.broadcast_to(jnp.sum(placed, axis=0, keepdims=True), (period, width))
+    piece = pltpu.roll(spread, 0, 1, stride=DECIM, stride_axis=0)
+    rows = []
+    for t in range(OUT_BLOCK // period):
+        left = jnp.zeros((period, t * LANES), F32)
+        right = jnp.zeros((period, STEP - LANES - t * LANES), F32)
+        rows.append(jnp.concatenate([p for p in (left, piece, right) if p.shape[1]], axis=1))
+    return jnp.concatenate(rows, axis=0)
 
 
 def rim_kernel(rec_hbm, rim_ref, tail_ref, sem):
@@ -110,9 +116,7 @@
     copy = pltpu.make_async_copy(rec_hbm.at[:, pl.ds(length - LANES, LANES)], tail_ref, sem)
     copy.start()
     copy.wait()
-    upper, lower = tail_ref[: LANES // 2], tail_ref[LANES // 2 :]
-    lane = lax.broadcasted_iota(jnp.int32, lower.shape, 1)
-    rim_ref[...] = jnp.where(lane < TAPS, pltpu.roll(upper, LANES - TAPS, 1), lower)
+    rim_ref[...] = tail_ref[...].T[LANES - TAPS :]
 
 
 def spectrum_kernel(taps_ref, rec_ref, tab_ref, twist_ref, spec_ref, mean_ref, head_ref):
@@ -137,7 +141,7 @@
         total = wide[:, :LANES] + wide[:, LANES:] + rest
         outputs += [total[t * LANES : (t + 1) * LANES].T for t in range(blocks // 2)]
     pieces = [jnp.concatenate(outputs[j : j + 2], axis=0) for j in range(0, blocks, 2)]
-    mean_ref[...] = jnp.broadcast_to(mean, mean_ref.shape)
+    mean_ref[...] = jnp.broadcast_to(mean, (LANES, LANES)).T[: mean_ref.shape[0]]
     even, odd = pieces[0] + pieces[2], pieces[1] + pieces[3]
     a, b = pieces[0] - pieces[2], pieces[1] - pieces[3]
     whole, half = even + odd, even - odd
@@ -182,12 +186,11 @@
     up_ref,
     down_ref,
 ):
-    head_high, head_low = split(head_ref[...])
-    rim = jnp.concatenate([pltpu.roll(rim_ref[...], LANES - TAPS, 1), rim_ref[...]], axis=0)
-    rim_high, rim_low = split(rim - mean_ref[...])
-    history = mm_nt(
+    head_high, head_low = split(head_ref[:, LANES - TAPS :])
+    rim_high, rim_low = split(rim_ref[...] - mean_ref[0:1, :])
+    history = mm(
         jnp.concatenate([head_high, head_high, head_low], axis=1),
-        jnp.concatenate([rim_high, rim_low, rim_high], axis=1),
+        jnp.concatenate([rim_high, rim_low, rim_high], axis=0),
     )
     high, low = split(history)
     stacked = jnp.concatenate([high, low, high], axis=0)
@@ -223,6 +226,7 @@
     for group in range(owners):
         for owner in range(owners):
             matrix[group, owner, :, owner, group, :] = np.eye(share)
+    matrix = matrix.reshape(owners, LANES, owners * LANES)[:, ::-1]
     return matrix.reshape(owners * LANES, owners * LANES).astype(jnp.bfloat16)
 
 
@@ -268,21 +272,20 @@
         near_ref[:, t, :] = total[t].T
 
 
-def loop_kernel(partner_ref, count_ref, flip_ref, pack_ref, white_ref, out_ref, turned_ref):
+def loop_kernel(partner_ref, count_ref, flip_ref, pack_ref, white_ref, out_ref):
     blocks, segs, _, bins, _ = white_ref.shape
     owners = out_ref.shape[1]
     slots = partner_ref.shape[0]
     rows = segs * 2 * bins
     packed_rows = 2 * bins // owners
-    flats = [white_ref[b].reshape(rows, LANES) for b in range(blocks)]
-    turned_ref[...] = mm(jnp.concatenate(flats, axis=0), flip_ref[...]).reshape(turned_ref.shape)
+    turned = mm(white_ref[...].reshape(blocks * rows, LANES), flip_ref[...])
     loops = []
     for b in range(blocks):
-        own = flats[b].astype(F32).reshape(segs, 2, bins, LANES)
+        own = turned[b * rows : (b + 1) * rows].reshape(segs, 2, bins, LANES)
         for k in range(slots):
             partner = jnp.clip(partner_ref[k, b], 0, blocks - 1)
             live = (k < count_ref[b]).astype(F32)
-            far = turned_ref[partner].reshape(segs, 2, bins, LANES)
+            far = white_ref[partner].astype(F32)
             real = jnp.sum(own[:, 0] * far[:, 0] + own[:, 1] * far[:, 1], axis=0)
             imag = jnp.sum(own[:, 1] * far[:, 0] - own[:, 0] * far[:, 1], axis=0)
             pair = jnp.concatenate([real, imag], axis=0) * live
@@ -367,7 +370,7 @@
     route = [(i, i + 1) for i in range(seg_count - 1)]
     rim = pl.pallas_call(
         rim_kernel,
-        out_shape=jax.ShapeDtypeStruct((chans // 2, LANES), F32),
+        out_shape=jax.ShapeDtypeStruct((TAPS, chans), F32),
         in_specs=hbm(1),
         out_specs=pl.BlockSpec(memory_space=pltpu.VMEM),
         scratch_shapes=[pltpu.VMEM((chans, LANES), F32), pltpu.SemaphoreType.DMA],
@@ -383,7 +386,7 @@
         spectrum_kernel,
         out_shape=[
             jax.ShapeDtypeStruct((2 * BINS, LANES), F32),
-            jax.ShapeDtypeStruct((LANES, LANES), F32),
+            jax.ShapeDtypeStruct((8, LANES), F32),
             jax.ShapeDtypeStruct((GROUP, LANES), F32),
         ],
         in_specs=vmem(4),
@@ -460,7 +463,6 @@
         out_shape=jax.ShapeDtypeStruct((chan_count, seg_count, out_rows, LANES), BF16),
         in_specs=smem(2) + vmem(3),
         out_specs=pl.BlockSpec(memory_space=pltpu.VMEM),
-        scratch_shapes=[pltpu.VMEM((chan_count, seg_count * 2 * bins, LANES), F32)],
         compiler_params=PARAMS,
         name="loop_spectra",
     )(loop_partner.T, loop_count, flip, pack_matrix(seg_count), moved)

time: 42.4 us -> 42.3 us (level)
  transfers between devices with their start and end apart: 7 -> 7, of which waited for: 2 -> 2; matrix products, arithmetic and copies ran while one was open for 0% -> 0% of each run, Pallas kernels for 13% -> 12%
where the time goes in v15:
time: 42.3 us; the launch traced here: 41.9 us
  starting transfers between devices  14.5 us (34%)
  blocking collectives  11.1 us (26%)
  Pallas kernels  8.78 us (21%)
  waiting for transfers between devices  6.53 us (15%)
  between operations  0.89 us (2%)
    all_to_all x1, blocking collectives, body(): summed = lax.all_to_all(crossed, ('chan', 'seg'), 0, 0, tiled=True)  11.1 us
    all_to_all x1, waiting for transfers between devices, body(): moved = lax.all_to_all(spread, ('chan', 'seg'), 0, 0, tiled=True)  5.64 us
    all_to_all x1, starting transfers between devices, body(): moved = lax.all_to_all(spread, ('chan', 'seg'), 0, 0, tiled=True)  4.73 us
    ppermute x1, starting transfers between devices, body(): after = lax.ppermute(down, 'chan', [(j, i) for i, j in ring])  3.04 us
    ppermute x1, starting transfers between devices, body(): rim = lax.ppermute(rim, 'seg', route)  2.49 us
    ppermute x1, starting transfers between devices, body(): before = lax.ppermute(up, 'chan', ring)  2.35 us
    pallas_call x1, Pallas kernels, body(): pl.pallas_call(near_kernel, out_shape=[jax.ShapeDtypeStruct((near_each, L...  2.07 us
    pallas_call x1, Pallas kernels, body(): pl.pallas_call(spectrum_kernel, out_shape=[jax.ShapeDtypeStruct((2 * BINS...  1.96 us
  transfers between devices with their start and end apart: 7, of which 2 were waited for; matrix products, arithmetic and copies ran while one was open for 0% of the time, Pallas kernels for 12%

profile of v15, /device:TPU:0, one launch (start us, length us, event | category | flops | bytes accessed | tf_op | source)
XLA Modules:
  0.0 41.9 jit_solution(1940702453439802918)
XLA Ops:
  0.6 0.0 copy-start.12
  0.6 0.0 copy-start.13
  0.7 0.0 copy-start.8
  0.7 0.0 copy-start.9
  0.7 1.1 %history.1 = f32[64,128]{1,0:T(8,128)S(1)} custom-call(f32[128,4096]{1,0:T(8,128)} %rec_hbm.1), custom_call_target="tpu_custom_call" | custom-call | flops 10000000000 | bytes 20000000 | tf_op jit(solution)/shard_map/history/pallas_call | solution.py:371
  1.8 0.0 copy-start.1
  1.8 0.0 copy-start.3
  1.8 0.0 copy-start.4
  1.8 2.5 %collective-permute-start = (f32[64,128]{1,0:T(8,128)S(1)}, f32[64,128]{1,0:T(8,128)S(1)}, u32[]{:S(2)}, u32[]{:S(2)}) collective-permute-start(f32[64,128]{1,0:T(8,128)S(1)} %history.1), channel_id=1, source_target_pairs={{0,1},{1,2},{2,3},{4,5},{5,6},{6,7},{8,9},{9,10},{10,11},{12,13},{... | collective-permute-start | bytes 98312 | tf_op jit(solution)/shard_map/ppermute | solution.py:383
  4.3 0.0 copy-done.12
  4.3 0.0 copy-done.13
  4.3 0.0 copy-done.8
  4.3 0.0 copy-done.9
  4.4 0.0 copy-start.10
  4.4 0.0 copy-start.11
  4.4 2.0 %filter_and_transform.1 = (f32[1024,128]{1,0:T(8,128)S(1)}, f32[8,128]{1,0:T(8,128)S(1)}, f32[16,128]{1,0:T(8,128)S(1)}) custom-call(f32[1,64]{1,0:T(1,128)S(1)} %bitcast.8, f32[128,4096]{1,0:T(8,128)S(1)} %copy-done.8, bf16[256,768]{1,0:T(8,128)(2,1)S(1)} %copy-done.12, f32[256,128]{1,0:T(8,128)S(1)} %copy-done.13), custom_call_target="tpu_custom_call" | custom-call | flops 1000000000 | bytes 5000000 | tf_op jit(solution)/shard_map/filter_and_transform/pallas_call | solution.py:385
  6.3 0.0 collective-permute-done.rim_ref
  6.4 0.0 copy-done.1
  6.4 0.0 copy-done.3
  6.4 0.0 copy-done.4
  6.4 1.4 %whiten.1 = (bf16[32,2,16,128]{3,2,1,0:T(8,128)(2,1)}, bf16[512,128]{1,0:T(8,128)(2,1)S(1)}, bf16[512,128]{1,0:T(8,128)(2,1)S(1)}) custom-call(f32[1024,128]{1,0:T(8,128)S(1)} %get-tuple-element.20.spec_ref, f32[64,128]{1,0:T(8,128)S(1)} %collective-permute-done.rim_ref, f32[8,128]{1,0:T(8,128)S(1)} %get-tuple-element.21.mean_ref, ...), custom_call_target="tpu_custom_call" | custom-call | tf_op jit(solution)/shard_map/whiten/pallas_call | solution.py:403
  7.8 2.4 %collective-permute-start.1 = (bf16[512,128]{1,0:T(8,128)(2,1)S(1)}, bf16[512,128]{1,0:T(8,128)(2,1)S(1)}, u32[]{:S(2)}, u32[]{:S(2)}) collective-permute-start(bf16[512,128]{1,0:T(8,128)(2,1)S(1)} %get-tuple-element.24), channel_id=1, source_target_pairs={{0,4},{4,8},{8,12},{12,16},{16,20},{20,24},{24,28},{28,0},{1,5},{5... | collective-permute-start | bytes 393224 | tf_op jit(solution)/shard_map/ppermute | solution.py:420
  10.2 3.0 %collective-permute-start.2 = (bf16[512,128]{1,0:T(8,128)(2,1)S(1)}, bf16[512,128]{1,0:T(8,128)(2,1)S(1)}, u32[]{:S(2)}, u32[]{:S(2)}) collective-permute-start(bf16[512,128]{1,0:T(8,128)(2,1)S(1)} %get-tuple-element.25), channel_id=1, source_target_pairs={{4,0},{8,4},{12,8},{16,12},{20,16},{24,20},{28,24},{0,28},{5,1},{9... | collective-permute-start | bytes 393224 | tf_op jit(solution)/shard_map/ppermute | solution.py:421
  13.2 4.7 %all-to-all-start = ((bf16[32,2,16,128]{3,2,1,0:T(8,128)(2,1)}), bf16[32,2,16,128]{3,2,1,0:T(8,128)(2,1)S(1)}, u32[]{:S(2)}, u32[]{:S(2)}) async-start(bf16[32,2,16,128]{3,2,1,0:T(8,128)(2,1)} %get-tuple-element.23.white_ref), calls=%async_computation | async-start | bytes 524288 | tf_op jit(solution)/shard_map/all_to_all | solution.py:416
  18.0 0.0 copy-start.2
  18.0 0.0 copy-start.5
  18.0 0.0 copy-start.6
  18.0 0.0 copy-start.7
  18.0 0.0 collective-permute-done.1.before_ref
  18.0 0.9 %collective-permute-done.2.after_ref = bf16[512,128]{1,0:T(8,128)(2,1)S(1)} collective-permute-done((bf16[512,128]{1,0:T(8,128)(2,1)S(1)}, bf16[512,128]{1,0:T(8,128)(2,1)S(1)}, u32[]{:S(2)}, u32[]{:S(2)}) %collective-permute-start.2) | collective-permute-done | bytes 131104 | tf_op jit(solution)/shard_map/ppermute | solution.py:421
  18.9 0.0 copy-done.10
  18.9 0.0 copy-done.11
  18.9 2.1 %near_lags.1 = (bf16[1,256,128]{2,1,0:T(8,128)(2,1)S(1)}, bf16[1,256,128]{2,1,0:T(8,128)(2,1)S(1)}, bf16[1,256,128]{2,1,0:T(8,128)(2,1)S(1)}, bf16[1,256,128]{2,1,0:T(8,128)(2,1)S(1)}) custom-call(s32[4]{0:T(128)S(1)} %copy-done.10, bf16[32,2,16,128]{3,2,1,0:T(8,128)(2,1)} %get-tuple-element.23.white_ref, ...), custom_call_target="tpu_custom_call" | custom-call | flops 20000000000 | bytes 20000000 | tf_op jit(solution)/shard_map/near_lags/pallas_call | solution.py:425
  21.0 0.0 copy-start
  21.0 0.4 collective-permute-start.3
  21.3 0.8 %collective-permute-start.4 = (bf16[1,256,128]{2,1,0:T(8,128)(2,1)S(1)}, bf16[1,256,128]{2,1,0:T(8,128)(2,1)S(1)}, u32[]{:S(2)}, u32[]{:S(2)}) collective-permute-start(bf16[1,256,128]{2,1,0:T(8,128)(2,1)S(1)} %get-tuple-element.29), channel_id=1, source_target_pairs={{0,2},{1,3},{2,0},{3,1},{4,6},{5,7},{6,4},{7,5},{8,10},{9,11},{10,... | collective-permute-start | bytes 196616 | tf_op jit(solution)/shard_map/ppermute | solution.py:440
  22.2 0.7 %collective-permute-start.5 = (bf16[1,256,128]{2,1,0:T(8,128)(2,1)S(1)}, bf16[1,256,128]{2,1,0:T(8,128)(2,1)S(1)}, u32[]{:S(2)}, u32[]{:S(2)}) collective-permute-start(bf16[1,256,128]{2,1,0:T(8,128)(2,1)S(1)} %get-tuple-element.30), channel_id=1, source_target_pairs={{0,3},{1,2},{2,1},{3,0},{4,7},{5,6},{6,5},{7,4},{8,11},{9,10},{10,... | collective-permute-start | bytes 196616 | tf_op jit(solution)/shard_map/ppermute | solution.py:440
  22.9 5.6 %all-to-all-done = bf16[32,2,16,128]{3,2,1,0:T(8,128)(2,1)S(1)} async-done(((bf16[32,2,16,128]{3,2,1,0:T(8,128)(2,1)}), bf16[32,2,16,128]{3,2,1,0:T(8,128)(2,1)S(1)}, u32[]{:S(2)}, u32[]{:S(2)}) %all-to-all-start) | async-done | bytes 262176 | tf_op jit(solution)/shard_map/all_to_all | solution.py:416
  28.6 0.0 copy-done.2
  28.6 0.0 copy-done.5
  28.6 0.0 copy-done.6
  28.6 0.0 copy-done.7
  28.6 1.2 %loop_spectra.1 = bf16[8,4,24,128]{3,2,1,0:T(8,128)(2,1)S(1)} custom-call(s32[3,8]{1,0:T(4,128)S(1)} %bitcast.7, s32[8]{0:T(128)S(1)} %copy-done.7, bf16[128,128]{1,0:T(8,128)(2,1)S(1)} %copy-done.5, bf16[512,512]{1,0:T(8,128)(2,1)S(1)} %copy-done.2, bf16[8,4,2,16,128]{4,3,2,1,0:T(8,128)(2,1)S(1)} %bitcast.5), custom_call_target="tpu_custom_call" | custom-call | tf_op jit(solution)/shard_map/loop_spectra/pallas_call | solution.py:461
  29.8 0.0 collective-permute-done.3.refs_1_
  29.8 0.0 collective-permute-done.4.refs_2_
  29.8 0.0 collective-permute-done.5.refs_3_
  29.8 11.1 %all_to_all.10.spec_ref = bf16[32,24,128]{2,1,0:T(8,128)(2,1)S(1)} all-to-all(bf16[32,24,128]{2,1,0:T(8,128)(2,1)S(1)} %bitcast.6), channel_id=1, replica_groups=mesh['chan'=8,'seg'=4] {'chan','seg'}, dimensions={0} | all-to-all | bytes 393216 | tf_op jit(solution)/shard_map/all_to_all | solution.py:471
  40.9 1.0 %lags.1 = (f32[128,1,256]{2,1,0:T(1,128)}, f32[96,256]{1,0:T(8,128)}) custom-call(bf16[32,24,128]{2,1,0:T(8,128)(2,1)S(1)} %all_to_all.10.spec_ref, bf16[1024,512]{1,0:T(8,128)(2,1)S(1)} %copy-done, bf16[1,256,128]{2,1,0:T(8,128)(2,1)S(1)} %get-tuple-element.32.refs_0_, bf16[1,256,128]{2,1,0:T(8,128)(2,1)S(1)} %collective-permute-done.3.refs_1_, ...), custom_call_target="tpu_custom_call" | custom-call | tf_op jit(solution)/shard_map/lags/pallas_call | solution.py:475
  (1 shorter events, 0.0 us)
Async XLA Ops:
  0.6 3.7 %copy-start.12 = (bf16[256,768]{1,0:T(8,128)(2,1)S(1)}, bf16[256,768]{1,0:T(8,128)(2,1)}, u32[]{:S(2)}) copy-start(bf16[256,768]{1,0:T(8,128)(2,1)} %constant.18.clone.tab_ref) | copy-start | bytes 1179652
  0.6 3.7 %copy-start.13 = (f32[256,128]{1,0:T(8,128)S(1)}, f32[256,128]{1,0:T(8,128)}, u32[]{:S(2)}) copy-start(f32[256,128]{1,0:T(8,128)} %constant.19.clone.twist_ref) | copy-start | bytes 393220
  0.7 3.7 %copy-start.8 = (f32[128,4096]{1,0:T(8,128)S(1)}, f32[128,4096]{1,0:T(8,128)}, u32[]{:S(2)}) copy-start(f32[128,4096]{1,0:T(8,128)} %rec_hbm.1) | copy-start | bytes 6291460
  0.7 3.7 %copy-start.9 = (f32[64]{0:T(128)S(1)}, f32[64]{0:T(128)}, u32[]{:S(2)}) copy-start(f32[64]{0:T(128)} %param.15) | copy-start | bytes 772
  1.8 4.6 %copy-start.1 = (bf16[512,512]{1,0:T(8,128)(2,1)S(1)}, bf16[512,512]{1,0:T(8,128)(2,1)}, u32[]{:S(2)}) copy-start(bf16[512,512]{1,0:T(8,128)(2,1)} %constant.21.clone.band_ref) | copy-start | bytes 1572868
  1.8 4.6 %copy-start.3 = (f32[512,128]{1,0:T(8,128)S(1)}, f32[512,128]{1,0:T(8,128)}, u32[]{:S(2)}) copy-start(f32[512,128]{1,0:T(8,128)} %constant.22.clone.share_ref) | copy-start | bytes 786436
  1.8 4.6 %copy-start.4 = (bf16[1024,128]{1,0:T(8,128)(2,1)S(1)}, bf16[1024,128]{1,0:T(8,128)(2,1)}, u32[]{:S(2)}) copy-start(bf16[1024,128]{1,0:T(8,128)(2,1)} %constant.20.clone.edge_ref) | copy-start | bytes 786436
  1.8 4.5 %collective-permute-start = (f32[64,128]{1,0:T(8,128)S(1)}, f32[64,128]{1,0:T(8,128)S(1)}, u32[]{:S(2)}, u32[]{:S(2)}) collective-permute-start(f32[64,128]{1,0:T(8,128)S(1)} %history.1), channel_id=1, source_target_pairs={{0,1},{1,2},{2,3},{4,5},{5,6},{6,7},{8,9},{9,10},{10,11},{12,13},{... | collective-permute-start | bytes 98312 | tf_op jit(solution)/shard_map/ppermute | solution.py:383
  4.4 14.5 %copy-start.10 = (s32[4]{0:T(128)S(1)}, s32[4]{0:T(128)}, u32[]{:S(2)}) copy-start(s32[4]{0:T(128)} %offs_ref.1) | copy-start | bytes 52
  4.4 14.5 %copy-start.11 = (bf16[512,1024]{1,0:T(8,128)(2,1)S(1)}, bf16[512,1024]{1,0:T(8,128)(2,1)}, u32[]{:S(2)}) copy-start(bf16[512,1024]{1,0:T(8,128)(2,1)} %constant.23.clone.inv_ref) | copy-start | bytes 3145732
  7.8 10.2 %collective-permute-start.1 = (bf16[512,128]{1,0:T(8,128)(2,1)S(1)}, bf16[512,128]{1,0:T(8,128)(2,1)S(1)}, u32[]{:S(2)}, u32[]{:S(2)}) collective-permute-start(bf16[512,128]{1,0:T(8,128)(2,1)S(1)} %get-tuple-element.24), channel_id=1, source_target_pairs={{0,4},{4,8},{8,12},{12,16},{16,20},{20,24},{24,28},{28,0},{1,5},{5... | collective-permute-start | bytes 393224 | tf_op jit(solution)/shard_map/ppermute | solution.py:420
  10.2 8.7 %collective-permute-start.2 = (bf16[512,128]{1,0:T(8,128)(2,1)S(1)}, bf16[512,128]{1,0:T(8,128)(2,1)S(1)}, u32[]{:S(2)}, u32[]{:S(2)}) collective-permute-start(bf16[512,128]{1,0:T(8,128)(2,1)S(1)} %get-tuple-element.25), channel_id=1, source_target_pairs={{4,0},{8,4},{12,8},{16,12},{20,16},{24,20},{28,24},{0,28},{5,1},{9... | collective-permute-start | bytes 393224 | tf_op jit(solution)/shard_map/ppermute | solution.py:421
  13.2 15.3 %all-to-all-start = ((bf16[32,2,16,128]{3,2,1,0:T(8,128)(2,1)}), bf16[32,2,16,128]{3,2,1,0:T(8,128)(2,1)S(1)}, u32[]{:S(2)}, u32[]{:S(2)}) async-start(bf16[32,2,16,128]{3,2,1,0:T(8,128)(2,1)} %get-tuple-element.23.white_ref), calls=%async_computation | async-start | bytes 524288 | tf_op jit(solution)/shard_map/all_to_all | solution.py:416
  18.0 10.6 %copy-start.2 = (bf16[512,512]{1,0:T(8,128)(2,1)S(1)}, bf16[512,512]{1,0:T(8,128)(2,1)}, u32[]{:S(2)}) copy-start(bf16[512,512]{1,0:T(8,128)(2,1)} %constant.25.clone.pack_ref) | copy-start | bytes 1572868
  18.0 10.6 %copy-start.5 = (bf16[128,128]{1,0:T(8,128)(2,1)S(1)}, bf16[128,128]{1,0:T(8,128)(2,1)}, u32[]{:S(2)}) copy-start(bf16[128,128]{1,0:T(8,128)(2,1)} %constant.24.clone.flip_ref) | copy-start | bytes 98308
  18.0 10.6 %copy-start.6 = (s32[8,3]{0,1:T(4,128)S(1)}, s32[8,3]{0,1:T(4,128)}, u32[]{:S(2)}) copy-start(s32[8,3]{0,1:T(4,128)} %param.17) | copy-start | bytes 292
  18.0 10.6 %copy-start.7 = (s32[8]{0:T(128)S(1)}, s32[8]{0:T(128)}, u32[]{:S(2)}) copy-start(s32[8]{0:T(128)} %count_ref.1) | copy-start | bytes 100
  21.0 19.9 %copy-start = (bf16[1024,512]{1,0:T(8,128)(2,1)S(1)}, bf16[1024,512]{1,0:T(8,128)(2,1)}, u32[]{:S(2)}) copy-start(bf16[1024,512]{1,0:T(8,128)(2,1)} %constant.26.clone.inv_ref) | copy-start | bytes 3145732
  21.0 8.8 %collective-permute-start.3 = (bf16[1,256,128]{2,1,0:T(8,128)(2,1)S(1)}, bf16[1,256,128]{2,1,0:T(8,128)(2,1)S(1)}, u32[]{:S(2)}, u32[]{:S(2)}) collective-permute-start(bf16[1,256,128]{2,1,0:T(8,128)(2,1)S(1)} %get-tuple-element.28), channel_id=1, source_target_pairs={{0,1},{1,0},{2,3},{3,2},{4,5},{5,4},{6,7},{7,6},{8,9},{9,8},{10,11... | collective-permute-start | bytes 196616 | tf_op jit(solution)/shard_map/ppermute | solution.py:440
  21.3 8.5 %collective-permute-start.4 = (bf16[1,256,128]{2,1,0:T(8,128)(2,1)S(1)}, bf16[1,256,128]{2,1,0:T(8,128)(2,1)S(1)}, u32[]{:S(2)}, u32[]{:S(2)}) collective-permute-start(bf16[1,256,128]{2,1,0:T(8,128)(2,1)S(1)} %get-tuple-element.29), channel_id=1, source_target_pairs={{0,2},{1,3},{2,0},{3,1},{4,6},{5,7},{6,4},{7,5},{8,10},{9,11},{10,... | collective-permute-start | bytes 196616 | tf_op jit(solution)/shard_map/ppermute | solution.py:440
  22.2 7.6 %collective-permute-start.5 = (bf16[1,256,128]{2,1,0:T(8,128)(2,1)S(1)}, bf16[1,256,128]{2,1,0:T(8,128)(2,1)S(1)}, u32[]{:S(2)}, u32[]{:S(2)}) collective-permute-start(bf16[1,256,128]{2,1,0:T(8,128)(2,1)S(1)} %get-tuple-element.30), channel_id=1, source_target_pairs={{0,3},{1,2},{2,1},{3,0},{4,7},{5,6},{6,5},{7,4},{8,11},{9,10},{10,... | collective-permute-start | bytes 196616 | tf_op jit(solution)/shard_map/ppermute | solution.py:440

commit v16 on v15

--- a/solution.py
+++ b/solution.py
@@ -273,19 +273,20 @@
 
 
 def loop_kernel(partner_ref, count_ref, flip_ref, pack_ref, white_ref, out_ref):
-    blocks, segs, _, bins, _ = white_ref.shape
-    owners = out_ref.shape[1]
+    segs, blocks, _, bins, _ = white_ref.shape
+    owners = out_ref.shape[0]
     slots = partner_ref.shape[0]
     rows = segs * 2 * bins
     packed_rows = 2 * bins // owners
     turned = mm(white_ref[...].reshape(blocks * rows, LANES), flip_ref[...])
+    turned = turned.reshape(white_ref.shape)
     loops = []
     for b in range(blocks):
-        own = turned[b * rows : (b + 1) * rows].reshape(segs, 2, bins, LANES)
+        own = turned[:, b]
         for k in range(slots):
             partner = jnp.clip(partner_ref[k, b], 0, blocks - 1)
             live = (k < count_ref[b]).astype(F32)
-            far = white_ref[partner].astype(F32)
+            far = white_ref[:, partner].astype(F32)
             real = jnp.sum(own[:, 0] * far[:, 0] + own[:, 1] * far[:, 1], axis=0)
             imag = jnp.sum(own[:, 1] * far[:, 0] - own[:, 0] * far[:, 1], axis=0)
             pair = jnp.concatenate([real, imag], axis=0) * live
@@ -296,7 +297,7 @@
     for b in range(blocks):
         for q in range(owners):
             tile = packed[b * depth : (b + 1) * depth, q * LANES : (q + 1) * LANES]
-            out_ref[b, q] = tile.astype(BF16)
+            out_ref[q, b] = tile.astype(BF16)
 
 
 def loop_lag_kernel(slots, spec_ref, inv_ref, loop_ref):
@@ -335,11 +336,11 @@
 
 
 def loops_plain(white, loop_partner, loop_count, owners, inverse):
-    blocks, _, _, bins, chans = white.shape
+    _, blocks, _, bins, chans = white.shape
     devices = blocks * owners
     slots = loop_partner.shape[1]
     share = chans // owners
-    wide = white.astype(F32)
+    wide = white.astype(F32).swapaxes(0, 1)
     loops = []
     for k in range(slots):
         far = jnp.flip(wide[loop_partner[:, k]], axis=4)
@@ -348,9 +349,9 @@
         imag = jnp.sum(wide[:, :, 1] * far[:, :, 0] - wide[:, :, 0] * far[:, :, 1], axis=1)
         pair = (jnp.stack([real, imag]) * live[None]).astype(BF16)
         loops.append(pair.reshape(2, blocks, bins, owners, share))
-    loop = jnp.transpose(jnp.stack(loops), (2, 4, 0, 1, 3, 5))
+    loop = jnp.transpose(jnp.stack(loops), (4, 2, 0, 1, 3, 5))
     loop = loop.reshape(devices, slots, 2 * bins, share)
-    summed = lax.all_to_all(loop, ("chan", "seg"), 0, 0, tiled=True).astype(F32)
+    summed = lax.all_to_all(loop, ("seg", "chan"), 0, 0, tiled=True).astype(F32)
     table = inverse.astype(np.float32).reshape(LAGS, devices, 2 * bins)
     lags = jnp.einsum("dtvc,ldv->tcl", summed, table, precision=lax.Precision.HIGHEST)
     return lags[None]
@@ -413,8 +414,8 @@
     if bins != GROUP:
         spread = jnp.moveaxis(white, 1, 0).reshape(2, devices, bins, LANES)
         spread = jnp.moveaxis(spread, 0, 1)
-    moved = lax.all_to_all(spread, ("chan", "seg"), 0, 0, tiled=True)
-    moved = moved.reshape(chan_count, seg_count, 2, bins, LANES)
+    moved = lax.all_to_all(spread, ("seg", "chan"), 0, 0, tiled=True)
+    moved = moved.reshape(seg_count, chan_count, 2, bins, LANES)
 
     ring = [(i, (i + 1) % chan_count) for i in range(chan_count)]
     before = lax.ppermute(up, "chan", ring)
@@ -460,7 +461,7 @@
     out_rows = slots * (2 * bins // seg_count)
     crossed = pl.pallas_call(
         loop_kernel,
-        out_shape=jax.ShapeDtypeStruct((chan_count, seg_count, out_rows, LANES), BF16),
+        out_shape=jax.ShapeDtypeStruct((seg_count, chan_count, out_rows, LANES), BF16),
         in_specs=smem(2) + vmem(3),
         out_specs=pl.BlockSpec(memory_space=pltpu.VMEM),
         compiler_params=PARAMS,
@@ -468,7 +469,7 @@
     )(loop_partner.T, loop_count, flip, pack_matrix(seg_count), moved)
     crossed, *lags[1:] = lax.optimization_barrier((crossed, *lags[1:]))
     crossed = crossed.reshape(devices, out_rows, LANES)
-    summed = lax.all_to_all(crossed, ("chan", "seg"), 0, 0, tiled=True)
+    summed = lax.all_to_all(crossed, ("seg", "chan"), 0, 0, tiled=True)
     columns = np.arange(2 * BINS).reshape(devices, seg_count, -1).swapaxes(0, 1).reshape(-1)
     loop_inverse = inverse_table(seg_count, order[columns], part[columns]).T
     loop_inverse = np.concatenate(split_np(loop_inverse), axis=1)

time: 42.3 us -> 41.9 us (level)
  transfers between devices with their start and end apart: 7 -> 7, of which waited for: 2 -> 2; matrix products, arithmetic and copies ran while one was open for 0% -> 0% of each run, Pallas kernels for 12% -> 13%
where the time goes in v16:
time: 41.9 us; the launch traced here: 41.6 us
  starting transfers between devices  14.5 us (35%)
  blocking collectives  10.7 us (26%)
  Pallas kernels  8.82 us (21%)
  waiting for transfers between devices  6.58 us (16%)
  between operations  0.89 us (2%)
    all_to_all x1, blocking collectives, body(): summed = lax.all_to_all(crossed, ('seg', 'chan'), 0, 0, tiled=True)  10.7 us
    all_to_all x1, waiting for transfers between devices, body(): moved = lax.all_to_all(spread, ('seg', 'chan'), 0, 0, tiled=True)  5.69 us
    all_to_all x1, starting transfers between devices, body(): moved = lax.all_to_all(spread, ('seg', 'chan'), 0, 0, tiled=True)  4.73 us
    ppermute x1, starting transfers between devices, body(): after = lax.ppermute(down, 'chan', [(j, i) for i, j in ring])  3.04 us
    ppermute x1, starting transfers between devices, body(): rim = lax.ppermute(rim, 'seg', route)  2.49 us
    ppermute x1, starting transfers between devices, body(): before = lax.ppermute(up, 'chan', ring)  2.35 us
    pallas_call x1, Pallas kernels, body(): pl.pallas_call(near_kernel, out_shape=[jax.ShapeDtypeStruct((near_each, L...  2.07 us
    pallas_call x1, Pallas kernels, body(): pl.pallas_call(spectrum_kernel, out_shape=[jax.ShapeDtypeStruct((2 * BINS...  1.96 us
  transfers between devices with their start and end apart: 7, of which 2 were waited for; matrix products, arithmetic and copies ran while one was open for 0% of the time, Pallas kernels for 13%

profile of v16, /device:TPU:0, one launch (start us, length us, event | category | flops | bytes accessed | tf_op | source)
XLA Modules:
  0.0 41.6 jit_solution(1660118489582636527)
XLA Ops:
  0.6 0.0 copy-start.12
  0.6 0.0 copy-start.13
  0.7 0.0 copy-start.8
  0.7 0.0 copy-start.9
  0.7 1.1 %history.1 = f32[64,128]{1,0:T(8,128)S(1)} custom-call(f32[128,4096]{1,0:T(8,128)} %rec_hbm.1), custom_call_target="tpu_custom_call" | custom-call | flops 10000000000 | bytes 20000000 | tf_op jit(solution)/shard_map/history/pallas_call | solution.py:372
  1.8 0.0 copy-start.1
  1.8 0.0 copy-start.3
  1.8 0.0 copy-start.4
  1.8 2.5 %collective-permute-start = (f32[64,128]{1,0:T(8,128)S(1)}, f32[64,128]{1,0:T(8,128)S(1)}, u32[]{:S(2)}, u32[]{:S(2)}) collective-permute-start(f32[64,128]{1,0:T(8,128)S(1)} %history.1), channel_id=1, source_target_pairs={{0,1},{1,2},{2,3},{4,5},{5,6},{6,7},{8,9},{9,10},{10,11},{12,13},{... | collective-permute-start | bytes 98312 | tf_op jit(solution)/shard_map/ppermute | solution.py:384
  4.3 0.0 copy-done.12
  4.3 0.0 copy-done.13
  4.3 0.0 copy-done.8
  4.3 0.0 copy-done.9
  4.4 0.0 copy-start.10
  4.4 0.0 copy-start.11
  4.4 2.0 %filter_and_transform.1 = (f32[1024,128]{1,0:T(8,128)S(1)}, f32[8,128]{1,0:T(8,128)S(1)}, f32[16,128]{1,0:T(8,128)S(1)}) custom-call(f32[1,64]{1,0:T(1,128)S(1)} %bitcast.8, f32[128,4096]{1,0:T(8,128)S(1)} %copy-done.8, bf16[256,768]{1,0:T(8,128)(2,1)S(1)} %copy-done.12, f32[256,128]{1,0:T(8,128)S(1)} %copy-done.13), custom_call_target="tpu_custom_call" | custom-call | flops 1000000000 | bytes 5000000 | tf_op jit(solution)/shard_map/filter_and_transform/pallas_call | solution.py:386
  6.3 0.0 collective-permute-done.rim_ref
  6.4 0.0 copy-done.1
  6.4 0.0 copy-done.3
  6.4 0.0 copy-done.4
  6.4 1.4 %whiten.1 = (bf16[32,2,16,128]{3,2,1,0:T(8,128)(2,1)}, bf16[512,128]{1,0:T(8,128)(2,1)S(1)}, bf16[512,128]{1,0:T(8,128)(2,1)S(1)}) custom-call(f32[1024,128]{1,0:T(8,128)S(1)} %get-tuple-element.20.spec_ref, f32[64,128]{1,0:T(8,128)S(1)} %collective-permute-done.rim_ref, f32[8,128]{1,0:T(8,128)S(1)} %get-tuple-element.21.mean_ref, ...), custom_call_target="tpu_custom_call" | custom-call | tf_op jit(solution)/shard_map/whiten/pallas_call | solution.py:404
  7.8 2.4 %collective-permute-start.1 = (bf16[512,128]{1,0:T(8,128)(2,1)S(1)}, bf16[512,128]{1,0:T(8,128)(2,1)S(1)}, u32[]{:S(2)}, u32[]{:S(2)}) collective-permute-start(bf16[512,128]{1,0:T(8,128)(2,1)S(1)} %get-tuple-element.24), channel_id=1, source_target_pairs={{0,4},{4,8},{8,12},{12,16},{16,20},{20,24},{24,28},{28,0},{1,5},{5... | collective-permute-start | bytes 393224 | tf_op jit(solution)/shard_map/ppermute | solution.py:421
  10.2 3.0 %collective-permute-start.2 = (bf16[512,128]{1,0:T(8,128)(2,1)S(1)}, bf16[512,128]{1,0:T(8,128)(2,1)S(1)}, u32[]{:S(2)}, u32[]{:S(2)}) collective-permute-start(bf16[512,128]{1,0:T(8,128)(2,1)S(1)} %get-tuple-element.25), channel_id=1, source_target_pairs={{4,0},{8,4},{12,8},{16,12},{20,16},{24,20},{28,24},{0,28},{5,1},{9... | collective-permute-start | bytes 393224 | tf_op jit(solution)/shard_map/ppermute | solution.py:422
  13.2 4.7 %all-to-all-start = ((bf16[32,2,16,128]{3,2,1,0:T(8,128)(2,1)}), bf16[32,2,16,128]{3,2,1,0:T(8,128)(2,1)S(1)}, u32[]{:S(2)}, u32[]{:S(2)}) async-start(bf16[32,2,16,128]{3,2,1,0:T(8,128)(2,1)} %get-tuple-element.23.white_ref), calls=%async_computation | async-start | bytes 524288 | tf_op jit(solution)/shard_map/all_to_all | solution.py:417
  18.0 0.0 copy-start.2
  18.0 0.0 copy-start.5
  18.0 0.0 copy-start.6
  18.0 0.0 copy-start.7
  18.0 0.0 collective-permute-done.1.before_ref
  18.0 0.9 %collective-permute-done.2.after_ref = bf16[512,128]{1,0:T(8,128)(2,1)S(1)} collective-permute-done((bf16[512,128]{1,0:T(8,128)(2,1)S(1)}, bf16[512,128]{1,0:T(8,128)(2,1)S(1)}, u32[]{:S(2)}, u32[]{:S(2)}) %collective-permute-start.2) | collective-permute-done | bytes 131104 | tf_op jit(solution)/shard_map/ppermute | solution.py:422
  18.9 0.0 copy-done.10
  18.9 0.0 copy-done.11
  18.9 2.1 %near_lags.1 = (bf16[1,256,128]{2,1,0:T(8,128)(2,1)S(1)}, bf16[1,256,128]{2,1,0:T(8,128)(2,1)S(1)}, bf16[1,256,128]{2,1,0:T(8,128)(2,1)S(1)}, bf16[1,256,128]{2,1,0:T(8,128)(2,1)S(1)}) custom-call(s32[4]{0:T(128)S(1)} %copy-done.10, bf16[32,2,16,128]{3,2,1,0:T(8,128)(2,1)} %get-tuple-element.23.white_ref, ...), custom_call_target="tpu_custom_call" | custom-call | flops 20000000000 | bytes 20000000 | tf_op jit(solution)/shard_map/near_lags/pallas_call | solution.py:426
  21.0 0.0 copy-start
  21.0 0.4 collective-permute-start.3
  21.3 0.8 %collective-permute-start.4 = (bf16[1,256,128]{2,1,0:T(8,128)(2,1)S(1)}, bf16[1,256,128]{2,1,0:T(8,128)(2,1)S(1)}, u32[]{:S(2)}, u32[]{:S(2)}) collective-permute-start(bf16[1,256,128]{2,1,0:T(8,128)(2,1)S(1)} %get-tuple-element.29), channel_id=1, source_target_pairs={{0,2},{1,3},{2,0},{3,1},{4,6},{5,7},{6,4},{7,5},{8,10},{9,11},{10,... | collective-permute-start | bytes 196616 | tf_op jit(solution)/shard_map/ppermute | solution.py:441
  22.2 0.7 %collective-permute-start.5 = (bf16[1,256,128]{2,1,0:T(8,128)(2,1)S(1)}, bf16[1,256,128]{2,1,0:T(8,128)(2,1)S(1)}, u32[]{:S(2)}, u32[]{:S(2)}) collective-permute-start(bf16[1,256,128]{2,1,0:T(8,128)(2,1)S(1)} %get-tuple-element.30), channel_id=1, source_target_pairs={{0,3},{1,2},{2,1},{3,0},{4,7},{5,6},{6,5},{7,4},{8,11},{9,10},{10,... | collective-permute-start | bytes 196616 | tf_op jit(solution)/shard_map/ppermute | solution.py:441
  22.9 5.7 %all-to-all-done = bf16[32,2,16,128]{3,2,1,0:T(8,128)(2,1)S(1)} async-done(((bf16[32,2,16,128]{3,2,1,0:T(8,128)(2,1)}), bf16[32,2,16,128]{3,2,1,0:T(8,128)(2,1)S(1)}, u32[]{:S(2)}, u32[]{:S(2)}) %all-to-all-start) | async-done | bytes 262176 | tf_op jit(solution)/shard_map/all_to_all | solution.py:417
  28.6 0.0 copy-done.2
  28.6 0.0 copy-done.5
  28.6 0.0 copy-done.6
  28.6 0.0 copy-done.7
  28.6 1.2 %loop_spectra.1 = bf16[4,8,24,128]{3,2,1,0:T(8,128)(2,1)S(1)} custom-call(s32[3,8]{1,0:T(4,128)S(1)} %bitcast.7, s32[8]{0:T(128)S(1)} %copy-done.7, bf16[128,128]{1,0:T(8,128)(2,1)S(1)} %copy-done.5, bf16[512,512]{1,0:T(8,128)(2,1)S(1)} %copy-done.2, bf16[4,8,2,16,128]{4,3,2,1,0:T(8,128)(2,1)S(1)} %bitcast.5), custom_call_target="tpu_custom_call" | custom-call | tf_op jit(solution)/shard_map/loop_spectra/pallas_call | solution.py:462
  29.9 0.0 collective-permute-done.3.refs_1_
  29.9 0.0 collective-permute-done.4.refs_2_
  29.9 0.0 collective-permute-done.5.refs_3_
  29.9 10.7 %all_to_all.10.spec_ref = bf16[32,24,128]{2,1,0:T(8,128)(2,1)S(1)} all-to-all(bf16[32,24,128]{2,1,0:T(8,128)(2,1)S(1)} %bitcast.6), channel_id=1, replica_groups=mesh['chan'=8,'seg'=4] {'seg','chan'}, dimensions={0} | all-to-all | bytes 393216 | tf_op jit(solution)/shard_map/all_to_all | solution.py:472
  40.6 1.0 %lags.1 = (f32[128,1,256]{2,1,0:T(1,128)}, f32[96,256]{1,0:T(8,128)}) custom-call(bf16[32,24,128]{2,1,0:T(8,128)(2,1)S(1)} %all_to_all.10.spec_ref, bf16[1024,512]{1,0:T(8,128)(2,1)S(1)} %copy-done, bf16[1,256,128]{2,1,0:T(8,128)(2,1)S(1)} %get-tuple-element.32.refs_0_, bf16[1,256,128]{2,1,0:T(8,128)(2,1)S(1)} %collective-permute-done.3.refs_1_, ...), custom_call_target="tpu_custom_call" | custom-call | tf_op jit(solution)/shard_map/lags/pallas_call | solution.py:476
  (1 shorter events, 0.0 us)
Async XLA Ops:
  0.6 3.7 %copy-start.12 = (bf16[256,768]{1,0:T(8,128)(2,1)S(1)}, bf16[256,768]{1,0:T(8,128)(2,1)}, u32[]{:S(2)}) copy-start(bf16[256,768]{1,0:T(8,128)(2,1)} %constant.18.clone.tab_ref) | copy-start | bytes 1179652
  0.6 3.7 %copy-start.13 = (f32[256,128]{1,0:T(8,128)S(1)}, f32[256,128]{1,0:T(8,128)}, u32[]{:S(2)}) copy-start(f32[256,128]{1,0:T(8,128)} %constant.19.clone.twist_ref) | copy-start | bytes 393220
  0.7 3.7 %copy-start.8 = (f32[128,4096]{1,0:T(8,128)S(1)}, f32[128,4096]{1,0:T(8,128)}, u32[]{:S(2)}) copy-start(f32[128,4096]{1,0:T(8,128)} %rec_hbm.1) | copy-start | bytes 6291460
  0.7 3.7 %copy-start.9 = (f32[64]{0:T(128)S(1)}, f32[64]{0:T(128)}, u32[]{:S(2)}) copy-start(f32[64]{0:T(128)} %param.15) | copy-start | bytes 772
  1.8 4.6 %copy-start.1 = (bf16[512,512]{1,0:T(8,128)(2,1)S(1)}, bf16[512,512]{1,0:T(8,128)(2,1)}, u32[]{:S(2)}) copy-start(bf16[512,512]{1,0:T(8,128)(2,1)} %constant.21.clone.band_ref) | copy-start | bytes 1572868
  1.8 4.6 %copy-start.3 = (f32[512,128]{1,0:T(8,128)S(1)}, f32[512,128]{1,0:T(8,128)}, u32[]{:S(2)}) copy-start(f32[512,128]{1,0:T(8,128)} %constant.22.clone.share_ref) | copy-start | bytes 786436
  1.8 4.6 %copy-start.4 = (bf16[1024,128]{1,0:T(8,128)(2,1)S(1)}, bf16[1024,128]{1,0:T(8,128)(2,1)}, u32[]{:S(2)}) copy-start(bf16[1024,128]{1,0:T(8,128)(2,1)} %constant.20.clone.edge_ref) | copy-start | bytes 786436
  1.8 4.5 %collective-permute-start = (f32[64,128]{1,0:T(8,128)S(1)}, f32[64,128]{1,0:T(8,128)S(1)}, u32[]{:S(2)}, u32[]{:S(2)}) collective-permute-start(f32[64,128]{1,0:T(8,128)S(1)} %history.1), channel_id=1, source_target_pairs={{0,1},{1,2},{2,3},{4,5},{5,6},{6,7},{8,9},{9,10},{10,11},{12,13},{... | collective-permute-start | bytes 98312 | tf_op jit(solution)/shard_map/ppermute | solution.py:384
  4.4 14.5 %copy-start.10 = (s32[4]{0:T(128)S(1)}, s32[4]{0:T(128)}, u32[]{:S(2)}) copy-start(s32[4]{0:T(128)} %offs_ref.1) | copy-start | bytes 52
  4.4 14.5 %copy-start.11 = (bf16[512,1024]{1,0:T(8,128)(2,1)S(1)}, bf16[512,1024]{1,0:T(8,128)(2,1)}, u32[]{:S(2)}) copy-start(bf16[512,1024]{1,0:T(8,128)(2,1)} %constant.23.clone.inv_ref) | copy-start | bytes 3145732
  7.8 10.2 %collective-permute-start.1 = (bf16[512,128]{1,0:T(8,128)(2,1)S(1)}, bf16[512,128]{1,0:T(8,128)(2,1)S(1)}, u32[]{:S(2)}, u32[]{:S(2)}) collective-permute-start(bf16[512,128]{1,0:T(8,128)(2,1)S(1)} %get-tuple-element.24), channel_id=1, source_target_pairs={{0,4},{4,8},{8,12},{12,16},{16,20},{20,24},{24,28},{28,0},{1,5},{5... | collective-permute-start | bytes 393224 | tf_op jit(solution)/shard_map/ppermute | solution.py:421
  10.2 8.7 %collective-permute-start.2 = (bf16[512,128]{1,0:T(8,128)(2,1)S(1)}, bf16[512,128]{1,0:T(8,128)(2,1)S(1)}, u32[]{:S(2)}, u32[]{:S(2)}) collective-permute-start(bf16[512,128]{1,0:T(8,128)(2,1)S(1)} %get-tuple-element.25), channel_id=1, source_target_pairs={{4,0},{8,4},{12,8},{16,12},{20,16},{24,20},{28,24},{0,28},{5,1},{9... | collective-permute-start | bytes 393224 | tf_op jit(solution)/shard_map/ppermute | solution.py:422
  13.2 15.4 %all-to-all-start = ((bf16[32,2,16,128]{3,2,1,0:T(8,128)(2,1)}), bf16[32,2,16,128]{3,2,1,0:T(8,128)(2,1)S(1)}, u32[]{:S(2)}, u32[]{:S(2)}) async-start(bf16[32,2,16,128]{3,2,1,0:T(8,128)(2,1)} %get-tuple-element.23.white_ref), calls=%async_computation | async-start | bytes 524288 | tf_op jit(solution)/shard_map/all_to_all | solution.py:417
  18.0 10.6 %copy-start.2 = (bf16[512,512]{1,0:T(8,128)(2,1)S(1)}, bf16[512,512]{1,0:T(8,128)(2,1)}, u32[]{:S(2)}) copy-start(bf16[512,512]{1,0:T(8,128)(2,1)} %constant.25.clone.pack_ref) | copy-start | bytes 1572868
  18.0 10.6 %copy-start.5 = (bf16[128,128]{1,0:T(8,128)(2,1)S(1)}, bf16[128,128]{1,0:T(8,128)(2,1)}, u32[]{:S(2)}) copy-start(bf16[128,128]{1,0:T(8,128)(2,1)} %constant.24.clone.flip_ref) | copy-start | bytes 98308
  18.0 10.6 %copy-start.6 = (s32[8,3]{0,1:T(4,128)S(1)}, s32[8,3]{0,1:T(4,128)}, u32[]{:S(2)}) copy-start(s32[8,3]{0,1:T(4,128)} %param.17) | copy-start | bytes 292
  18.0 10.6 %copy-start.7 = (s32[8]{0:T(128)S(1)}, s32[8]{0:T(128)}, u32[]{:S(2)}) copy-start(s32[8]{0:T(128)} %count_ref.1) | copy-start | bytes 100
  21.0 19.6 %copy-start = (bf16[1024,512]{1,0:T(8,128)(2,1)S(1)}, bf16[1024,512]{1,0:T(8,128)(2,1)}, u32[]{:S(2)}) copy-start(bf16[1024,512]{1,0:T(8,128)(2,1)} %constant.26.clone.inv_ref) | copy-start | bytes 3145732
  21.0 8.9 %collective-permute-start.3 = (bf16[1,256,128]{2,1,0:T(8,128)(2,1)S(1)}, bf16[1,256,128]{2,1,0:T(8,128)(2,1)S(1)}, u32[]{:S(2)}, u32[]{:S(2)}) collective-permute-start(bf16[1,256,128]{2,1,0:T(8,128)(2,1)S(1)} %get-tuple-element.28), channel_id=1, source_target_pairs={{0,1},{1,0},{2,3},{3,2},{4,5},{5,4},{6,7},{7,6},{8,9},{9,8},{10,11... | collective-permute-start | bytes 196616 | tf_op jit(solution)/shard_map/ppermute | solution.py:441
  21.3 8.5 %collective-permute-start.4 = (bf16[1,256,128]{2,1,0:T(8,128)(2,1)S(1)}, bf16[1,256,128]{2,1,0:T(8,128)(2,1)S(1)}, u32[]{:S(2)}, u32[]{:S(2)}) collective-permute-start(bf16[1,256,128]{2,1,0:T(8,128)(2,1)S(1)} %get-tuple-element.29), channel_id=1, source_target_pairs={{0,2},{1,3},{2,0},{3,1},{4,6},{5,7},{6,4},{7,5},{8,10},{9,11},{10,... | collective-permute-start | bytes 196616 | tf_op jit(solution)/shard_map/ppermute | solution.py:441
  22.2 7.7 %collective-permute-start.5 = (bf16[1,256,128]{2,1,0:T(8,128)(2,1)S(1)}, bf16[1,256,128]{2,1,0:T(8,128)(2,1)S(1)}, u32[]{:S(2)}, u32[]{:S(2)}) collective-permute-start(bf16[1,256,128]{2,1,0:T(8,128)(2,1)S(1)} %get-tuple-element.30), channel_id=1, source_target_pairs={{0,3},{1,2},{2,1},{3,0},{4,7},{5,6},{6,5},{7,4},{8,11},{9,10},{10,... | collective-permute-start | bytes 196616 | tf_op jit(solution)/shard_map/ppermute | solution.py:441

commit v17 on v16

--- a/solution.py
+++ b/solution.py
@@ -54,7 +54,7 @@
 def twiddle_table():
     angles = np.arange(DEPTH)[:, None] * np.arange(1, RADIX) * (2.0 * np.pi / NFFT)
     columns = np.stack([np.cos(angles), np.sin(angles)], axis=2).reshape(DEPTH, -1)
-    return np.pad(columns, ((0, 0), (0, LANES - columns.shape[1]))).astype(np.float32)
+    return np.repeat(columns, LANES, axis=1).astype(np.float32)
 
 
 def edge_table():
@@ -126,27 +126,25 @@
     taps_high, taps_low = split(table.T)
     taps_both = jnp.concatenate([taps_high, taps_low], axis=1)
     before = [jnp.zeros((LANES, LANES), BF16)] * 2
-    outputs = []
-    for first in range(0, blocks, blocks // 2):
-        windows = ([], [])
-        for j in range(first, first + blocks // 2):
-            chunk = rec_ref[:, j * STEP : (j + 1) * STEP]
-            if j == 0:
-                mean = jnp.sum(chunk, axis=1, keepdims=True) * (1.0 / STEP)
-            for i, value in enumerate(split(chunk - mean)):
-                windows[i].append(jnp.concatenate([before[i], value], axis=1))
-                before[i] = value[:, STEP - LANES :]
-        wide = mm(jnp.concatenate(windows[0], axis=0), taps_both)
-        rest = mm(jnp.concatenate(windows[1], axis=0), taps_high)
-        total = wide[:, :LANES] + wide[:, LANES:] + rest
-        outputs += [total[t * LANES : (t + 1) * LANES].T for t in range(blocks // 2)]
+    windows = ([], [])
+    for j in range(blocks):
+        chunk = rec_ref[:, j * STEP : (j + 1) * STEP]
+        if j == 0:
+            mean = jnp.sum(chunk, axis=1, keepdims=True) * (1.0 / STEP)
+        for i, value in enumerate(split(chunk - mean)):
+            windows[i].append(jnp.concatenate([before[i], value], axis=1))
+            before[i] = value[:, STEP - LANES :]
+    wide = mm(jnp.concatenate(windows[0], axis=0), taps_both)
+    rest = mm(jnp.concatenate(windows[1], axis=0), taps_high)
+    total = wide[:, :LANES] + wide[:, LANES:] + rest
+    outputs = [total[t * LANES : (t + 1) * LANES].T for t in range(blocks)]
     pieces = [jnp.concatenate(outputs[j : j + 2], axis=0) for j in range(0, blocks, 2)]
     mean_ref[...] = jnp.broadcast_to(mean, (LANES, LANES)).T[: mean_ref.shape[0]]
     even, odd = pieces[0] + pieces[2], pieces[1] + pieces[3]
     a, b = pieces[0] - pieces[2], pieces[1] - pieces[3]
     whole, half = even + odd, even - odd
     whole = whole - jnp.sum(whole, axis=0, keepdims=True) * (1.0 / DEPTH)
-    c1, s1, c2, s2, c3, s3 = [twist_ref[:, i : i + 1] for i in range(6)]
+    c1, s1, c2, s2, c3, s3 = [twist_ref[:, i * LANES : (i + 1) * LANES] for i in range(6)]
     inputs = [
         whole,
         a * c1 - b * s1,

time: 41.9 us -> 41.9 us (level)
  no operation moved by 1% of the time
where the time goes in v17:
time: 41.9 us; the launch traced here: 41.6 us
  starting transfers between devices  14.5 us (35%)
  blocking collectives  10.7 us (26%)
  Pallas kernels  8.91 us (21%)
  waiting for transfers between devices  6.57 us (16%)
  between operations  0.89 us (2%)
    all_to_all x1, blocking collectives, body(): summed = lax.all_to_all(crossed, ('seg', 'chan'), 0, 0, tiled=True)  10.7 us
    all_to_all x1, waiting for transfers between devices, body(): moved = lax.all_to_all(spread, ('seg', 'chan'), 0, 0, tiled=True)  5.59 us
    all_to_all x1, starting transfers between devices, body(): moved = lax.all_to_all(spread, ('seg', 'chan'), 0, 0, tiled=True)  4.66 us
    ppermute x1, starting transfers between devices, body(): after = lax.ppermute(down, 'chan', [(j, i) for i, j in ring])  3.04 us
    ppermute x1, starting transfers between devices, body(): rim = lax.ppermute(rim, 'seg', route)  2.49 us
    ppermute x1, starting transfers between devices, body(): before = lax.ppermute(up, 'chan', ring)  2.35 us
    pallas_call x1, Pallas kernels, body(): pl.pallas_call(near_kernel, out_shape=[jax.ShapeDtypeStruct((near_each, L...  2.08 us
    pallas_call x1, Pallas kernels, body(): pl.pallas_call(spectrum_kernel, out_shape=[jax.ShapeDtypeStruct((2 * BINS...  2.05 us
  transfers between devices with their start and end apart: 7, of which 2 were waited for; matrix products, arithmetic and copies ran while one was open for 0% of the time, Pallas kernels for 13%

profile of v17, /device:TPU:0, one launch (start us, length us, event | category | flops | bytes accessed | tf_op | source)
XLA Modules:
  0.0 41.6 jit_solution(3168047330331298890)
XLA Ops:
  0.6 0.0 copy-start.12
  0.6 0.0 copy-start.13
  0.7 0.0 copy-start.8
  0.7 0.0 copy-start.9
  0.7 1.1 %history.1 = f32[64,128]{1,0:T(8,128)S(1)} custom-call(f32[128,4096]{1,0:T(8,128)} %rec_hbm.1), custom_call_target="tpu_custom_call" | custom-call | flops 10000000000 | bytes 20000000 | tf_op jit(solution)/shard_map/history/pallas_call | solution.py:370
  1.8 0.0 copy-start.1
  1.8 0.0 copy-start.3
  1.8 0.0 copy-start.4
  1.8 2.5 %collective-permute-start = (f32[64,128]{1,0:T(8,128)S(1)}, f32[64,128]{1,0:T(8,128)S(1)}, u32[]{:S(2)}, u32[]{:S(2)}) collective-permute-start(f32[64,128]{1,0:T(8,128)S(1)} %history.1), channel_id=1, source_target_pairs={{0,1},{1,2},{2,3},{4,5},{5,6},{6,7},{8,9},{9,10},{10,11},{12,13},{... | collective-permute-start | bytes 98312 | tf_op jit(solution)/shard_map/ppermute | solution.py:382
  4.3 0.0 copy-done.12
  4.3 0.0 copy-done.13
  4.3 0.0 copy-done.8
  4.3 0.0 copy-done.9
  4.4 0.0 copy-start.10
  4.4 0.0 copy-start.11
  4.4 2.0 %filter_and_transform.1 = (f32[1024,128]{1,0:T(8,128)S(1)}, f32[8,128]{1,0:T(8,128)S(1)}, f32[16,128]{1,0:T(8,128)S(1)}) custom-call(f32[1,64]{1,0:T(1,128)S(1)} %bitcast.8, f32[128,4096]{1,0:T(8,128)S(1)} %copy-done.8, bf16[256,768]{1,0:T(8,128)(2,1)S(1)} %copy-done.13, f32[256,768]{1,0:T(8,128)S(1)} %copy-done.12), custom_call_target="tpu_custom_call" | custom-call | flops 1000000000 | bytes 5000000 | tf_op jit(solution)/shard_map/filter_and_transform/pallas_call | solution.py:384
  6.4 0.0 collective-permute-done.rim_ref
  6.4 0.0 copy-done.1
  6.5 0.0 copy-done.3
  6.5 0.0 copy-done.4
  6.5 1.4 %whiten.1 = (bf16[32,2,16,128]{3,2,1,0:T(8,128)(2,1)}, bf16[512,128]{1,0:T(8,128)(2,1)S(1)}, bf16[512,128]{1,0:T(8,128)(2,1)S(1)}) custom-call(f32[1024,128]{1,0:T(8,128)S(1)} %get-tuple-element.20.spec_ref, f32[64,128]{1,0:T(8,128)S(1)} %collective-permute-done.rim_ref, f32[8,128]{1,0:T(8,128)S(1)} %get-tuple-element.21.mean_ref, ...), custom_call_target="tpu_custom_call" | custom-call | tf_op jit(solution)/shard_map/whiten/pallas_call | solution.py:402
  7.9 2.4 %collective-permute-start.1 = (bf16[512,128]{1,0:T(8,128)(2,1)S(1)}, bf16[512,128]{1,0:T(8,128)(2,1)S(1)}, u32[]{:S(2)}, u32[]{:S(2)}) collective-permute-start(bf16[512,128]{1,0:T(8,128)(2,1)S(1)} %get-tuple-element.24), channel_id=1, source_target_pairs={{0,4},{4,8},{8,12},{12,16},{16,20},{20,24},{24,28},{28,0},{1,5},{5... | collective-permute-start | bytes 393224 | tf_op jit(solution)/shard_map/ppermute | solution.py:419
  10.3 3.0 %collective-permute-start.2 = (bf16[512,128]{1,0:T(8,128)(2,1)S(1)}, bf16[512,128]{1,0:T(8,128)(2,1)S(1)}, u32[]{:S(2)}, u32[]{:S(2)}) collective-permute-start(bf16[512,128]{1,0:T(8,128)(2,1)S(1)} %get-tuple-element.25), channel_id=1, source_target_pairs={{4,0},{8,4},{12,8},{16,12},{20,16},{24,20},{28,24},{0,28},{5,1},{9... | collective-permute-start | bytes 393224 | tf_op jit(solution)/shard_map/ppermute | solution.py:420
  13.3 4.7 %all-to-all-start = ((bf16[32,2,16,128]{3,2,1,0:T(8,128)(2,1)}), bf16[32,2,16,128]{3,2,1,0:T(8,128)(2,1)S(1)}, u32[]{:S(2)}, u32[]{:S(2)}) async-start(bf16[32,2,16,128]{3,2,1,0:T(8,128)(2,1)} %get-tuple-element.23.white_ref), calls=%async_computation | async-start | bytes 524288 | tf_op jit(solution)/shard_map/all_to_all | solution.py:415
  18.0 0.0 copy-start.2
  18.0 0.0 copy-start.5
  18.0 0.0 copy-start.6
  18.0 0.0 copy-start.7
  18.0 0.0 collective-permute-done.1.before_ref
  18.0 1.0 %collective-permute-done.2.after_ref = bf16[512,128]{1,0:T(8,128)(2,1)S(1)} collective-permute-done((bf16[512,128]{1,0:T(8,128)(2,1)S(1)}, bf16[512,128]{1,0:T(8,128)(2,1)S(1)}, u32[]{:S(2)}, u32[]{:S(2)}) %collective-permute-start.2) | collective-permute-done | bytes 131104 | tf_op jit(solution)/shard_map/ppermute | solution.py:420
  19.0 0.0 copy-done.10
  19.0 0.0 copy-done.11
  19.0 2.1 %near_lags.1 = (bf16[1,256,128]{2,1,0:T(8,128)(2,1)S(1)}, bf16[1,256,128]{2,1,0:T(8,128)(2,1)S(1)}, bf16[1,256,128]{2,1,0:T(8,128)(2,1)S(1)}, bf16[1,256,128]{2,1,0:T(8,128)(2,1)S(1)}) custom-call(s32[4]{0:T(128)S(1)} %copy-done.10, bf16[32,2,16,128]{3,2,1,0:T(8,128)(2,1)} %get-tuple-element.23.white_ref, ...), custom_call_target="tpu_custom_call" | custom-call | flops 20000000000 | bytes 20000000 | tf_op jit(solution)/shard_map/near_lags/pallas_call | solution.py:424
  21.1 0.0 copy-start
  21.1 0.3 collective-permute-start.3
  21.4 0.8 %collective-permute-start.4 = (bf16[1,256,128]{2,1,0:T(8,128)(2,1)S(1)}, bf16[1,256,128]{2,1,0:T(8,128)(2,1)S(1)}, u32[]{:S(2)}, u32[]{:S(2)}) collective-permute-start(bf16[1,256,128]{2,1,0:T(8,128)(2,1)S(1)} %get-tuple-element.29), channel_id=1, source_target_pairs={{0,2},{1,3},{2,0},{3,1},{4,6},{5,7},{6,4},{7,5},{8,10},{9,11},{10,... | collective-permute-start | bytes 196616 | tf_op jit(solution)/shard_map/ppermute | solution.py:439
  22.2 0.8 %collective-permute-start.5 = (bf16[1,256,128]{2,1,0:T(8,128)(2,1)S(1)}, bf16[1,256,128]{2,1,0:T(8,128)(2,1)S(1)}, u32[]{:S(2)}, u32[]{:S(2)}) collective-permute-start(bf16[1,256,128]{2,1,0:T(8,128)(2,1)S(1)} %get-tuple-element.30), channel_id=1, source_target_pairs={{0,3},{1,2},{2,1},{3,0},{4,7},{5,6},{6,5},{7,4},{8,11},{9,10},{10,... | collective-permute-start | bytes 196616 | tf_op jit(solution)/shard_map/ppermute | solution.py:439
  23.0 5.6 %all-to-all-done = bf16[32,2,16,128]{3,2,1,0:T(8,128)(2,1)S(1)} async-done(((bf16[32,2,16,128]{3,2,1,0:T(8,128)(2,1)}), bf16[32,2,16,128]{3,2,1,0:T(8,128)(2,1)S(1)}, u32[]{:S(2)}, u32[]{:S(2)}) %all-to-all-start) | async-done | bytes 262176 | tf_op jit(solution)/shard_map/all_to_all | solution.py:415
  28.6 0.0 copy-done.2
  28.6 0.0 copy-done.5
  28.6 0.0 copy-done.6
  28.6 0.0 copy-done.7
  28.6 1.2 %loop_spectra.1 = bf16[4,8,24,128]{3,2,1,0:T(8,128)(2,1)S(1)} custom-call(s32[3,8]{1,0:T(4,128)S(1)} %bitcast.7, s32[8]{0:T(128)S(1)} %copy-done.7, bf16[128,128]{1,0:T(8,128)(2,1)S(1)} %copy-done.5, bf16[512,512]{1,0:T(8,128)(2,1)S(1)} %copy-done.2, bf16[4,8,2,16,128]{4,3,2,1,0:T(8,128)(2,1)S(1)} %bitcast.5), custom_call_target="tpu_custom_call" | custom-call | tf_op jit(solution)/shard_map/loop_spectra/pallas_call | solution.py:460
  29.9 0.0 collective-permute-done.3.refs_1_
  29.9 0.0 collective-permute-done.4.refs_2_
  29.9 0.0 collective-permute-done.5.refs_3_
  29.9 10.7 %all_to_all.10.spec_ref = bf16[32,24,128]{2,1,0:T(8,128)(2,1)S(1)} all-to-all(bf16[32,24,128]{2,1,0:T(8,128)(2,1)S(1)} %bitcast.6), channel_id=1, replica_groups=mesh['chan'=8,'seg'=4] {'seg','chan'}, dimensions={0} | all-to-all | bytes 393216 | tf_op jit(solution)/shard_map/all_to_all | solution.py:470
  40.6 1.0 %lags.1 = (f32[128,1,256]{2,1,0:T(1,128)}, f32[96,256]{1,0:T(8,128)}) custom-call(bf16[32,24,128]{2,1,0:T(8,128)(2,1)S(1)} %all_to_all.10.spec_ref, bf16[1024,512]{1,0:T(8,128)(2,1)S(1)} %copy-done, bf16[1,256,128]{2,1,0:T(8,128)(2,1)S(1)} %get-tuple-element.32.refs_0_, bf16[1,256,128]{2,1,0:T(8,128)(2,1)S(1)} %collective-permute-done.3.refs_1_, ...), custom_call_target="tpu_custom_call" | custom-call | tf_op jit(solution)/shard_map/lags/pallas_call | solution.py:474
  (1 shorter events, 0.0 us)
Async XLA Ops:
  0.6 3.7 %copy-start.12 = (f32[256,768]{1,0:T(8,128)S(1)}, f32[256,768]{1,0:T(8,128)}, u32[]{:S(2)}) copy-start(f32[256,768]{1,0:T(8,128)} %constant.19.clone.twist_ref) | copy-start | bytes 2359300
  0.6 3.7 %copy-start.13 = (bf16[256,768]{1,0:T(8,128)(2,1)S(1)}, bf16[256,768]{1,0:T(8,128)(2,1)}, u32[]{:S(2)}) copy-start(bf16[256,768]{1,0:T(8,128)(2,1)} %constant.18.clone.tab_ref) | copy-start | bytes 1179652
  0.7 3.7 %copy-start.8 = (f32[128,4096]{1,0:T(8,128)S(1)}, f32[128,4096]{1,0:T(8,128)}, u32[]{:S(2)}) copy-start(f32[128,4096]{1,0:T(8,128)} %rec_hbm.1) | copy-start | bytes 6291460
  0.7 3.7 %copy-start.9 = (f32[64]{0:T(128)S(1)}, f32[64]{0:T(128)}, u32[]{:S(2)}) copy-start(f32[64]{0:T(128)} %param.15) | copy-start | bytes 772
  1.8 4.7 %copy-start.1 = (bf16[512,512]{1,0:T(8,128)(2,1)S(1)}, bf16[512,512]{1,0:T(8,128)(2,1)}, u32[]{:S(2)}) copy-start(bf16[512,512]{1,0:T(8,128)(2,1)} %constant.21.clone.band_ref) | copy-start | bytes 1572868
  1.8 4.7 %copy-start.3 = (f32[512,128]{1,0:T(8,128)S(1)}, f32[512,128]{1,0:T(8,128)}, u32[]{:S(2)}) copy-start(f32[512,128]{1,0:T(8,128)} %constant.22.clone.share_ref) | copy-start | bytes 786436
  1.8 4.7 %copy-start.4 = (bf16[1024,128]{1,0:T(8,128)(2,1)S(1)}, bf16[1024,128]{1,0:T(8,128)(2,1)}, u32[]{:S(2)}) copy-start(bf16[1024,128]{1,0:T(8,128)(2,1)} %constant.20.clone.edge_ref) | copy-start | bytes 786436
  1.8 4.6 %collective-permute-start = (f32[64,128]{1,0:T(8,128)S(1)}, f32[64,128]{1,0:T(8,128)S(1)}, u32[]{:S(2)}, u32[]{:S(2)}) collective-permute-start(f32[64,128]{1,0:T(8,128)S(1)} %history.1), channel_id=1, source_target_pairs={{0,1},{1,2},{2,3},{4,5},{5,6},{6,7},{8,9},{9,10},{10,11},{12,13},{... | collective-permute-start | bytes 98312 | tf_op jit(solution)/shard_map/ppermute | solution.py:382
  4.4 14.6 %copy-start.10 = (s32[4]{0:T(128)S(1)}, s32[4]{0:T(128)}, u32[]{:S(2)}) copy-start(s32[4]{0:T(128)} %offs_ref.1) | copy-start | bytes 52
  4.4 14.6 %copy-start.11 = (bf16[512,1024]{1,0:T(8,128)(2,1)S(1)}, bf16[512,1024]{1,0:T(8,128)(2,1)}, u32[]{:S(2)}) copy-start(bf16[512,1024]{1,0:T(8,128)(2,1)} %constant.23.clone.inv_ref) | copy-start | bytes 3145732
  7.9 10.1 %collective-permute-start.1 = (bf16[512,128]{1,0:T(8,128)(2,1)S(1)}, bf16[512,128]{1,0:T(8,128)(2,1)S(1)}, u32[]{:S(2)}, u32[]{:S(2)}) collective-permute-start(bf16[512,128]{1,0:T(8,128)(2,1)S(1)} %get-tuple-element.24), channel_id=1, source_target_pairs={{0,4},{4,8},{8,12},{12,16},{16,20},{20,24},{24,28},{28,0},{1,5},{5... | collective-permute-start | bytes 393224 | tf_op jit(solution)/shard_map/ppermute | solution.py:419
  10.3 8.7 %collective-permute-start.2 = (bf16[512,128]{1,0:T(8,128)(2,1)S(1)}, bf16[512,128]{1,0:T(8,128)(2,1)S(1)}, u32[]{:S(2)}, u32[]{:S(2)}) collective-permute-start(bf16[512,128]{1,0:T(8,128)(2,1)S(1)} %get-tuple-element.25), channel_id=1, source_target_pairs={{4,0},{8,4},{12,8},{16,12},{20,16},{24,20},{28,24},{0,28},{5,1},{9... | collective-permute-start | bytes 393224 | tf_op jit(solution)/shard_map/ppermute | solution.py:420
  13.3 15.3 %all-to-all-start = ((bf16[32,2,16,128]{3,2,1,0:T(8,128)(2,1)}), bf16[32,2,16,128]{3,2,1,0:T(8,128)(2,1)S(1)}, u32[]{:S(2)}, u32[]{:S(2)}) async-start(bf16[32,2,16,128]{3,2,1,0:T(8,128)(2,1)} %get-tuple-element.23.white_ref), calls=%async_computation | async-start | bytes 524288 | tf_op jit(solution)/shard_map/all_to_all | solution.py:415
  18.0 10.6 %copy-start.2 = (bf16[512,512]{1,0:T(8,128)(2,1)S(1)}, bf16[512,512]{1,0:T(8,128)(2,1)}, u32[]{:S(2)}) copy-start(bf16[512,512]{1,0:T(8,128)(2,1)} %constant.25.clone.pack_ref) | copy-start | bytes 1572868
  18.0 10.6 %copy-start.5 = (bf16[128,128]{1,0:T(8,128)(2,1)S(1)}, bf16[128,128]{1,0:T(8,128)(2,1)}, u32[]{:S(2)}) copy-start(bf16[128,128]{1,0:T(8,128)(2,1)} %constant.24.clone.flip_ref) | copy-start | bytes 98308
  18.0 10.6 %copy-start.6 = (s32[8,3]{0,1:T(4,128)S(1)}, s32[8,3]{0,1:T(4,128)}, u32[]{:S(2)}) copy-start(s32[8,3]{0,1:T(4,128)} %param.17) | copy-start | bytes 292
  18.0 10.6 %copy-start.7 = (s32[8]{0:T(128)S(1)}, s32[8]{0:T(128)}, u32[]{:S(2)}) copy-start(s32[8]{0:T(128)} %count_ref.1) | copy-start | bytes 100
  21.1 19.5 %copy-start = (bf16[1024,512]{1,0:T(8,128)(2,1)S(1)}, bf16[1024,512]{1,0:T(8,128)(2,1)}, u32[]{:S(2)}) copy-start(bf16[1024,512]{1,0:T(8,128)(2,1)} %constant.26.clone.inv_ref) | copy-start | bytes 3145732
  21.1 8.8 %collective-permute-start.3 = (bf16[1,256,128]{2,1,0:T(8,128)(2,1)S(1)}, bf16[1,256,128]{2,1,0:T(8,128)(2,1)S(1)}, u32[]{:S(2)}, u32[]{:S(2)}) collective-permute-start(bf16[1,256,128]{2,1,0:T(8,128)(2,1)S(1)} %get-tuple-element.28), channel_id=1, source_target_pairs={{0,1},{1,0},{2,3},{3,2},{4,5},{5,4},{6,7},{7,6},{8,9},{9,8},{10,11... | collective-permute-start | bytes 196616 | tf_op jit(solution)/shard_map/ppermute | solution.py:439
  21.4 8.5 %collective-permute-start.4 = (bf16[1,256,128]{2,1,0:T(8,128)(2,1)S(1)}, bf16[1,256,128]{2,1,0:T(8,128)(2,1)S(1)}, u32[]{:S(2)}, u32[]{:S(2)}) collective-permute-start(bf16[1,256,128]{2,1,0:T(8,128)(2,1)S(1)} %get-tuple-element.29), channel_id=1, source_target_pairs={{0,2},{1,3},{2,0},{3,1},{4,6},{5,7},{6,4},{7,5},{8,10},{9,11},{10,... | collective-permute-start | bytes 196616 | tf_op jit(solution)/shard_map/ppermute | solution.py:439
  22.2 7.7 %collective-permute-start.5 = (bf16[1,256,128]{2,1,0:T(8,128)(2,1)S(1)}, bf16[1,256,128]{2,1,0:T(8,128)(2,1)S(1)}, u32[]{:S(2)}, u32[]{:S(2)}) collective-permute-start(bf16[1,256,128]{2,1,0:T(8,128)(2,1)S(1)} %get-tuple-element.30), channel_id=1, source_target_pairs={{0,3},{1,2},{2,1},{3,0},{4,7},{5,6},{6,5},{7,4},{8,11},{9,10},{10,... | collective-permute-start | bytes 196616 | tf_op jit(solution)/shard_map/ppermute | solution.py:439

commit v18 on v16

--- a/solution.py
+++ b/solution.py
@@ -116,7 +116,16 @@
     copy = pltpu.make_async_copy(rec_hbm.at[:, pl.ds(length - LANES, LANES)], tail_ref, sem)
     copy.start()
     copy.wait()
-    rim_ref[...] = tail_ref[...].T[LANES - TAPS :]
+    tail = tail_ref[...].T[LANES - TAPS :]
+    mean = jnp.sum(tail, axis=0, keepdims=True) * (1.0 / TAPS)
+    high, _ = split(mean)
+    middle, low = split(mean - high.astype(F32))
+    parts = [high, middle, low]
+    row = lax.broadcasted_iota(jnp.int32, (GROUP, LANES), 0)
+    means = jnp.zeros((GROUP, LANES), F32)
+    for i, part in enumerate(parts):
+        means = jnp.where(row == i, part.astype(F32), means)
+    rim_ref[...] = jnp.concatenate([tail - mean, means], axis=0).astype(BF16)
 
 
 def spectrum_kernel(taps_ref, rec_ref, tab_ref, twist_ref, spec_ref, mean_ref, head_ref):
@@ -187,7 +196,9 @@
     down_ref,
 ):
     head_high, head_low = split(head_ref[:, LANES - TAPS :])
-    rim_high, rim_low = split(rim_ref[...] - mean_ref[0:1, :])
+    rim = rim_ref[...].astype(F32)
+    offset = jnp.sum(rim[TAPS:], axis=0, keepdims=True) - mean_ref[0:1, :]
+    rim_high, rim_low = split(rim[:TAPS] + offset)
     history = mm(
         jnp.concatenate([head_high, head_high, head_low], axis=1),
         jnp.concatenate([rim_high, rim_low, rim_high], axis=0),
@@ -371,7 +382,7 @@
     route = [(i, i + 1) for i in range(seg_count - 1)]
     rim = pl.pallas_call(
         rim_kernel,
-        out_shape=jax.ShapeDtypeStruct((TAPS, chans), F32),
+        out_shape=jax.ShapeDtypeStruct((TAPS + GROUP, chans), BF16),
         in_specs=hbm(1),
         out_specs=pl.BlockSpec(memory_space=pltpu.VMEM),
         scratch_shapes=[pltpu.VMEM((chans, LANES), F32), pltpu.SemaphoreType.DMA],

time: 41.9 us -> 41.8 us (level)
  no operation moved by 1% of the time
where the time goes in v18:
time: 41.8 us; the launch traced here: 41.5 us
  starting transfers between devices  14.4 us (34%)
  blocking collectives  10.7 us (26%)
  Pallas kernels  8.85 us (21%)
  waiting for transfers between devices  6.58 us (16%)
  between operations  0.89 us (2%)
    all_to_all x1, blocking collectives, body(): summed = lax.all_to_all(crossed, ('seg', 'chan'), 0, 0, tiled=True)  10.7 us
    all_to_all x1, waiting for transfers between devices, body(): moved = lax.all_to_all(spread, ('seg', 'chan'), 0, 0, tiled=True)  5.52 us
    all_to_all x1, starting transfers between devices, body(): moved = lax.all_to_all(spread, ('seg', 'chan'), 0, 0, tiled=True)  4.58 us
    ppermute x1, starting transfers between devices, body(): after = lax.ppermute(down, 'chan', [(j, i) for i, j in ring])  3.04 us
    ppermute x1, starting transfers between devices, body(): rim = lax.ppermute(rim, 'seg', route)  2.49 us
    ppermute x1, starting transfers between devices, body(): before = lax.ppermute(up, 'chan', ring)  2.35 us
    pallas_call x1, Pallas kernels, body(): pl.pallas_call(near_kernel, out_shape=[jax.ShapeDtypeStruct((near_each, L...  2.07 us
    pallas_call x1, Pallas kernels, body(): pl.pallas_call(spectrum_kernel, out_shape=[jax.ShapeDtypeStruct((2 * BINS...  1.98 us
  transfers between devices with their start and end apart: 7, of which 2 were waited for; matrix products, arithmetic and copies ran while one was open for 0% of the time, Pallas kernels for 13%

profile of v18, /device:TPU:0, one launch (start us, length us, event | category | flops | bytes accessed | tf_op | source)
XLA Modules:
  0.0 41.5 jit_solution(17097375212387343329)
XLA Ops:
  0.6 0.0 copy-start.12
  0.6 0.0 copy-start.13
  0.7 0.0 copy-start.8
  0.7 0.0 copy-start.9
  0.7 1.1 %history.1 = bf16[80,128]{1,0:T(8,128)(2,1)S(1)} custom-call(f32[128,4096]{1,0:T(8,128)} %rec_hbm.1), custom_call_target="tpu_custom_call" | custom-call | flops 10000000000 | bytes 20000000 | tf_op jit(solution)/shard_map/history/pallas_call | solution.py:383
  1.8 0.0 copy-start.1
  1.8 0.0 copy-start.3
  1.8 0.0 copy-start.4
  1.8 2.5 %collective-permute-start = (bf16[80,128]{1,0:T(8,128)(2,1)S(1)}, bf16[80,128]{1,0:T(8,128)(2,1)S(1)}, u32[]{:S(2)}, u32[]{:S(2)}) collective-permute-start(bf16[80,128]{1,0:T(8,128)(2,1)S(1)} %history.1), channel_id=1, source_target_pairs={{0,1},{1,2},{2,3},{4,5},{5,6},{6,7},{8,9},{9,10},{10,11},{12,13},{... | collective-permute-start | bytes 61448 | tf_op jit(solution)/shard_map/ppermute | solution.py:395
  4.3 0.0 copy-done.12
  4.3 0.0 copy-done.13
  4.4 0.0 copy-done.8
  4.4 0.0 copy-done.9
  4.4 0.0 copy-start.10
  4.4 0.0 copy-start.11
  4.4 2.0 %filter_and_transform.1 = (f32[1024,128]{1,0:T(8,128)S(1)}, f32[8,128]{1,0:T(8,128)S(1)}, f32[16,128]{1,0:T(8,128)S(1)}) custom-call(f32[1,64]{1,0:T(1,128)S(1)} %bitcast.8, f32[128,4096]{1,0:T(8,128)S(1)} %copy-done.8, bf16[256,768]{1,0:T(8,128)(2,1)S(1)} %copy-done.12, f32[256,128]{1,0:T(8,128)S(1)} %copy-done.13), custom_call_target="tpu_custom_call" | custom-call | flops 1000000000 | bytes 5000000 | tf_op jit(solution)/shard_map/filter_and_transform/pallas_call | solution.py:397
  6.4 0.0 collective-permute-done.rim_ref
  6.4 0.0 copy-done.1
  6.4 0.0 copy-done.3
  6.4 0.0 copy-done.4
  6.4 1.4 %whiten.1 = (bf16[32,2,16,128]{3,2,1,0:T(8,128)(2,1)}, bf16[512,128]{1,0:T(8,128)(2,1)S(1)}, bf16[512,128]{1,0:T(8,128)(2,1)S(1)}) custom-call(f32[1024,128]{1,0:T(8,128)S(1)} %get-tuple-element.20.spec_ref, bf16[80,128]{1,0:T(8,128)(2,1)S(1)} %collective-permute-done.rim_ref, f32[8,128]{1,0:T(8,128)S(1)} %get-tuple-element.21.mean_ref, ...), custom_call_target="tpu_custom_call" | custom-call | tf_op jit(solution)/shard_map/whiten/pallas_call | solution.py:415
  7.9 2.4 %collective-permute-start.1 = (bf16[512,128]{1,0:T(8,128)(2,1)S(1)}, bf16[512,128]{1,0:T(8,128)(2,1)S(1)}, u32[]{:S(2)}, u32[]{:S(2)}) collective-permute-start(bf16[512,128]{1,0:T(8,128)(2,1)S(1)} %get-tuple-element.24), channel_id=1, source_target_pairs={{0,4},{4,8},{8,12},{12,16},{16,20},{20,24},{24,28},{28,0},{1,5},{5... | collective-permute-start | bytes 393224 | tf_op jit(solution)/shard_map/ppermute | solution.py:432
  10.2 3.0 %collective-permute-start.2 = (bf16[512,128]{1,0:T(8,128)(2,1)S(1)}, bf16[512,128]{1,0:T(8,128)(2,1)S(1)}, u32[]{:S(2)}, u32[]{:S(2)}) collective-permute-start(bf16[512,128]{1,0:T(8,128)(2,1)S(1)} %get-tuple-element.25), channel_id=1, source_target_pairs={{4,0},{8,4},{12,8},{16,12},{20,16},{24,20},{28,24},{0,28},{5,1},{9... | collective-permute-start | bytes 393224 | tf_op jit(solution)/shard_map/ppermute | solution.py:433
  13.3 4.6 %all-to-all-start = ((bf16[32,2,16,128]{3,2,1,0:T(8,128)(2,1)}), bf16[32,2,16,128]{3,2,1,0:T(8,128)(2,1)S(1)}, u32[]{:S(2)}, u32[]{:S(2)}) async-start(bf16[32,2,16,128]{3,2,1,0:T(8,128)(2,1)} %get-tuple-element.23.white_ref), calls=%async_computation | async-start | bytes 524288 | tf_op jit(solution)/shard_map/all_to_all | solution.py:428
  17.8 0.0 copy-start.2
  17.9 0.0 copy-start.5
  17.9 0.0 copy-start.6
  17.9 0.0 copy-start.7
  17.9 0.0 collective-permute-done.1.before_ref
  17.9 1.0 %collective-permute-done.2.after_ref = bf16[512,128]{1,0:T(8,128)(2,1)S(1)} collective-permute-done((bf16[512,128]{1,0:T(8,128)(2,1)S(1)}, bf16[512,128]{1,0:T(8,128)(2,1)S(1)}, u32[]{:S(2)}, u32[]{:S(2)}) %collective-permute-start.2) | collective-permute-done | bytes 131104 | tf_op jit(solution)/shard_map/ppermute | solution.py:433
  19.0 0.0 copy-done.10
  19.0 0.0 copy-done.11
  19.0 2.1 %near_lags.1 = (bf16[1,256,128]{2,1,0:T(8,128)(2,1)S(1)}, bf16[1,256,128]{2,1,0:T(8,128)(2,1)S(1)}, bf16[1,256,128]{2,1,0:T(8,128)(2,1)S(1)}, bf16[1,256,128]{2,1,0:T(8,128)(2,1)S(1)}) custom-call(s32[4]{0:T(128)S(1)} %copy-done.10, bf16[32,2,16,128]{3,2,1,0:T(8,128)(2,1)} %get-tuple-element.23.white_ref, ...), custom_call_target="tpu_custom_call" | custom-call | flops 20000000000 | bytes 20000000 | tf_op jit(solution)/shard_map/near_lags/pallas_call | solution.py:437
  21.0 0.0 copy-start
  21.0 0.3 collective-permute-start.3
  21.4 0.7 %collective-permute-start.4 = (bf16[1,256,128]{2,1,0:T(8,128)(2,1)S(1)}, bf16[1,256,128]{2,1,0:T(8,128)(2,1)S(1)}, u32[]{:S(2)}, u32[]{:S(2)}) collective-permute-start(bf16[1,256,128]{2,1,0:T(8,128)(2,1)S(1)} %get-tuple-element.29), channel_id=1, source_target_pairs={{0,2},{1,3},{2,0},{3,1},{4,6},{5,7},{6,4},{7,5},{8,10},{9,11},{10,... | collective-permute-start | bytes 196616 | tf_op jit(solution)/shard_map/ppermute | solution.py:452
  22.1 0.9 %collective-permute-start.5 = (bf16[1,256,128]{2,1,0:T(8,128)(2,1)S(1)}, bf16[1,256,128]{2,1,0:T(8,128)(2,1)S(1)}, u32[]{:S(2)}, u32[]{:S(2)}) collective-permute-start(bf16[1,256,128]{2,1,0:T(8,128)(2,1)S(1)} %get-tuple-element.30), channel_id=1, source_target_pairs={{0,3},{1,2},{2,1},{3,0},{4,7},{5,6},{6,5},{7,4},{8,11},{9,10},{10,... | collective-permute-start | bytes 196616 | tf_op jit(solution)/shard_map/ppermute | solution.py:452
  23.0 5.5 %all-to-all-done = bf16[32,2,16,128]{3,2,1,0:T(8,128)(2,1)S(1)} async-done(((bf16[32,2,16,128]{3,2,1,0:T(8,128)(2,1)}), bf16[32,2,16,128]{3,2,1,0:T(8,128)(2,1)S(1)}, u32[]{:S(2)}, u32[]{:S(2)}) %all-to-all-start) | async-done | bytes 262176 | tf_op jit(solution)/shard_map/all_to_all | solution.py:428
  28.5 0.0 copy-done.2
  28.5 0.0 copy-done.5
  28.5 0.0 copy-done.6
  28.5 1.2 %loop_spectra.1 = bf16[4,8,24,128]{3,2,1,0:T(8,128)(2,1)S(1)} custom-call(s32[3,8]{1,0:T(4,128)S(1)} %bitcast.7, s32[8]{0:T(128)S(1)} %copy-done.7, bf16[128,128]{1,0:T(8,128)(2,1)S(1)} %copy-done.5, bf16[512,512]{1,0:T(8,128)(2,1)S(1)} %copy-done.2, bf16[4,8,2,16,128]{4,3,2,1,0:T(8,128)(2,1)S(1)} %bitcast.5), custom_call_target="tpu_custom_call" | custom-call | tf_op jit(solution)/shard_map/loop_spectra/pallas_call | solution.py:473
  29.8 0.0 collective-permute-done.3.refs_1_
  29.8 0.0 collective-permute-done.4.refs_2_
  29.8 0.0 collective-permute-done.5.refs_3_
  29.8 10.7 %all_to_all.10.spec_ref = bf16[32,24,128]{2,1,0:T(8,128)(2,1)S(1)} all-to-all(bf16[32,24,128]{2,1,0:T(8,128)(2,1)S(1)} %bitcast.6), channel_id=1, replica_groups=mesh['chan'=8,'seg'=4] {'seg','chan'}, dimensions={0} | all-to-all | bytes 393216 | tf_op jit(solution)/shard_map/all_to_all | solution.py:483
  40.5 0.0 copy-done
  40.5 1.0 %lags.1 = (f32[128,1,256]{2,1,0:T(1,128)}, f32[96,256]{1,0:T(8,128)}) custom-call(bf16[32,24,128]{2,1,0:T(8,128)(2,1)S(1)} %all_to_all.10.spec_ref, bf16[1024,512]{1,0:T(8,128)(2,1)S(1)} %copy-done, bf16[1,256,128]{2,1,0:T(8,128)(2,1)S(1)} %get-tuple-element.32.refs_0_, bf16[1,256,128]{2,1,0:T(8,128)(2,1)S(1)} %collective-permute-done.3.refs_1_, ...), custom_call_target="tpu_custom_call" | custom-call | tf_op jit(solution)/shard_map/lags/pallas_call | solution.py:487
  (1 shorter events, 0.0 us)
Async XLA Ops:
  0.6 3.7 %copy-start.12 = (bf16[256,768]{1,0:T(8,128)(2,1)S(1)}, bf16[256,768]{1,0:T(8,128)(2,1)}, u32[]{:S(2)}) copy-start(bf16[256,768]{1,0:T(8,128)(2,1)} %constant.18.clone.tab_ref) | copy-start | bytes 1179652
  0.6 3.7 %copy-start.13 = (f32[256,128]{1,0:T(8,128)S(1)}, f32[256,128]{1,0:T(8,128)}, u32[]{:S(2)}) copy-start(f32[256,128]{1,0:T(8,128)} %constant.19.clone.twist_ref) | copy-start | bytes 393220
  0.7 3.7 %copy-start.8 = (f32[128,4096]{1,0:T(8,128)S(1)}, f32[128,4096]{1,0:T(8,128)}, u32[]{:S(2)}) copy-start(f32[128,4096]{1,0:T(8,128)} %rec_hbm.1) | copy-start | bytes 6291460
  0.7 3.7 %copy-start.9 = (f32[64]{0:T(128)S(1)}, f32[64]{0:T(128)}, u32[]{:S(2)}) copy-start(f32[64]{0:T(128)} %param.15) | copy-start | bytes 772
  1.8 4.6 %copy-start.1 = (bf16[512,512]{1,0:T(8,128)(2,1)S(1)}, bf16[512,512]{1,0:T(8,128)(2,1)}, u32[]{:S(2)}) copy-start(bf16[512,512]{1,0:T(8,128)(2,1)} %constant.21.clone.band_ref) | copy-start | bytes 1572868
  1.8 4.6 %copy-start.3 = (f32[512,128]{1,0:T(8,128)S(1)}, f32[512,128]{1,0:T(8,128)}, u32[]{:S(2)}) copy-start(f32[512,128]{1,0:T(8,128)} %constant.22.clone.share_ref) | copy-start | bytes 786436
  1.8 4.6 %copy-start.4 = (bf16[1024,128]{1,0:T(8,128)(2,1)S(1)}, bf16[1024,128]{1,0:T(8,128)(2,1)}, u32[]{:S(2)}) copy-start(bf16[1024,128]{1,0:T(8,128)(2,1)} %constant.20.clone.edge_ref) | copy-start | bytes 786436
  1.8 4.6 %collective-permute-start = (bf16[80,128]{1,0:T(8,128)(2,1)S(1)}, bf16[80,128]{1,0:T(8,128)(2,1)S(1)}, u32[]{:S(2)}, u32[]{:S(2)}) collective-permute-start(bf16[80,128]{1,0:T(8,128)(2,1)S(1)} %history.1), channel_id=1, source_target_pairs={{0,1},{1,2},{2,3},{4,5},{5,6},{6,7},{8,9},{9,10},{10,11},{12,13},{... | collective-permute-start | bytes 61448 | tf_op jit(solution)/shard_map/ppermute | solution.py:395
  4.4 14.6 %copy-start.10 = (s32[4]{0:T(128)S(1)}, s32[4]{0:T(128)}, u32[]{:S(2)}) copy-start(s32[4]{0:T(128)} %offs_ref.1) | copy-start | bytes 52
  4.4 14.6 %copy-start.11 = (bf16[512,1024]{1,0:T(8,128)(2,1)S(1)}, bf16[512,1024]{1,0:T(8,128)(2,1)}, u32[]{:S(2)}) copy-start(bf16[512,1024]{1,0:T(8,128)(2,1)} %constant.23.clone.inv_ref) | copy-start | bytes 3145732
  7.9 10.0 %collective-permute-start.1 = (bf16[512,128]{1,0:T(8,128)(2,1)S(1)}, bf16[512,128]{1,0:T(8,128)(2,1)S(1)}, u32[]{:S(2)}, u32[]{:S(2)}) collective-permute-start(bf16[512,128]{1,0:T(8,128)(2,1)S(1)} %get-tuple-element.24), channel_id=1, source_target_pairs={{0,4},{4,8},{8,12},{12,16},{16,20},{20,24},{24,28},{28,0},{1,5},{5... | collective-permute-start | bytes 393224 | tf_op jit(solution)/shard_map/ppermute | solution.py:432
  10.2 8.7 %collective-permute-start.2 = (bf16[512,128]{1,0:T(8,128)(2,1)S(1)}, bf16[512,128]{1,0:T(8,128)(2,1)S(1)}, u32[]{:S(2)}, u32[]{:S(2)}) collective-permute-start(bf16[512,128]{1,0:T(8,128)(2,1)S(1)} %get-tuple-element.25), channel_id=1, source_target_pairs={{4,0},{8,4},{12,8},{16,12},{20,16},{24,20},{28,24},{0,28},{5,1},{9... | collective-permute-start | bytes 393224 | tf_op jit(solution)/shard_map/ppermute | solution.py:433
  13.3 15.2 %all-to-all-start = ((bf16[32,2,16,128]{3,2,1,0:T(8,128)(2,1)}), bf16[32,2,16,128]{3,2,1,0:T(8,128)(2,1)S(1)}, u32[]{:S(2)}, u32[]{:S(2)}) async-start(bf16[32,2,16,128]{3,2,1,0:T(8,128)(2,1)} %get-tuple-element.23.white_ref), calls=%async_computation | async-start | bytes 524288 | tf_op jit(solution)/shard_map/all_to_all | solution.py:428
  17.8 10.6 %copy-start.2 = (bf16[512,512]{1,0:T(8,128)(2,1)S(1)}, bf16[512,512]{1,0:T(8,128)(2,1)}, u32[]{:S(2)}) copy-start(bf16[512,512]{1,0:T(8,128)(2,1)} %constant.25.clone.pack_ref) | copy-start | bytes 1572868
  17.9 10.6 %copy-start.5 = (bf16[128,128]{1,0:T(8,128)(2,1)S(1)}, bf16[128,128]{1,0:T(8,128)(2,1)}, u32[]{:S(2)}) copy-start(bf16[128,128]{1,0:T(8,128)(2,1)} %constant.24.clone.flip_ref) | copy-start | bytes 98308
  17.9 10.6 %copy-start.6 = (s32[8,3]{0,1:T(4,128)S(1)}, s32[8,3]{0,1:T(4,128)}, u32[]{:S(2)}) copy-start(s32[8,3]{0,1:T(4,128)} %param.17) | copy-start | bytes 292
  17.9 10.6 %copy-start.7 = (s32[8]{0:T(128)S(1)}, s32[8]{0:T(128)}, u32[]{:S(2)}) copy-start(s32[8]{0:T(128)} %count_ref.1) | copy-start | bytes 100
  21.0 19.5 %copy-start = (bf16[1024,512]{1,0:T(8,128)(2,1)S(1)}, bf16[1024,512]{1,0:T(8,128)(2,1)}, u32[]{:S(2)}) copy-start(bf16[1024,512]{1,0:T(8,128)(2,1)} %constant.26.clone.inv_ref) | copy-start | bytes 3145732
  21.0 8.7 %collective-permute-start.3 = (bf16[1,256,128]{2,1,0:T(8,128)(2,1)S(1)}, bf16[1,256,128]{2,1,0:T(8,128)(2,1)S(1)}, u32[]{:S(2)}, u32[]{:S(2)}) collective-permute-start(bf16[1,256,128]{2,1,0:T(8,128)(2,1)S(1)} %get-tuple-element.28), channel_id=1, source_target_pairs={{0,1},{1,0},{2,3},{3,2},{4,5},{5,4},{6,7},{7,6},{8,9},{9,8},{10,11... | collective-permute-start | bytes 196616 | tf_op jit(solution)/shard_map/ppermute | solution.py:452
  21.4 8.4 %collective-permute-start.4 = (bf16[1,256,128]{2,1,0:T(8,128)(2,1)S(1)}, bf16[1,256,128]{2,1,0:T(8,128)(2,1)S(1)}, u32[]{:S(2)}, u32[]{:S(2)}) collective-permute-start(bf16[1,256,128]{2,1,0:T(8,128)(2,1)S(1)} %get-tuple-element.29), channel_id=1, source_target_pairs={{0,2},{1,3},{2,0},{3,1},{4,6},{5,7},{6,4},{7,5},{8,10},{9,11},{10,... | collective-permute-start | bytes 196616 | tf_op jit(solution)/shard_map/ppermute | solution.py:452
  22.1 7.7 %collective-permute-start.5 = (bf16[1,256,128]{2,1,0:T(8,128)(2,1)S(1)}, bf16[1,256,128]{2,1,0:T(8,128)(2,1)S(1)}, u32[]{:S(2)}, u32[]{:S(2)}) collective-permute-start(bf16[1,256,128]{2,1,0:T(8,128)(2,1)S(1)} %get-tuple-element.30), channel_id=1, source_target_pairs={{0,3},{1,2},{2,1},{3,0},{4,7},{5,6},{6,5},{7,4},{8,11},{9,10},{10,... | collective-permute-start | bytes 196616 | tf_op jit(solution)/shard_map/ppermute | solution.py:452

commit v19 on v16

--- a/solution.py
+++ b/solution.py
@@ -183,8 +183,6 @@
     band_ref,
     share_ref,
     white_ref,
-    up_ref,
-    down_ref,
 ):
     head_high, head_low = split(head_ref[:, LANES - TAPS :])
     rim_high, rim_low = split(rim_ref[...] - mean_ref[0:1, :])
@@ -205,18 +203,14 @@
     scale = 1.0 / (smoothed + (WATER * level + 1e-06))
     white = parted * scale.reshape(GROUPS, 1, GROUP, LANES)
     white_ref[...] = white.astype(BF16)
-    flat = white.reshape(2 * BINS, LANES)
-    turned = pltpu.roll(flat, SPAN, 1)
-    lane = lax.broadcasted_iota(jnp.int32, (BINS, LANES), 1)
-    up_ref[...] = jnp.where(lane < SPAN, turned[:BINS], flat[BINS:]).astype(BF16)
-    down_ref[...] = jnp.where(lane < SPAN, flat[:BINS], turned[BINS:]).astype(BF16)
 
 
 def offset_moves(offs_ref):
     row = lax.broadcasted_iota(jnp.int32, (2 * LANES, LANES), 0)
     channel = lax.broadcasted_iota(jnp.int32, (2 * LANES, LANES), 1)
-    distance = jnp.where(row < LANES + SPAN, row, row - 2 * LANES) - channel
-    hits = [(distance == offs_ref[o]).astype(F32) for o in range(offs_ref.shape[0])]
+    distance = row - (channel + SPAN)
+    offsets = [0] + [offs_ref[o] for o in range(offs_ref.shape[0])]
+    hits = [(distance == offset).astype(F32) for offset in offsets]
     return jnp.concatenate(hits, axis=1).astype(BF16)
 
 
@@ -234,22 +228,16 @@
     return place ^ r if owners & (owners - 1) == 0 else (place + r) % owners
 
 
-def near_kernel(offs_ref, white_ref, before_ref, after_ref, inv_ref, *refs):
+def near_kernel(offs_ref, white_ref, before_ref, inv_ref, *refs):
     out_refs, lags_ref = refs[:-1], refs[-1]
     rows = white_ref.shape[0] * 2 * GROUP
-    half = rows // 2
     noff = lags_ref.shape[0]
-    before, after = before_ref[...].astype(F32), after_ref[...].astype(F32)
-    lane = lax.broadcasted_iota(jnp.int32, (half, LANES), 1)
-    upper = jnp.where(lane < SPAN, after, pltpu.roll(before, SPAN, 1))
-    lower = jnp.where(lane < SPAN, pltpu.roll(after, SPAN, 1), before)
-    edge = jnp.concatenate([upper, lower], axis=0).astype(BF16)
-    own = white_ref[...].reshape(rows, LANES)
-    far = mm(jnp.concatenate([own, edge], axis=1), offset_moves(offs_ref))
-    own = own.astype(F32).reshape(-1, 2, GROUP, LANES)
+    blocks = [ref[...].reshape(rows, LANES) for ref in (before_ref, white_ref)]
+    far = mm(jnp.concatenate(blocks, axis=1), offset_moves(offs_ref))
+    own = far[:, :LANES].reshape(-1, 2, GROUP, LANES)
     columns = []
     for o in range(noff):
-        other = far[:, o * LANES : (o + 1) * LANES].reshape(own.shape)
+        other = far[:, (o + 1) * LANES : (o + 2) * LANES].reshape(own.shape)
         real = own[:, 0] * other[:, 0] + own[:, 1] * other[:, 1]
         imag = own[:, 1] * other[:, 0] - own[:, 0] * other[:, 1]
         columns.append(jnp.stack([real, imag], axis=1).reshape(rows, LANES).astype(BF16))
@@ -257,19 +245,31 @@
     lags = both[:LAGS] + both[LAGS:]
     for o in range(noff):
         lags_ref[o] = lags[:, o * LANES : (o + 1) * LANES]
-    owners = len(out_refs)
+    owners = len(out_refs) // 2
     each = noff // owners
     place = lax.axis_index("seg")
+    half = LAGS // 2
+    lane = lax.broadcasted_iota(jnp.int32, (half, LANES), 1)
     for r in range(owners):
         first = partner_of(place, r, owners) * each
-        out_refs[r][...] = lags_ref[pl.ds(first, each)].astype(BF16)
+        for t in range(each):
+            upper, lower = lags_ref[first + t, :half], lags_ref[first + t, half:]
+            mine = jnp.where(lane < SPAN, pltpu.roll(upper, SPAN, 1), lower)
+            theirs = jnp.where(lane < SPAN, upper, pltpu.roll(lower, SPAN, 1))
+            out_refs[r][t] = mine.astype(BF16)
+            out_refs[owners + r][t] = theirs.astype(BF16)
 
 
 def turn_kernel(*refs):
     near_ref = refs[-1]
-    total = sum(ref[...].astype(F32) for ref in refs[:-1])
+    owners = (len(refs) - 1) // 2
+    first = sum(ref[...].astype(F32) for ref in refs[:owners])
+    second = sum(ref[...].astype(F32) for ref in refs[owners:-1])
+    lane = lax.broadcasted_iota(jnp.int32, first.shape[1:], 1)
     for t in range(near_ref.shape[1]):
-        near_ref[:, t, :] = total[t].T
+        upper = jnp.where(lane < SPAN, first[t], pltpu.roll(second[t], SPAN, 1))
+        lower = jnp.where(lane < SPAN, pltpu.roll(first[t], SPAN, 1), second[t])
+        near_ref[:, t, :] = jnp.concatenate([upper, lower], axis=0).T
 
 
 def loop_kernel(partner_ref, count_ref, flip_ref, pack_ref, white_ref, out_ref):
@@ -400,12 +400,11 @@
     )(taps, recording, short_table(), twiddle_table())
 
     band, band_share = band_tables()
-    half = jax.ShapeDtypeStruct((BINS, LANES), BF16)
-    white, up, down = pl.pallas_call(
+    white = pl.pallas_call(
         whiten_kernel,
-        out_shape=[jax.ShapeDtypeStruct((GROUPS, 2, GROUP, LANES), BF16), half, half],
+        out_shape=jax.ShapeDtypeStruct((GROUPS, 2, GROUP, LANES), BF16),
         in_specs=vmem(7),
-        out_specs=vmem(3),
+        out_specs=pl.BlockSpec(memory_space=pltpu.VMEM),
         compiler_params=PARAMS,
         name="whiten",
     )(spec, rim, mean, head, edge_table(), band, band_share)
@@ -418,27 +417,33 @@
     moved = moved.reshape(seg_count, chan_count, 2, bins, LANES)
 
     ring = [(i, (i + 1) % chan_count) for i in range(chan_count)]
-    before = lax.ppermute(up, "chan", ring)
-    after = lax.ppermute(down, "chan", [(j, i) for i, j in ring])
+    before = lax.ppermute(white, "chan", ring)
     order = np.repeat(bin_order().reshape(GROUPS, 1, GROUP), 2, axis=1).reshape(-1)
     part = np.broadcast_to(np.arange(2).reshape(1, 2, 1), (GROUPS, 2, GROUP)).reshape(-1)
     inverse = np.concatenate(split_np(inverse_table(seg_count, order, part)), axis=0)
     lags = pl.pallas_call(
         near_kernel,
-        out_shape=[jax.ShapeDtypeStruct((near_each, LAGS, LANES), BF16)] * seg_count,
-        in_specs=smem(1) + vmem(4),
-        out_specs=vmem(seg_count),
+        out_shape=[jax.ShapeDtypeStruct((near_each, LAGS // 2, LANES), BF16)] * (2 * seg_count),
+        in_specs=smem(1) + vmem(3),
+        out_specs=vmem(2 * seg_count),
         scratch_shapes=[pltpu.VMEM((noff, LAGS, LANES), F32)],
         compiler_params=PARAMS,
         cost_estimate=pl.CostEstimate(
             flops=20_000_000_000, bytes_accessed=20_000_000, transcendentals=0
         ),
         name="near_lags",
-    )(offsets, white, before, after, inverse)
+    )(offsets, white, before, inverse)
     lags = list(lags)
     for r in range(seg_count - 1, 0, -1):
         route = [(i, partner_of(i, r, seg_count)) for i in range(seg_count)]
         lags[r] = lax.ppermute(lags[r], "seg", route)
+    for r in range(seg_count - 1, -1, -1):
+        route = [
+            (c * seg_count + i, (c - 1) % chan_count * seg_count + partner_of(i, r, seg_count))
+            for c in range(chan_count)
+            for i in range(seg_count)
+        ]
+        lags[seg_count + r] = lax.ppermute(lags[seg_count + r], ("chan", "seg"), route)
     moved, lags[0] = lax.optimization_barrier((moved, lags[0]))
 
     near_shape = jax.ShapeDtypeStruct((chans, near_each, LAGS), F32)
@@ -450,7 +455,7 @@
         near = pl.pallas_call(
             turn_kernel,
             out_shape=near_shape,
-            in_specs=vmem(seg_count),
+            in_specs=vmem(2 * seg_count),
             out_specs=pl.BlockSpec(memory_space=pltpu.VMEM),
             compiler_params=PARAMS,
             name="near_turn",
@@ -476,7 +481,7 @@
     near, loop = pl.pallas_call(
         functools.partial(last_kernel, slots),
         out_shape=[near_shape, jax.ShapeDtypeStruct((slots * share, LAGS), F32)],
-        in_specs=vmem(2 + seg_count),
+        in_specs=vmem(2 + 2 * seg_count),
         out_specs=vmem(2),
         compiler_params=PARAMS,
         name="lags",

time: 41.9 us -> 47.7 us (1.14)
  starting transfers between devices: 14.5 us -> 19.2 us
  blocking collectives: 10.7 us -> 13.7 us
  waiting for transfers between devices: 6.58 us -> 4.55 us
    all_to_all x1, waiting for transfers between devices: 5.69 us -> 0.01 us  [body(): moved = lax.all_to_all(spread, ('seg', 'chan'), 0, 0, tiled=True)]
    ppermute x2 -> x5, waiting for transfers between devices: 0.88 us -> 4.54 us  [the longest x1 2.94 us: body(): before = lax.ppermute(white, 'chan', ring)]
    all_to_all x1, blocking collectives: 10.7 us -> 13.7 us  [body(): summed = lax.all_to_all(crossed, ('seg', 'chan'), 0, 0, tiled=True)]
    ppermute x2 -> x5, starting transfers between devices: 5.4 us -> 7.73 us  [the longest x4 5.37 us: body(): lax.ppermute(lags[seg_count + r], ('chan', 'seg'), route)]
    all_to_all x1, starting transfers between devices: 4.73 us -> 6.32 us  [body(): moved = lax.all_to_all(spread, ('seg', 'chan'), 0, 0, tiled=True)]
    ppermute x3, starting transfers between devices: 1.93 us -> 2.72 us  [body(): lags[r] = lax.ppermute(lags[r], 'seg', route)]
  transfers between devices with their start and end apart: 7 -> 10, of which waited for: 2 -> 2; matrix products, arithmetic and copies ran while one was open for 0% -> 0% of each run, Pallas kernels for 13% -> 11%
where the time goes in v19:
time: 47.7 us; the launch traced here: 47.4 us
  starting transfers between devices  19.2 us (40%)
  blocking collectives  13.7 us (29%)
  Pallas kernels  8.98 us (19%)
  waiting for transfers between devices  4.55 us (10%)
  between operations  0.89 us (2%)
    all_to_all x1, blocking collectives, body(): summed = lax.all_to_all(crossed, ('seg', 'chan'), 0, 0, tiled=True)  13.7 us
    all_to_all x1, starting transfers between devices, body(): moved = lax.all_to_all(spread, ('seg', 'chan'), 0, 0, tiled=True)  6.32 us
    ppermute x4, starting transfers between devices, body(): lax.ppermute(lags[seg_count + r], ('chan', 'seg'), route)  5.37 us
    ppermute x1, waiting for transfers between devices, body(): before = lax.ppermute(white, 'chan', ring)  2.94 us
    ppermute x3, starting transfers between devices, body(): lags[r] = lax.ppermute(lags[r], 'seg', route)  2.72 us
    ppermute x1, starting transfers between devices, body(): rim = lax.ppermute(rim, 'seg', route)  2.49 us
    ppermute x1, starting transfers between devices, body(): before = lax.ppermute(white, 'chan', ring)  2.35 us
    pallas_call x1, Pallas kernels, body(): pl.pallas_call(near_kernel, out_shape=[jax.ShapeDtypeStruct((near_each, L...  2.24 us
  transfers between devices with their start and end apart: 10, of which 2 were waited for; matrix products, arithmetic and copies ran while one was open for 0% of the time, Pallas kernels for 11%

profile of v19, /device:TPU:0, one launch (start us, length us, event | category | flops | bytes accessed | tf_op | source)
XLA Modules:
  0.0 47.4 jit_solution(17561837582016560294)
XLA Ops:
  0.6 0.0 copy-start.12
  0.6 0.0 copy-start.13
  0.7 0.0 copy-start.8
  0.7 0.0 copy-start.9
  0.7 1.1 %history.1 = f32[64,128]{1,0:T(8,128)S(1)} custom-call(f32[128,4096]{1,0:T(8,128)} %rec_hbm.1), custom_call_target="tpu_custom_call" | custom-call | flops 10000000000 | bytes 20000000 | tf_op jit(solution)/shard_map/history/pallas_call | solution.py:372
  1.8 0.0 copy-start.1
  1.8 0.0 copy-start.3
  1.8 0.0 copy-start.4
  1.8 2.5 %collective-permute-start = (f32[64,128]{1,0:T(8,128)S(1)}, f32[64,128]{1,0:T(8,128)S(1)}, u32[]{:S(2)}, u32[]{:S(2)}) collective-permute-start(f32[64,128]{1,0:T(8,128)S(1)} %history.1), channel_id=1, source_target_pairs={{0,1},{1,2},{2,3},{4,5},{5,6},{6,7},{8,9},{9,10},{10,11},{12,13},{... | collective-permute-start | bytes 98312 | tf_op jit(solution)/shard_map/ppermute | solution.py:384
  4.3 0.0 copy-done.12
  4.3 0.0 copy-done.13
  4.3 0.0 copy-done.8
  4.3 0.0 copy-done.9
  4.4 2.0 %filter_and_transform.1 = (f32[1024,128]{1,0:T(8,128)S(1)}, f32[8,128]{1,0:T(8,128)S(1)}, f32[16,128]{1,0:T(8,128)S(1)}) custom-call(f32[1,64]{1,0:T(1,128)S(1)} %bitcast.8, f32[128,4096]{1,0:T(8,128)S(1)} %copy-done.8, bf16[256,768]{1,0:T(8,128)(2,1)S(1)} %copy-done.12, f32[256,128]{1,0:T(8,128)S(1)} %copy-done.13), custom_call_target="tpu_custom_call" | custom-call | flops 1000000000 | bytes 5000000 | tf_op jit(solution)/shard_map/filter_and_transform/pallas_call | solution.py:386
  6.3 0.0 copy-start.10
  6.3 0.0 copy-start.11
  6.3 0.0 collective-permute-done.rim_ref
  6.4 0.0 copy-done.1
  6.4 0.0 copy-done.3
  6.4 1.4 %whiten.1.white_ref = bf16[32,2,16,128]{3,2,1,0:T(8,128)(2,1)} custom-call(f32[1024,128]{1,0:T(8,128)S(1)} %get-tuple-element.25.spec_ref, f32[64,128]{1,0:T(8,128)S(1)} %collective-permute-done.rim_ref, f32[8,128]{1,0:T(8,128)S(1)} %get-tuple-element.26.mean_ref, f32[16,128]{1,0:T(8,128)S(1)} %get-tuple-element.27.head_ref, ...), custom_call_target="tpu_custom_call" | custom-call | tf_op jit(solution)/shard_map/whiten/pallas_call | solution.py:403
  7.8 2.4 %collective-permute-start.1 = (bf16[32,2,16,128]{3,2,1,0:T(8,128)(2,1)}, bf16[32,2,16,128]{3,2,1,0:T(8,128)(2,1)S(1)}, u32[]{:S(2)}, u32[]{:S(2)}) collective-permute-start(bf16[32,2,16,128]{3,2,1,0:T(8,128)(2,1)} %whiten.1.white_ref), channel_id=1, source_target_pairs={{0,4},{4,8},{8,12},{12,16},{16,20},{20,24},{24,28},{28,0},{1,5},{5... | collective-permute-start | bytes 786440 | tf_op jit(solution)/shard_map/ppermute | solution.py:420
  10.2 6.3 %all-to-all-start = ((bf16[32,2,16,128]{3,2,1,0:T(8,128)(2,1)}), bf16[32,2,16,128]{3,2,1,0:T(8,128)(2,1)S(1)}, u32[]{:S(2)}, u32[]{:S(2)}) async-start(bf16[32,2,16,128]{3,2,1,0:T(8,128)(2,1)} %whiten.1.white_ref), calls=%async_computation | async-start | bytes 524288 | tf_op jit(solution)/shard_map/all_to_all | solution.py:416
  16.5 0.0 copy-start.2
  16.5 0.0 copy-start.5
  16.5 0.0 copy-start.6
  16.5 0.0 copy-start.7
  16.5 2.9 %collective-permute-done.1.before_ref = bf16[32,2,16,128]{3,2,1,0:T(8,128)(2,1)S(1)} collective-permute-done((bf16[32,2,16,128]{3,2,1,0:T(8,128)(2,1)}, bf16[32,2,16,128]{3,2,1,0:T(8,128)(2,1)S(1)}, u32[]{:S(2)}, u32[]{:S(2)}) %collective-permute-start.1) | collective-permute-done | bytes 262176 | tf_op jit(solution)/shard_map/ppermute | solution.py:420
  19.5 0.0 copy-done.11
  19.5 2.2 %near_lags.1 = (bf16[1,128,128]{2,1,0:T(8,128)(2,1)S(1)}, bf16[1,128,128]{2,1,0:T(8,128)(2,1)S(1)}, bf16[1,128,128]{2,1,0:T(8,128)(2,1)S(1)}, bf16[1,128,128]{2,...) custom-call(s32[4]{0:T(128)S(1)} %copy-done.10, ...), custom_call_target="tpu_custom_call" | custom-call | flops 20000000000 | bytes 20000000 | tf_op jit(solution)/shard_map/near_lags/pallas_call | solution.py:424
  21.7 0.0 copy-start
  21.7 1.3 %collective-permute-start.2 = (bf16[1,128,128]{2,1,0:T(8,128)(2,1)S(1)}, bf16[1,128,128]{2,1,0:T(8,128)(2,1)S(1)}, u32[]{:S(2)}, u32[]{:S(2)}) collective-permute-start(bf16[1,128,128]{2,1,0:T(8,128)(2,1)S(1)} %get-tuple-element.30), channel_id=1, source_target_pairs={{0,1},{1,0},{2,3},{3,2},{4,5},{5,4},{6,7},{7,6},{8,9},{9,8},{10,11... | collective-permute-start | bytes 98312 | tf_op jit(solution)/shard_map/ppermute | solution.py:439
  23.0 0.2 collective-permute-start.3
  23.3 1.2 %collective-permute-start.4 = (bf16[1,128,128]{2,1,0:T(8,128)(2,1)S(1)}, bf16[1,128,128]{2,1,0:T(8,128)(2,1)S(1)}, u32[]{:S(2)}, u32[]{:S(2)}) collective-permute-start(bf16[1,128,128]{2,1,0:T(8,128)(2,1)S(1)} %get-tuple-element.32), channel_id=1, source_target_pairs={{0,3},{1,2},{2,1},{3,0},{4,7},{5,6},{6,5},{7,4},{8,11},{9,10},{10,... | collective-permute-start | bytes 98312 | tf_op jit(solution)/shard_map/ppermute | solution.py:439
  24.5 2.0 %collective-permute-start.5 = (bf16[1,128,128]{2,1,0:T(8,128)(2,1)S(1)}, bf16[1,128,128]{2,1,0:T(8,128)(2,1)S(1)}, u32[]{:S(2)}, u32[]{:S(2)}) collective-permute-start(bf16[1,128,128]{2,1,0:T(8,128)(2,1)S(1)} %get-tuple-element.33), channel_id=1, source_target_pairs={{0,28},{1,29},{2,30},{3,31},{4,0},{5,1},{6,2},{7,3},{8,4},{9,5},{1... | collective-permute-start | bytes 98312 | tf_op jit(solution)/shard_map/ppermute | solution.py:446
  26.5 1.4 %collective-permute-start.6 = (bf16[1,128,128]{2,1,0:T(8,128)(2,1)S(1)}, bf16[1,128,128]{2,1,0:T(8,128)(2,1)S(1)}, u32[]{:S(2)}, u32[]{:S(2)}) collective-permute-start(bf16[1,128,128]{2,1,0:T(8,128)(2,1)S(1)} %get-tuple-element.34), channel_id=1, source_target_pairs={{0,29},{1,28},{2,31},{3,30},{4,1},{5,0},{6,3},{7,2},{8,5},{9,4},{1... | collective-permute-start | bytes 98312 | tf_op jit(solution)/shard_map/ppermute | solution.py:446
  27.9 0.0 collective-permute-done.2.refs_1_
  27.9 0.1 collective-permute-start.7
  28.0 0.0 collective-permute-done.3.refs_2_
  28.0 1.8 %collective-permute-start.8 = (bf16[1,128,128]{2,1,0:T(8,128)(2,1)S(1)}, bf16[1,128,128]{2,1,0:T(8,128)(2,1)S(1)}, u32[]{:S(2)}, u32[]{:S(2)}) collective-permute-start(bf16[1,128,128]{2,1,0:T(8,128)(2,1)S(1)} %get-tuple-element.36), channel_id=1, source_target_pairs={{0,31},{1,30},{2,29},{3,28},{4,3},{5,2},{6,1},{7,0},{8,7},{9,6},{1... | collective-permute-start | bytes 98312 | tf_op jit(solution)/shard_map/ppermute | solution.py:446
  29.8 0.0 all-to-all-done
  29.9 1.2 %loop_spectra.1 = bf16[4,8,24,128]{3,2,1,0:T(8,128)(2,1)S(1)} custom-call(s32[3,8]{1,0:T(4,128)S(1)} %bitcast.7, s32[8]{0:T(128)S(1)} %copy-done.7, bf16[128,128]{1,0:T(8,128)(2,1)S(1)} %copy-done.5, bf16[512,512]{1,0:T(8,128)(2,1)S(1)} %copy-done.2, bf16[4,8,2,16,128]{4,3,2,1,0:T(8,128)(2,1)S(1)} %bitcast.5), custom_call_target="tpu_custom_call" | custom-call | tf_op jit(solution)/shard_map/loop_spectra/pallas_call | solution.py:467
  31.1 0.0 collective-permute-done.4.refs_3_
  31.1 0.0 collective-permute-done.5.refs_4_
  31.1 0.0 collective-permute-done.6.refs_5_
  31.2 1.6 %collective-permute-done.7.refs_6_ = bf16[1,128,128]{2,1,0:T(8,128)(2,1)S(1)} collective-permute-done((bf16[1,128,128]{2,1,0:T(8,128)(2,1)S(1)}, bf16[1,128,128]{2,1,0:T(8,128)(2,1)S(1)}, u32[]{:S(2)}, u32[]{:S(2)}) %collective-permute-start.7) | collective-permute-done | bytes 32800 | tf_op jit(solution)/shard_map/ppermute | solution.py:446
  32.7 0.0 collective-permute-done.8.refs_7_
  32.7 13.7 %all_to_all.10.spec_ref = bf16[32,24,128]{2,1,0:T(8,128)(2,1)S(1)} all-to-all(bf16[32,24,128]{2,1,0:T(8,128)(2,1)S(1)} %bitcast.6), channel_id=1, replica_groups=mesh['chan'=8,'seg'=4] {'seg','chan'}, dimensions={0} | all-to-all | bytes 393216 | tf_op jit(solution)/shard_map/all_to_all | solution.py:477
  46.4 1.0 %lags.1 = (f32[128,1,256]{2,1,0:T(1,128)}, f32[96,256]{1,0:T(8,128)}) custom-call(bf16[32,24,128]{2,1,0:T(8,128)(2,1)S(1)} %all_to_all.10.spec_ref, bf16[1024,512]{1,0:T(8,128)(2,1)S(1)} %copy-done, bf16[1,128,128]{2,1,0:T(8,128)(2,1)S(1)} %get-tuple-element.38.refs_0_, bf16[1,128,128]{2,1,0:T(8,128)(2,1)S(1)} %collective-permute-done.2.refs_1_, ...), custom_call_target="tpu_custom_call" | custom-call | tf_op jit(solution)/shard_map/lags/pallas_call | solution.py:481
  (7 shorter events, 0.0 us)
Async XLA Ops:
  0.6 3.7 %copy-start.12 = (bf16[256,768]{1,0:T(8,128)(2,1)S(1)}, bf16[256,768]{1,0:T(8,128)(2,1)}, u32[]{:S(2)}) copy-start(bf16[256,768]{1,0:T(8,128)(2,1)} %constant.18.clone.tab_ref) | copy-start | bytes 1179652
  0.6 3.7 %copy-start.13 = (f32[256,128]{1,0:T(8,128)S(1)}, f32[256,128]{1,0:T(8,128)}, u32[]{:S(2)}) copy-start(f32[256,128]{1,0:T(8,128)} %constant.19.clone.twist_ref) | copy-start | bytes 393220
  0.7 3.7 %copy-start.8 = (f32[128,4096]{1,0:T(8,128)S(1)}, f32[128,4096]{1,0:T(8,128)}, u32[]{:S(2)}) copy-start(f32[128,4096]{1,0:T(8,128)} %rec_hbm.1) | copy-start | bytes 6291460
  0.7 3.7 %copy-start.9 = (f32[64]{0:T(128)S(1)}, f32[64]{0:T(128)}, u32[]{:S(2)}) copy-start(f32[64]{0:T(128)} %param.15) | copy-start | bytes 772
  1.8 4.6 %copy-start.1 = (bf16[512,512]{1,0:T(8,128)(2,1)S(1)}, bf16[512,512]{1,0:T(8,128)(2,1)}, u32[]{:S(2)}) copy-start(bf16[512,512]{1,0:T(8,128)(2,1)} %constant.21.clone.band_ref) | copy-start | bytes 1572868
  1.8 4.6 %copy-start.3 = (bf16[1024,128]{1,0:T(8,128)(2,1)S(1)}, bf16[1024,128]{1,0:T(8,128)(2,1)}, u32[]{:S(2)}) copy-start(bf16[1024,128]{1,0:T(8,128)(2,1)} %constant.20.clone.edge_ref) | copy-start | bytes 786436
  1.8 4.6 %copy-start.4 = (f32[512,128]{1,0:T(8,128)S(1)}, f32[512,128]{1,0:T(8,128)}, u32[]{:S(2)}) copy-start(f32[512,128]{1,0:T(8,128)} %constant.22.clone.share_ref) | copy-start | bytes 786436
  1.8 4.5 %collective-permute-start = (f32[64,128]{1,0:T(8,128)S(1)}, f32[64,128]{1,0:T(8,128)S(1)}, u32[]{:S(2)}, u32[]{:S(2)}) collective-permute-start(f32[64,128]{1,0:T(8,128)S(1)} %history.1), channel_id=1, source_target_pairs={{0,1},{1,2},{2,3},{4,5},{5,6},{6,7},{8,9},{9,10},{10,11},{12,13},{... | collective-permute-start | bytes 98312 | tf_op jit(solution)/shard_map/ppermute | solution.py:384
  6.3 13.2 %copy-start.10 = (s32[4]{0:T(128)S(1)}, s32[4]{0:T(128)}, u32[]{:S(2)}) copy-start(s32[4]{0:T(128)} %offs_ref.1) | copy-start | bytes 52
  6.3 13.2 %copy-start.11 = (bf16[512,1024]{1,0:T(8,128)(2,1)S(1)}, bf16[512,1024]{1,0:T(8,128)(2,1)}, u32[]{:S(2)}) copy-start(bf16[512,1024]{1,0:T(8,128)(2,1)} %constant.23.clone.inv_ref) | copy-start | bytes 3145732
  7.8 11.7 %collective-permute-start.1 = (bf16[32,2,16,128]{3,2,1,0:T(8,128)(2,1)}, bf16[32,2,16,128]{3,2,1,0:T(8,128)(2,1)S(1)}, u32[]{:S(2)}, u32[]{:S(2)}) collective-permute-start(bf16[32,2,16,128]{3,2,1,0:T(8,128)(2,1)} %whiten.1.white_ref), channel_id=1, source_target_pairs={{0,4},{4,8},{8,12},{12,16},{16,20},{20,24},{24,28},{28,0},{1,5},{5... | collective-permute-start | bytes 786440 | tf_op jit(solution)/shard_map/ppermute | solution.py:420
  10.2 19.7 %all-to-all-start = ((bf16[32,2,16,128]{3,2,1,0:T(8,128)(2,1)}), bf16[32,2,16,128]{3,2,1,0:T(8,128)(2,1)S(1)}, u32[]{:S(2)}, u32[]{:S(2)}) async-start(bf16[32,2,16,128]{3,2,1,0:T(8,128)(2,1)} %whiten.1.white_ref), calls=%async_computation | async-start | bytes 524288 | tf_op jit(solution)/shard_map/all_to_all | solution.py:416
  16.5 13.4 %copy-start.2 = (bf16[512,512]{1,0:T(8,128)(2,1)S(1)}, bf16[512,512]{1,0:T(8,128)(2,1)}, u32[]{:S(2)}) copy-start(bf16[512,512]{1,0:T(8,128)(2,1)} %constant.25.clone.pack_ref) | copy-start | bytes 1572868
  16.5 13.4 %copy-start.5 = (bf16[128,128]{1,0:T(8,128)(2,1)S(1)}, bf16[128,128]{1,0:T(8,128)(2,1)}, u32[]{:S(2)}) copy-start(bf16[128,128]{1,0:T(8,128)(2,1)} %constant.24.clone.flip_ref) | copy-start | bytes 98308
  16.5 13.3 %copy-start.6 = (s32[8,3]{0,1:T(4,128)S(1)}, s32[8,3]{0,1:T(4,128)}, u32[]{:S(2)}) copy-start(s32[8,3]{0,1:T(4,128)} %param.17) | copy-start | bytes 292
  16.5 13.3 %copy-start.7 = (s32[8]{0:T(128)S(1)}, s32[8]{0:T(128)}, u32[]{:S(2)}) copy-start(s32[8]{0:T(128)} %count_ref.1) | copy-start | bytes 100
  21.7 24.7 %copy-start = (bf16[1024,512]{1,0:T(8,128)(2,1)S(1)}, bf16[1024,512]{1,0:T(8,128)(2,1)}, u32[]{:S(2)}) copy-start(bf16[1024,512]{1,0:T(8,128)(2,1)} %constant.26.clone.inv_ref) | copy-start | bytes 3145732
  21.7 6.2 %collective-permute-start.2 = (bf16[1,128,128]{2,1,0:T(8,128)(2,1)S(1)}, bf16[1,128,128]{2,1,0:T(8,128)(2,1)S(1)}, u32[]{:S(2)}, u32[]{:S(2)}) collective-permute-start(bf16[1,128,128]{2,1,0:T(8,128)(2,1)S(1)} %get-tuple-element.30), channel_id=1, source_target_pairs={{0,1},{1,0},{2,3},{3,2},{4,5},{5,4},{6,7},{7,6},{8,9},{9,8},{10,11... | collective-permute-start | bytes 98312 | tf_op jit(solution)/shard_map/ppermute | solution.py:439
  23.0 5.0 %collective-permute-start.3 = (bf16[1,128,128]{2,1,0:T(8,128)(2,1)S(1)}, bf16[1,128,128]{2,1,0:T(8,128)(2,1)S(1)}, u32[]{:S(2)}, u32[]{:S(2)}) collective-permute-start(bf16[1,128,128]{2,1,0:T(8,128)(2,1)S(1)} %get-tuple-element.31), channel_id=1, source_target_pairs={{0,2},{1,3},{2,0},{3,1},{4,6},{5,7},{6,4},{7,5},{8,10},{9,11},{10,... | collective-permute-start | bytes 98312 | tf_op jit(solution)/shard_map/ppermute | solution.py:439
  23.3 7.9 %collective-permute-start.4 = (bf16[1,128,128]{2,1,0:T(8,128)(2,1)S(1)}, bf16[1,128,128]{2,1,0:T(8,128)(2,1)S(1)}, u32[]{:S(2)}, u32[]{:S(2)}) collective-permute-start(bf16[1,128,128]{2,1,0:T(8,128)(2,1)S(1)} %get-tuple-element.32), channel_id=1, source_target_pairs={{0,3},{1,2},{2,1},{3,0},{4,7},{5,6},{6,5},{7,4},{8,11},{9,10},{10,... | collective-permute-start | bytes 98312 | tf_op jit(solution)/shard_map/ppermute | solution.py:439
  24.5 6.7 %collective-permute-start.5 = (bf16[1,128,128]{2,1,0:T(8,128)(2,1)S(1)}, bf16[1,128,128]{2,1,0:T(8,128)(2,1)S(1)}, u32[]{:S(2)}, u32[]{:S(2)}) collective-permute-start(bf16[1,128,128]{2,1,0:T(8,128)(2,1)S(1)} %get-tuple-element.33), channel_id=1, source_target_pairs={{0,28},{1,29},{2,30},{3,31},{4,0},{5,1},{6,2},{7,3},{8,4},{9,5},{1... | collective-permute-start | bytes 98312 | tf_op jit(solution)/shard_map/ppermute | solution.py:446
  26.5 4.7 %collective-permute-start.6 = (bf16[1,128,128]{2,1,0:T(8,128)(2,1)S(1)}, bf16[1,128,128]{2,1,0:T(8,128)(2,1)S(1)}, u32[]{:S(2)}, u32[]{:S(2)}) collective-permute-start(bf16[1,128,128]{2,1,0:T(8,128)(2,1)S(1)} %get-tuple-element.34), channel_id=1, source_target_pairs={{0,29},{1,28},{2,31},{3,30},{4,1},{5,0},{6,3},{7,2},{8,5},{9,4},{1... | collective-permute-start | bytes 98312 | tf_op jit(solution)/shard_map/ppermute | solution.py:446
  27.9 4.8 %collective-permute-start.7 = (bf16[1,128,128]{2,1,0:T(8,128)(2,1)S(1)}, bf16[1,128,128]{2,1,0:T(8,128)(2,1)S(1)}, u32[]{:S(2)}, u32[]{:S(2)}) collective-permute-start(bf16[1,128,128]{2,1,0:T(8,128)(2,1)S(1)} %get-tuple-element.35), channel_id=1, source_target_pairs={{0,30},{1,31},{2,28},{3,29},{4,2},{5,3},{6,0},{7,1},{8,6},{9,7},{1... | collective-permute-start | bytes 98312 | tf_op jit(solution)/shard_map/ppermute | solution.py:446
  28.0 4.7 %collective-permute-start.8 = (bf16[1,128,128]{2,1,0:T(8,128)(2,1)S(1)}, bf16[1,128,128]{2,1,0:T(8,128)(2,1)S(1)}, u32[]{:S(2)}, u32[]{:S(2)}) collective-permute-start(bf16[1,128,128]{2,1,0:T(8,128)(2,1)S(1)} %get-tuple-element.36), channel_id=1, source_target_pairs={{0,31},{1,30},{2,29},{3,28},{4,3},{5,2},{6,1},{7,0},{8,7},{9,6},{1... | collective-permute-start | bytes 98312 | tf_op jit(solution)/shard_map/ppermute | solution.py:446

commit v20 on v16

--- a/solution.py
+++ b/solution.py
@@ -183,8 +183,8 @@
     band_ref,
     share_ref,
     white_ref,
-    up_ref,
-    down_ref,
+    first_ref,
+    second_ref,
 ):
     head_high, head_low = split(head_ref[:, LANES - TAPS :])
     rim_high, rim_low = split(rim_ref[...] - mean_ref[0:1, :])
@@ -208,8 +208,27 @@
     flat = white.reshape(2 * BINS, LANES)
     turned = pltpu.roll(flat, SPAN, 1)
     lane = lax.broadcasted_iota(jnp.int32, (BINS, LANES), 1)
-    up_ref[...] = jnp.where(lane < SPAN, turned[:BINS], flat[BINS:]).astype(BF16)
-    down_ref[...] = jnp.where(lane < SPAN, flat[:BINS], turned[BINS:]).astype(BF16)
+    up = jnp.where(lane < SPAN, turned[:BINS], flat[BINS:])
+    down = jnp.where(lane < SPAN, flat[:BINS], turned[BINS:])
+    place = lax.axis_index("chan")
+    up_first = halo_order(place, lax.axis_size("chan"))[0]
+    first_ref[...] = jnp.where(up_first, up, down).astype(BF16)
+    second_ref[...] = jnp.where(up_first, down, up).astype(BF16)
+
+
+def halo_order(place, count):
+    if count % 2:
+        return place >= 0, place >= 0
+    return place % 2 == 0, place % 2 == 1
+
+
+def halo_routes(count):
+    if count % 2:
+        ring = [(i, (i + 1) % count) for i in range(count)]
+        return ring, [(j, i) for i, j in ring]
+    first = [(i, i + 1 - 2 * (i % 2)) for i in range(count)]
+    second = [(i, (i - 1 + 2 * (i % 2)) % count) for i in range(count)]
+    return first, second
 
 
 def offset_moves(offs_ref):
@@ -234,12 +253,15 @@
     return place ^ r if owners & (owners - 1) == 0 else (place + r) % owners
 
 
-def near_kernel(offs_ref, white_ref, before_ref, after_ref, inv_ref, *refs):
+def near_kernel(offs_ref, white_ref, first_ref, second_ref, inv_ref, *refs):
     out_refs, lags_ref = refs[:-1], refs[-1]
     rows = white_ref.shape[0] * 2 * GROUP
     half = rows // 2
     noff = lags_ref.shape[0]
-    before, after = before_ref[...].astype(F32), after_ref[...].astype(F32)
+    before_first = halo_order(lax.axis_index("chan"), lax.axis_size("chan"))[1]
+    first, second = first_ref[...].astype(F32), second_ref[...].astype(F32)
+    before = jnp.where(before_first, first, second)
+    after = jnp.where(before_first, second, first)
     lane = lax.broadcasted_iota(jnp.int32, (half, LANES), 1)
     upper = jnp.where(lane < SPAN, after, pltpu.roll(before, SPAN, 1))
     lower = jnp.where(lane < SPAN, pltpu.roll(after, SPAN, 1), before)
@@ -401,7 +423,7 @@
 
     band, band_share = band_tables()
     half = jax.ShapeDtypeStruct((BINS, LANES), BF16)
-    white, up, down = pl.pallas_call(
+    white, first, second = pl.pallas_call(
         whiten_kernel,
         out_shape=[jax.ShapeDtypeStruct((GROUPS, 2, GROUP, LANES), BF16), half, half],
         in_specs=vmem(7),
@@ -417,9 +439,9 @@
     moved = lax.all_to_all(spread, ("seg", "chan"), 0, 0, tiled=True)
     moved = moved.reshape(seg_count, chan_count, 2, bins, LANES)
 
-    ring = [(i, (i + 1) % chan_count) for i in range(chan_count)]
-    before = lax.ppermute(up, "chan", ring)
-    after = lax.ppermute(down, "chan", [(j, i) for i, j in ring])
+    routes = halo_routes(chan_count)
+    first = lax.ppermute(first, "chan", routes[0])
+    second = lax.ppermute(second, "chan", routes[1])
     order = np.repeat(bin_order().reshape(GROUPS, 1, GROUP), 2, axis=1).reshape(-1)
     part = np.broadcast_to(np.arange(2).reshape(1, 2, 1), (GROUPS, 2, GROUP)).reshape(-1)
     inverse = np.concatenate(split_np(inverse_table(seg_count, order, part)), axis=0)
@@ -434,7 +456,7 @@
             flops=20_000_000_000, bytes_accessed=20_000_000, transcendentals=0
         ),
         name="near_lags",
-    )(offsets, white, before, after, inverse)
+    )(offsets, white, first, second, inverse)
     lags = list(lags)
     for r in range(seg_count - 1, 0, -1):
         route = [(i, partner_of(i, r, seg_count)) for i in range(seg_count)]

time: 41.9 us -> 41.9 us (level)
    ppermute x2, starting transfers between devices: 5.4 us -> 5.89 us  [the longest x1 3.54 us: body(): second = lax.ppermute(second, 'chan', routes[1])]
    all_to_all x1, starting transfers between devices: 4.73 us -> 4.24 us  [body(): moved = lax.all_to_all(spread, ('seg', 'chan'), 0, 0, tiled=True)]
where the time goes in v20:
time: 41.9 us; the launch traced here: 41.6 us
  starting transfers between devices  14.8 us (35%)
  blocking collectives  10.7 us (26%)
  Pallas kernels  8.83 us (21%)
  waiting for transfers between devices  6.28 us (15%)
  between operations  0.89 us (2%)
    all_to_all x1, blocking collectives, body(): summed = lax.all_to_all(crossed, ('seg', 'chan'), 0, 0, tiled=True)  10.7 us
    all_to_all x1, waiting for transfers between devices, body(): moved = lax.all_to_all(spread, ('seg', 'chan'), 0, 0, tiled=True)  5.5 us
    all_to_all x1, starting transfers between devices, body(): moved = lax.all_to_all(spread, ('seg', 'chan'), 0, 0, tiled=True)  4.24 us
    ppermute x1, starting transfers between devices, body(): second = lax.ppermute(second, 'chan', routes[1])  3.54 us
    ppermute x1, starting transfers between devices, body(): rim = lax.ppermute(rim, 'seg', route)  2.49 us
    ppermute x1, starting transfers between devices, body(): first = lax.ppermute(first, 'chan', routes[0])  2.35 us
    ppermute x3, starting transfers between devices, body(): lags[r] = lax.ppermute(lags[r], 'seg', route)  2.21 us
    pallas_call x1, Pallas kernels, body(): pl.pallas_call(near_kernel, out_shape=[jax.ShapeDtypeStruct((near_each, L...  2.08 us
  transfers between devices with their start and end apart: 7, of which 2 were waited for; matrix products, arithmetic and copies ran while one was open for 0% of the time, Pallas kernels for 13%

profile of v20, /device:TPU:0, one launch (start us, length us, event | category | flops | bytes accessed | tf_op | source)
XLA Modules:
  0.0 41.6 jit_solution(7934440764236728485)
XLA Ops:
  0.6 0.0 copy-start.12
  0.6 0.0 copy-start.13
  0.7 0.0 copy-start.8
  0.7 0.0 copy-start.9
  0.7 1.1 %history.1 = f32[64,128]{1,0:T(8,128)S(1)} custom-call(f32[128,4096]{1,0:T(8,128)} %rec_hbm.1), custom_call_target="tpu_custom_call" | custom-call | flops 10000000000 | bytes 20000000 | tf_op jit(solution)/shard_map/history/pallas_call | solution.py:394
  1.8 0.0 copy-start.1
  1.8 0.0 copy-start.3
  1.8 0.0 copy-start.4
  1.8 2.5 %collective-permute-start = (f32[64,128]{1,0:T(8,128)S(1)}, f32[64,128]{1,0:T(8,128)S(1)}, u32[]{:S(2)}, u32[]{:S(2)}) collective-permute-start(f32[64,128]{1,0:T(8,128)S(1)} %history.1), channel_id=1, source_target_pairs={{0,1},{1,2},{2,3},{4,5},{5,6},{6,7},{8,9},{9,10},{10,11},{12,13},{... | collective-permute-start | bytes 98312 | tf_op jit(solution)/shard_map/ppermute | solution.py:406
  4.3 0.0 copy-done.12
  4.3 0.0 copy-done.13
  4.3 0.0 copy-done.8
  4.3 0.0 copy-done.9
  4.4 0.0 copy-start.10
  4.4 0.0 copy-start.11
  4.4 2.0 %filter_and_transform.1 = (f32[1024,128]{1,0:T(8,128)S(1)}, f32[8,128]{1,0:T(8,128)S(1)}, f32[16,128]{1,0:T(8,128)S(1)}) custom-call(f32[1,64]{1,0:T(1,128)S(1)} %bitcast.8, f32[128,4096]{1,0:T(8,128)S(1)} %copy-done.8, bf16[256,768]{1,0:T(8,128)(2,1)S(1)} %copy-done.12, f32[256,128]{1,0:T(8,128)S(1)} %copy-done.13), custom_call_target="tpu_custom_call" | custom-call | flops 1000000000 | bytes 5000000 | tf_op jit(solution)/shard_map/filter_and_transform/pallas_call | solution.py:408
  6.3 0.0 collective-permute-done.rim_ref
  6.4 0.0 copy-done.1
  6.4 0.0 copy-done.3
  6.4 0.0 copy-done.4
  6.4 1.4 %whiten.1 = (bf16[32,2,16,128]{3,2,1,0:T(8,128)(2,1)}, bf16[512,128]{1,0:T(8,128)(2,1)S(1)}, bf16[512,128]{1,0:T(8,128)(2,1)S(1)}) custom-call(f32[1024,128]{1,0:T(8,128)S(1)} %get-tuple-element.20.spec_ref, f32[64,128]{1,0:T(8,128)S(1)} %collective-permute-done.rim_ref, f32[8,128]{1,0:T(8,128)S(1)} %get-tuple-element.21.mean_ref, ...), custom_call_target="tpu_custom_call" | custom-call | tf_op jit(solution)/shard_map/whiten/pallas_call | solution.py:426
  7.8 2.4 %collective-permute-start.1 = (bf16[512,128]{1,0:T(8,128)(2,1)S(1)}, bf16[512,128]{1,0:T(8,128)(2,1)S(1)}, u32[]{:S(2)}, u32[]{:S(2)}) collective-permute-start(bf16[512,128]{1,0:T(8,128)(2,1)S(1)} %get-tuple-element.24), channel_id=1, source_target_pairs={{0,4},{4,0},{8,12},{12,8},{16,20},{20,16},{24,28},{28,24},{1,5},{5... | collective-permute-start | bytes 393224 | tf_op jit(solution)/shard_map/ppermute | solution.py:443
  10.2 3.5 %collective-permute-start.2 = (bf16[512,128]{1,0:T(8,128)(2,1)S(1)}, bf16[512,128]{1,0:T(8,128)(2,1)S(1)}, u32[]{:S(2)}, u32[]{:S(2)}) collective-permute-start(bf16[512,128]{1,0:T(8,128)(2,1)S(1)} %get-tuple-element.25), channel_id=1, source_target_pairs={{0,28},{4,8},{8,4},{12,16},{16,12},{20,24},{24,20},{28,0},{1,29},{... | collective-permute-start | bytes 393224 | tf_op jit(solution)/shard_map/ppermute | solution.py:444
  13.7 4.2 %all-to-all-start = ((bf16[32,2,16,128]{3,2,1,0:T(8,128)(2,1)}), bf16[32,2,16,128]{3,2,1,0:T(8,128)(2,1)S(1)}, u32[]{:S(2)}, u32[]{:S(2)}) async-start(bf16[32,2,16,128]{3,2,1,0:T(8,128)(2,1)} %get-tuple-element.23.white_ref), calls=%async_computation | async-start | bytes 524288 | tf_op jit(solution)/shard_map/all_to_all | solution.py:439
  18.0 0.0 copy-start.2
  18.0 0.0 copy-start.5
  18.0 0.0 copy-start.6
  18.0 0.0 copy-start.7
  18.0 0.0 collective-permute-done.1.first_ref
  18.0 0.8 %collective-permute-done.2.second_ref = bf16[512,128]{1,0:T(8,128)(2,1)S(1)} collective-permute-done((bf16[512,128]{1,0:T(8,128)(2,1)S(1)}, bf16[512,128]{1,0:T(8,128)(2,1)S(1)}, u32[]{:S(2)}, u32[]{:S(2)}) %collective-permute-start.2) | collective-permute-done | bytes 131104 | tf_op jit(solution)/shard_map/ppermute | solution.py:444
  18.8 0.0 copy-done.10
  18.8 0.0 copy-done.11
  18.8 2.1 %near_lags.1 = (bf16[1,256,128]{2,1,0:T(8,128)(2,1)S(1)}, bf16[1,256,128]{2,1,0:T(8,128)(2,1)S(1)}, bf16[1,256,128]{2,1,0:T(8,128)(2,1)S(1)}, bf16[1,256,128]{2,1,0:T(8,128)(2,1)S(1)}) custom-call(s32[4]{0:T(128)S(1)} %copy-done.10, bf16[32,2,16,128]{3,2,1,0:T(8,128)(2,1)} %get-tuple-element.23.white_ref, ...), custom_call_target="tpu_custom_call" | custom-call | flops 20000000000 | bytes 20000000 | tf_op jit(solution)/shard_map/near_lags/pallas_call | solution.py:448
  20.9 0.0 copy-start
  20.9 0.4 collective-permute-start.3
  21.3 1.8 %collective-permute-start.4 = (bf16[1,256,128]{2,1,0:T(8,128)(2,1)S(1)}, bf16[1,256,128]{2,1,0:T(8,128)(2,1)S(1)}, u32[]{:S(2)}, u32[]{:S(2)}) collective-permute-start(bf16[1,256,128]{2,1,0:T(8,128)(2,1)S(1)} %get-tuple-element.29), channel_id=1, source_target_pairs={{0,2},{1,3},{2,0},{3,1},{4,6},{5,7},{6,4},{7,5},{8,10},{9,11},{10,... | collective-permute-start | bytes 196616 | tf_op jit(solution)/shard_map/ppermute | solution.py:463
  23.0 0.1 collective-permute-start.5
  23.1 5.5 %all-to-all-done = bf16[32,2,16,128]{3,2,1,0:T(8,128)(2,1)S(1)} async-done(((bf16[32,2,16,128]{3,2,1,0:T(8,128)(2,1)}), bf16[32,2,16,128]{3,2,1,0:T(8,128)(2,1)S(1)}, u32[]{:S(2)}, u32[]{:S(2)}) %all-to-all-start) | async-done | bytes 262176 | tf_op jit(solution)/shard_map/all_to_all | solution.py:439
  28.6 0.0 copy-done.2
  28.6 0.0 copy-done.5
  28.6 0.0 copy-done.6
  28.6 0.0 copy-done.7
  28.6 1.2 %loop_spectra.1 = bf16[4,8,24,128]{3,2,1,0:T(8,128)(2,1)S(1)} custom-call(s32[3,8]{1,0:T(4,128)S(1)} %bitcast.7, s32[8]{0:T(128)S(1)} %copy-done.7, bf16[128,128]{1,0:T(8,128)(2,1)S(1)} %copy-done.5, bf16[512,512]{1,0:T(8,128)(2,1)S(1)} %copy-done.2, bf16[4,8,2,16,128]{4,3,2,1,0:T(8,128)(2,1)S(1)} %bitcast.5), custom_call_target="tpu_custom_call" | custom-call | tf_op jit(solution)/shard_map/loop_spectra/pallas_call | solution.py:484
  29.9 0.0 collective-permute-done.3.refs_1_
  29.9 0.0 collective-permute-done.4.refs_2_
  29.9 0.0 collective-permute-done.5.refs_3_
  29.9 10.7 %all_to_all.10.spec_ref = bf16[32,24,128]{2,1,0:T(8,128)(2,1)S(1)} all-to-all(bf16[32,24,128]{2,1,0:T(8,128)(2,1)S(1)} %bitcast.6), channel_id=1, replica_groups=mesh['chan'=8,'seg'=4] {'seg','chan'}, dimensions={0} | all-to-all | bytes 393216 | tf_op jit(solution)/shard_map/all_to_all | solution.py:494
  40.6 1.0 %lags.1 = (f32[128,1,256]{2,1,0:T(1,128)}, f32[96,256]{1,0:T(8,128)}) custom-call(bf16[32,24,128]{2,1,0:T(8,128)(2,1)S(1)} %all_to_all.10.spec_ref, bf16[1024,512]{1,0:T(8,128)(2,1)S(1)} %copy-done, bf16[1,256,128]{2,1,0:T(8,128)(2,1)S(1)} %get-tuple-element.32.refs_0_, bf16[1,256,128]{2,1,0:T(8,128)(2,1)S(1)} %collective-permute-done.3.refs_1_, ...), custom_call_target="tpu_custom_call" | custom-call | tf_op jit(solution)/shard_map/lags/pallas_call | solution.py:498
  (1 shorter events, 0.0 us)
Async XLA Ops:
  0.6 3.7 %copy-start.12 = (bf16[256,768]{1,0:T(8,128)(2,1)S(1)}, bf16[256,768]{1,0:T(8,128)(2,1)}, u32[]{:S(2)}) copy-start(bf16[256,768]{1,0:T(8,128)(2,1)} %constant.18.clone.tab_ref) | copy-start | bytes 1179652
  0.6 3.7 %copy-start.13 = (f32[256,128]{1,0:T(8,128)S(1)}, f32[256,128]{1,0:T(8,128)}, u32[]{:S(2)}) copy-start(f32[256,128]{1,0:T(8,128)} %constant.19.clone.twist_ref) | copy-start | bytes 393220
  0.7 3.7 %copy-start.8 = (f32[128,4096]{1,0:T(8,128)S(1)}, f32[128,4096]{1,0:T(8,128)}, u32[]{:S(2)}) copy-start(f32[128,4096]{1,0:T(8,128)} %rec_hbm.1) | copy-start | bytes 6291460
  0.7 3.7 %copy-start.9 = (f32[64]{0:T(128)S(1)}, f32[64]{0:T(128)}, u32[]{:S(2)}) copy-start(f32[64]{0:T(128)} %param.15) | copy-start | bytes 772
  1.8 4.6 %copy-start.1 = (bf16[512,512]{1,0:T(8,128)(2,1)S(1)}, bf16[512,512]{1,0:T(8,128)(2,1)}, u32[]{:S(2)}) copy-start(bf16[512,512]{1,0:T(8,128)(2,1)} %constant.21.clone.band_ref) | copy-start | bytes 1572868
  1.8 4.6 %copy-start.3 = (f32[512,128]{1,0:T(8,128)S(1)}, f32[512,128]{1,0:T(8,128)}, u32[]{:S(2)}) copy-start(f32[512,128]{1,0:T(8,128)} %constant.22.clone.share_ref) | copy-start | bytes 786436
  1.8 4.6 %copy-start.4 = (bf16[1024,128]{1,0:T(8,128)(2,1)S(1)}, bf16[1024,128]{1,0:T(8,128)(2,1)}, u32[]{:S(2)}) copy-start(bf16[1024,128]{1,0:T(8,128)(2,1)} %constant.20.clone.edge_ref) | copy-start | bytes 786436
  1.8 4.5 %collective-permute-start = (f32[64,128]{1,0:T(8,128)S(1)}, f32[64,128]{1,0:T(8,128)S(1)}, u32[]{:S(2)}, u32[]{:S(2)}) collective-permute-start(f32[64,128]{1,0:T(8,128)S(1)} %history.1), channel_id=1, source_target_pairs={{0,1},{1,2},{2,3},{4,5},{5,6},{6,7},{8,9},{9,10},{10,11},{12,13},{... | collective-permute-start | bytes 98312 | tf_op jit(solution)/shard_map/ppermute | solution.py:406
  4.4 14.4 %copy-start.10 = (s32[4]{0:T(128)S(1)}, s32[4]{0:T(128)}, u32[]{:S(2)}) copy-start(s32[4]{0:T(128)} %offs_ref.1) | copy-start | bytes 52
  4.4 14.4 %copy-start.11 = (bf16[512,1024]{1,0:T(8,128)(2,1)S(1)}, bf16[512,1024]{1,0:T(8,128)(2,1)}, u32[]{:S(2)}) copy-start(bf16[512,1024]{1,0:T(8,128)(2,1)} %constant.23.clone.inv_ref) | copy-start | bytes 3145732
  7.8 10.2 %collective-permute-start.1 = (bf16[512,128]{1,0:T(8,128)(2,1)S(1)}, bf16[512,128]{1,0:T(8,128)(2,1)S(1)}, u32[]{:S(2)}, u32[]{:S(2)}) collective-permute-start(bf16[512,128]{1,0:T(8,128)(2,1)S(1)} %get-tuple-element.24), channel_id=1, source_target_pairs={{0,4},{4,0},{8,12},{12,8},{16,20},{20,16},{24,28},{28,24},{1,5},{5... | collective-permute-start | bytes 393224 | tf_op jit(solution)/shard_map/ppermute | solution.py:443
  10.2 8.6 %collective-permute-start.2 = (bf16[512,128]{1,0:T(8,128)(2,1)S(1)}, bf16[512,128]{1,0:T(8,128)(2,1)S(1)}, u32[]{:S(2)}, u32[]{:S(2)}) collective-permute-start(bf16[512,128]{1,0:T(8,128)(2,1)S(1)} %get-tuple-element.25), channel_id=1, source_target_pairs={{0,28},{4,8},{8,4},{12,16},{16,12},{20,24},{24,20},{28,0},{1,29},{... | collective-permute-start | bytes 393224 | tf_op jit(solution)/shard_map/ppermute | solution.py:444
  13.7 14.9 %all-to-all-start = ((bf16[32,2,16,128]{3,2,1,0:T(8,128)(2,1)}), bf16[32,2,16,128]{3,2,1,0:T(8,128)(2,1)S(1)}, u32[]{:S(2)}, u32[]{:S(2)}) async-start(bf16[32,2,16,128]{3,2,1,0:T(8,128)(2,1)} %get-tuple-element.23.white_ref), calls=%async_computation | async-start | bytes 524288 | tf_op jit(solution)/shard_map/all_to_all | solution.py:439
  18.0 10.6 %copy-start.2 = (bf16[512,512]{1,0:T(8,128)(2,1)S(1)}, bf16[512,512]{1,0:T(8,128)(2,1)}, u32[]{:S(2)}) copy-start(bf16[512,512]{1,0:T(8,128)(2,1)} %constant.25.clone.pack_ref) | copy-start | bytes 1572868
  18.0 10.6 %copy-start.5 = (bf16[128,128]{1,0:T(8,128)(2,1)S(1)}, bf16[128,128]{1,0:T(8,128)(2,1)}, u32[]{:S(2)}) copy-start(bf16[128,128]{1,0:T(8,128)(2,1)} %constant.24.clone.flip_ref) | copy-start | bytes 98308
  18.0 10.6 %copy-start.6 = (s32[8,3]{0,1:T(4,128)S(1)}, s32[8,3]{0,1:T(4,128)}, u32[]{:S(2)}) copy-start(s32[8,3]{0,1:T(4,128)} %param.17) | copy-start | bytes 292
  18.0 10.6 %copy-start.7 = (s32[8]{0:T(128)S(1)}, s32[8]{0:T(128)}, u32[]{:S(2)}) copy-start(s32[8]{0:T(128)} %count_ref.1) | copy-start | bytes 100
  20.9 19.7 %copy-start = (bf16[1024,512]{1,0:T(8,128)(2,1)S(1)}, bf16[1024,512]{1,0:T(8,128)(2,1)}, u32[]{:S(2)}) copy-start(bf16[1024,512]{1,0:T(8,128)(2,1)} %constant.26.clone.inv_ref) | copy-start | bytes 3145732
  20.9 9.0 %collective-permute-start.3 = (bf16[1,256,128]{2,1,0:T(8,128)(2,1)S(1)}, bf16[1,256,128]{2,1,0:T(8,128)(2,1)S(1)}, u32[]{:S(2)}, u32[]{:S(2)}) collective-permute-start(bf16[1,256,128]{2,1,0:T(8,128)(2,1)S(1)} %get-tuple-element.28), channel_id=1, source_target_pairs={{0,1},{1,0},{2,3},{3,2},{4,5},{5,4},{6,7},{7,6},{8,9},{9,8},{10,11... | collective-permute-start | bytes 196616 | tf_op jit(solution)/shard_map/ppermute | solution.py:463
  21.3 8.6 %collective-permute-start.4 = (bf16[1,256,128]{2,1,0:T(8,128)(2,1)S(1)}, bf16[1,256,128]{2,1,0:T(8,128)(2,1)S(1)}, u32[]{:S(2)}, u32[]{:S(2)}) collective-permute-start(bf16[1,256,128]{2,1,0:T(8,128)(2,1)S(1)} %get-tuple-element.29), channel_id=1, source_target_pairs={{0,2},{1,3},{2,0},{3,1},{4,6},{5,7},{6,4},{7,5},{8,10},{9,11},{10,... | collective-permute-start | bytes 196616 | tf_op jit(solution)/shard_map/ppermute | solution.py:463
  23.0 6.9 %collective-permute-start.5 = (bf16[1,256,128]{2,1,0:T(8,128)(2,1)S(1)}, bf16[1,256,128]{2,1,0:T(8,128)(2,1)S(1)}, u32[]{:S(2)}, u32[]{:S(2)}) collective-permute-start(bf16[1,256,128]{2,1,0:T(8,128)(2,1)S(1)} %get-tuple-element.30), channel_id=1, source_target_pairs={{0,3},{1,2},{2,1},{3,0},{4,7},{5,6},{6,5},{7,4},{8,11},{9,10},{10,... | collective-permute-start | bytes 196616 | tf_op jit(solution)/shard_map/ppermute | solution.py:463

commit v21 on v20

--- a/solution.py
+++ b/solution.py
@@ -219,15 +219,15 @@
 def halo_order(place, count):
     if count % 2:
         return place >= 0, place >= 0
-    return place % 2 == 0, place % 2 == 1
+    return place % 2 == 1, place % 2 == 0
 
 
 def halo_routes(count):
     if count % 2:
         ring = [(i, (i + 1) % count) for i in range(count)]
         return ring, [(j, i) for i, j in ring]
-    first = [(i, i + 1 - 2 * (i % 2)) for i in range(count)]
-    second = [(i, (i - 1 + 2 * (i % 2)) % count) for i in range(count)]
+    first = [(i, (i - 1 + 2 * (i % 2)) % count) for i in range(count)]
+    second = [(i, i + 1 - 2 * (i % 2)) for i in range(count)]
     return first, second
 
 

time: 41.9 us -> 41.9 us (level)
    ppermute x1, starting transfers between devices: 3.54 us -> 0.01 us  [body(): second = lax.ppermute(second, 'chan', routes[1])]
    ppermute x1, starting transfers between devices: 2.35 us -> 5.39 us  [body(): first = lax.ppermute(first, 'chan', routes[0])]
    ppermute x1, waiting for transfers between devices: 0.77 us -> 2.3 us  [body(): second = lax.ppermute(second, 'chan', routes[1])]
    all_to_all x1, waiting for transfers between devices: 5.5 us -> 4.25 us  [body(): moved = lax.all_to_all(spread, ('seg', 'chan'), 0, 0, tiled=True)]
    all_to_all x1, starting transfers between devices: 4.24 us -> 4.73 us  [body(): moved = lax.all_to_all(spread, ('seg', 'chan'), 0, 0, tiled=True)]
where the time goes in v21:
time: 41.9 us; the launch traced here: 41.6 us
  starting transfers between devices  14.5 us (35%)
  blocking collectives  10.7 us (26%)
  Pallas kernels  8.83 us (21%)
  waiting for transfers between devices  6.57 us (16%)
  between operations  0.89 us (2%)
    all_to_all x1, blocking collectives, body(): summed = lax.all_to_all(crossed, ('seg', 'chan'), 0, 0, tiled=True)  10.7 us
    ppermute x1, starting transfers between devices, body(): first = lax.ppermute(first, 'chan', routes[0])  5.39 us
    all_to_all x1, starting transfers between devices, body(): moved = lax.all_to_all(spread, ('seg', 'chan'), 0, 0, tiled=True)  4.73 us
    all_to_all x1, waiting for transfers between devices, body(): moved = lax.all_to_all(spread, ('seg', 'chan'), 0, 0, tiled=True)  4.25 us
    ppermute x1, starting transfers between devices, body(): rim = lax.ppermute(rim, 'seg', route)  2.49 us
    ppermute x1, waiting for transfers between devices, body(): second = lax.ppermute(second, 'chan', routes[1])  2.3 us
    pallas_call x1, Pallas kernels, body(): pl.pallas_call(near_kernel, out_shape=[jax.ShapeDtypeStruct((near_each, L...  2.08 us
    pallas_call x1, Pallas kernels, body(): pl.pallas_call(spectrum_kernel, out_shape=[jax.ShapeDtypeStruct((2 * BINS...  1.96 us
  transfers between devices with their start and end apart: 7, of which 2 were waited for; matrix products, arithmetic and copies ran while one was open for 0% of the time, Pallas kernels for 13%

profile of v21, /device:TPU:0, one launch (start us, length us, event | category | flops | bytes accessed | tf_op | source)
XLA Modules:
  0.0 41.6 jit_solution(5748933670496380952)
XLA Ops:
  0.6 0.0 copy-start.12
  0.6 0.0 copy-start.13
  0.7 0.0 copy-start.8
  0.7 0.0 copy-start.9
  0.7 1.1 %history.1 = f32[64,128]{1,0:T(8,128)S(1)} custom-call(f32[128,4096]{1,0:T(8,128)} %rec_hbm.1), custom_call_target="tpu_custom_call" | custom-call | flops 10000000000 | bytes 20000000 | tf_op jit(solution)/shard_map/history/pallas_call | solution.py:394
  1.8 0.0 copy-start.1
  1.8 0.0 copy-start.3
  1.8 0.0 copy-start.4
  1.8 2.5 %collective-permute-start = (f32[64,128]{1,0:T(8,128)S(1)}, f32[64,128]{1,0:T(8,128)S(1)}, u32[]{:S(2)}, u32[]{:S(2)}) collective-permute-start(f32[64,128]{1,0:T(8,128)S(1)} %history.1), channel_id=1, source_target_pairs={{0,1},{1,2},{2,3},{4,5},{5,6},{6,7},{8,9},{9,10},{10,11},{12,13},{... | collective-permute-start | bytes 98312 | tf_op jit(solution)/shard_map/ppermute | solution.py:406
  4.3 0.0 copy-done.12
  4.3 0.0 copy-done.13
  4.3 0.0 copy-done.8
  4.3 0.0 copy-done.9
  4.4 0.0 copy-start.10
  4.4 0.0 copy-start.11
  4.4 2.0 %filter_and_transform.1 = (f32[1024,128]{1,0:T(8,128)S(1)}, f32[8,128]{1,0:T(8,128)S(1)}, f32[16,128]{1,0:T(8,128)S(1)}) custom-call(f32[1,64]{1,0:T(1,128)S(1)} %bitcast.8, f32[128,4096]{1,0:T(8,128)S(1)} %copy-done.8, bf16[256,768]{1,0:T(8,128)(2,1)S(1)} %copy-done.12, f32[256,128]{1,0:T(8,128)S(1)} %copy-done.13), custom_call_target="tpu_custom_call" | custom-call | flops 1000000000 | bytes 5000000 | tf_op jit(solution)/shard_map/filter_and_transform/pallas_call | solution.py:408
  6.3 0.0 collective-permute-done.rim_ref
  6.4 0.0 copy-done.1
  6.4 0.0 copy-done.3
  6.4 0.0 copy-done.4
  6.4 1.4 %whiten.1 = (bf16[32,2,16,128]{3,2,1,0:T(8,128)(2,1)}, bf16[512,128]{1,0:T(8,128)(2,1)S(1)}, bf16[512,128]{1,0:T(8,128)(2,1)S(1)}) custom-call(f32[1024,128]{1,0:T(8,128)S(1)} %get-tuple-element.20.spec_ref, f32[64,128]{1,0:T(8,128)S(1)} %collective-permute-done.rim_ref, f32[8,128]{1,0:T(8,128)S(1)} %get-tuple-element.21.mean_ref, ...), custom_call_target="tpu_custom_call" | custom-call | tf_op jit(solution)/shard_map/whiten/pallas_call | solution.py:426
  7.8 5.4 %collective-permute-start.1 = (bf16[512,128]{1,0:T(8,128)(2,1)S(1)}, bf16[512,128]{1,0:T(8,128)(2,1)S(1)}, u32[]{:S(2)}, u32[]{:S(2)}) collective-permute-start(bf16[512,128]{1,0:T(8,128)(2,1)S(1)} %get-tuple-element.24), channel_id=1, source_target_pairs={{0,28},{4,8},{8,4},{12,16},{16,12},{20,24},{24,20},{28,0},{1,29},{... | collective-permute-start | bytes 393224 | tf_op jit(solution)/shard_map/ppermute | solution.py:443
  13.2 0.0 collective-permute-start.2
  13.2 4.7 %all-to-all-start = ((bf16[32,2,16,128]{3,2,1,0:T(8,128)(2,1)}), bf16[32,2,16,128]{3,2,1,0:T(8,128)(2,1)S(1)}, u32[]{:S(2)}, u32[]{:S(2)}) async-start(bf16[32,2,16,128]{3,2,1,0:T(8,128)(2,1)} %get-tuple-element.23.white_ref), calls=%async_computation | async-start | bytes 524288 | tf_op jit(solution)/shard_map/all_to_all | solution.py:439
  18.0 0.0 copy-start.2
  18.0 0.0 copy-start.5
  18.0 0.0 copy-start.6
  18.0 0.0 copy-start.7
  18.0 0.0 collective-permute-done.1.first_ref
  18.0 2.3 %collective-permute-done.2.second_ref = bf16[512,128]{1,0:T(8,128)(2,1)S(1)} collective-permute-done((bf16[512,128]{1,0:T(8,128)(2,1)S(1)}, bf16[512,128]{1,0:T(8,128)(2,1)S(1)}, u32[]{:S(2)}, u32[]{:S(2)}) %collective-permute-start.2) | collective-permute-done | bytes 131104 | tf_op jit(solution)/shard_map/ppermute | solution.py:444
  20.3 0.0 copy-done.10
  20.3 0.0 copy-done.11
  20.3 2.1 %near_lags.1 = (bf16[1,256,128]{2,1,0:T(8,128)(2,1)S(1)}, bf16[1,256,128]{2,1,0:T(8,128)(2,1)S(1)}, bf16[1,256,128]{2,1,0:T(8,128)(2,1)S(1)}, bf16[1,256,128]{2,1,0:T(8,128)(2,1)S(1)}) custom-call(s32[4]{0:T(128)S(1)} %copy-done.10, bf16[32,2,16,128]{3,2,1,0:T(8,128)(2,1)} %get-tuple-element.23.white_ref, ...), custom_call_target="tpu_custom_call" | custom-call | flops 20000000000 | bytes 20000000 | tf_op jit(solution)/shard_map/near_lags/pallas_call | solution.py:448
  22.4 0.0 copy-start
  22.4 0.2 collective-permute-start.3
  22.6 0.7 %collective-permute-start.4 = (bf16[1,256,128]{2,1,0:T(8,128)(2,1)S(1)}, bf16[1,256,128]{2,1,0:T(8,128)(2,1)S(1)}, u32[]{:S(2)}, u32[]{:S(2)}) collective-permute-start(bf16[1,256,128]{2,1,0:T(8,128)(2,1)S(1)} %get-tuple-element.29), channel_id=1, source_target_pairs={{0,2},{1,3},{2,0},{3,1},{4,6},{5,7},{6,4},{7,5},{8,10},{9,11},{10,... | collective-permute-start | bytes 196616 | tf_op jit(solution)/shard_map/ppermute | solution.py:463
  23.4 1.0 %collective-permute-start.5 = (bf16[1,256,128]{2,1,0:T(8,128)(2,1)S(1)}, bf16[1,256,128]{2,1,0:T(8,128)(2,1)S(1)}, u32[]{:S(2)}, u32[]{:S(2)}) collective-permute-start(bf16[1,256,128]{2,1,0:T(8,128)(2,1)S(1)} %get-tuple-element.30), channel_id=1, source_target_pairs={{0,3},{1,2},{2,1},{3,0},{4,7},{5,6},{6,5},{7,4},{8,11},{9,10},{10,... | collective-permute-start | bytes 196616 | tf_op jit(solution)/shard_map/ppermute | solution.py:463
  24.4 4.3 %all-to-all-done = bf16[32,2,16,128]{3,2,1,0:T(8,128)(2,1)S(1)} async-done(((bf16[32,2,16,128]{3,2,1,0:T(8,128)(2,1)}), bf16[32,2,16,128]{3,2,1,0:T(8,128)(2,1)S(1)}, u32[]{:S(2)}, u32[]{:S(2)}) %all-to-all-start) | async-done | bytes 262176 | tf_op jit(solution)/shard_map/all_to_all | solution.py:439
  28.6 0.0 copy-done.2
  28.6 0.0 copy-done.5
  28.6 0.0 copy-done.6
  28.6 0.0 copy-done.7
  28.6 1.2 %loop_spectra.1 = bf16[4,8,24,128]{3,2,1,0:T(8,128)(2,1)S(1)} custom-call(s32[3,8]{1,0:T(4,128)S(1)} %bitcast.7, s32[8]{0:T(128)S(1)} %copy-done.7, bf16[128,128]{1,0:T(8,128)(2,1)S(1)} %copy-done.5, bf16[512,512]{1,0:T(8,128)(2,1)S(1)} %copy-done.2, bf16[4,8,2,16,128]{4,3,2,1,0:T(8,128)(2,1)S(1)} %bitcast.5), custom_call_target="tpu_custom_call" | custom-call | tf_op jit(solution)/shard_map/loop_spectra/pallas_call | solution.py:484
  29.9 0.0 collective-permute-done.3.refs_1_
  29.9 0.0 collective-permute-done.4.refs_2_
  29.9 0.0 collective-permute-done.5.refs_3_
  29.9 10.7 %all_to_all.10.spec_ref = bf16[32,24,128]{2,1,0:T(8,128)(2,1)S(1)} all-to-all(bf16[32,24,128]{2,1,0:T(8,128)(2,1)S(1)} %bitcast.6), channel_id=1, replica_groups=mesh['chan'=8,'seg'=4] {'seg','chan'}, dimensions={0} | all-to-all | bytes 393216 | tf_op jit(solution)/shard_map/all_to_all | solution.py:494
  40.6 1.0 %lags.1 = (f32[128,1,256]{2,1,0:T(1,128)}, f32[96,256]{1,0:T(8,128)}) custom-call(bf16[32,24,128]{2,1,0:T(8,128)(2,1)S(1)} %all_to_all.10.spec_ref, bf16[1024,512]{1,0:T(8,128)(2,1)S(1)} %copy-done, bf16[1,256,128]{2,1,0:T(8,128)(2,1)S(1)} %get-tuple-element.32.refs_0_, bf16[1,256,128]{2,1,0:T(8,128)(2,1)S(1)} %collective-permute-done.3.refs_1_, ...), custom_call_target="tpu_custom_call" | custom-call | tf_op jit(solution)/shard_map/lags/pallas_call | solution.py:498
  (1 shorter events, 0.0 us)
Async XLA Ops:
  0.6 3.7 %copy-start.12 = (bf16[256,768]{1,0:T(8,128)(2,1)S(1)}, bf16[256,768]{1,0:T(8,128)(2,1)}, u32[]{:S(2)}) copy-start(bf16[256,768]{1,0:T(8,128)(2,1)} %constant.18.clone.tab_ref) | copy-start | bytes 1179652
  0.6 3.7 %copy-start.13 = (f32[256,128]{1,0:T(8,128)S(1)}, f32[256,128]{1,0:T(8,128)}, u32[]{:S(2)}) copy-start(f32[256,128]{1,0:T(8,128)} %constant.19.clone.twist_ref) | copy-start | bytes 393220
  0.7 3.7 %copy-start.8 = (f32[128,4096]{1,0:T(8,128)S(1)}, f32[128,4096]{1,0:T(8,128)}, u32[]{:S(2)}) copy-start(f32[128,4096]{1,0:T(8,128)} %rec_hbm.1) | copy-start | bytes 6291460
  0.7 3.7 %copy-start.9 = (f32[64]{0:T(128)S(1)}, f32[64]{0:T(128)}, u32[]{:S(2)}) copy-start(f32[64]{0:T(128)} %param.15) | copy-start | bytes 772
  1.8 4.6 %copy-start.1 = (bf16[512,512]{1,0:T(8,128)(2,1)S(1)}, bf16[512,512]{1,0:T(8,128)(2,1)}, u32[]{:S(2)}) copy-start(bf16[512,512]{1,0:T(8,128)(2,1)} %constant.21.clone.band_ref) | copy-start | bytes 1572868
  1.8 4.6 %copy-start.3 = (f32[512,128]{1,0:T(8,128)S(1)}, f32[512,128]{1,0:T(8,128)}, u32[]{:S(2)}) copy-start(f32[512,128]{1,0:T(8,128)} %constant.22.clone.share_ref) | copy-start | bytes 786436
  1.8 4.6 %copy-start.4 = (bf16[1024,128]{1,0:T(8,128)(2,1)S(1)}, bf16[1024,128]{1,0:T(8,128)(2,1)}, u32[]{:S(2)}) copy-start(bf16[1024,128]{1,0:T(8,128)(2,1)} %constant.20.clone.edge_ref) | copy-start | bytes 786436
  1.8 4.5 %collective-permute-start = (f32[64,128]{1,0:T(8,128)S(1)}, f32[64,128]{1,0:T(8,128)S(1)}, u32[]{:S(2)}, u32[]{:S(2)}) collective-permute-start(f32[64,128]{1,0:T(8,128)S(1)} %history.1), channel_id=1, source_target_pairs={{0,1},{1,2},{2,3},{4,5},{5,6},{6,7},{8,9},{9,10},{10,11},{12,13},{... | collective-permute-start | bytes 98312 | tf_op jit(solution)/shard_map/ppermute | solution.py:406
  4.4 16.0 %copy-start.10 = (s32[4]{0:T(128)S(1)}, s32[4]{0:T(128)}, u32[]{:S(2)}) copy-start(s32[4]{0:T(128)} %offs_ref.1) | copy-start | bytes 52
  4.4 16.0 %copy-start.11 = (bf16[512,1024]{1,0:T(8,128)(2,1)S(1)}, bf16[512,1024]{1,0:T(8,128)(2,1)}, u32[]{:S(2)}) copy-start(bf16[512,1024]{1,0:T(8,128)(2,1)} %constant.23.clone.inv_ref) | copy-start | bytes 3145732
  7.8 10.2 %collective-permute-start.1 = (bf16[512,128]{1,0:T(8,128)(2,1)S(1)}, bf16[512,128]{1,0:T(8,128)(2,1)S(1)}, u32[]{:S(2)}, u32[]{:S(2)}) collective-permute-start(bf16[512,128]{1,0:T(8,128)(2,1)S(1)} %get-tuple-element.24), channel_id=1, source_target_pairs={{0,28},{4,8},{8,4},{12,16},{16,12},{20,24},{24,20},{28,0},{1,29},{... | collective-permute-start | bytes 393224 | tf_op jit(solution)/shard_map/ppermute | solution.py:443
  13.2 7.1 %collective-permute-start.2 = (bf16[512,128]{1,0:T(8,128)(2,1)S(1)}, bf16[512,128]{1,0:T(8,128)(2,1)S(1)}, u32[]{:S(2)}, u32[]{:S(2)}) collective-permute-start(bf16[512,128]{1,0:T(8,128)(2,1)S(1)} %get-tuple-element.25), channel_id=1, source_target_pairs={{0,4},{4,0},{8,12},{12,8},{16,20},{20,16},{24,28},{28,24},{1,5},{5... | collective-permute-start | bytes 393224 | tf_op jit(solution)/shard_map/ppermute | solution.py:444
  13.2 15.4 %all-to-all-start = ((bf16[32,2,16,128]{3,2,1,0:T(8,128)(2,1)}), bf16[32,2,16,128]{3,2,1,0:T(8,128)(2,1)S(1)}, u32[]{:S(2)}, u32[]{:S(2)}) async-start(bf16[32,2,16,128]{3,2,1,0:T(8,128)(2,1)} %get-tuple-element.23.white_ref), calls=%async_computation | async-start | bytes 524288 | tf_op jit(solution)/shard_map/all_to_all | solution.py:439
  18.0 10.7 %copy-start.2 = (bf16[512,512]{1,0:T(8,128)(2,1)S(1)}, bf16[512,512]{1,0:T(8,128)(2,1)}, u32[]{:S(2)}) copy-start(bf16[512,512]{1,0:T(8,128)(2,1)} %constant.25.clone.pack_ref) | copy-start | bytes 1572868
  18.0 10.6 %copy-start.5 = (bf16[128,128]{1,0:T(8,128)(2,1)S(1)}, bf16[128,128]{1,0:T(8,128)(2,1)}, u32[]{:S(2)}) copy-start(bf16[128,128]{1,0:T(8,128)(2,1)} %constant.24.clone.flip_ref) | copy-start | bytes 98308
  18.0 10.6 %copy-start.6 = (s32[8,3]{0,1:T(4,128)S(1)}, s32[8,3]{0,1:T(4,128)}, u32[]{:S(2)}) copy-start(s32[8,3]{0,1:T(4,128)} %param.17) | copy-start | bytes 292
  18.0 10.6 %copy-start.7 = (s32[8]{0:T(128)S(1)}, s32[8]{0:T(128)}, u32[]{:S(2)}) copy-start(s32[8]{0:T(128)} %count_ref.1) | copy-start | bytes 100
  22.4 18.2 %copy-start = (bf16[1024,512]{1,0:T(8,128)(2,1)S(1)}, bf16[1024,512]{1,0:T(8,128)(2,1)}, u32[]{:S(2)}) copy-start(bf16[1024,512]{1,0:T(8,128)(2,1)} %constant.26.clone.inv_ref) | copy-start | bytes 3145732
  22.4 7.4 %collective-permute-start.3 = (bf16[1,256,128]{2,1,0:T(8,128)(2,1)S(1)}, bf16[1,256,128]{2,1,0:T(8,128)(2,1)S(1)}, u32[]{:S(2)}, u32[]{:S(2)}) collective-permute-start(bf16[1,256,128]{2,1,0:T(8,128)(2,1)S(1)} %get-tuple-element.28), channel_id=1, source_target_pairs={{0,1},{1,0},{2,3},{3,2},{4,5},{5,4},{6,7},{7,6},{8,9},{9,8},{10,11... | collective-permute-start | bytes 196616 | tf_op jit(solution)/shard_map/ppermute | solution.py:463
  22.6 7.2 %collective-permute-start.4 = (bf16[1,256,128]{2,1,0:T(8,128)(2,1)S(1)}, bf16[1,256,128]{2,1,0:T(8,128)(2,1)S(1)}, u32[]{:S(2)}, u32[]{:S(2)}) collective-permute-start(bf16[1,256,128]{2,1,0:T(8,128)(2,1)S(1)} %get-tuple-element.29), channel_id=1, source_target_pairs={{0,2},{1,3},{2,0},{3,1},{4,6},{5,7},{6,4},{7,5},{8,10},{9,11},{10,... | collective-permute-start | bytes 196616 | tf_op jit(solution)/shard_map/ppermute | solution.py:463
  23.4 6.5 %collective-permute-start.5 = (bf16[1,256,128]{2,1,0:T(8,128)(2,1)S(1)}, bf16[1,256,128]{2,1,0:T(8,128)(2,1)S(1)}, u32[]{:S(2)}, u32[]{:S(2)}) collective-permute-start(bf16[1,256,128]{2,1,0:T(8,128)(2,1)S(1)} %get-tuple-element.30), channel_id=1, source_target_pairs={{0,3},{1,2},{2,1},{3,0},{4,7},{5,6},{6,5},{7,4},{8,11},{9,10},{10,... | collective-permute-start | bytes 196616 | tf_op jit(solution)/shard_map/ppermute | solution.py:463

commit v22 on v16

--- a/solution.py
+++ b/solution.py
@@ -310,8 +310,7 @@
         turned = loop[:, k * step : (k + 1) * step].reshape(sources * step, LANES).T
         groups = [turned[g * share : (g + 1) * share] for g in range(LANES // share)]
         rows.append(jnp.concatenate(groups, axis=1))
-    both = mm(jnp.concatenate(rows, axis=0).astype(BF16), inv_ref[...])
-    loop_ref[...] = both[:, :LAGS] + both[:, LAGS:]
+    loop_ref[...] = mm(jnp.concatenate(rows, axis=0).astype(BF16), inv_ref[...])
 
 
 def last_kernel(slots, spec_ref, inv_ref, *refs):
@@ -472,7 +471,7 @@
     summed = lax.all_to_all(crossed, ("seg", "chan"), 0, 0, tiled=True)
     columns = np.arange(2 * BINS).reshape(devices, seg_count, -1).swapaxes(0, 1).reshape(-1)
     loop_inverse = inverse_table(seg_count, order[columns], part[columns]).T
-    loop_inverse = np.concatenate(split_np(loop_inverse), axis=1)
+    loop_inverse = loop_inverse.astype(jnp.bfloat16)
     near, loop = pl.pallas_call(
         functools.partial(last_kernel, slots),
         out_shape=[near_shape, jax.ShapeDtypeStruct((slots * share, LAGS), F32)],

time: 41.9 us -> 41.8 us (level)
  no operation moved by 1% of the time
where the time goes in v22:
time: 41.8 us; the launch traced here: 41.5 us
  starting transfers between devices  14.5 us (35%)
  blocking collectives  10.7 us (26%)
  Pallas kernels  8.72 us (21%)
  waiting for transfers between devices  6.58 us (16%)
  between operations  0.89 us (2%)
    all_to_all x1, blocking collectives, body(): summed = lax.all_to_all(crossed, ('seg', 'chan'), 0, 0, tiled=True)  10.7 us
    all_to_all x1, waiting for transfers between devices, body(): moved = lax.all_to_all(spread, ('seg', 'chan'), 0, 0, tiled=True)  5.7 us
    all_to_all x1, starting transfers between devices, body(): moved = lax.all_to_all(spread, ('seg', 'chan'), 0, 0, tiled=True)  4.73 us
    ppermute x1, starting transfers between devices, body(): after = lax.ppermute(down, 'chan', [(j, i) for i, j in ring])  3.04 us
    ppermute x1, starting transfers between devices, body(): rim = lax.ppermute(rim, 'seg', route)  2.49 us
    ppermute x1, starting transfers between devices, body(): before = lax.ppermute(up, 'chan', ring)  2.35 us
    pallas_call x1, Pallas kernels, body(): pl.pallas_call(near_kernel, out_shape=[jax.ShapeDtypeStruct((near_each, L...  2.06 us
    pallas_call x1, Pallas kernels, body(): pl.pallas_call(spectrum_kernel, out_shape=[jax.ShapeDtypeStruct((2 * BINS...  1.96 us
  transfers between devices with their start and end apart: 7, of which 2 were waited for; matrix products, arithmetic and copies ran while one was open for 0% of the time, Pallas kernels for 13%

profile of v22, /device:TPU:0, one launch (start us, length us, event | category | flops | bytes accessed | tf_op | source)
XLA Modules:
  0.0 41.5 jit_solution(1660886088686197349)
XLA Ops:
  0.6 0.0 copy-start.12
  0.6 0.0 copy-start.13
  0.7 0.0 copy-start.8
  0.7 0.0 copy-start.9
  0.7 1.1 %history.1 = f32[64,128]{1,0:T(8,128)S(1)} custom-call(f32[128,4096]{1,0:T(8,128)} %rec_hbm.1), custom_call_target="tpu_custom_call" | custom-call | flops 10000000000 | bytes 20000000 | tf_op jit(solution)/shard_map/history/pallas_call | solution.py:371
  1.8 0.0 copy-start
  1.8 0.0 copy-start.3
  1.8 0.0 copy-start.4
  1.8 2.5 %collective-permute-start = (f32[64,128]{1,0:T(8,128)S(1)}, f32[64,128]{1,0:T(8,128)S(1)}, u32[]{:S(2)}, u32[]{:S(2)}) collective-permute-start(f32[64,128]{1,0:T(8,128)S(1)} %history.1), channel_id=1, source_target_pairs={{0,1},{1,2},{2,3},{4,5},{5,6},{6,7},{8,9},{9,10},{10,11},{12,13},{... | collective-permute-start | bytes 98312 | tf_op jit(solution)/shard_map/ppermute | solution.py:383
  4.3 0.0 copy-done.12
  4.3 0.0 copy-done.13
  4.3 0.0 copy-done.8
  4.3 0.0 copy-done.9
  4.4 0.0 copy-start.10
  4.4 0.0 copy-start.11
  4.4 2.0 %filter_and_transform.1 = (f32[1024,128]{1,0:T(8,128)S(1)}, f32[8,128]{1,0:T(8,128)S(1)}, f32[16,128]{1,0:T(8,128)S(1)}) custom-call(f32[1,64]{1,0:T(1,128)S(1)} %bitcast.8, f32[128,4096]{1,0:T(8,128)S(1)} %copy-done.8, bf16[256,768]{1,0:T(8,128)(2,1)S(1)} %copy-done.12, f32[256,128]{1,0:T(8,128)S(1)} %copy-done.13), custom_call_target="tpu_custom_call" | custom-call | flops 1000000000 | bytes 5000000 | tf_op jit(solution)/shard_map/filter_and_transform/pallas_call | solution.py:385
  6.3 0.0 collective-permute-done.rim_ref
  6.4 0.0 copy-done
  6.4 0.0 copy-done.3
  6.4 0.0 copy-done.4
  6.4 1.4 %whiten.1 = (bf16[32,2,16,128]{3,2,1,0:T(8,128)(2,1)}, bf16[512,128]{1,0:T(8,128)(2,1)S(1)}, bf16[512,128]{1,0:T(8,128)(2,1)S(1)}) custom-call(f32[1024,128]{1,0:T(8,128)S(1)} %get-tuple-element.20.spec_ref, f32[64,128]{1,0:T(8,128)S(1)} %collective-permute-done.rim_ref, f32[8,128]{1,0:T(8,128)S(1)} %get-tuple-element.21.mean_ref, ...), custom_call_target="tpu_custom_call" | custom-call | tf_op jit(solution)/shard_map/whiten/pallas_call | solution.py:403
  7.8 2.4 %collective-permute-start.1 = (bf16[512,128]{1,0:T(8,128)(2,1)S(1)}, bf16[512,128]{1,0:T(8,128)(2,1)S(1)}, u32[]{:S(2)}, u32[]{:S(2)}) collective-permute-start(bf16[512,128]{1,0:T(8,128)(2,1)S(1)} %get-tuple-element.24), channel_id=1, source_target_pairs={{0,4},{4,8},{8,12},{12,16},{16,20},{20,24},{24,28},{28,0},{1,5},{5... | collective-permute-start | bytes 393224 | tf_op jit(solution)/shard_map/ppermute | solution.py:420
  10.2 3.0 %collective-permute-start.2 = (bf16[512,128]{1,0:T(8,128)(2,1)S(1)}, bf16[512,128]{1,0:T(8,128)(2,1)S(1)}, u32[]{:S(2)}, u32[]{:S(2)}) collective-permute-start(bf16[512,128]{1,0:T(8,128)(2,1)S(1)} %get-tuple-element.25), channel_id=1, source_target_pairs={{4,0},{8,4},{12,8},{16,12},{20,16},{24,20},{28,24},{0,28},{5,1},{9... | collective-permute-start | bytes 393224 | tf_op jit(solution)/shard_map/ppermute | solution.py:421
  13.2 4.7 %all-to-all-start = ((bf16[32,2,16,128]{3,2,1,0:T(8,128)(2,1)}), bf16[32,2,16,128]{3,2,1,0:T(8,128)(2,1)S(1)}, u32[]{:S(2)}, u32[]{:S(2)}) async-start(bf16[32,2,16,128]{3,2,1,0:T(8,128)(2,1)} %get-tuple-element.23.white_ref), calls=%async_computation | async-start | bytes 524288 | tf_op jit(solution)/shard_map/all_to_all | solution.py:416
  18.0 0.0 copy-start.1
  18.0 0.0 copy-start.5
  18.0 0.0 copy-start.6
  18.0 0.0 copy-start.7
  18.0 0.0 copy-start.2
  18.0 0.0 collective-permute-done.1.before_ref
  18.0 0.9 %collective-permute-done.2.after_ref = bf16[512,128]{1,0:T(8,128)(2,1)S(1)} collective-permute-done((bf16[512,128]{1,0:T(8,128)(2,1)S(1)}, bf16[512,128]{1,0:T(8,128)(2,1)S(1)}, u32[]{:S(2)}, u32[]{:S(2)}) %collective-permute-start.2) | collective-permute-done | bytes 131104 | tf_op jit(solution)/shard_map/ppermute | solution.py:421
  18.9 0.0 copy-done.10
  18.9 0.0 copy-done.11
  18.9 2.1 %near_lags.1 = (bf16[1,256,128]{2,1,0:T(8,128)(2,1)S(1)}, bf16[1,256,128]{2,1,0:T(8,128)(2,1)S(1)}, bf16[1,256,128]{2,1,0:T(8,128)(2,1)S(1)}, bf16[1,256,128]{2,1,0:T(8,128)(2,1)S(1)}) custom-call(s32[4]{0:T(128)S(1)} %copy-done.10, bf16[32,2,16,128]{3,2,1,0:T(8,128)(2,1)} %get-tuple-element.23.white_ref, ...), custom_call_target="tpu_custom_call" | custom-call | flops 20000000000 | bytes 20000000 | tf_op jit(solution)/shard_map/near_lags/pallas_call | solution.py:425
  21.0 0.4 collective-permute-start.3
  21.3 0.9 %collective-permute-start.4 = (bf16[1,256,128]{2,1,0:T(8,128)(2,1)S(1)}, bf16[1,256,128]{2,1,0:T(8,128)(2,1)S(1)}, u32[]{:S(2)}, u32[]{:S(2)}) collective-permute-start(bf16[1,256,128]{2,1,0:T(8,128)(2,1)S(1)} %get-tuple-element.29), channel_id=1, source_target_pairs={{0,2},{1,3},{2,0},{3,1},{4,6},{5,7},{6,4},{7,5},{8,10},{9,11},{10,... | collective-permute-start | bytes 196616 | tf_op jit(solution)/shard_map/ppermute | solution.py:440
  22.2 0.7 %collective-permute-start.5 = (bf16[1,256,128]{2,1,0:T(8,128)(2,1)S(1)}, bf16[1,256,128]{2,1,0:T(8,128)(2,1)S(1)}, u32[]{:S(2)}, u32[]{:S(2)}) collective-permute-start(bf16[1,256,128]{2,1,0:T(8,128)(2,1)S(1)} %get-tuple-element.30), channel_id=1, source_target_pairs={{0,3},{1,2},{2,1},{3,0},{4,7},{5,6},{6,5},{7,4},{8,11},{9,10},{10,... | collective-permute-start | bytes 196616 | tf_op jit(solution)/shard_map/ppermute | solution.py:440
  22.9 5.7 %all-to-all-done = bf16[32,2,16,128]{3,2,1,0:T(8,128)(2,1)S(1)} async-done(((bf16[32,2,16,128]{3,2,1,0:T(8,128)(2,1)}), bf16[32,2,16,128]{3,2,1,0:T(8,128)(2,1)S(1)}, u32[]{:S(2)}, u32[]{:S(2)}) %all-to-all-start) | async-done | bytes 262176 | tf_op jit(solution)/shard_map/all_to_all | solution.py:416
  28.6 0.0 copy-done.1
  28.6 0.0 copy-done.5
  28.6 0.0 copy-done.6
  28.6 0.0 copy-done.7
  28.6 1.2 %loop_spectra.1 = bf16[4,8,24,128]{3,2,1,0:T(8,128)(2,1)S(1)} custom-call(s32[3,8]{1,0:T(4,128)S(1)} %bitcast.7, s32[8]{0:T(128)S(1)} %copy-done.7, bf16[128,128]{1,0:T(8,128)(2,1)S(1)} %copy-done.5, bf16[512,512]{1,0:T(8,128)(2,1)S(1)} %copy-done.1, bf16[4,8,2,16,128]{4,3,2,1,0:T(8,128)(2,1)S(1)} %bitcast.5), custom_call_target="tpu_custom_call" | custom-call | tf_op jit(solution)/shard_map/loop_spectra/pallas_call | solution.py:461
  29.9 0.0 collective-permute-done.3.refs_1_
  29.9 0.0 collective-permute-done.4.refs_2_
  29.9 0.0 collective-permute-done.5.refs_3_
  29.9 10.7 %all_to_all.10.spec_ref = bf16[32,24,128]{2,1,0:T(8,128)(2,1)S(1)} all-to-all(bf16[32,24,128]{2,1,0:T(8,128)(2,1)S(1)} %bitcast.6), channel_id=1, replica_groups=mesh['chan'=8,'seg'=4] {'seg','chan'}, dimensions={0} | all-to-all | bytes 393216 | tf_op jit(solution)/shard_map/all_to_all | solution.py:471
  40.6 0.9 %lags.1 = (f32[128,1,256]{2,1,0:T(1,128)}, f32[96,256]{1,0:T(8,128)}) custom-call(bf16[32,24,128]{2,1,0:T(8,128)(2,1)S(1)} %all_to_all.10.spec_ref, bf16[1024,256]{1,0:T(8,128)(2,1)S(1)} %copy-done.2, bf16[1,256,128]{2,1,0:T(8,128)(2,1)S(1)} %get-tuple-element.32.refs_0_, bf16[1,256,128]{2,1,0:T(8,128)(2,1)S(1)} %collective-permute-done.3.refs_1_, ...), custom_call_target="tpu_custom_call" | custom-call | tf_op jit(solution)/shard_map/lags/pallas_call | solution.py:475
  (1 shorter events, 0.0 us)
Async XLA Ops:
  0.6 3.7 %copy-start.12 = (bf16[256,768]{1,0:T(8,128)(2,1)S(1)}, bf16[256,768]{1,0:T(8,128)(2,1)}, u32[]{:S(2)}) copy-start(bf16[256,768]{1,0:T(8,128)(2,1)} %constant.18.clone.tab_ref) | copy-start | bytes 1179652
  0.6 3.7 %copy-start.13 = (f32[256,128]{1,0:T(8,128)S(1)}, f32[256,128]{1,0:T(8,128)}, u32[]{:S(2)}) copy-start(f32[256,128]{1,0:T(8,128)} %constant.19.clone.twist_ref) | copy-start | bytes 393220
  0.7 3.7 %copy-start.8 = (f32[128,4096]{1,0:T(8,128)S(1)}, f32[128,4096]{1,0:T(8,128)}, u32[]{:S(2)}) copy-start(f32[128,4096]{1,0:T(8,128)} %rec_hbm.1) | copy-start | bytes 6291460
  0.7 3.7 %copy-start.9 = (f32[64]{0:T(128)S(1)}, f32[64]{0:T(128)}, u32[]{:S(2)}) copy-start(f32[64]{0:T(128)} %param.15) | copy-start | bytes 772
  1.8 4.6 %copy-start = (bf16[512,512]{1,0:T(8,128)(2,1)S(1)}, bf16[512,512]{1,0:T(8,128)(2,1)}, u32[]{:S(2)}) copy-start(bf16[512,512]{1,0:T(8,128)(2,1)} %constant.21.clone.band_ref) | copy-start | bytes 1572868
  1.8 4.6 %copy-start.3 = (f32[512,128]{1,0:T(8,128)S(1)}, f32[512,128]{1,0:T(8,128)}, u32[]{:S(2)}) copy-start(f32[512,128]{1,0:T(8,128)} %constant.22.clone.share_ref) | copy-start | bytes 786436
  1.8 4.6 %copy-start.4 = (bf16[1024,128]{1,0:T(8,128)(2,1)S(1)}, bf16[1024,128]{1,0:T(8,128)(2,1)}, u32[]{:S(2)}) copy-start(bf16[1024,128]{1,0:T(8,128)(2,1)} %constant.20.clone.edge_ref) | copy-start | bytes 786436
  1.8 4.5 %collective-permute-start = (f32[64,128]{1,0:T(8,128)S(1)}, f32[64,128]{1,0:T(8,128)S(1)}, u32[]{:S(2)}, u32[]{:S(2)}) collective-permute-start(f32[64,128]{1,0:T(8,128)S(1)} %history.1), channel_id=1, source_target_pairs={{0,1},{1,2},{2,3},{4,5},{5,6},{6,7},{8,9},{9,10},{10,11},{12,13},{... | collective-permute-start | bytes 98312 | tf_op jit(solution)/shard_map/ppermute | solution.py:383
  4.4 14.5 %copy-start.10 = (s32[4]{0:T(128)S(1)}, s32[4]{0:T(128)}, u32[]{:S(2)}) copy-start(s32[4]{0:T(128)} %offs_ref.1) | copy-start | bytes 52
  4.4 14.5 %copy-start.11 = (bf16[512,1024]{1,0:T(8,128)(2,1)S(1)}, bf16[512,1024]{1,0:T(8,128)(2,1)}, u32[]{:S(2)}) copy-start(bf16[512,1024]{1,0:T(8,128)(2,1)} %constant.23.clone.inv_ref) | copy-start | bytes 3145732
  7.8 10.2 %collective-permute-start.1 = (bf16[512,128]{1,0:T(8,128)(2,1)S(1)}, bf16[512,128]{1,0:T(8,128)(2,1)S(1)}, u32[]{:S(2)}, u32[]{:S(2)}) collective-permute-start(bf16[512,128]{1,0:T(8,128)(2,1)S(1)} %get-tuple-element.24), channel_id=1, source_target_pairs={{0,4},{4,8},{8,12},{12,16},{16,20},{20,24},{24,28},{28,0},{1,5},{5... | collective-permute-start | bytes 393224 | tf_op jit(solution)/shard_map/ppermute | solution.py:420
  10.2 8.7 %collective-permute-start.2 = (bf16[512,128]{1,0:T(8,128)(2,1)S(1)}, bf16[512,128]{1,0:T(8,128)(2,1)S(1)}, u32[]{:S(2)}, u32[]{:S(2)}) collective-permute-start(bf16[512,128]{1,0:T(8,128)(2,1)S(1)} %get-tuple-element.25), channel_id=1, source_target_pairs={{4,0},{8,4},{12,8},{16,12},{20,16},{24,20},{28,24},{0,28},{5,1},{9... | collective-permute-start | bytes 393224 | tf_op jit(solution)/shard_map/ppermute | solution.py:421
  13.2 15.4 %all-to-all-start = ((bf16[32,2,16,128]{3,2,1,0:T(8,128)(2,1)}), bf16[32,2,16,128]{3,2,1,0:T(8,128)(2,1)S(1)}, u32[]{:S(2)}, u32[]{:S(2)}) async-start(bf16[32,2,16,128]{3,2,1,0:T(8,128)(2,1)} %get-tuple-element.23.white_ref), calls=%async_computation | async-start | bytes 524288 | tf_op jit(solution)/shard_map/all_to_all | solution.py:416
  18.0 10.6 %copy-start.1 = (bf16[512,512]{1,0:T(8,128)(2,1)S(1)}, bf16[512,512]{1,0:T(8,128)(2,1)}, u32[]{:S(2)}) copy-start(bf16[512,512]{1,0:T(8,128)(2,1)} %constant.25.clone.pack_ref) | copy-start | bytes 1572868
  18.0 10.6 %copy-start.5 = (bf16[128,128]{1,0:T(8,128)(2,1)S(1)}, bf16[128,128]{1,0:T(8,128)(2,1)}, u32[]{:S(2)}) copy-start(bf16[128,128]{1,0:T(8,128)(2,1)} %constant.24.clone.flip_ref) | copy-start | bytes 98308
  18.0 10.6 %copy-start.6 = (s32[8,3]{0,1:T(4,128)S(1)}, s32[8,3]{0,1:T(4,128)}, u32[]{:S(2)}) copy-start(s32[8,3]{0,1:T(4,128)} %param.17) | copy-start | bytes 292
  18.0 10.6 %copy-start.7 = (s32[8]{0:T(128)S(1)}, s32[8]{0:T(128)}, u32[]{:S(2)}) copy-start(s32[8]{0:T(128)} %count_ref.1) | copy-start | bytes 100
  18.0 22.6 %copy-start.2 = (bf16[1024,256]{1,0:T(8,128)(2,1)S(1)}, bf16[1024,256]{1,0:T(8,128)(2,1)}, u32[]{:S(2)}) copy-start(bf16[1024,256]{1,0:T(8,128)(2,1)} %constant.26.clone.inv_ref) | copy-start | bytes 1572868
  21.0 8.9 %collective-permute-start.3 = (bf16[1,256,128]{2,1,0:T(8,128)(2,1)S(1)}, bf16[1,256,128]{2,1,0:T(8,128)(2,1)S(1)}, u32[]{:S(2)}, u32[]{:S(2)}) collective-permute-start(bf16[1,256,128]{2,1,0:T(8,128)(2,1)S(1)} %get-tuple-element.28), channel_id=1, source_target_pairs={{0,1},{1,0},{2,3},{3,2},{4,5},{5,4},{6,7},{7,6},{8,9},{9,8},{10,11... | collective-permute-start | bytes 196616 | tf_op jit(solution)/shard_map/ppermute | solution.py:440
  21.3 8.6 %collective-permute-start.4 = (bf16[1,256,128]{2,1,0:T(8,128)(2,1)S(1)}, bf16[1,256,128]{2,1,0:T(8,128)(2,1)S(1)}, u32[]{:S(2)}, u32[]{:S(2)}) collective-permute-start(bf16[1,256,128]{2,1,0:T(8,128)(2,1)S(1)} %get-tuple-element.29), channel_id=1, source_target_pairs={{0,2},{1,3},{2,0},{3,1},{4,6},{5,7},{6,4},{7,5},{8,10},{9,11},{10,... | collective-permute-start | bytes 196616 | tf_op jit(solution)/shard_map/ppermute | solution.py:440
  22.2 7.7 %collective-permute-start.5 = (bf16[1,256,128]{2,1,0:T(8,128)(2,1)S(1)}, bf16[1,256,128]{2,1,0:T(8,128)(2,1)S(1)}, u32[]{:S(2)}, u32[]{:S(2)}) collective-permute-start(bf16[1,256,128]{2,1,0:T(8,128)(2,1)S(1)} %get-tuple-element.30), channel_id=1, source_target_pairs={{0,3},{1,2},{2,1},{3,0},{4,7},{5,6},{6,5},{7,4},{8,11},{9,10},{10,... | collective-permute-start | bytes 196616 | tf_op jit(solution)/shard_map/ppermute | solution.py:440

commit v23 on v22

--- a/solution.py
+++ b/solution.py
@@ -113,9 +113,14 @@
 
 def rim_kernel(rec_hbm, rim_ref, tail_ref, sem):
     length = rec_hbm.shape[1]
-    copy = pltpu.make_async_copy(rec_hbm.at[:, pl.ds(length - LANES, LANES)], tail_ref, sem)
-    copy.start()
-    copy.wait()
+    copies = []
+    for i in range(4):
+        part = pl.ds(i * LANES // 4, LANES // 4)
+        source = rec_hbm.at[part, pl.ds(length - LANES, LANES)]
+        copies.append(pltpu.make_async_copy(source, tail_ref.at[part], sem.at[i]))
+        copies[i].start()
+    for copy in copies:
+        copy.wait()
     rim_ref[...] = tail_ref[...].T[LANES - TAPS :]
 
 
@@ -314,8 +319,12 @@
 
 
 def last_kernel(slots, spec_ref, inv_ref, *refs):
-    turn_kernel(*refs[:-1])
-    loop_lag_kernel(slots, spec_ref, inv_ref, refs[-1])
+    lag_refs, (near_hbm, loop_ref, near_ref, sem) = refs[:-4], refs[-4:]
+    turn_kernel(*lag_refs, near_ref)
+    copy = pltpu.make_async_copy(near_ref, near_hbm, sem)
+    copy.start()
+    loop_lag_kernel(slots, spec_ref, inv_ref, loop_ref)
+    copy.wait()
 
 
 def vmem(count):
@@ -373,7 +382,7 @@
         out_shape=jax.ShapeDtypeStruct((TAPS, chans), F32),
         in_specs=hbm(1),
         out_specs=pl.BlockSpec(memory_space=pltpu.VMEM),
-        scratch_shapes=[pltpu.VMEM((chans, LANES), F32), pltpu.SemaphoreType.DMA],
+        scratch_shapes=[pltpu.VMEM((chans, LANES), F32), pltpu.SemaphoreType.DMA((4,))],
         compiler_params=PARAMS,
         cost_estimate=pl.CostEstimate(
             flops=10_000_000_000, bytes_accessed=20_000_000, transcendentals=0
@@ -476,7 +485,11 @@
         functools.partial(last_kernel, slots),
         out_shape=[near_shape, jax.ShapeDtypeStruct((slots * share, LAGS), F32)],
         in_specs=vmem(2 + seg_count),
-        out_specs=vmem(2),
+        out_specs=hbm(1) + vmem(1),
+        scratch_shapes=[
+            pltpu.VMEM((chans, near_each, LAGS), F32),
+            pltpu.SemaphoreType.DMA,
+        ],
         compiler_params=PARAMS,
         name="lags",
     )(summed, loop_inverse, *lags)

time: 41.8 us -> 42.4 us (1.014)
  Pallas kernels: 8.72 us -> 9.29 us
    pallas_call x1, Pallas kernels: 0.92 us -> 1.52 us  [body(): pl.pallas_call(functools.partial(last_kernel, slots), out_shape=[near_sha...]
where the time goes in v23:
time: 42.4 us; the launch traced here: 42.1 us
  starting transfers between devices  14.5 us (34%)
  blocking collectives  10.7 us (25%)
  Pallas kernels  9.29 us (22%)
  waiting for transfers between devices  6.58 us (16%)
  between operations  0.89 us (2%)
    all_to_all x1, blocking collectives, body(): summed = lax.all_to_all(crossed, ('seg', 'chan'), 0, 0, tiled=True)  10.7 us
    all_to_all x1, waiting for transfers between devices, body(): moved = lax.all_to_all(spread, ('seg', 'chan'), 0, 0, tiled=True)  5.7 us
    all_to_all x1, starting transfers between devices, body(): moved = lax.all_to_all(spread, ('seg', 'chan'), 0, 0, tiled=True)  4.74 us
    ppermute x1, starting transfers between devices, body(): after = lax.ppermute(down, 'chan', [(j, i) for i, j in ring])  3.05 us
    ppermute x1, starting transfers between devices, body(): rim = lax.ppermute(rim, 'seg', route)  2.49 us
    ppermute x1, starting transfers between devices, body(): before = lax.ppermute(up, 'chan', ring)  2.34 us
    pallas_call x1, Pallas kernels, body(): pl.pallas_call(near_kernel, out_shape=[jax.ShapeDtypeStruct((near_each, L...  2.07 us
    pallas_call x1, Pallas kernels, body(): pl.pallas_call(spectrum_kernel, out_shape=[jax.ShapeDtypeStruct((2 * BINS...  1.97 us
  transfers between devices with their start and end apart: 7, of which 2 were waited for; matrix products, arithmetic and copies ran while one was open for 0% of the time, Pallas kernels for 13%

profile of v23, /device:TPU:0, one launch (start us, length us, event | category | flops | bytes accessed | tf_op | source)
XLA Modules:
  0.0 42.1 jit_solution(15770625456700805146)
XLA Ops:
  0.6 0.0 copy-start.12
  0.6 0.0 copy-start.13
  0.7 0.0 copy-start.8
  0.7 0.0 copy-start.9
  0.7 1.1 %history.1 = f32[64,128]{1,0:T(8,128)S(1)} custom-call(f32[128,4096]{1,0:T(8,128)} %rec_hbm.1), custom_call_target="tpu_custom_call" | custom-call | flops 10000000000 | bytes 20000000 | tf_op jit(solution)/shard_map/history/pallas_call | solution.py:380
  1.7 0.0 copy-start
  1.7 0.0 copy-start.3
  1.8 0.0 copy-start.4
  1.8 2.5 %collective-permute-start = (f32[64,128]{1,0:T(8,128)S(1)}, f32[64,128]{1,0:T(8,128)S(1)}, u32[]{:S(2)}, u32[]{:S(2)}) collective-permute-start(f32[64,128]{1,0:T(8,128)S(1)} %history.1), channel_id=1, source_target_pairs={{0,1},{1,2},{2,3},{4,5},{5,6},{6,7},{8,9},{9,10},{10,11},{12,13},{... | collective-permute-start | bytes 98312 | tf_op jit(solution)/shard_map/ppermute | solution.py:392
  4.3 0.0 copy-done.12
  4.3 0.0 copy-done.13
  4.3 0.0 copy-done.8
  4.3 0.0 copy-done.9
  4.3 0.0 copy-start.10
  4.3 0.0 copy-start.11
  4.3 2.0 %filter_and_transform.1 = (f32[1024,128]{1,0:T(8,128)S(1)}, f32[8,128]{1,0:T(8,128)S(1)}, f32[16,128]{1,0:T(8,128)S(1)}) custom-call(f32[1,64]{1,0:T(1,128)S(1)} %bitcast.8, f32[128,4096]{1,0:T(8,128)S(1)} %copy-done.8, bf16[256,768]{1,0:T(8,128)(2,1)S(1)} %copy-done.12, f32[256,128]{1,0:T(8,128)S(1)} %copy-done.13), custom_call_target="tpu_custom_call" | custom-call | flops 1000000000 | bytes 5000000 | tf_op jit(solution)/shard_map/filter_and_transform/pallas_call | solution.py:394
  6.3 0.0 collective-permute-done.rim_ref
  6.3 0.0 copy-done
  6.3 0.0 copy-done.3
  6.3 0.0 copy-done.4
  6.3 1.4 %whiten.1 = (bf16[32,2,16,128]{3,2,1,0:T(8,128)(2,1)}, bf16[512,128]{1,0:T(8,128)(2,1)S(1)}, bf16[512,128]{1,0:T(8,128)(2,1)S(1)}) custom-call(f32[1024,128]{1,0:T(8,128)S(1)} %get-tuple-element.20.spec_ref, f32[64,128]{1,0:T(8,128)S(1)} %collective-permute-done.rim_ref, f32[8,128]{1,0:T(8,128)S(1)} %get-tuple-element.21.mean_ref, ...), custom_call_target="tpu_custom_call" | custom-call | tf_op jit(solution)/shard_map/whiten/pallas_call | solution.py:412
  7.8 2.3 %collective-permute-start.1 = (bf16[512,128]{1,0:T(8,128)(2,1)S(1)}, bf16[512,128]{1,0:T(8,128)(2,1)S(1)}, u32[]{:S(2)}, u32[]{:S(2)}) collective-permute-start(bf16[512,128]{1,0:T(8,128)(2,1)S(1)} %get-tuple-element.24), channel_id=1, source_target_pairs={{0,4},{4,8},{8,12},{12,16},{16,20},{20,24},{24,28},{28,0},{1,5},{5... | collective-permute-start | bytes 393224 | tf_op jit(solution)/shard_map/ppermute | solution.py:429
  10.1 3.0 %collective-permute-start.2 = (bf16[512,128]{1,0:T(8,128)(2,1)S(1)}, bf16[512,128]{1,0:T(8,128)(2,1)S(1)}, u32[]{:S(2)}, u32[]{:S(2)}) collective-permute-start(bf16[512,128]{1,0:T(8,128)(2,1)S(1)} %get-tuple-element.25), channel_id=1, source_target_pairs={{4,0},{8,4},{12,8},{16,12},{20,16},{24,20},{28,24},{0,28},{5,1},{9... | collective-permute-start | bytes 393224 | tf_op jit(solution)/shard_map/ppermute | solution.py:430
  13.2 4.7 %all-to-all-start = ((bf16[32,2,16,128]{3,2,1,0:T(8,128)(2,1)}), bf16[32,2,16,128]{3,2,1,0:T(8,128)(2,1)S(1)}, u32[]{:S(2)}, u32[]{:S(2)}) async-start(bf16[32,2,16,128]{3,2,1,0:T(8,128)(2,1)} %get-tuple-element.23.white_ref), calls=%async_computation | async-start | bytes 524288 | tf_op jit(solution)/shard_map/all_to_all | solution.py:425
  17.9 0.0 copy-start.1
  17.9 0.0 copy-start.5
  17.9 0.0 copy-start.6
  17.9 0.0 copy-start.7
  18.0 0.0 copy-start.2
  18.0 0.0 collective-permute-done.1.before_ref
  18.0 0.9 %collective-permute-done.2.after_ref = bf16[512,128]{1,0:T(8,128)(2,1)S(1)} collective-permute-done((bf16[512,128]{1,0:T(8,128)(2,1)S(1)}, bf16[512,128]{1,0:T(8,128)(2,1)S(1)}, u32[]{:S(2)}, u32[]{:S(2)}) %collective-permute-start.2) | collective-permute-done | bytes 131104 | tf_op jit(solution)/shard_map/ppermute | solution.py:430
  18.8 0.0 copy-done.10
  18.9 0.0 copy-done.11
  18.9 2.1 %near_lags.1 = (bf16[1,256,128]{2,1,0:T(8,128)(2,1)S(1)}, bf16[1,256,128]{2,1,0:T(8,128)(2,1)S(1)}, bf16[1,256,128]{2,1,0:T(8,128)(2,1)S(1)}, bf16[1,256,128]{2,1,0:T(8,128)(2,1)S(1)}) custom-call(s32[4]{0:T(128)S(1)} %copy-done.10, bf16[32,2,16,128]{3,2,1,0:T(8,128)(2,1)} %get-tuple-element.23.white_ref, ...), custom_call_target="tpu_custom_call" | custom-call | flops 20000000000 | bytes 20000000 | tf_op jit(solution)/shard_map/near_lags/pallas_call | solution.py:434
  20.9 0.4 collective-permute-start.3
  21.3 0.9 %collective-permute-start.4 = (bf16[1,256,128]{2,1,0:T(8,128)(2,1)S(1)}, bf16[1,256,128]{2,1,0:T(8,128)(2,1)S(1)}, u32[]{:S(2)}, u32[]{:S(2)}) collective-permute-start(bf16[1,256,128]{2,1,0:T(8,128)(2,1)S(1)} %get-tuple-element.29), channel_id=1, source_target_pairs={{0,2},{1,3},{2,0},{3,1},{4,6},{5,7},{6,4},{7,5},{8,10},{9,11},{10,... | collective-permute-start | bytes 196616 | tf_op jit(solution)/shard_map/ppermute | solution.py:449
  22.2 0.7 %collective-permute-start.5 = (bf16[1,256,128]{2,1,0:T(8,128)(2,1)S(1)}, bf16[1,256,128]{2,1,0:T(8,128)(2,1)S(1)}, u32[]{:S(2)}, u32[]{:S(2)}) collective-permute-start(bf16[1,256,128]{2,1,0:T(8,128)(2,1)S(1)} %get-tuple-element.30), channel_id=1, source_target_pairs={{0,3},{1,2},{2,1},{3,0},{4,7},{5,6},{6,5},{7,4},{8,11},{9,10},{10,... | collective-permute-start | bytes 196616 | tf_op jit(solution)/shard_map/ppermute | solution.py:449
  22.9 5.7 %all-to-all-done = bf16[32,2,16,128]{3,2,1,0:T(8,128)(2,1)S(1)} async-done(((bf16[32,2,16,128]{3,2,1,0:T(8,128)(2,1)}), bf16[32,2,16,128]{3,2,1,0:T(8,128)(2,1)S(1)}, u32[]{:S(2)}, u32[]{:S(2)}) %all-to-all-start) | async-done | bytes 262176 | tf_op jit(solution)/shard_map/all_to_all | solution.py:425
  28.6 0.0 copy-done.1
  28.6 0.0 copy-done.5
  28.6 0.0 copy-done.6
  28.6 0.0 copy-done.7
  28.6 1.2 %loop_spectra.1 = bf16[4,8,24,128]{3,2,1,0:T(8,128)(2,1)S(1)} custom-call(s32[3,8]{1,0:T(4,128)S(1)} %bitcast.7, s32[8]{0:T(128)S(1)} %copy-done.7, bf16[128,128]{1,0:T(8,128)(2,1)S(1)} %copy-done.5, bf16[512,512]{1,0:T(8,128)(2,1)S(1)} %copy-done.1, bf16[4,8,2,16,128]{4,3,2,1,0:T(8,128)(2,1)S(1)} %bitcast.5), custom_call_target="tpu_custom_call" | custom-call | tf_op jit(solution)/shard_map/loop_spectra/pallas_call | solution.py:470
  29.8 0.0 collective-permute-done.3.refs_1_
  29.8 0.0 collective-permute-done.4.refs_2_
  29.8 0.0 collective-permute-done.5.refs_3_
  29.9 10.7 %all_to_all.10.spec_ref = bf16[32,24,128]{2,1,0:T(8,128)(2,1)S(1)} all-to-all(bf16[32,24,128]{2,1,0:T(8,128)(2,1)S(1)} %bitcast.6), channel_id=1, replica_groups=mesh['chan'=8,'seg'=4] {'seg','chan'}, dimensions={0} | all-to-all | bytes 393216 | tf_op jit(solution)/shard_map/all_to_all | solution.py:480
  40.6 1.5 %lags.1 = (f32[128,1,256]{2,1,0:T(1,128)}, f32[96,256]{1,0:T(8,128)}) custom-call(bf16[32,24,128]{2,1,0:T(8,128)(2,1)S(1)} %all_to_all.10.spec_ref, bf16[1024,256]{1,0:T(8,128)(2,1)S(1)} %copy-done.2, bf16[1,256,128]{2,1,0:T(8,128)(2,1)S(1)} %get-tuple-element.32.refs_0_, bf16[1,256,128]{2,1,0:T(8,128)(2,1)S(1)} %collective-permute-done.3.refs_1_, ...), custom_call_target="tpu_custom_call" | custom-call | tf_op jit(solution)/shard_map/lags/pallas_call | solution.py:484
  (1 shorter events, 0.0 us)
Async XLA Ops:
  0.6 3.6 %copy-start.12 = (bf16[256,768]{1,0:T(8,128)(2,1)S(1)}, bf16[256,768]{1,0:T(8,128)(2,1)}, u32[]{:S(2)}) copy-start(bf16[256,768]{1,0:T(8,128)(2,1)} %constant.18.clone.tab_ref) | copy-start | bytes 1179652
  0.6 3.6 %copy-start.13 = (f32[256,128]{1,0:T(8,128)S(1)}, f32[256,128]{1,0:T(8,128)}, u32[]{:S(2)}) copy-start(f32[256,128]{1,0:T(8,128)} %constant.19.clone.twist_ref) | copy-start | bytes 393220
  0.7 3.6 %copy-start.8 = (f32[128,4096]{1,0:T(8,128)S(1)}, f32[128,4096]{1,0:T(8,128)}, u32[]{:S(2)}) copy-start(f32[128,4096]{1,0:T(8,128)} %rec_hbm.1) | copy-start | bytes 6291460
  0.7 3.6 %copy-start.9 = (f32[64]{0:T(128)S(1)}, f32[64]{0:T(128)}, u32[]{:S(2)}) copy-start(f32[64]{0:T(128)} %param.15) | copy-start | bytes 772
  1.7 4.6 %copy-start = (bf16[512,512]{1,0:T(8,128)(2,1)S(1)}, bf16[512,512]{1,0:T(8,128)(2,1)}, u32[]{:S(2)}) copy-start(bf16[512,512]{1,0:T(8,128)(2,1)} %constant.21.clone.band_ref) | copy-start | bytes 1572868
  1.7 4.6 %copy-start.3 = (f32[512,128]{1,0:T(8,128)S(1)}, f32[512,128]{1,0:T(8,128)}, u32[]{:S(2)}) copy-start(f32[512,128]{1,0:T(8,128)} %constant.22.clone.share_ref) | copy-start | bytes 786436
  1.8 4.6 %copy-start.4 = (bf16[1024,128]{1,0:T(8,128)(2,1)S(1)}, bf16[1024,128]{1,0:T(8,128)(2,1)}, u32[]{:S(2)}) copy-start(bf16[1024,128]{1,0:T(8,128)(2,1)} %constant.20.clone.edge_ref) | copy-start | bytes 786436
  1.8 4.5 %collective-permute-start = (f32[64,128]{1,0:T(8,128)S(1)}, f32[64,128]{1,0:T(8,128)S(1)}, u32[]{:S(2)}, u32[]{:S(2)}) collective-permute-start(f32[64,128]{1,0:T(8,128)S(1)} %history.1), channel_id=1, source_target_pairs={{0,1},{1,2},{2,3},{4,5},{5,6},{6,7},{8,9},{9,10},{10,11},{12,13},{... | collective-permute-start | bytes 98312 | tf_op jit(solution)/shard_map/ppermute | solution.py:392
  4.3 14.5 %copy-start.10 = (s32[4]{0:T(128)S(1)}, s32[4]{0:T(128)}, u32[]{:S(2)}) copy-start(s32[4]{0:T(128)} %offs_ref.1) | copy-start | bytes 52
  4.3 14.5 %copy-start.11 = (bf16[512,1024]{1,0:T(8,128)(2,1)S(1)}, bf16[512,1024]{1,0:T(8,128)(2,1)}, u32[]{:S(2)}) copy-start(bf16[512,1024]{1,0:T(8,128)(2,1)} %constant.23.clone.inv_ref) | copy-start | bytes 3145732
  7.8 10.2 %collective-permute-start.1 = (bf16[512,128]{1,0:T(8,128)(2,1)S(1)}, bf16[512,128]{1,0:T(8,128)(2,1)S(1)}, u32[]{:S(2)}, u32[]{:S(2)}) collective-permute-start(bf16[512,128]{1,0:T(8,128)(2,1)S(1)} %get-tuple-element.24), channel_id=1, source_target_pairs={{0,4},{4,8},{8,12},{12,16},{16,20},{20,24},{24,28},{28,0},{1,5},{5... | collective-permute-start | bytes 393224 | tf_op jit(solution)/shard_map/ppermute | solution.py:429
  10.1 8.7 %collective-permute-start.2 = (bf16[512,128]{1,0:T(8,128)(2,1)S(1)}, bf16[512,128]{1,0:T(8,128)(2,1)S(1)}, u32[]{:S(2)}, u32[]{:S(2)}) collective-permute-start(bf16[512,128]{1,0:T(8,128)(2,1)S(1)} %get-tuple-element.25), channel_id=1, source_target_pairs={{4,0},{8,4},{12,8},{16,12},{20,16},{24,20},{28,24},{0,28},{5,1},{9... | collective-permute-start | bytes 393224 | tf_op jit(solution)/shard_map/ppermute | solution.py:430
  13.2 15.4 %all-to-all-start = ((bf16[32,2,16,128]{3,2,1,0:T(8,128)(2,1)}), bf16[32,2,16,128]{3,2,1,0:T(8,128)(2,1)S(1)}, u32[]{:S(2)}, u32[]{:S(2)}) async-start(bf16[32,2,16,128]{3,2,1,0:T(8,128)(2,1)} %get-tuple-element.23.white_ref), calls=%async_computation | async-start | bytes 524288 | tf_op jit(solution)/shard_map/all_to_all | solution.py:425
  17.9 10.6 %copy-start.1 = (bf16[512,512]{1,0:T(8,128)(2,1)S(1)}, bf16[512,512]{1,0:T(8,128)(2,1)}, u32[]{:S(2)}) copy-start(bf16[512,512]{1,0:T(8,128)(2,1)} %constant.25.clone.pack_ref) | copy-start | bytes 1572868
  17.9 10.6 %copy-start.5 = (bf16[128,128]{1,0:T(8,128)(2,1)S(1)}, bf16[128,128]{1,0:T(8,128)(2,1)}, u32[]{:S(2)}) copy-start(bf16[128,128]{1,0:T(8,128)(2,1)} %constant.24.clone.flip_ref) | copy-start | bytes 98308
  17.9 10.6 %copy-start.6 = (s32[8,3]{0,1:T(4,128)S(1)}, s32[8,3]{0,1:T(4,128)}, u32[]{:S(2)}) copy-start(s32[8,3]{0,1:T(4,128)} %param.17) | copy-start | bytes 292
  17.9 10.6 %copy-start.7 = (s32[8]{0:T(128)S(1)}, s32[8]{0:T(128)}, u32[]{:S(2)}) copy-start(s32[8]{0:T(128)} %count_ref.1) | copy-start | bytes 100
  18.0 22.6 %copy-start.2 = (bf16[1024,256]{1,0:T(8,128)(2,1)S(1)}, bf16[1024,256]{1,0:T(8,128)(2,1)}, u32[]{:S(2)}) copy-start(bf16[1024,256]{1,0:T(8,128)(2,1)} %constant.26.clone.inv_ref) | copy-start | bytes 1572868
  20.9 8.9 %collective-permute-start.3 = (bf16[1,256,128]{2,1,0:T(8,128)(2,1)S(1)}, bf16[1,256,128]{2,1,0:T(8,128)(2,1)S(1)}, u32[]{:S(2)}, u32[]{:S(2)}) collective-permute-start(bf16[1,256,128]{2,1,0:T(8,128)(2,1)S(1)} %get-tuple-element.28), channel_id=1, source_target_pairs={{0,1},{1,0},{2,3},{3,2},{4,5},{5,4},{6,7},{7,6},{8,9},{9,8},{10,11... | collective-permute-start | bytes 196616 | tf_op jit(solution)/shard_map/ppermute | solution.py:449
  21.3 8.6 %collective-permute-start.4 = (bf16[1,256,128]{2,1,0:T(8,128)(2,1)S(1)}, bf16[1,256,128]{2,1,0:T(8,128)(2,1)S(1)}, u32[]{:S(2)}, u32[]{:S(2)}) collective-permute-start(bf16[1,256,128]{2,1,0:T(8,128)(2,1)S(1)} %get-tuple-element.29), channel_id=1, source_target_pairs={{0,2},{1,3},{2,0},{3,1},{4,6},{5,7},{6,4},{7,5},{8,10},{9,11},{10,... | collective-permute-start | bytes 196616 | tf_op jit(solution)/shard_map/ppermute | solution.py:449
  22.2 7.7 %collective-permute-start.5 = (bf16[1,256,128]{2,1,0:T(8,128)(2,1)S(1)}, bf16[1,256,128]{2,1,0:T(8,128)(2,1)S(1)}, u32[]{:S(2)}, u32[]{:S(2)}) collective-permute-start(bf16[1,256,128]{2,1,0:T(8,128)(2,1)S(1)} %get-tuple-element.30), channel_id=1, source_target_pairs={{0,3},{1,2},{2,1},{3,0},{4,7},{5,6},{6,5},{7,4},{8,11},{9,10},{10,... | collective-permute-start | bytes 196616 | tf_op jit(solution)/shard_map/ppermute | solution.py:449

commit v24 on v22

--- a/solution.py
+++ b/solution.py
@@ -113,9 +113,14 @@
 
 def rim_kernel(rec_hbm, rim_ref, tail_ref, sem):
     length = rec_hbm.shape[1]
-    copy = pltpu.make_async_copy(rec_hbm.at[:, pl.ds(length - LANES, LANES)], tail_ref, sem)
-    copy.start()
-    copy.wait()
+    copies = []
+    for i in range(4):
+        part = pl.ds(i * LANES // 4, LANES // 4)
+        source = rec_hbm.at[part, pl.ds(length - LANES, LANES)]
+        copies.append(pltpu.make_async_copy(source, tail_ref.at[part], sem.at[i]))
+        copies[i].start()
+    for copy in copies:
+        copy.wait()
     rim_ref[...] = tail_ref[...].T[LANES - TAPS :]
 
 
@@ -373,7 +378,7 @@
         out_shape=jax.ShapeDtypeStruct((TAPS, chans), F32),
         in_specs=hbm(1),
         out_specs=pl.BlockSpec(memory_space=pltpu.VMEM),
-        scratch_shapes=[pltpu.VMEM((chans, LANES), F32), pltpu.SemaphoreType.DMA],
+        scratch_shapes=[pltpu.VMEM((chans, LANES), F32), pltpu.SemaphoreType.DMA((4,))],
         compiler_params=PARAMS,
         cost_estimate=pl.CostEstimate(
             flops=10_000_000_000, bytes_accessed=20_000_000, transcendentals=0

time: 41.8 us -> 41.8 us (level)
  no operation moved by 1% of the time
where the time goes in v24:
time: 41.8 us; the launch traced here: 41.5 us
  starting transfers between devices  14.5 us (35%)
  blocking collectives  10.7 us (26%)
  Pallas kernels  8.68 us (21%)
  waiting for transfers between devices  6.58 us (16%)
  between operations  0.89 us (2%)
    all_to_all x1, blocking collectives, body(): summed = lax.all_to_all(crossed, ('seg', 'chan'), 0, 0, tiled=True)  10.7 us
    all_to_all x1, waiting for transfers between devices, body(): moved = lax.all_to_all(spread, ('seg', 'chan'), 0, 0, tiled=True)  5.7 us
    all_to_all x1, starting transfers between devices, body(): moved = lax.all_to_all(spread, ('seg', 'chan'), 0, 0, tiled=True)  4.74 us
    ppermute x1, starting transfers between devices, body(): after = lax.ppermute(down, 'chan', [(j, i) for i, j in ring])  3.05 us
    ppermute x1, starting transfers between devices, body(): rim = lax.ppermute(rim, 'seg', route)  2.49 us
    ppermute x1, starting transfers between devices, body(): before = lax.ppermute(up, 'chan', ring)  2.34 us
    pallas_call x1, Pallas kernels, body(): pl.pallas_call(near_kernel, out_shape=[jax.ShapeDtypeStruct((near_each, L...  2.07 us
    pallas_call x1, Pallas kernels, body(): pl.pallas_call(spectrum_kernel, out_shape=[jax.ShapeDtypeStruct((2 * BINS...  1.97 us
  transfers between devices with their start and end apart: 7, of which 2 were waited for; matrix products, arithmetic and copies ran while one was open for 0% of the time, Pallas kernels for 13%

profile of v24, /device:TPU:0, one launch (start us, length us, event | category | flops | bytes accessed | tf_op | source)
XLA Modules:
  0.0 41.5 jit_solution(15566413464736918581)
XLA Ops:
  0.6 0.0 copy-start.12
  0.6 0.0 copy-start.13
  0.7 0.0 copy-start.8
  0.7 0.0 copy-start.9
  0.7 1.1 %history.1 = f32[64,128]{1,0:T(8,128)S(1)} custom-call(f32[128,4096]{1,0:T(8,128)} %rec_hbm.1), custom_call_target="tpu_custom_call" | custom-call | flops 10000000000 | bytes 20000000 | tf_op jit(solution)/shard_map/history/pallas_call | solution.py:376
  1.7 0.0 copy-start
  1.7 0.0 copy-start.3
  1.8 0.0 copy-start.4
  1.8 2.5 %collective-permute-start = (f32[64,128]{1,0:T(8,128)S(1)}, f32[64,128]{1,0:T(8,128)S(1)}, u32[]{:S(2)}, u32[]{:S(2)}) collective-permute-start(f32[64,128]{1,0:T(8,128)S(1)} %history.1), channel_id=1, source_target_pairs={{0,1},{1,2},{2,3},{4,5},{5,6},{6,7},{8,9},{9,10},{10,11},{12,13},{... | collective-permute-start | bytes 98312 | tf_op jit(solution)/shard_map/ppermute | solution.py:388
  4.3 0.0 copy-done.12
  4.3 0.0 copy-done.13
  4.3 0.0 copy-done.8
  4.3 0.0 copy-done.9
  4.3 0.0 copy-start.10
  4.3 0.0 copy-start.11
  4.3 2.0 %filter_and_transform.1 = (f32[1024,128]{1,0:T(8,128)S(1)}, f32[8,128]{1,0:T(8,128)S(1)}, f32[16,128]{1,0:T(8,128)S(1)}) custom-call(f32[1,64]{1,0:T(1,128)S(1)} %bitcast.8, f32[128,4096]{1,0:T(8,128)S(1)} %copy-done.8, bf16[256,768]{1,0:T(8,128)(2,1)S(1)} %copy-done.12, f32[256,128]{1,0:T(8,128)S(1)} %copy-done.13), custom_call_target="tpu_custom_call" | custom-call | flops 1000000000 | bytes 5000000 | tf_op jit(solution)/shard_map/filter_and_transform/pallas_call | solution.py:390
  6.3 0.0 collective-permute-done.rim_ref
  6.3 0.0 copy-done
  6.3 0.0 copy-done.3
  6.3 0.0 copy-done.4
  6.3 1.4 %whiten.1 = (bf16[32,2,16,128]{3,2,1,0:T(8,128)(2,1)}, bf16[512,128]{1,0:T(8,128)(2,1)S(1)}, bf16[512,128]{1,0:T(8,128)(2,1)S(1)}) custom-call(f32[1024,128]{1,0:T(8,128)S(1)} %get-tuple-element.20.spec_ref, f32[64,128]{1,0:T(8,128)S(1)} %collective-permute-done.rim_ref, f32[8,128]{1,0:T(8,128)S(1)} %get-tuple-element.21.mean_ref, ...), custom_call_target="tpu_custom_call" | custom-call | tf_op jit(solution)/shard_map/whiten/pallas_call | solution.py:408
  7.8 2.3 %collective-permute-start.1 = (bf16[512,128]{1,0:T(8,128)(2,1)S(1)}, bf16[512,128]{1,0:T(8,128)(2,1)S(1)}, u32[]{:S(2)}, u32[]{:S(2)}) collective-permute-start(bf16[512,128]{1,0:T(8,128)(2,1)S(1)} %get-tuple-element.24), channel_id=1, source_target_pairs={{0,4},{4,8},{8,12},{12,16},{16,20},{20,24},{24,28},{28,0},{1,5},{5... | collective-permute-start | bytes 393224 | tf_op jit(solution)/shard_map/ppermute | solution.py:425
  10.1 3.0 %collective-permute-start.2 = (bf16[512,128]{1,0:T(8,128)(2,1)S(1)}, bf16[512,128]{1,0:T(8,128)(2,1)S(1)}, u32[]{:S(2)}, u32[]{:S(2)}) collective-permute-start(bf16[512,128]{1,0:T(8,128)(2,1)S(1)} %get-tuple-element.25), channel_id=1, source_target_pairs={{4,0},{8,4},{12,8},{16,12},{20,16},{24,20},{28,24},{0,28},{5,1},{9... | collective-permute-start | bytes 393224 | tf_op jit(solution)/shard_map/ppermute | solution.py:426
  13.2 4.7 %all-to-all-start = ((bf16[32,2,16,128]{3,2,1,0:T(8,128)(2,1)}), bf16[32,2,16,128]{3,2,1,0:T(8,128)(2,1)S(1)}, u32[]{:S(2)}, u32[]{:S(2)}) async-start(bf16[32,2,16,128]{3,2,1,0:T(8,128)(2,1)} %get-tuple-element.23.white_ref), calls=%async_computation | async-start | bytes 524288 | tf_op jit(solution)/shard_map/all_to_all | solution.py:421
  17.9 0.0 copy-start.1
  17.9 0.0 copy-start.5
  17.9 0.0 copy-start.6
  17.9 0.0 copy-start.7
  18.0 0.0 copy-start.2
  18.0 0.0 collective-permute-done.1.before_ref
  18.0 0.9 %collective-permute-done.2.after_ref = bf16[512,128]{1,0:T(8,128)(2,1)S(1)} collective-permute-done((bf16[512,128]{1,0:T(8,128)(2,1)S(1)}, bf16[512,128]{1,0:T(8,128)(2,1)S(1)}, u32[]{:S(2)}, u32[]{:S(2)}) %collective-permute-start.2) | collective-permute-done | bytes 131104 | tf_op jit(solution)/shard_map/ppermute | solution.py:426
  18.8 0.0 copy-done.10
  18.9 0.0 copy-done.11
  18.9 2.1 %near_lags.1 = (bf16[1,256,128]{2,1,0:T(8,128)(2,1)S(1)}, bf16[1,256,128]{2,1,0:T(8,128)(2,1)S(1)}, bf16[1,256,128]{2,1,0:T(8,128)(2,1)S(1)}, bf16[1,256,128]{2,1,0:T(8,128)(2,1)S(1)}) custom-call(s32[4]{0:T(128)S(1)} %copy-done.10, bf16[32,2,16,128]{3,2,1,0:T(8,128)(2,1)} %get-tuple-element.23.white_ref, ...), custom_call_target="tpu_custom_call" | custom-call | flops 20000000000 | bytes 20000000 | tf_op jit(solution)/shard_map/near_lags/pallas_call | solution.py:430
  20.9 0.4 collective-permute-start.3
  21.3 0.9 %collective-permute-start.4 = (bf16[1,256,128]{2,1,0:T(8,128)(2,1)S(1)}, bf16[1,256,128]{2,1,0:T(8,128)(2,1)S(1)}, u32[]{:S(2)}, u32[]{:S(2)}) collective-permute-start(bf16[1,256,128]{2,1,0:T(8,128)(2,1)S(1)} %get-tuple-element.29), channel_id=1, source_target_pairs={{0,2},{1,3},{2,0},{3,1},{4,6},{5,7},{6,4},{7,5},{8,10},{9,11},{10,... | collective-permute-start | bytes 196616 | tf_op jit(solution)/shard_map/ppermute | solution.py:445
  22.2 0.7 %collective-permute-start.5 = (bf16[1,256,128]{2,1,0:T(8,128)(2,1)S(1)}, bf16[1,256,128]{2,1,0:T(8,128)(2,1)S(1)}, u32[]{:S(2)}, u32[]{:S(2)}) collective-permute-start(bf16[1,256,128]{2,1,0:T(8,128)(2,1)S(1)} %get-tuple-element.30), channel_id=1, source_target_pairs={{0,3},{1,2},{2,1},{3,0},{4,7},{5,6},{6,5},{7,4},{8,11},{9,10},{10,... | collective-permute-start | bytes 196616 | tf_op jit(solution)/shard_map/ppermute | solution.py:445
  22.9 5.7 %all-to-all-done = bf16[32,2,16,128]{3,2,1,0:T(8,128)(2,1)S(1)} async-done(((bf16[32,2,16,128]{3,2,1,0:T(8,128)(2,1)}), bf16[32,2,16,128]{3,2,1,0:T(8,128)(2,1)S(1)}, u32[]{:S(2)}, u32[]{:S(2)}) %all-to-all-start) | async-done | bytes 262176 | tf_op jit(solution)/shard_map/all_to_all | solution.py:421
  28.6 0.0 copy-done.1
  28.6 0.0 copy-done.5
  28.6 0.0 copy-done.6
  28.6 0.0 copy-done.7
  28.6 1.2 %loop_spectra.1 = bf16[4,8,24,128]{3,2,1,0:T(8,128)(2,1)S(1)} custom-call(s32[3,8]{1,0:T(4,128)S(1)} %bitcast.7, s32[8]{0:T(128)S(1)} %copy-done.7, bf16[128,128]{1,0:T(8,128)(2,1)S(1)} %copy-done.5, bf16[512,512]{1,0:T(8,128)(2,1)S(1)} %copy-done.1, bf16[4,8,2,16,128]{4,3,2,1,0:T(8,128)(2,1)S(1)} %bitcast.5), custom_call_target="tpu_custom_call" | custom-call | tf_op jit(solution)/shard_map/loop_spectra/pallas_call | solution.py:466
  29.8 0.0 collective-permute-done.3.refs_1_
  29.8 0.0 collective-permute-done.4.refs_2_
  29.8 0.0 collective-permute-done.5.refs_3_
  29.9 10.7 %all_to_all.10.spec_ref = bf16[32,24,128]{2,1,0:T(8,128)(2,1)S(1)} all-to-all(bf16[32,24,128]{2,1,0:T(8,128)(2,1)S(1)} %bitcast.6), channel_id=1, replica_groups=mesh['chan'=8,'seg'=4] {'seg','chan'}, dimensions={0} | all-to-all | bytes 393216 | tf_op jit(solution)/shard_map/all_to_all | solution.py:476
  40.6 0.9 %lags.1 = (f32[128,1,256]{2,1,0:T(1,128)}, f32[96,256]{1,0:T(8,128)}) custom-call(bf16[32,24,128]{2,1,0:T(8,128)(2,1)S(1)} %all_to_all.10.spec_ref, bf16[1024,256]{1,0:T(8,128)(2,1)S(1)} %copy-done.2, bf16[1,256,128]{2,1,0:T(8,128)(2,1)S(1)} %get-tuple-element.32.refs_0_, bf16[1,256,128]{2,1,0:T(8,128)(2,1)S(1)} %collective-permute-done.3.refs_1_, ...), custom_call_target="tpu_custom_call" | custom-call | tf_op jit(solution)/shard_map/lags/pallas_call | solution.py:480
  (1 shorter events, 0.0 us)
Async XLA Ops:
  0.6 3.6 %copy-start.12 = (bf16[256,768]{1,0:T(8,128)(2,1)S(1)}, bf16[256,768]{1,0:T(8,128)(2,1)}, u32[]{:S(2)}) copy-start(bf16[256,768]{1,0:T(8,128)(2,1)} %constant.18.clone.tab_ref) | copy-start | bytes 1179652
  0.6 3.6 %copy-start.13 = (f32[256,128]{1,0:T(8,128)S(1)}, f32[256,128]{1,0:T(8,128)}, u32[]{:S(2)}) copy-start(f32[256,128]{1,0:T(8,128)} %constant.19.clone.twist_ref) | copy-start | bytes 393220
  0.7 3.6 %copy-start.8 = (f32[128,4096]{1,0:T(8,128)S(1)}, f32[128,4096]{1,0:T(8,128)}, u32[]{:S(2)}) copy-start(f32[128,4096]{1,0:T(8,128)} %rec_hbm.1) | copy-start | bytes 6291460
  0.7 3.6 %copy-start.9 = (f32[64]{0:T(128)S(1)}, f32[64]{0:T(128)}, u32[]{:S(2)}) copy-start(f32[64]{0:T(128)} %param.15) | copy-start | bytes 772
  1.7 4.6 %copy-start = (bf16[512,512]{1,0:T(8,128)(2,1)S(1)}, bf16[512,512]{1,0:T(8,128)(2,1)}, u32[]{:S(2)}) copy-start(bf16[512,512]{1,0:T(8,128)(2,1)} %constant.21.clone.band_ref) | copy-start | bytes 1572868
  1.7 4.6 %copy-start.3 = (f32[512,128]{1,0:T(8,128)S(1)}, f32[512,128]{1,0:T(8,128)}, u32[]{:S(2)}) copy-start(f32[512,128]{1,0:T(8,128)} %constant.22.clone.share_ref) | copy-start | bytes 786436
  1.8 4.6 %copy-start.4 = (bf16[1024,128]{1,0:T(8,128)(2,1)S(1)}, bf16[1024,128]{1,0:T(8,128)(2,1)}, u32[]{:S(2)}) copy-start(bf16[1024,128]{1,0:T(8,128)(2,1)} %constant.20.clone.edge_ref) | copy-start | bytes 786436
  1.8 4.5 %collective-permute-start = (f32[64,128]{1,0:T(8,128)S(1)}, f32[64,128]{1,0:T(8,128)S(1)}, u32[]{:S(2)}, u32[]{:S(2)}) collective-permute-start(f32[64,128]{1,0:T(8,128)S(1)} %history.1), channel_id=1, source_target_pairs={{0,1},{1,2},{2,3},{4,5},{5,6},{6,7},{8,9},{9,10},{10,11},{12,13},{... | collective-permute-start | bytes 98312 | tf_op jit(solution)/shard_map/ppermute | solution.py:388
  4.3 14.5 %copy-start.10 = (s32[4]{0:T(128)S(1)}, s32[4]{0:T(128)}, u32[]{:S(2)}) copy-start(s32[4]{0:T(128)} %offs_ref.1) | copy-start | bytes 52
  4.3 14.5 %copy-start.11 = (bf16[512,1024]{1,0:T(8,128)(2,1)S(1)}, bf16[512,1024]{1,0:T(8,128)(2,1)}, u32[]{:S(2)}) copy-start(bf16[512,1024]{1,0:T(8,128)(2,1)} %constant.23.clone.inv_ref) | copy-start | bytes 3145732
  7.8 10.2 %collective-permute-start.1 = (bf16[512,128]{1,0:T(8,128)(2,1)S(1)}, bf16[512,128]{1,0:T(8,128)(2,1)S(1)}, u32[]{:S(2)}, u32[]{:S(2)}) collective-permute-start(bf16[512,128]{1,0:T(8,128)(2,1)S(1)} %get-tuple-element.24), channel_id=1, source_target_pairs={{0,4},{4,8},{8,12},{12,16},{16,20},{20,24},{24,28},{28,0},{1,5},{5... | collective-permute-start | bytes 393224 | tf_op jit(solution)/shard_map/ppermute | solution.py:425
  10.1 8.7 %collective-permute-start.2 = (bf16[512,128]{1,0:T(8,128)(2,1)S(1)}, bf16[512,128]{1,0:T(8,128)(2,1)S(1)}, u32[]{:S(2)}, u32[]{:S(2)}) collective-permute-start(bf16[512,128]{1,0:T(8,128)(2,1)S(1)} %get-tuple-element.25), channel_id=1, source_target_pairs={{4,0},{8,4},{12,8},{16,12},{20,16},{24,20},{28,24},{0,28},{5,1},{9... | collective-permute-start | bytes 393224 | tf_op jit(solution)/shard_map/ppermute | solution.py:426
  13.2 15.4 %all-to-all-start = ((bf16[32,2,16,128]{3,2,1,0:T(8,128)(2,1)}), bf16[32,2,16,128]{3,2,1,0:T(8,128)(2,1)S(1)}, u32[]{:S(2)}, u32[]{:S(2)}) async-start(bf16[32,2,16,128]{3,2,1,0:T(8,128)(2,1)} %get-tuple-element.23.white_ref), calls=%async_computation | async-start | bytes 524288 | tf_op jit(solution)/shard_map/all_to_all | solution.py:421
  17.9 10.6 %copy-start.1 = (bf16[512,512]{1,0:T(8,128)(2,1)S(1)}, bf16[512,512]{1,0:T(8,128)(2,1)}, u32[]{:S(2)}) copy-start(bf16[512,512]{1,0:T(8,128)(2,1)} %constant.25.clone.pack_ref) | copy-start | bytes 1572868
  17.9 10.6 %copy-start.5 = (bf16[128,128]{1,0:T(8,128)(2,1)S(1)}, bf16[128,128]{1,0:T(8,128)(2,1)}, u32[]{:S(2)}) copy-start(bf16[128,128]{1,0:T(8,128)(2,1)} %constant.24.clone.flip_ref) | copy-start | bytes 98308
  17.9 10.6 %copy-start.6 = (s32[8,3]{0,1:T(4,128)S(1)}, s32[8,3]{0,1:T(4,128)}, u32[]{:S(2)}) copy-start(s32[8,3]{0,1:T(4,128)} %param.17) | copy-start | bytes 292
  17.9 10.6 %copy-start.7 = (s32[8]{0:T(128)S(1)}, s32[8]{0:T(128)}, u32[]{:S(2)}) copy-start(s32[8]{0:T(128)} %count_ref.1) | copy-start | bytes 100
  18.0 22.6 %copy-start.2 = (bf16[1024,256]{1,0:T(8,128)(2,1)S(1)}, bf16[1024,256]{1,0:T(8,128)(2,1)}, u32[]{:S(2)}) copy-start(bf16[1024,256]{1,0:T(8,128)(2,1)} %constant.26.clone.inv_ref) | copy-start | bytes 1572868
  20.9 8.9 %collective-permute-start.3 = (bf16[1,256,128]{2,1,0:T(8,128)(2,1)S(1)}, bf16[1,256,128]{2,1,0:T(8,128)(2,1)S(1)}, u32[]{:S(2)}, u32[]{:S(2)}) collective-permute-start(bf16[1,256,128]{2,1,0:T(8,128)(2,1)S(1)} %get-tuple-element.28), channel_id=1, source_target_pairs={{0,1},{1,0},{2,3},{3,2},{4,5},{5,4},{6,7},{7,6},{8,9},{9,8},{10,11... | collective-permute-start | bytes 196616 | tf_op jit(solution)/shard_map/ppermute | solution.py:445
  21.3 8.6 %collective-permute-start.4 = (bf16[1,256,128]{2,1,0:T(8,128)(2,1)S(1)}, bf16[1,256,128]{2,1,0:T(8,128)(2,1)S(1)}, u32[]{:S(2)}, u32[]{:S(2)}) collective-permute-start(bf16[1,256,128]{2,1,0:T(8,128)(2,1)S(1)} %get-tuple-element.29), channel_id=1, source_target_pairs={{0,2},{1,3},{2,0},{3,1},{4,6},{5,7},{6,4},{7,5},{8,10},{9,11},{10,... | collective-permute-start | bytes 196616 | tf_op jit(solution)/shard_map/ppermute | solution.py:445
  22.2 7.7 %collective-permute-start.5 = (bf16[1,256,128]{2,1,0:T(8,128)(2,1)S(1)}, bf16[1,256,128]{2,1,0:T(8,128)(2,1)S(1)}, u32[]{:S(2)}, u32[]{:S(2)}) collective-permute-start(bf16[1,256,128]{2,1,0:T(8,128)(2,1)S(1)} %get-tuple-element.30), channel_id=1, source_target_pairs={{0,3},{1,2},{2,1},{3,0},{4,7},{5,6},{6,5},{7,4},{8,11},{9,10},{10,... | collective-permute-start | bytes 196616 | tf_op jit(solution)/shard_map/ppermute | solution.py:445

commit v25 on v24

--- a/solution.py
+++ b/solution.py
@@ -121,7 +121,15 @@
         copies[i].start()
     for copy in copies:
         copy.wait()
-    rim_ref[...] = tail_ref[...].T[LANES - TAPS :]
+    tail = tail_ref[...].T[LANES - TAPS :]
+    mean = jnp.sum(tail, axis=0, keepdims=True) * (1.0 / TAPS)
+    high, _ = split(mean)
+    middle, low = split(mean - high.astype(F32))
+    row = lax.broadcasted_iota(jnp.int32, (GROUP, LANES), 0)
+    means = jnp.zeros((GROUP, LANES), F32)
+    for i, part in enumerate((high, middle, low)):
+        means = jnp.where(row == i, part.astype(F32), means)
+    rim_ref[...] = jnp.concatenate([tail - mean, means], axis=0).astype(BF16)
 
 
 def spectrum_kernel(taps_ref, rec_ref, tab_ref, twist_ref, spec_ref, mean_ref, head_ref):
@@ -192,7 +200,9 @@
     down_ref,
 ):
     head_high, head_low = split(head_ref[:, LANES - TAPS :])
-    rim_high, rim_low = split(rim_ref[...] - mean_ref[0:1, :])
+    rim = rim_ref[...].astype(F32)
+    offset = jnp.sum(rim[TAPS:], axis=0, keepdims=True) - mean_ref[0:1, :]
+    rim_high, rim_low = split(rim[:TAPS] + offset)
     history = mm(
         jnp.concatenate([head_high, head_high, head_low], axis=1),
         jnp.concatenate([rim_high, rim_low, rim_high], axis=0),
@@ -375,7 +385,7 @@
     route = [(i, i + 1) for i in range(seg_count - 1)]
     rim = pl.pallas_call(
         rim_kernel,
-        out_shape=jax.ShapeDtypeStruct((TAPS, chans), F32),
+        out_shape=jax.ShapeDtypeStruct((TAPS + GROUP, chans), BF16),
         in_specs=hbm(1),
         out_specs=pl.BlockSpec(memory_space=pltpu.VMEM),
         scratch_shapes=[pltpu.VMEM((chans, LANES), F32), pltpu.SemaphoreType.DMA((4,))],

time: 41.8 us -> 41.6 us (level)
  no operation moved by 1% of the time
where the time goes in v25:
time: 41.6 us; the launch traced here: 41.4 us
  starting transfers between devices  14.4 us (35%)
  blocking collectives  10.7 us (26%)
  Pallas kernels  8.72 us (21%)
  waiting for transfers between devices  6.58 us (16%)
  between operations  0.89 us (2%)
    all_to_all x1, blocking collectives, body(): summed = lax.all_to_all(crossed, ('seg', 'chan'), 0, 0, tiled=True)  10.7 us
    all_to_all x1, waiting for transfers between devices, body(): moved = lax.all_to_all(spread, ('seg', 'chan'), 0, 0, tiled=True)  5.54 us
    all_to_all x1, starting transfers between devices, body(): moved = lax.all_to_all(spread, ('seg', 'chan'), 0, 0, tiled=True)  4.57 us
    ppermute x1, starting transfers between devices, body(): after = lax.ppermute(down, 'chan', [(j, i) for i, j in ring])  3.04 us
    ppermute x1, starting transfers between devices, body(): rim = lax.ppermute(rim, 'seg', route)  2.49 us
    ppermute x1, starting transfers between devices, body(): before = lax.ppermute(up, 'chan', ring)  2.35 us
    pallas_call x1, Pallas kernels, body(): pl.pallas_call(near_kernel, out_shape=[jax.ShapeDtypeStruct((near_each, L...  2.06 us
    pallas_call x1, Pallas kernels, body(): pl.pallas_call(spectrum_kernel, out_shape=[jax.ShapeDtypeStruct((2 * BINS...  2 us
  transfers between devices with their start and end apart: 7, of which 2 were waited for; matrix products, arithmetic and copies ran while one was open for 0% of the time, Pallas kernels for 13%

profile of v25, /device:TPU:0, one launch (start us, length us, event | category | flops | bytes accessed | tf_op | source)
XLA Modules:
  0.0 41.4 jit_solution(640681852525518784)
XLA Ops:
  0.6 0.0 copy-start.12
  0.6 0.0 copy-start.13
  0.7 0.0 copy-start.8
  0.7 0.0 copy-start.9
  0.7 1.1 %history.1 = bf16[80,128]{1,0:T(8,128)(2,1)S(1)} custom-call(f32[128,4096]{1,0:T(8,128)} %rec_hbm.1), custom_call_target="tpu_custom_call" | custom-call | flops 10000000000 | bytes 20000000 | tf_op jit(solution)/shard_map/history/pallas_call | solution.py:386
  1.8 0.0 copy-start
  1.8 0.0 copy-start.3
  1.8 0.0 copy-start.4
  1.8 2.5 %collective-permute-start = (bf16[80,128]{1,0:T(8,128)(2,1)S(1)}, bf16[80,128]{1,0:T(8,128)(2,1)S(1)}, u32[]{:S(2)}, u32[]{:S(2)}) collective-permute-start(bf16[80,128]{1,0:T(8,128)(2,1)S(1)} %history.1), channel_id=1, source_target_pairs={{0,1},{1,2},{2,3},{4,5},{5,6},{6,7},{8,9},{9,10},{10,11},{12,13},{... | collective-permute-start | bytes 61448 | tf_op jit(solution)/shard_map/ppermute | solution.py:398
  4.3 0.0 copy-done.12
  4.3 0.0 copy-done.13
  4.3 0.0 copy-done.8
  4.3 0.0 copy-done.9
  4.3 0.0 copy-start.10
  4.3 0.0 copy-start.11
  4.3 2.0 %filter_and_transform.1 = (f32[1024,128]{1,0:T(8,128)S(1)}, f32[8,128]{1,0:T(8,128)S(1)}, f32[16,128]{1,0:T(8,128)S(1)}) custom-call(f32[1,64]{1,0:T(1,128)S(1)} %bitcast.8, f32[128,4096]{1,0:T(8,128)S(1)} %copy-done.8, bf16[256,768]{1,0:T(8,128)(2,1)S(1)} %copy-done.12, f32[256,128]{1,0:T(8,128)S(1)} %copy-done.13), custom_call_target="tpu_custom_call" | custom-call | flops 1000000000 | bytes 5000000 | tf_op jit(solution)/shard_map/filter_and_transform/pallas_call | solution.py:400
  6.4 0.0 collective-permute-done.rim_ref
  6.4 0.0 copy-done
  6.4 0.0 copy-done.3
  6.4 0.0 copy-done.4
  6.4 1.4 %whiten.1 = (bf16[32,2,16,128]{3,2,1,0:T(8,128)(2,1)}, bf16[512,128]{1,0:T(8,128)(2,1)S(1)}, bf16[512,128]{1,0:T(8,128)(2,1)S(1)}) custom-call(f32[1024,128]{1,0:T(8,128)S(1)} %get-tuple-element.20.spec_ref, bf16[80,128]{1,0:T(8,128)(2,1)S(1)} %collective-permute-done.rim_ref, f32[8,128]{1,0:T(8,128)S(1)} %get-tuple-element.21.mean_ref, ...), custom_call_target="tpu_custom_call" | custom-call | tf_op jit(solution)/shard_map/whiten/pallas_call | solution.py:418
  7.8 2.3 %collective-permute-start.1 = (bf16[512,128]{1,0:T(8,128)(2,1)S(1)}, bf16[512,128]{1,0:T(8,128)(2,1)S(1)}, u32[]{:S(2)}, u32[]{:S(2)}) collective-permute-start(bf16[512,128]{1,0:T(8,128)(2,1)S(1)} %get-tuple-element.24), channel_id=1, source_target_pairs={{0,4},{4,8},{8,12},{12,16},{16,20},{20,24},{24,28},{28,0},{1,5},{5... | collective-permute-start | bytes 393224 | tf_op jit(solution)/shard_map/ppermute | solution.py:435
  10.2 3.0 %collective-permute-start.2 = (bf16[512,128]{1,0:T(8,128)(2,1)S(1)}, bf16[512,128]{1,0:T(8,128)(2,1)S(1)}, u32[]{:S(2)}, u32[]{:S(2)}) collective-permute-start(bf16[512,128]{1,0:T(8,128)(2,1)S(1)} %get-tuple-element.25), channel_id=1, source_target_pairs={{4,0},{8,4},{12,8},{16,12},{20,16},{24,20},{28,24},{0,28},{5,1},{9... | collective-permute-start | bytes 393224 | tf_op jit(solution)/shard_map/ppermute | solution.py:436
  13.2 4.6 %all-to-all-start = ((bf16[32,2,16,128]{3,2,1,0:T(8,128)(2,1)}), bf16[32,2,16,128]{3,2,1,0:T(8,128)(2,1)S(1)}, u32[]{:S(2)}, u32[]{:S(2)}) async-start(bf16[32,2,16,128]{3,2,1,0:T(8,128)(2,1)} %get-tuple-element.23.white_ref), calls=%async_computation | async-start | bytes 524288 | tf_op jit(solution)/shard_map/all_to_all | solution.py:431
  17.8 0.0 copy-start.1
  17.8 0.0 copy-start.5
  17.8 0.0 copy-start.6
  17.8 0.0 copy-start.7
  17.8 0.0 copy-start.2
  17.9 0.0 collective-permute-done.1.before_ref
  17.9 1.0 %collective-permute-done.2.after_ref = bf16[512,128]{1,0:T(8,128)(2,1)S(1)} collective-permute-done((bf16[512,128]{1,0:T(8,128)(2,1)S(1)}, bf16[512,128]{1,0:T(8,128)(2,1)S(1)}, u32[]{:S(2)}, u32[]{:S(2)}) %collective-permute-start.2) | collective-permute-done | bytes 131104 | tf_op jit(solution)/shard_map/ppermute | solution.py:436
  18.9 0.0 copy-done.10
  18.9 0.0 copy-done.11
  18.9 2.1 %near_lags.1 = (bf16[1,256,128]{2,1,0:T(8,128)(2,1)S(1)}, bf16[1,256,128]{2,1,0:T(8,128)(2,1)S(1)}, bf16[1,256,128]{2,1,0:T(8,128)(2,1)S(1)}, bf16[1,256,128]{2,1,0:T(8,128)(2,1)S(1)}) custom-call(s32[4]{0:T(128)S(1)} %copy-done.10, bf16[32,2,16,128]{3,2,1,0:T(8,128)(2,1)} %get-tuple-element.23.white_ref, ...), custom_call_target="tpu_custom_call" | custom-call | flops 20000000000 | bytes 20000000 | tf_op jit(solution)/shard_map/near_lags/pallas_call | solution.py:440
  21.0 0.4 collective-permute-start.3
  21.3 0.7 %collective-permute-start.4 = (bf16[1,256,128]{2,1,0:T(8,128)(2,1)S(1)}, bf16[1,256,128]{2,1,0:T(8,128)(2,1)S(1)}, u32[]{:S(2)}, u32[]{:S(2)}) collective-permute-start(bf16[1,256,128]{2,1,0:T(8,128)(2,1)S(1)} %get-tuple-element.29), channel_id=1, source_target_pairs={{0,2},{1,3},{2,0},{3,1},{4,6},{5,7},{6,4},{7,5},{8,10},{9,11},{10,... | collective-permute-start | bytes 196616 | tf_op jit(solution)/shard_map/ppermute | solution.py:455
  22.0 0.9 %collective-permute-start.5 = (bf16[1,256,128]{2,1,0:T(8,128)(2,1)S(1)}, bf16[1,256,128]{2,1,0:T(8,128)(2,1)S(1)}, u32[]{:S(2)}, u32[]{:S(2)}) collective-permute-start(bf16[1,256,128]{2,1,0:T(8,128)(2,1)S(1)} %get-tuple-element.30), channel_id=1, source_target_pairs={{0,3},{1,2},{2,1},{3,0},{4,7},{5,6},{6,5},{7,4},{8,11},{9,10},{10,... | collective-permute-start | bytes 196616 | tf_op jit(solution)/shard_map/ppermute | solution.py:455
  22.9 5.5 %all-to-all-done = bf16[32,2,16,128]{3,2,1,0:T(8,128)(2,1)S(1)} async-done(((bf16[32,2,16,128]{3,2,1,0:T(8,128)(2,1)}), bf16[32,2,16,128]{3,2,1,0:T(8,128)(2,1)S(1)}, u32[]{:S(2)}, u32[]{:S(2)}) %all-to-all-start) | async-done | bytes 262176 | tf_op jit(solution)/shard_map/all_to_all | solution.py:431
  28.4 0.0 copy-done.1
  28.4 0.0 copy-done.5
  28.4 0.0 copy-done.6
  28.5 0.0 copy-done.7
  28.5 1.2 %loop_spectra.1 = bf16[4,8,24,128]{3,2,1,0:T(8,128)(2,1)S(1)} custom-call(s32[3,8]{1,0:T(4,128)S(1)} %bitcast.7, s32[8]{0:T(128)S(1)} %copy-done.7, bf16[128,128]{1,0:T(8,128)(2,1)S(1)} %copy-done.5, bf16[512,512]{1,0:T(8,128)(2,1)S(1)} %copy-done.1, bf16[4,8,2,16,128]{4,3,2,1,0:T(8,128)(2,1)S(1)} %bitcast.5), custom_call_target="tpu_custom_call" | custom-call | tf_op jit(solution)/shard_map/loop_spectra/pallas_call | solution.py:476
  29.7 0.0 collective-permute-done.3.refs_1_
  29.7 0.0 collective-permute-done.4.refs_2_
  29.7 0.0 collective-permute-done.5.refs_3_
  29.7 10.7 %all_to_all.10.spec_ref = bf16[32,24,128]{2,1,0:T(8,128)(2,1)S(1)} all-to-all(bf16[32,24,128]{2,1,0:T(8,128)(2,1)S(1)} %bitcast.6), channel_id=1, replica_groups=mesh['chan'=8,'seg'=4] {'seg','chan'}, dimensions={0} | all-to-all | bytes 393216 | tf_op jit(solution)/shard_map/all_to_all | solution.py:486
  40.4 0.9 %lags.1 = (f32[128,1,256]{2,1,0:T(1,128)}, f32[96,256]{1,0:T(8,128)}) custom-call(bf16[32,24,128]{2,1,0:T(8,128)(2,1)S(1)} %all_to_all.10.spec_ref, bf16[1024,256]{1,0:T(8,128)(2,1)S(1)} %copy-done.2, bf16[1,256,128]{2,1,0:T(8,128)(2,1)S(1)} %get-tuple-element.32.refs_0_, bf16[1,256,128]{2,1,0:T(8,128)(2,1)S(1)} %collective-permute-done.3.refs_1_, ...), custom_call_target="tpu_custom_call" | custom-call | tf_op jit(solution)/shard_map/lags/pallas_call | solution.py:490
  (1 shorter events, 0.0 us)
Async XLA Ops:
  0.6 3.7 %copy-start.12 = (bf16[256,768]{1,0:T(8,128)(2,1)S(1)}, bf16[256,768]{1,0:T(8,128)(2,1)}, u32[]{:S(2)}) copy-start(bf16[256,768]{1,0:T(8,128)(2,1)} %constant.18.clone.tab_ref) | copy-start | bytes 1179652
  0.6 3.7 %copy-start.13 = (f32[256,128]{1,0:T(8,128)S(1)}, f32[256,128]{1,0:T(8,128)}, u32[]{:S(2)}) copy-start(f32[256,128]{1,0:T(8,128)} %constant.19.clone.twist_ref) | copy-start | bytes 393220
  0.7 3.7 %copy-start.8 = (f32[128,4096]{1,0:T(8,128)S(1)}, f32[128,4096]{1,0:T(8,128)}, u32[]{:S(2)}) copy-start(f32[128,4096]{1,0:T(8,128)} %rec_hbm.1) | copy-start | bytes 6291460
  0.7 3.7 %copy-start.9 = (f32[64]{0:T(128)S(1)}, f32[64]{0:T(128)}, u32[]{:S(2)}) copy-start(f32[64]{0:T(128)} %param.15) | copy-start | bytes 772
  1.8 4.6 %copy-start = (bf16[512,512]{1,0:T(8,128)(2,1)S(1)}, bf16[512,512]{1,0:T(8,128)(2,1)}, u32[]{:S(2)}) copy-start(bf16[512,512]{1,0:T(8,128)(2,1)} %constant.21.clone.band_ref) | copy-start | bytes 1572868
  1.8 4.6 %copy-start.3 = (f32[512,128]{1,0:T(8,128)S(1)}, f32[512,128]{1,0:T(8,128)}, u32[]{:S(2)}) copy-start(f32[512,128]{1,0:T(8,128)} %constant.22.clone.share_ref) | copy-start | bytes 786436
  1.8 4.6 %copy-start.4 = (bf16[1024,128]{1,0:T(8,128)(2,1)S(1)}, bf16[1024,128]{1,0:T(8,128)(2,1)}, u32[]{:S(2)}) copy-start(bf16[1024,128]{1,0:T(8,128)(2,1)} %constant.20.clone.edge_ref) | copy-start | bytes 786436
  1.8 4.6 %collective-permute-start = (bf16[80,128]{1,0:T(8,128)(2,1)S(1)}, bf16[80,128]{1,0:T(8,128)(2,1)S(1)}, u32[]{:S(2)}, u32[]{:S(2)}) collective-permute-start(bf16[80,128]{1,0:T(8,128)(2,1)S(1)} %history.1), channel_id=1, source_target_pairs={{0,1},{1,2},{2,3},{4,5},{5,6},{6,7},{8,9},{9,10},{10,11},{12,13},{... | collective-permute-start | bytes 61448 | tf_op jit(solution)/shard_map/ppermute | solution.py:398
  4.3 14.6 %copy-start.10 = (s32[4]{0:T(128)S(1)}, s32[4]{0:T(128)}, u32[]{:S(2)}) copy-start(s32[4]{0:T(128)} %offs_ref.1) | copy-start | bytes 52
  4.3 14.6 %copy-start.11 = (bf16[512,1024]{1,0:T(8,128)(2,1)S(1)}, bf16[512,1024]{1,0:T(8,128)(2,1)}, u32[]{:S(2)}) copy-start(bf16[512,1024]{1,0:T(8,128)(2,1)} %constant.23.clone.inv_ref) | copy-start | bytes 3145732
  7.8 10.0 %collective-permute-start.1 = (bf16[512,128]{1,0:T(8,128)(2,1)S(1)}, bf16[512,128]{1,0:T(8,128)(2,1)S(1)}, u32[]{:S(2)}, u32[]{:S(2)}) collective-permute-start(bf16[512,128]{1,0:T(8,128)(2,1)S(1)} %get-tuple-element.24), channel_id=1, source_target_pairs={{0,4},{4,8},{8,12},{12,16},{16,20},{20,24},{24,28},{28,0},{1,5},{5... | collective-permute-start | bytes 393224 | tf_op jit(solution)/shard_map/ppermute | solution.py:435
  10.2 8.7 %collective-permute-start.2 = (bf16[512,128]{1,0:T(8,128)(2,1)S(1)}, bf16[512,128]{1,0:T(8,128)(2,1)S(1)}, u32[]{:S(2)}, u32[]{:S(2)}) collective-permute-start(bf16[512,128]{1,0:T(8,128)(2,1)S(1)} %get-tuple-element.25), channel_id=1, source_target_pairs={{4,0},{8,4},{12,8},{16,12},{20,16},{24,20},{28,24},{0,28},{5,1},{9... | collective-permute-start | bytes 393224 | tf_op jit(solution)/shard_map/ppermute | solution.py:436
  13.2 15.2 %all-to-all-start = ((bf16[32,2,16,128]{3,2,1,0:T(8,128)(2,1)}), bf16[32,2,16,128]{3,2,1,0:T(8,128)(2,1)S(1)}, u32[]{:S(2)}, u32[]{:S(2)}) async-start(bf16[32,2,16,128]{3,2,1,0:T(8,128)(2,1)} %get-tuple-element.23.white_ref), calls=%async_computation | async-start | bytes 524288 | tf_op jit(solution)/shard_map/all_to_all | solution.py:431
  17.8 10.6 %copy-start.1 = (bf16[512,512]{1,0:T(8,128)(2,1)S(1)}, bf16[512,512]{1,0:T(8,128)(2,1)}, u32[]{:S(2)}) copy-start(bf16[512,512]{1,0:T(8,128)(2,1)} %constant.25.clone.pack_ref) | copy-start | bytes 1572868
  17.8 10.6 %copy-start.5 = (bf16[128,128]{1,0:T(8,128)(2,1)S(1)}, bf16[128,128]{1,0:T(8,128)(2,1)}, u32[]{:S(2)}) copy-start(bf16[128,128]{1,0:T(8,128)(2,1)} %constant.24.clone.flip_ref) | copy-start | bytes 98308
  17.8 10.6 %copy-start.6 = (s32[8,3]{0,1:T(4,128)S(1)}, s32[8,3]{0,1:T(4,128)}, u32[]{:S(2)}) copy-start(s32[8,3]{0,1:T(4,128)} %param.17) | copy-start | bytes 292
  17.8 10.6 %copy-start.7 = (s32[8]{0:T(128)S(1)}, s32[8]{0:T(128)}, u32[]{:S(2)}) copy-start(s32[8]{0:T(128)} %count_ref.1) | copy-start | bytes 100
  17.8 22.6 %copy-start.2 = (bf16[1024,256]{1,0:T(8,128)(2,1)S(1)}, bf16[1024,256]{1,0:T(8,128)(2,1)}, u32[]{:S(2)}) copy-start(bf16[1024,256]{1,0:T(8,128)(2,1)} %constant.26.clone.inv_ref) | copy-start | bytes 1572868
  21.0 8.7 %collective-permute-start.3 = (bf16[1,256,128]{2,1,0:T(8,128)(2,1)S(1)}, bf16[1,256,128]{2,1,0:T(8,128)(2,1)S(1)}, u32[]{:S(2)}, u32[]{:S(2)}) collective-permute-start(bf16[1,256,128]{2,1,0:T(8,128)(2,1)S(1)} %get-tuple-element.28), channel_id=1, source_target_pairs={{0,1},{1,0},{2,3},{3,2},{4,5},{5,4},{6,7},{7,6},{8,9},{9,8},{10,11... | collective-permute-start | bytes 196616 | tf_op jit(solution)/shard_map/ppermute | solution.py:455
  21.3 8.4 %collective-permute-start.4 = (bf16[1,256,128]{2,1,0:T(8,128)(2,1)S(1)}, bf16[1,256,128]{2,1,0:T(8,128)(2,1)S(1)}, u32[]{:S(2)}, u32[]{:S(2)}) collective-permute-start(bf16[1,256,128]{2,1,0:T(8,128)(2,1)S(1)} %get-tuple-element.29), channel_id=1, source_target_pairs={{0,2},{1,3},{2,0},{3,1},{4,6},{5,7},{6,4},{7,5},{8,10},{9,11},{10,... | collective-permute-start | bytes 196616 | tf_op jit(solution)/shard_map/ppermute | solution.py:455
  22.0 7.7 %collective-permute-start.5 = (bf16[1,256,128]{2,1,0:T(8,128)(2,1)S(1)}, bf16[1,256,128]{2,1,0:T(8,128)(2,1)S(1)}, u32[]{:S(2)}, u32[]{:S(2)}) collective-permute-start(bf16[1,256,128]{2,1,0:T(8,128)(2,1)S(1)} %get-tuple-element.30), channel_id=1, source_target_pairs={{0,3},{1,2},{2,1},{3,0},{4,7},{5,6},{6,5},{7,4},{8,11},{9,10},{10,... | collective-permute-start | bytes 196616 | tf_op jit(solution)/shard_map/ppermute | solution.py:455

commit v26 on v20

--- a/solution.py
+++ b/solution.py
@@ -332,8 +332,7 @@
         turned = loop[:, k * step : (k + 1) * step].reshape(sources * step, LANES).T
         groups = [turned[g * share : (g + 1) * share] for g in range(LANES // share)]
         rows.append(jnp.concatenate(groups, axis=1))
-    both = mm(jnp.concatenate(rows, axis=0).astype(BF16), inv_ref[...])
-    loop_ref[...] = both[:, :LAGS] + both[:, LAGS:]
+    loop_ref[...] = mm(jnp.concatenate(rows, axis=0).astype(BF16), inv_ref[...])
 
 
 def last_kernel(slots, spec_ref, inv_ref, *refs):
@@ -494,7 +493,7 @@
     summed = lax.all_to_all(crossed, ("seg", "chan"), 0, 0, tiled=True)
     columns = np.arange(2 * BINS).reshape(devices, seg_count, -1).swapaxes(0, 1).reshape(-1)
     loop_inverse = inverse_table(seg_count, order[columns], part[columns]).T
-    loop_inverse = np.concatenate(split_np(loop_inverse), axis=1)
+    loop_inverse = loop_inverse.astype(jnp.bfloat16)
     near, loop = pl.pallas_call(
         functools.partial(last_kernel, slots),
         out_shape=[near_shape, jax.ShapeDtypeStruct((slots * share, LAGS), F32)],

time: 41.9 us -> 41.8 us (level)
  no operation moved by 1% of the time
where the time goes in v26:
time: 41.8 us; the launch traced here: 41.5 us
  starting transfers between devices  14.8 us (35%)
  blocking collectives  10.7 us (26%)
  Pallas kernels  8.72 us (21%)
  waiting for transfers between devices  6.29 us (15%)
  between operations  0.89 us (2%)
    all_to_all x1, blocking collectives, body(): summed = lax.all_to_all(crossed, ('seg', 'chan'), 0, 0, tiled=True)  10.7 us
    all_to_all x1, waiting for transfers between devices, body(): moved = lax.all_to_all(spread, ('seg', 'chan'), 0, 0, tiled=True)  5.52 us
    all_to_all x1, starting transfers between devices, body(): moved = lax.all_to_all(spread, ('seg', 'chan'), 0, 0, tiled=True)  4.24 us
    ppermute x1, starting transfers between devices, body(): second = lax.ppermute(second, 'chan', routes[1])  3.54 us
    ppermute x1, starting transfers between devices, body(): rim = lax.ppermute(rim, 'seg', route)  2.49 us
    ppermute x1, starting transfers between devices, body(): first = lax.ppermute(first, 'chan', routes[0])  2.35 us
    ppermute x3, starting transfers between devices, body(): lags[r] = lax.ppermute(lags[r], 'seg', route)  2.21 us
    pallas_call x1, Pallas kernels, body(): pl.pallas_call(near_kernel, out_shape=[jax.ShapeDtypeStruct((near_each, L...  2.07 us
  transfers between devices with their start and end apart: 7, of which 2 were waited for; matrix products, arithmetic and copies ran while one was open for 0% of the time, Pallas kernels for 13%

profile of v26, /device:TPU:0, one launch (start us, length us, event | category | flops | bytes accessed | tf_op | source)
XLA Modules:
  0.0 41.5 jit_solution(3633300343861847137)
XLA Ops:
  0.6 0.0 copy-start.12
  0.6 0.0 copy-start.13
  0.7 0.0 copy-start.8
  0.7 0.0 copy-start.9
  0.7 1.1 %history.1 = f32[64,128]{1,0:T(8,128)S(1)} custom-call(f32[128,4096]{1,0:T(8,128)} %rec_hbm.1), custom_call_target="tpu_custom_call" | custom-call | flops 10000000000 | bytes 20000000 | tf_op jit(solution)/shard_map/history/pallas_call | solution.py:393
  1.8 0.0 copy-start
  1.8 0.0 copy-start.3
  1.8 0.0 copy-start.4
  1.8 2.5 %collective-permute-start = (f32[64,128]{1,0:T(8,128)S(1)}, f32[64,128]{1,0:T(8,128)S(1)}, u32[]{:S(2)}, u32[]{:S(2)}) collective-permute-start(f32[64,128]{1,0:T(8,128)S(1)} %history.1), channel_id=1, source_target_pairs={{0,1},{1,2},{2,3},{4,5},{5,6},{6,7},{8,9},{9,10},{10,11},{12,13},{... | collective-permute-start | bytes 98312 | tf_op jit(solution)/shard_map/ppermute | solution.py:405
  4.3 0.0 copy-done.12
  4.3 0.0 copy-done.13
  4.3 0.0 copy-done.8
  4.3 0.0 copy-done.9
  4.4 0.0 copy-start.10
  4.4 0.0 copy-start.11
  4.4 2.0 %filter_and_transform.1 = (f32[1024,128]{1,0:T(8,128)S(1)}, f32[8,128]{1,0:T(8,128)S(1)}, f32[16,128]{1,0:T(8,128)S(1)}) custom-call(f32[1,64]{1,0:T(1,128)S(1)} %bitcast.8, f32[128,4096]{1,0:T(8,128)S(1)} %copy-done.8, bf16[256,768]{1,0:T(8,128)(2,1)S(1)} %copy-done.12, f32[256,128]{1,0:T(8,128)S(1)} %copy-done.13), custom_call_target="tpu_custom_call" | custom-call | flops 1000000000 | bytes 5000000 | tf_op jit(solution)/shard_map/filter_and_transform/pallas_call | solution.py:407
  6.3 0.0 collective-permute-done.rim_ref
  6.4 0.0 copy-done
  6.4 0.0 copy-done.3
  6.4 0.0 copy-done.4
  6.4 1.4 %whiten.1 = (bf16[32,2,16,128]{3,2,1,0:T(8,128)(2,1)}, bf16[512,128]{1,0:T(8,128)(2,1)S(1)}, bf16[512,128]{1,0:T(8,128)(2,1)S(1)}) custom-call(f32[1024,128]{1,0:T(8,128)S(1)} %get-tuple-element.20.spec_ref, f32[64,128]{1,0:T(8,128)S(1)} %collective-permute-done.rim_ref, f32[8,128]{1,0:T(8,128)S(1)} %get-tuple-element.21.mean_ref, ...), custom_call_target="tpu_custom_call" | custom-call | tf_op jit(solution)/shard_map/whiten/pallas_call | solution.py:425
  7.8 2.4 %collective-permute-start.1 = (bf16[512,128]{1,0:T(8,128)(2,1)S(1)}, bf16[512,128]{1,0:T(8,128)(2,1)S(1)}, u32[]{:S(2)}, u32[]{:S(2)}) collective-permute-start(bf16[512,128]{1,0:T(8,128)(2,1)S(1)} %get-tuple-element.24), channel_id=1, source_target_pairs={{0,4},{4,0},{8,12},{12,8},{16,20},{20,16},{24,28},{28,24},{1,5},{5... | collective-permute-start | bytes 393224 | tf_op jit(solution)/shard_map/ppermute | solution.py:442
  10.2 3.5 %collective-permute-start.2 = (bf16[512,128]{1,0:T(8,128)(2,1)S(1)}, bf16[512,128]{1,0:T(8,128)(2,1)S(1)}, u32[]{:S(2)}, u32[]{:S(2)}) collective-permute-start(bf16[512,128]{1,0:T(8,128)(2,1)S(1)} %get-tuple-element.25), channel_id=1, source_target_pairs={{0,28},{4,8},{8,4},{12,16},{16,12},{20,24},{24,20},{28,0},{1,29},{... | collective-permute-start | bytes 393224 | tf_op jit(solution)/shard_map/ppermute | solution.py:443
  13.7 4.2 %all-to-all-start = ((bf16[32,2,16,128]{3,2,1,0:T(8,128)(2,1)}), bf16[32,2,16,128]{3,2,1,0:T(8,128)(2,1)S(1)}, u32[]{:S(2)}, u32[]{:S(2)}) async-start(bf16[32,2,16,128]{3,2,1,0:T(8,128)(2,1)} %get-tuple-element.23.white_ref), calls=%async_computation | async-start | bytes 524288 | tf_op jit(solution)/shard_map/all_to_all | solution.py:438
  18.0 0.0 copy-start.1
  18.0 0.0 copy-start.5
  18.0 0.0 copy-start.6
  18.0 0.0 copy-start.7
  18.0 0.0 copy-start.2
  18.0 0.0 collective-permute-done.1.first_ref
  18.0 0.8 %collective-permute-done.2.second_ref = bf16[512,128]{1,0:T(8,128)(2,1)S(1)} collective-permute-done((bf16[512,128]{1,0:T(8,128)(2,1)S(1)}, bf16[512,128]{1,0:T(8,128)(2,1)S(1)}, u32[]{:S(2)}, u32[]{:S(2)}) %collective-permute-start.2) | collective-permute-done | bytes 131104 | tf_op jit(solution)/shard_map/ppermute | solution.py:443
  18.8 0.0 copy-done.10
  18.8 0.0 copy-done.11
  18.8 2.1 %near_lags.1 = (bf16[1,256,128]{2,1,0:T(8,128)(2,1)S(1)}, bf16[1,256,128]{2,1,0:T(8,128)(2,1)S(1)}, bf16[1,256,128]{2,1,0:T(8,128)(2,1)S(1)}, bf16[1,256,128]{2,1,0:T(8,128)(2,1)S(1)}) custom-call(s32[4]{0:T(128)S(1)} %copy-done.10, bf16[32,2,16,128]{3,2,1,0:T(8,128)(2,1)} %get-tuple-element.23.white_ref, ...), custom_call_target="tpu_custom_call" | custom-call | flops 20000000000 | bytes 20000000 | tf_op jit(solution)/shard_map/near_lags/pallas_call | solution.py:447
  20.9 0.4 collective-permute-start.3
  21.2 1.8 %collective-permute-start.4 = (bf16[1,256,128]{2,1,0:T(8,128)(2,1)S(1)}, bf16[1,256,128]{2,1,0:T(8,128)(2,1)S(1)}, u32[]{:S(2)}, u32[]{:S(2)}) collective-permute-start(bf16[1,256,128]{2,1,0:T(8,128)(2,1)S(1)} %get-tuple-element.29), channel_id=1, source_target_pairs={{0,2},{1,3},{2,0},{3,1},{4,6},{5,7},{6,4},{7,5},{8,10},{9,11},{10,... | collective-permute-start | bytes 196616 | tf_op jit(solution)/shard_map/ppermute | solution.py:462
  23.0 0.1 collective-permute-start.5
  23.1 5.5 %all-to-all-done = bf16[32,2,16,128]{3,2,1,0:T(8,128)(2,1)S(1)} async-done(((bf16[32,2,16,128]{3,2,1,0:T(8,128)(2,1)}), bf16[32,2,16,128]{3,2,1,0:T(8,128)(2,1)S(1)}, u32[]{:S(2)}, u32[]{:S(2)}) %all-to-all-start) | async-done | bytes 262176 | tf_op jit(solution)/shard_map/all_to_all | solution.py:438
  28.6 0.0 copy-done.1
  28.6 0.0 copy-done.5
  28.6 0.0 copy-done.6
  28.6 0.0 copy-done.7
  28.6 1.2 %loop_spectra.1 = bf16[4,8,24,128]{3,2,1,0:T(8,128)(2,1)S(1)} custom-call(s32[3,8]{1,0:T(4,128)S(1)} %bitcast.7, s32[8]{0:T(128)S(1)} %copy-done.7, bf16[128,128]{1,0:T(8,128)(2,1)S(1)} %copy-done.5, bf16[512,512]{1,0:T(8,128)(2,1)S(1)} %copy-done.1, bf16[4,8,2,16,128]{4,3,2,1,0:T(8,128)(2,1)S(1)} %bitcast.5), custom_call_target="tpu_custom_call" | custom-call | tf_op jit(solution)/shard_map/loop_spectra/pallas_call | solution.py:483
  29.9 0.0 collective-permute-done.3.refs_1_
  29.9 0.0 collective-permute-done.4.refs_2_
  29.9 0.0 collective-permute-done.5.refs_3_
  29.9 10.7 %all_to_all.10.spec_ref = bf16[32,24,128]{2,1,0:T(8,128)(2,1)S(1)} all-to-all(bf16[32,24,128]{2,1,0:T(8,128)(2,1)S(1)} %bitcast.6), channel_id=1, replica_groups=mesh['chan'=8,'seg'=4] {'seg','chan'}, dimensions={0} | all-to-all | bytes 393216 | tf_op jit(solution)/shard_map/all_to_all | solution.py:493
  40.6 0.9 %lags.1 = (f32[128,1,256]{2,1,0:T(1,128)}, f32[96,256]{1,0:T(8,128)}) custom-call(bf16[32,24,128]{2,1,0:T(8,128)(2,1)S(1)} %all_to_all.10.spec_ref, bf16[1024,256]{1,0:T(8,128)(2,1)S(1)} %copy-done.2, bf16[1,256,128]{2,1,0:T(8,128)(2,1)S(1)} %get-tuple-element.32.refs_0_, bf16[1,256,128]{2,1,0:T(8,128)(2,1)S(1)} %collective-permute-done.3.refs_1_, ...), custom_call_target="tpu_custom_call" | custom-call | tf_op jit(solution)/shard_map/lags/pallas_call | solution.py:497
  (1 shorter events, 0.0 us)
Async XLA Ops:
  0.6 3.7 %copy-start.12 = (bf16[256,768]{1,0:T(8,128)(2,1)S(1)}, bf16[256,768]{1,0:T(8,128)(2,1)}, u32[]{:S(2)}) copy-start(bf16[256,768]{1,0:T(8,128)(2,1)} %constant.18.clone.tab_ref) | copy-start | bytes 1179652
  0.6 3.7 %copy-start.13 = (f32[256,128]{1,0:T(8,128)S(1)}, f32[256,128]{1,0:T(8,128)}, u32[]{:S(2)}) copy-start(f32[256,128]{1,0:T(8,128)} %constant.19.clone.twist_ref) | copy-start | bytes 393220
  0.7 3.7 %copy-start.8 = (f32[128,4096]{1,0:T(8,128)S(1)}, f32[128,4096]{1,0:T(8,128)}, u32[]{:S(2)}) copy-start(f32[128,4096]{1,0:T(8,128)} %rec_hbm.1) | copy-start | bytes 6291460
  0.7 3.7 %copy-start.9 = (f32[64]{0:T(128)S(1)}, f32[64]{0:T(128)}, u32[]{:S(2)}) copy-start(f32[64]{0:T(128)} %param.15) | copy-start | bytes 772
  1.8 4.6 %copy-start = (bf16[512,512]{1,0:T(8,128)(2,1)S(1)}, bf16[512,512]{1,0:T(8,128)(2,1)}, u32[]{:S(2)}) copy-start(bf16[512,512]{1,0:T(8,128)(2,1)} %constant.21.clone.band_ref) | copy-start | bytes 1572868
  1.8 4.6 %copy-start.3 = (f32[512,128]{1,0:T(8,128)S(1)}, f32[512,128]{1,0:T(8,128)}, u32[]{:S(2)}) copy-start(f32[512,128]{1,0:T(8,128)} %constant.22.clone.share_ref) | copy-start | bytes 786436
  1.8 4.6 %copy-start.4 = (bf16[1024,128]{1,0:T(8,128)(2,1)S(1)}, bf16[1024,128]{1,0:T(8,128)(2,1)}, u32[]{:S(2)}) copy-start(bf16[1024,128]{1,0:T(8,128)(2,1)} %constant.20.clone.edge_ref) | copy-start | bytes 786436
  1.8 4.5 %collective-permute-start = (f32[64,128]{1,0:T(8,128)S(1)}, f32[64,128]{1,0:T(8,128)S(1)}, u32[]{:S(2)}, u32[]{:S(2)}) collective-permute-start(f32[64,128]{1,0:T(8,128)S(1)} %history.1), channel_id=1, source_target_pairs={{0,1},{1,2},{2,3},{4,5},{5,6},{6,7},{8,9},{9,10},{10,11},{12,13},{... | collective-permute-start | bytes 98312 | tf_op jit(solution)/shard_map/ppermute | solution.py:405
  4.4 14.4 %copy-start.10 = (s32[4]{0:T(128)S(1)}, s32[4]{0:T(128)}, u32[]{:S(2)}) copy-start(s32[4]{0:T(128)} %offs_ref.1) | copy-start | bytes 52
  4.4 14.4 %copy-start.11 = (bf16[512,1024]{1,0:T(8,128)(2,1)S(1)}, bf16[512,1024]{1,0:T(8,128)(2,1)}, u32[]{:S(2)}) copy-start(bf16[512,1024]{1,0:T(8,128)(2,1)} %constant.23.clone.inv_ref) | copy-start | bytes 3145732
  7.8 10.2 %collective-permute-start.1 = (bf16[512,128]{1,0:T(8,128)(2,1)S(1)}, bf16[512,128]{1,0:T(8,128)(2,1)S(1)}, u32[]{:S(2)}, u32[]{:S(2)}) collective-permute-start(bf16[512,128]{1,0:T(8,128)(2,1)S(1)} %get-tuple-element.24), channel_id=1, source_target_pairs={{0,4},{4,0},{8,12},{12,8},{16,20},{20,16},{24,28},{28,24},{1,5},{5... | collective-permute-start | bytes 393224 | tf_op jit(solution)/shard_map/ppermute | solution.py:442
  10.2 8.6 %collective-permute-start.2 = (bf16[512,128]{1,0:T(8,128)(2,1)S(1)}, bf16[512,128]{1,0:T(8,128)(2,1)S(1)}, u32[]{:S(2)}, u32[]{:S(2)}) collective-permute-start(bf16[512,128]{1,0:T(8,128)(2,1)S(1)} %get-tuple-element.25), channel_id=1, source_target_pairs={{0,28},{4,8},{8,4},{12,16},{16,12},{20,24},{24,20},{28,0},{1,29},{... | collective-permute-start | bytes 393224 | tf_op jit(solution)/shard_map/ppermute | solution.py:443
  13.7 14.9 %all-to-all-start = ((bf16[32,2,16,128]{3,2,1,0:T(8,128)(2,1)}), bf16[32,2,16,128]{3,2,1,0:T(8,128)(2,1)S(1)}, u32[]{:S(2)}, u32[]{:S(2)}) async-start(bf16[32,2,16,128]{3,2,1,0:T(8,128)(2,1)} %get-tuple-element.23.white_ref), calls=%async_computation | async-start | bytes 524288 | tf_op jit(solution)/shard_map/all_to_all | solution.py:438
  18.0 10.6 %copy-start.1 = (bf16[512,512]{1,0:T(8,128)(2,1)S(1)}, bf16[512,512]{1,0:T(8,128)(2,1)}, u32[]{:S(2)}) copy-start(bf16[512,512]{1,0:T(8,128)(2,1)} %constant.25.clone.pack_ref) | copy-start | bytes 1572868
  18.0 10.6 %copy-start.5 = (bf16[128,128]{1,0:T(8,128)(2,1)S(1)}, bf16[128,128]{1,0:T(8,128)(2,1)}, u32[]{:S(2)}) copy-start(bf16[128,128]{1,0:T(8,128)(2,1)} %constant.24.clone.flip_ref) | copy-start | bytes 98308
  18.0 10.6 %copy-start.6 = (s32[8,3]{0,1:T(4,128)S(1)}, s32[8,3]{0,1:T(4,128)}, u32[]{:S(2)}) copy-start(s32[8,3]{0,1:T(4,128)} %param.17) | copy-start | bytes 292
  18.0 10.6 %copy-start.7 = (s32[8]{0:T(128)S(1)}, s32[8]{0:T(128)}, u32[]{:S(2)}) copy-start(s32[8]{0:T(128)} %count_ref.1) | copy-start | bytes 100
  18.0 22.6 %copy-start.2 = (bf16[1024,256]{1,0:T(8,128)(2,1)S(1)}, bf16[1024,256]{1,0:T(8,128)(2,1)}, u32[]{:S(2)}) copy-start(bf16[1024,256]{1,0:T(8,128)(2,1)} %constant.26.clone.inv_ref) | copy-start | bytes 1572868
  20.9 9.0 %collective-permute-start.3 = (bf16[1,256,128]{2,1,0:T(8,128)(2,1)S(1)}, bf16[1,256,128]{2,1,0:T(8,128)(2,1)S(1)}, u32[]{:S(2)}, u32[]{:S(2)}) collective-permute-start(bf16[1,256,128]{2,1,0:T(8,128)(2,1)S(1)} %get-tuple-element.28), channel_id=1, source_target_pairs={{0,1},{1,0},{2,3},{3,2},{4,5},{5,4},{6,7},{7,6},{8,9},{9,8},{10,11... | collective-permute-start | bytes 196616 | tf_op jit(solution)/shard_map/ppermute | solution.py:462
  21.2 8.7 %collective-permute-start.4 = (bf16[1,256,128]{2,1,0:T(8,128)(2,1)S(1)}, bf16[1,256,128]{2,1,0:T(8,128)(2,1)S(1)}, u32[]{:S(2)}, u32[]{:S(2)}) collective-permute-start(bf16[1,256,128]{2,1,0:T(8,128)(2,1)S(1)} %get-tuple-element.29), channel_id=1, source_target_pairs={{0,2},{1,3},{2,0},{3,1},{4,6},{5,7},{6,4},{7,5},{8,10},{9,11},{10,... | collective-permute-start | bytes 196616 | tf_op jit(solution)/shard_map/ppermute | solution.py:462
  23.0 6.9 %collective-permute-start.5 = (bf16[1,256,128]{2,1,0:T(8,128)(2,1)S(1)}, bf16[1,256,128]{2,1,0:T(8,128)(2,1)S(1)}, u32[]{:S(2)}, u32[]{:S(2)}) collective-permute-start(bf16[1,256,128]{2,1,0:T(8,128)(2,1)S(1)} %get-tuple-element.30), channel_id=1, source_target_pairs={{0,3},{1,2},{2,1},{3,0},{4,7},{5,6},{6,5},{7,4},{8,11},{9,10},{10,... | collective-permute-start | bytes 196616 | tf_op jit(solution)/shard_map/ppermute | solution.py:462
